TPU v7x, 32 devices: a whole 2x2x4 slice. The times are simulated.
32 devices in a mesh: rows: 8 (over y, x, core), batch: 4 (over z).
Axes of the slice: x: 2, y: 2, z: 4, core: 2. Of those that a mesh axis runs over, the one named last changes fastest.
Arguments:
- section_four: bfloat16 [8, 64, 128, 1024], P('batch', 'rows'), may hold values from -6 to 6
- section_five: bfloat16 [8, 32, 64, 2048], P('batch', 'rows'), may hold values from -6 to 6
- target_four: float32 [8, 64, 128, 12], P('batch', 'rows'), may hold values from -6 to 6
- target_five: float32 [8, 32, 64, 12], P('batch', 'rows'), may hold values from -6 to 6
- target_six: float32 [8, 16, 32, 12], P('batch', 'rows'), may hold values from -6 to 6
- anchor_four: int32 [8, 64, 128, 3], P('batch', 'rows'), may hold values from 0 to 1, as said below
- anchor_five: int32 [8, 32, 64, 3], P('batch', 'rows'), may hold values from 0 to 1, as said below
- anchor_six: int32 [8, 16, 32, 3], P('batch', 'rows'), may hold values from 0 to 1, as said below
- lateral_four: float32 [1024, 256], P(('rows', 'batch')), may hold values from -0.1875 to 0.1875
- lateral_five: float32 [2048, 256], P(('rows', 'batch')), may hold values from -0.125 to 0.125
- output_conv: float32 [2, 2304, 256], P(None, ('rows', 'batch')), may hold values from -0.125 to 0.125
- delta_head: float32 [2304, 12], P(('rows', 'batch')), may hold values from -0.125 to 0.125
- mean_four: float32 [1024, 256], P(('rows', 'batch')), may hold values from -0.00390625 to 0.00390625
- mean_five: float32 [2048, 256], P(('rows', 'batch')), may hold values from -0.00390625 to 0.00390625
- mean_conv: float32 [2, 2304, 256], P(None, ('rows', 'batch')), may hold values from -0.00390625 to 0.00390625
- mean_head: float32 [2304, 12], P(('rows', 'batch')), may hold values from -0.02734375 to 0.02734375
- square_four: float32 [1024, 256], P(('rows', 'batch')), may hold values from 7.6293944e-08 to 3.0517577e-07
- square_five: float32 [2048, 256], P(('rows', 'batch')), may hold values from 7.6293944e-08 to 3.0517577e-07
- square_conv: float32 [2, 2304, 256], P(None, ('rows', 'batch')), may hold values from 7.6293944e-08 to 3.0517577e-07
- square_head: float32 [2304, 12], P(('rows', 'batch')), may hold values from 3.0517579e-06 to 1.2207031e-05
Outputs:
- loss_sum: float32 [], replicated
- positives: float32 [], replicated
- first_four: float32 [1024, 256], P(('rows', 'batch'))
- first_five: float32 [2048, 256], P(('rows', 'batch'))
- first_conv: float32 [2, 2304, 256], P(None, ('rows', 'batch'))
- first_head: float32 [2304, 12], P(('rows', 'batch'))
- second_four: float32 [1024, 256], P(('rows', 'batch'))
- second_five: float32 [2048, 256], P(('rows', 'batch'))
- second_conv: float32 [2, 2304, 256], P(None, ('rows', 'batch'))
- second_head: float32 [2304, 12], P(('rows', 'batch'))
- weight_four: float32 [1024, 256], P(('rows', 'batch'))
- weight_five: float32 [2048, 256], P(('rows', 'batch'))
- weight_conv: float32 [2, 2304, 256], P(None, ('rows', 'batch'))
- weight_head: float32 [2304, 12], P(('rows', 'batch'))
Inputs may be any that keep to these rules, and one draw needn't show every extreme that they name: `anchor_four`: 1 marks a positive anchor. `anchor_five`: 1 marks a positive anchor. `anchor_six`: 1 marks a positive anchor.
All inputs are finite; a program needn't handle non-finite values.
Results may differ from a plain program's by a relative error of at most 0.012.
The roundings to bfloat16 on the way count: a program that leaves them out, or rounds other values in their place, can miss the bound.
Values may be sent and summed in bfloat16 or wider, within the bound.
No kernel may reach another device: no remote copies, remote signals or barrier semaphores. Data moves between devices by JAX's collectives and lax.ppermute only.
A program may use at most 128 MiB of HBM per device.

v0:
```python
import jax
import jax.numpy as jnp
from jax import lax
from jax.sharding import PartitionSpec as P

STEP = 5


box_beta = 1.0 / 9.0
beta_one = 0.5
beta_two = 0.5
learn_rate = 0.02
weight_decay = 0.01
epsilon = 1e-08


def with_halo(value, sides, width):
    for axis, dim in sides:
        count, length = (lax.axis_size(axis), value.shape[dim])
        up = [(i, (i + 1) % count) for i in range(count - 1)]
        down = [(j, i) for i, j in up]
        last = lax.slice_in_dim(value, length - width, length, axis=dim)
        first = lax.slice_in_dim(value, 0, width, axis=dim)
        before = lax.ppermute(last, axis, up)
        after = lax.ppermute(first, axis, down)
        value = jnp.concatenate([before, value, after], axis=dim)
    return value


def widened(field):
    return jnp.pad(field, ((0, 0), (0, 0), (1, 1), (0, 0)))


def conv_taps(padded, kernel):
    height = padded.shape[1] - 2
    extent = padded.shape[2]
    channels = padded.shape[3]
    spread = widened(padded)
    summed = jnp.zeros((padded.shape[0], height, extent, kernel.shape[1]), jnp.float32)
    for offset in range(9):
        row_step, col_step = divmod(offset, 3)
        window = spread[:, row_step : row_step + height, col_step : col_step + extent]
        summed = summed + jnp.dot(
            window,
            kernel[offset * channels : (offset + 1) * channels],
            preferred_element_type=jnp.float32,
        )
    return summed


def conv_back(padded_grad, kernel):
    height = padded_grad.shape[1] - 2
    extent = padded_grad.shape[2]
    channels = kernel.shape[0] // 9
    spread = widened(padded_grad)
    summed = jnp.zeros((padded_grad.shape[0], height, extent, channels), jnp.float32)
    for offset in range(9):
        row_step, col_step = divmod(offset, 3)
        window = spread[
            :, 2 - row_step : 2 - row_step + height, 2 - col_step : 2 - col_step + extent
        ]
        summed = summed + jnp.dot(
            window,
            kernel[offset * channels : (offset + 1) * channels].T,
            preferred_element_type=jnp.float32,
        )
    return summed


def weight_grad(padded, gradient):
    height = gradient.shape[1]
    extent = gradient.shape[2]
    spread = widened(padded)
    pieces = []
    for offset in range(9):
        row_step, col_step = divmod(offset, 3)
        window = spread[:, row_step : row_step + height, col_step : col_step + extent]
        pieces.append(
            jnp.einsum("bhwc,bhwo->co", window, gradient, preferred_element_type=jnp.float32)
        )
    return jnp.concatenate(pieces, axis=0)


def rim_forward(field):
    return with_halo(field, (("rows", 1),), 1)


def rim_backward(field):
    return with_halo(field, (("rows", 1),), 1)


def spread_up(field):
    return jnp.repeat(jnp.repeat(field, 2, axis=1), 2, axis=2)


def pooled(field):
    count_b, height, extent, channels = field.shape
    return jnp.mean(field.reshape(count_b, height // 2, 2, extent // 2, 2, channels), axis=(2, 4))


def folded(field):
    count_b, height, extent, channels = field.shape
    return jnp.sum(field.reshape(count_b, height // 2, 2, extent // 2, 2, channels), axis=(2, 4))


def smooth_box(mismatch):
    magnitude = jnp.abs(mismatch)
    return jnp.where(
        magnitude < box_beta, 0.5 * mismatch * mismatch / box_beta, magnitude - 0.5 * box_beta
    )


def adamw_update(weight, gradient, mean, square):
    first = beta_one * mean + (1.0 - beta_one) * gradient
    second = beta_two * square + (1.0 - beta_two) * gradient * gradient
    corrected_first = first / (1.0 - beta_one**STEP)
    corrected_second = second / (1.0 - beta_two**STEP)
    return (
        first,
        second,
        weight
        - learn_rate
        * (corrected_first / (jnp.sqrt(corrected_second) + epsilon) + weight_decay * weight),
    )


def on_device(
    section_four,
    section_five,
    target_four,
    target_five,
    target_six,
    anchor_four,
    anchor_five,
    anchor_six,
    lateral_four,
    lateral_five,
    output_conv,
    delta_head,
    mean_four,
    mean_five,
    mean_conv,
    mean_head,
    square_four,
    square_five,
    square_conv,
    square_head,
):
    full_four, full_five, full_conv, full_head = (
        lax.all_gather(lateral_four.astype(jnp.bfloat16), ("rows", "batch"), axis=0, tiled=True),
        lax.all_gather(lateral_five.astype(jnp.bfloat16), ("rows", "batch"), axis=0, tiled=True),
        lax.all_gather(output_conv.astype(jnp.bfloat16), ("rows", "batch"), axis=1, tiled=True),
        lax.all_gather(delta_head.astype(jnp.bfloat16), ("rows", "batch"), axis=0, tiled=True),
    )
    lat_five = jnp.dot(section_five, full_five, preferred_element_type=jnp.float32)
    merged = jnp.dot(section_four, full_four, preferred_element_type=jnp.float32) + spread_up(
        lat_five
    )
    input_four = rim_forward(merged.astype(jnp.bfloat16))
    input_five = rim_forward(lat_five.astype(jnp.bfloat16))
    level_four = conv_taps(input_four, full_conv[0])
    level_five = conv_taps(input_five, full_conv[1])
    level_six = pooled(level_five)
    head_inputs = [
        rim_forward(level.astype(jnp.bfloat16)) for level in (level_four, level_five, level_six)
    ]
    anchors = [anchor.astype(jnp.float32) for anchor in (anchor_four, anchor_five, anchor_six)]
    masks = [jnp.repeat(anchor, 4, axis=3) for anchor in anchors]
    mismatches = [
        conv_taps(head_in, full_head) - target
        for head_in, target in zip(head_inputs, (target_four, target_five, target_six))
    ]
    local_loss = sum(
        (jnp.sum(mask * smooth_box(mismatch)) for mask, mismatch in zip(masks, mismatches))
    )
    local_count = sum((jnp.sum(anchor) for anchor in anchors))
    positives, loss_sum = lax.psum((local_count, local_loss), ("rows", "batch"))
    inverse = 1.0 / jnp.maximum(positives, 1.0)
    delta_grads = [
        (mask * jnp.clip(mismatch / box_beta, -1.0, 1.0) * inverse).astype(jnp.bfloat16)
        for mask, mismatch in zip(masks, mismatches)
    ]
    head_grad = jnp.zeros(full_head.shape, jnp.float32)
    for head_in, delta_grad in zip(head_inputs, delta_grads):
        head_grad = head_grad + weight_grad(head_in, delta_grad)
    delta_padded = [rim_backward(delta_grad) for delta_grad in delta_grads]
    level_backs = [conv_back(padded, full_head) for padded in delta_padded]
    grad_four = level_backs[0].astype(jnp.bfloat16)
    grad_five = (level_backs[1] + 0.25 * spread_up(level_backs[2])).astype(jnp.bfloat16)
    conv_grad = jnp.stack([weight_grad(input_four, grad_four), weight_grad(input_five, grad_five)])
    padded_four = rim_backward(grad_four)
    padded_five = rim_backward(grad_five)
    back_merged = conv_back(padded_four, full_conv[0])
    back_five = conv_back(padded_five, full_conv[1])
    grad_lat_four = back_merged.astype(jnp.bfloat16)
    grad_lat_five = (back_five + folded(back_merged)).astype(jnp.bfloat16)
    four_grad = jnp.einsum(
        "bhwc,bhwo->co", section_four, grad_lat_four, preferred_element_type=jnp.float32
    )
    five_grad = jnp.einsum(
        "bhwc,bhwo->co", section_five, grad_lat_five, preferred_element_type=jnp.float32
    )
    four_part, five_part, conv_part, head_part = (
        lax.psum_scatter(four_grad, ("rows", "batch"), scatter_dimension=0, tiled=True),
        lax.psum_scatter(five_grad, ("rows", "batch"), scatter_dimension=0, tiled=True),
        lax.psum_scatter(conv_grad, ("rows", "batch"), scatter_dimension=1, tiled=True),
        lax.psum_scatter(head_grad, ("rows", "batch"), scatter_dimension=0, tiled=True),
    )
    first_four, second_four, weight_four = adamw_update(
        lateral_four, four_part, mean_four, square_four
    )
    first_five, second_five, weight_five = adamw_update(
        lateral_five, five_part, mean_five, square_five
    )
    first_conv, second_conv, weight_conv = adamw_update(
        output_conv, conv_part, mean_conv, square_conv
    )
    first_head, second_head, weight_head = adamw_update(
        delta_head, head_part, mean_head, square_head
    )
    return (
        loss_sum,
        positives,
        first_four,
        first_five,
        first_conv,
        first_head,
        second_four,
        second_five,
        second_conv,
        second_head,
        weight_four,
        weight_five,
        weight_conv,
        weight_head,
    )


def solution(mesh):
    return jax.shard_map(
        on_device,
        mesh=mesh,
        in_specs=(
            P("batch", "rows", None, None),
            P("batch", "rows", None, None),
            P("batch", "rows", None, None),
            P("batch", "rows", None, None),
            P("batch", "rows", None, None),
            P("batch", "rows", None, None),
            P("batch", "rows", None, None),
            P("batch", "rows", None, None),
            P(("rows", "batch"), None),
            P(("rows", "batch"), None),
            P(None, ("rows", "batch"), None),
            P(("rows", "batch"), None),
            P(("rows", "batch"), None),
            P(("rows", "batch"), None),
            P(None, ("rows", "batch"), None),
            P(("rows", "batch"), None),
            P(("rows", "batch"), None),
            P(("rows", "batch"), None),
            P(None, ("rows", "batch"), None),
            P(("rows", "batch"), None),
        ),
        out_specs=(
            P(),
            P(),
            P(("rows", "batch"), None),
            P(("rows", "batch"), None),
            P(None, ("rows", "batch"), None),
            P(("rows", "batch"), None),
            P(("rows", "batch"), None),
            P(("rows", "batch"), None),
            P(None, ("rows", "batch"), None),
            P(("rows", "batch"), None),
            P(("rows", "batch"), None),
            P(("rows", "batch"), None),
            P(None, ("rows", "batch"), None),
            P(("rows", "batch"), None),
        ),
        check_vma=False,
    )
```

profile of v0, /device:TPU:0, one launch (start us, length us, event | category | flops | bytes accessed | tf_op | source)
XLA Modules:
  0.0 824.5 jit_solution(10135135274103917104)
XLA Ops:
  7.2 1.6 convert_element_type.80
  8.9 1.6 convert_element_type.82
  11.3 1.3 convert_reduce_fusion
  12.6 1.3 convert_reduce_fusion.1
  13.9 1.3 convert_reduce_fusion.2
  16.0 74.2 %all_gather.12 = bf16[1024,256]{1,0:T(8,128)(2,1)S(1)} all-gather(bf16[32,256]{1,0:T(8,128)(2,1)S(1)} %convert_element_type.79), channel_id=1, replica_groups=mesh['rows'=8,'batch'=4] {'rows','batch'}, dimensions={0}, use_global_device_ids=true | all-gather | bytes 540672 | tf_op jit(solution)/shard_map/all_gather | solution.py:150
  90.2 1.9 fusion.349
  92.2 1.3 collective-permute-start.4
  94.9 2.1 broadcast_in_dim.23
  97.0 3.6 reshape.75
  100.6 4.1 add_convert_fusion.2
  105.8 3.1 collective-permute-start
  108.8 1.3 collective-permute-start.1
  110.1 66.4 %all-gather = bf16[32,72,12]{1,2,0:T(8,128)(2,1)S(1)} all-gather(bf16[1,72,12]{1,2,0:T(8,128)(2,1)S(1)} %convert_bitcast_fusion), channel_id=1, replica_groups=mesh['rows'=8,'batch'=4] {'rows','batch'}, dimensions={0}, use_global_device_ids=true | all-gather | bytes 57024 | tf_op jit(solution)/shard_map/all_gather | solution.py:153
  182.8 1.8 fusion.5
  184.7 1.7 fusion.189
  194.7 2.0 fusion.350
  196.7 2.2 reshape.78
  198.9 2.1 reduce_sum.74
  205.4 3.0 collective-permute-start.6
  208.4 1.3 collective-permute-start.7
  209.7 1.3 fusion.122
  211.1 1.3 fusion.125
  212.4 1.4 fusion.128
  213.8 1.3 fusion.131
  215.1 1.4 fusion.119
  216.6 1.3 fusion.135
  217.9 1.4 fusion.134
  219.3 1.3 fusion.209
  220.7 2.0 add_convert_fusion.1
  222.8 3.2 collective-permute-start.2
  226.4 1.5 collective-permute-start.3
  232.9 2.0 collective-permute-done.3
  241.5 48.7 %all-reduce.11 = (f32[]{:T(128)}, f32[]{:T(128)}) all-reduce(f32[]{:T(128)S(6)} %add.404, f32[]{:T(128)S(6)} %add.406), channel_id=1, replica_groups=mesh['rows'=8,'batch'=4] {'rows','batch'}, use_global_device_ids=true, to_apply=%region_4.5 | all-reduce | flops 2 | bytes 16 | tf_op jit(solution)/shard_map/psum | solution.py:177
  291.0 1.5 fusion.79
  293.1 1.8 fusion.333
  302.7 3.0 collective-permute-start.16
  307.8 4.4 collective-permute-start.10
  312.2 1.3 collective-permute-start.15
  313.5 4.3 collective-permute-start.14
  325.8 4.5 collective-permute-start.18
  337.1 4.3 collective-permute-start.12
  348.9 1.3 copy-done.8
  350.9 2.3 convolution_bitcast_fusion.1
  353.2 2.6 copy.243
  356.1 1.3 fusion.144
  357.5 1.3 convolution_add_fusion.14
  363.5 2.0 convolution_add_fusion.9
  365.4 3.4 reshape.79
  368.9 3.9 reduce_sum.79
  372.8 4.0 convolution_bitcast_fusion
  376.8 2.9 copy.245
  379.8 2.0 fusion.26
  381.8 2.0 fusion.25
  390.3 1.4 fusion.30
  393.3 2.5 pad_maximum_fusion
  396.0 32.1 %all-reduce.14.cloned.1.call-done = f32[2304,12]{0,1:T(8,128)} async-done(((f32[2304,12]{0,1:T(8,128)}), f32[2304,12]{0,1:T(8,128)}) %all-reduce.14.cloned.1.call-update) | async-done | bytes 110608
  428.1 1.4 multiply_subtract_fusion.3
  429.5 138.0 %reduce-scatter.11.cloned.1.call-done = f32[32,256]{1,0:T(8,128)} async-done(((f32[1024,256]{1,0:T(8,128)}), f32[32,256]{1,0:T(8,128)}) %reduce-scatter.11.cloned.1.call-update) | async-done | bytes 32784 | tf_op jit(solution)/shard_map/reduce_scatter | solution.py:204
  567.5 1.4 multiply_subtract_fusion.2
  568.9 136.2 %reduce-scatter.13.cloned.1.call-done = f32[64,256]{1,0:T(8,128)} async-done(((f32[2048,256]{1,0:T(8,128)}), f32[64,256]{1,0:T(8,128)}) %reduce-scatter.13.cloned.1.call-update) | async-done | bytes 65552 | tf_op jit(solution)/shard_map/reduce_scatter | solution.py:205
  705.1 1.5 multiply_subtract_fusion.1
  706.6 108.9 %reduce-scatter.9.cloned.1.call-done = f32[2,72,256]{2,1,0:T(8,128)} async-done(((f32[2,2304,256]{2,1,0:T(8,128)}), f32[2,72,256]{2,1,0:T(8,128)}) %reduce-scatter.9.cloned.1.call-update) | async-done | bytes 147472 | tf_op jit(solution)/shard_map/reduce_scatter | solution.py:206
  815.5 1.7 multiply_subtract_fusion
  (343 shorter events, 77.0 us)
Async XLA Ops:
  7.2 83.0 %copy-start = (bf16[2,4,64,2048]{3,2,1,0:T(8,128)(2,1)S(1)}, bf16[2,4,64,2048]{3,2,1,0:T(8,128)(2,1)}, u32[]{:S(2)}) copy-start(bf16[2,4,64,2048]{3,2,1,0:T(8,128)(2,1)} %param.21) | copy-start | bytes 6291460
  7.2 83.0 %all-gather.4.cloned.1.call-start = ((), (), s32[]{:S(2)}) async-start(), calls=%async_computation.3 | async-start | bytes 1081344 | tf_op jit(solution)/shard_map/all_gather | solution.py:151
  8.9 175.8 %all-gather.6.cloned.1.call-start = ((), (), s32[]{:S(2)}) async-start(), calls=%async_computation.4 | async-start | bytes 2433024 | tf_op jit(solution)/shard_map/all_gather | solution.py:152
  10.5 417.6 %all-reduce.14.cloned.1.call-start = ((), (), s32[]{:S(2)}) async-start(), calls=%async_computation.8 | async-start | bytes 294912
  92.1 89.1 %copy-start.15 = (bf16[2,4,64,256]{3,2,1,0:T(8,128)(2,1)}, bf16[2,4,64,256]{3,2,1,0:T(8,128)(2,1)S(1)}, u32[]{:S(2)}) copy-start(bf16[2,4,64,256]{3,2,1,0:T(8,128)(2,1)S(1)} %get-tuple-element.92) | copy-start | bytes 786436
  92.2 89.0 %collective-permute-start.4 = (bf16[2,1,64,256]{3,2,1,0:T(8,128)(2,1)S(1)}, bf16[2,1,64,256]{3,2,1,0:T(8,128)(2,1)S(1)}, u32[]{:S(2)}, u32[]{:S(2)}) collective-permute-start(bf16[2,1,64,256]{3,2,1,0:T(8,128)(2,1)S(1)} %get-tuple-element.80), channel_id=1, source_target_pairs={{0,4},{4,8},{8,12},{12,16},{16,20},{20,24},{24,28},{1,5},{5,9},{9,... | collective-permute-start | bytes 196616 | tf_op jit(solution)/shard_map/ppermute | solution.py:24
  93.5 87.7 %collective-permute-start.5 = (bf16[2,1,64,256]{3,2,1,0:T(8,128)(2,1)S(1)}, bf16[2,1,64,256]{3,2,1,0:T(8,128)(2,1)S(1)}, u32[]{:S(2)}, u32[]{:S(2)}) collective-permute-start(bf16[2,1,64,256]{3,2,1,0:T(8,128)(2,1)S(1)} %get-tuple-element.81), channel_id=1, source_target_pairs={{4,0},{8,4},{12,8},{16,12},{20,16},{24,20},{28,24},{5,1},{9,5},{13... | collective-permute-start | bytes 196616 | tf_op jit(solution)/shard_map/ppermute | solution.py:25
  100.6 76.0 %copy-start.69 = (s32[2,2,32,3]{2,1,3,0:T(2,128)S(1)}, s32[2,2,32,3]{2,1,3,0:T(2,128)}, u32[]{:S(2)}) copy-start(s32[2,2,32,3]{2,1,3,0:T(2,128)} %param.27) | copy-start | bytes 4612
  100.6 76.6 %copy-start.61 = (s32[2,4,64,3]{2,1,3,0:T(4,128)S(1)}, s32[2,4,64,3]{2,1,3,0:T(4,128)}, u32[]{:S(2)}) copy-start(s32[2,4,64,3]{2,1,3,0:T(4,128)} %param.26) | copy-start | bytes 18436
  100.6 77.2 %copy-start.50 = (s32[2,8,128,3]{2,1,3,0:T(8,128)S(1)}, s32[2,8,128,3]{2,1,3,0:T(8,128)}, u32[]{:S(2)}) copy-start(s32[2,8,128,3]{2,1,3,0:T(8,128)} %param.25) | copy-start | bytes 73732
  105.8 76.4 %collective-permute-start = (bf16[2,1,128,256]{3,2,1,0:T(8,128)(2,1)S(1)}, bf16[2,1,128,256]{3,2,1,0:T(8,128)(2,1)S(1)}, u32[]{:S(2)}, u32[]{:S(2)}) collective-permute-start(bf16[2,1,128,256]{3,2,1,0:T(8,128)(2,1)S(1)} %get-tuple-element.74), channel_id=1, source_target_pairs={{0,4},{4,8},{8,12},{12,16},{16,20},{20,24},{24,28},{1,5},{5,9},{9,... | collective-permute-start | bytes 393224 | tf_op jit(solution)/shard_map/ppermute | solution.py:24
  108.8 74.0 %collective-permute-start.1 = (bf16[2,1,128,256]{3,2,1,0:T(8,128)(2,1)S(1)}, bf16[2,1,128,256]{3,2,1,0:T(8,128)(2,1)}, u32[]{:S(2)}, u32[]{:S(2)}) collective-permute-start(bf16[2,1,128,256]{3,2,1,0:T(8,128)(2,1)S(1)} %get-tuple-element.75), channel_id=1, source_target_pairs={{4,0},{8,4},{12,8},{16,12},{20,16},{24,20},{28,24},{5,1},{9,5},{13... | collective-permute-start | bytes 393224 | tf_op jit(solution)/shard_map/ppermute | solution.py:25
  181.2 13.5 %copy-start.36 = (bf16[2,1,64,256]{3,2,1,0:T(8,128)(2,1)}, bf16[2,1,64,256]{3,2,1,0:T(8,128)(2,1)S(1)}, u32[]{:S(2)}) copy-start(bf16[2,1,64,256]{3,2,1,0:T(8,128)(2,1)S(1)} %collective-permute-done.5) | copy-start | bytes 196612
  184.7 36.0 %copy-start.1 = (bf16[2,10,130,256]{3,2,1,0:T(8,128)(2,1)}, bf16[2,10,130,256]{3,2,1,0:T(8,128)(2,1)S(1)}, u32[]{:S(2)}) copy-start(bf16[2,10,130,256]{3,2,1,0:T(8,128)(2,1)S(1)} %fusion.5) | copy-start | bytes 3993604
  184.7 4.3 copy-start.9
  201.9 24.5 %collective-permute-start.8 = (bf16[2,1,32,256]{3,2,1,0:T(8,128)(2,1)S(1)}, bf16[2,1,32,256]{3,2,1,0:T(8,128)(2,1)S(1)}, u32[]{:S(2)}, u32[]{:S(2)}) collective-permute-start(bf16[2,1,32,256]{3,2,1,0:T(8,128)(2,1)S(1)} %get-tuple-element.84), channel_id=1, source_target_pairs={{0,4},{4,8},{8,12},{12,16},{16,20},{20,24},{24,28},{1,5},{5,9},{9,... | collective-permute-start | bytes 98312 | tf_op jit(solution)/shard_map/ppermute | solution.py:24
  203.2 24.6 %collective-permute-start.9 = (bf16[2,1,32,256]{3,2,1,0:T(8,128)(2,1)S(1)}, bf16[2,1,32,256]{3,2,1,0:T(8,128)(2,1)S(1)}, u32[]{:S(2)}, u32[]{:S(2)}) collective-permute-start(bf16[2,1,32,256]{3,2,1,0:T(8,128)(2,1)S(1)} %get-tuple-element.85), channel_id=1, source_target_pairs={{4,0},{8,4},{12,8},{16,12},{20,16},{24,20},{28,24},{5,1},{9,5},{13... | collective-permute-start | bytes 98312 | tf_op jit(solution)/shard_map/ppermute | solution.py:25
  205.4 24.7 %collective-permute-start.6 = (bf16[2,1,64,256]{3,2,1,0:T(8,128)(2,1)S(1)}, bf16[2,1,64,256]{3,2,1,0:T(8,128)(2,1)S(1)}, u32[]{:S(2)}, u32[]{:S(2)}) collective-permute-start(bf16[2,1,64,256]{3,2,1,0:T(8,128)(2,1)S(1)} %get-tuple-element.78), channel_id=1, source_target_pairs={{0,4},{4,8},{8,12},{12,16},{16,20},{20,24},{24,28},{1,5},{5,9},{9,... | collective-permute-start | bytes 196616 | tf_op jit(solution)/shard_map/ppermute | solution.py:24
  208.4 21.6 %collective-permute-start.7 = (bf16[2,1,64,256]{3,2,1,0:T(8,128)(2,1)S(1)}, bf16[2,1,64,256]{3,2,1,0:T(8,128)(2,1)S(1)}, u32[]{:S(2)}, u32[]{:S(2)}) collective-permute-start(bf16[2,1,64,256]{3,2,1,0:T(8,128)(2,1)S(1)} %get-tuple-element.79), channel_id=1, source_target_pairs={{4,0},{8,4},{12,8},{16,12},{20,16},{24,20},{28,24},{5,1},{9,5},{13... | collective-permute-start | bytes 196616 | tf_op jit(solution)/shard_map/ppermute | solution.py:25
  220.7 5.3 copy-start.28
  222.7 15.3 %copy-start.6 = (bf16[2,8,128,256]{3,2,1,0:T(8,128)(2,1)}, bf16[2,8,128,256]{3,2,1,0:T(8,128)(2,1)S(1)}, u32[]{:S(2)}) copy-start(bf16[2,8,128,256]{3,2,1,0:T(8,128)(2,1)S(1)} %add_convert_fusion.1) | copy-start | bytes 3145732
  222.7 6.5 copy-start.63
  222.7 6.7 copy-start.70
  222.8 7.3 copy-start.19
  222.8 10.1 %collective-permute-start.2 = (bf16[2,1,128,256]{3,2,1,0:T(8,128)(2,1)S(1)}, bf16[2,1,128,256]{3,2,1,0:T(8,128)(2,1)S(1)}, u32[]{:S(2)}, u32[]{:S(2)}) collective-permute-start(bf16[2,1,128,256]{3,2,1,0:T(8,128)(2,1)S(1)} %get-tuple-element.72), channel_id=1, source_target_pairs={{0,4},{4,8},{8,12},{12,16},{16,20},{20,24},{24,28},{1,5},{5,9},{9,... | collective-permute-start | bytes 393224 | tf_op jit(solution)/shard_map/ppermute | solution.py:24
  226.4 4.5 copy-start.66
  226.4 8.6 %collective-permute-start.3 = (bf16[2,1,128,256]{3,2,1,0:T(8,128)(2,1)S(1)}, bf16[2,1,128,256]{3,2,1,0:T(8,128)(2,1)S(1)}, u32[]{:S(2)}, u32[]{:S(2)}) collective-permute-start(bf16[2,1,128,256]{3,2,1,0:T(8,128)(2,1)S(1)} %get-tuple-element.73), channel_id=1, source_target_pairs={{4,0},{8,4},{12,8},{16,12},{20,16},{24,20},{28,24},{5,1},{9,5},{13... | collective-permute-start | bytes 393224 | tf_op jit(solution)/shard_map/ppermute | solution.py:25
  232.9 4.3 copy-start.48
  238.5 54.6 %copy-start.29 = (bf16[2304,12]{0,1:T(8,128)(2,1)S(1)}, bf16[2304,12]{0,1:T(8,128)(2,1)}, u32[]{:S(2)}) copy-start(bf16[2304,12]{0,1:T(8,128)(2,1)} %reshape.81) | copy-start | bytes 165892
  290.9 15.5 %copy-start.30 = (bf16[2,4,64,12]{2,3,1,0:T(8,128)(2,1)}, bf16[2,4,64,12]{2,3,1,0:T(8,128)(2,1)S(1)}, u32[]{:S(2)}) copy-start(bf16[2,4,64,12]{2,3,1,0:T(8,128)(2,1)S(1)} %fusion.221) | copy-start | bytes 36868
  291.0 4.3 copy-start.58
  301.4 12.1 %collective-permute-start.17 = (bf16[2,1,32,12]{2,3,1,0:T(8,128)(2,1)S(1)}, bf16[2,1,32,12]{2,3,1,0:T(8,128)(2,1)S(1)}, u32[]{:S(2)}, u32[]{:S(2)}) collective-permute-start(bf16[2,1,32,12]{2,3,1,0:T(8,128)(2,1)S(1)} %get-tuple-element.89), channel_id=1, source_target_pairs={{4,0},{8,4},{12,8},{16,12},{20,16},{24,20},{28,24},{5,1},{9,5},{13... | collective-permute-start | bytes 4616 | tf_op jit(solution)/shard_map/ppermute | solution.py:25
  302.7 15.1 %collective-permute-start.16 = (bf16[2,1,32,12]{2,3,1,0:T(8,128)(2,1)S(1)}, bf16[2,1,32,12]{2,3,1,0:T(8,128)(2,1)S(1)}, u32[]{:S(2)}, u32[]{:S(2)}) collective-permute-start(bf16[2,1,32,12]{2,3,1,0:T(8,128)(2,1)S(1)} %get-tuple-element.88), channel_id=1, source_target_pairs={{0,4},{4,8},{8,12},{12,16},{16,20},{20,24},{24,28},{1,5},{5,9},{9,... | collective-permute-start | bytes 4616 | tf_op jit(solution)/shard_map/ppermute | solution.py:24
  306.4 261.1 %reduce-scatter.11.cloned.1.call-start = ((), (), s32[]{:S(2)}) async-start(), calls=%async_computation.6 | async-start | bytes 1081344 | tf_op jit(solution)/shard_map/reduce_scatter | solution.py:204
  306.5 23.8 %collective-permute-start.11 = (bf16[2,1,128,12]{2,3,1,0:T(8,128)(2,1)}, bf16[2,1,128,12]{2,3,1,0:T(8,128)(2,1)S(1)}, u32[]{:S(2)}, u32[]{:S(2)}) collective-permute-start(bf16[2,1,128,12]{2,3,1,0:T(8,128)(2,1)} %get-tuple-element.82), channel_id=1, source_target_pairs={{4,0},{8,4},{12,8},{16,12},{20,16},{24,20},{28,24},{5,1},{9,5},{13... | collective-permute-start | bytes 18440 | tf_op jit(solution)/shard_map/ppermute | solution.py:25
  307.8 22.6 %collective-permute-start.10 = (bf16[2,1,128,12]{2,3,1,0:T(8,128)(2,1)}, bf16[2,1,128,12]{2,3,1,0:T(8,128)(2,1)S(1)}, u32[]{:S(2)}, u32[]{:S(2)}) collective-permute-start(bf16[2,1,128,12]{2,3,1,0:T(8,128)(2,1)} %get-tuple-element.83), channel_id=1, source_target_pairs={{0,4},{4,8},{8,12},{12,16},{16,20},{20,24},{24,28},{1,5},{5,9},{9,... | collective-permute-start | bytes 18440 | tf_op jit(solution)/shard_map/ppermute | solution.py:24
  312.2 8.3 %collective-permute-start.15 = (bf16[2,1,64,12]{2,3,1,0:T(8,128)(2,1)S(1)}, bf16[2,1,64,12]{2,3,1,0:T(8,128)(2,1)S(1)}, u32[]{:S(2)}, u32[]{:S(2)}) collective-permute-start(bf16[2,1,64,12]{2,3,1,0:T(8,128)(2,1)S(1)} %get-tuple-element.87), channel_id=1, source_target_pairs={{4,0},{8,4},{12,8},{16,12},{20,16},{24,20},{28,24},{5,1},{9,5},{13... | collective-permute-start | bytes 9224 | tf_op jit(solution)/shard_map/ppermute | solution.py:25
  313.5 7.0 collective-permute-start.14
  323.3 18.6 %copy-start.20 = (bf16[2,4,64,256]{3,2,1,0:T(8,128)(2,1)}, bf16[2,4,64,256]{3,2,1,0:T(8,128)(2,1)S(1)}, u32[]{:S(2)}) copy-start(bf16[2,4,64,256]{3,2,1,0:T(8,128)(2,1)S(1)} %fusion.12) | copy-start | bytes 786436
  324.5 5.8 copy-start.26
  324.5 17.4 %collective-permute-start.19 = (bf16[2,1,64,256]{3,2,1,0:T(8,128)(2,1)S(1)}, bf16[2,1,64,256]{3,2,1,0:T(8,128)(2,1)S(1)}, u32[]{:S(2)}, u32[]{:S(2)}) collective-permute-start(bf16[2,1,64,256]{3,2,1,0:T(8,128)(2,1)S(1)} %get-tuple-element.77), channel_id=1, source_target_pairs={{4,0},{8,4},{12,8},{16,12},{20,16},{24,20},{28,24},{5,1},{9,5},{13... | collective-permute-start | bytes 196616 | tf_op jit(solution)/shard_map/ppermute | solution.py:25
  325.8 16.1 %collective-permute-start.18 = (bf16[2,1,64,256]{3,2,1,0:T(8,128)(2,1)S(1)}, bf16[2,1,64,256]{3,2,1,0:T(8,128)(2,1)S(1)}, u32[]{:S(2)}, u32[]{:S(2)}) collective-permute-start(bf16[2,1,64,256]{3,2,1,0:T(8,128)(2,1)S(1)} %get-tuple-element.76), channel_id=1, source_target_pairs={{0,4},{4,8},{8,12},{12,16},{16,20},{20,24},{24,28},{1,5},{5,9},{9,... | collective-permute-start | bytes 196616 | tf_op jit(solution)/shard_map/ppermute | solution.py:24
  334.9 6.5 copy-start.18
  335.8 8.1 collective-permute-start.13
  337.1 7.2 collective-permute-start.12
  355.8 349.2 %reduce-scatter.13.cloned.1.call-start = ((), (), s32[]{:S(2)}) async-start(), calls=%async_computation.7 | async-start | bytes 2162688 | tf_op jit(solution)/shard_map/reduce_scatter | solution.py:205
  357.5 3.7 copy-start.21
  368.9 3.9 copy-start.60
  379.7 5.1 copy-start.37
  379.8 435.7 %reduce-scatter.9.cloned.1.call-start = ((), (), s32[]{:S(2)}) async-start(), calls=%async_computation.5 | async-start | bytes 4866048 | tf_op jit(solution)/shard_map/reduce_scatter | solution.py:206
  379.8 4.1 copy-start.11
  379.8 4.1 copy-start.22
  395.8 32.2 %copy-start.68 = (f32[72,12]{0,1:T(8,128)S(1)}, f32[72,12]{0,1:T(8,128)}, u32[]{:S(2)}) copy-start(f32[72,12]{0,1:T(8,128)} %param.31) | copy-start | bytes 10372
  395.8 32.2 %copy-start.71 = (f32[72,12]{0,1:T(8,128)S(1)}, f32[72,12]{0,1:T(8,128)}, u32[]{:S(2)}) copy-start(f32[72,12]{0,1:T(8,128)} %param.39) | copy-start | bytes 10372
  395.8 32.2 %copy-start.72 = (f32[72,12]{0,1:T(8,128)S(1)}, f32[72,12]{0,1:T(8,128)}, u32[]{:S(2)}) copy-start(f32[72,12]{0,1:T(8,128)} %param.35) | copy-start | bytes 10372
  395.8 171.6 %copy-start.43 = (f32[32,256]{1,0:T(8,128)S(1)}, f32[32,256]{1,0:T(8,128)}, u32[]{:S(2)}) copy-start(f32[32,256]{1,0:T(8,128)} %param.28) | copy-start | bytes 98308
  395.8 171.6 %copy-start.64 = (f32[32,256]{1,0:T(8,128)S(1)}, f32[32,256]{1,0:T(8,128)}, u32[]{:S(2)}) copy-start(f32[32,256]{1,0:T(8,128)} %param.36) | copy-start | bytes 98308
  395.9 171.6 %copy-start.65 = (f32[32,256]{1,0:T(8,128)S(1)}, f32[32,256]{1,0:T(8,128)}, u32[]{:S(2)}) copy-start(f32[32,256]{1,0:T(8,128)} %param.32) | copy-start | bytes 98308
  395.9 309.2 %copy-start.38 = (f32[64,256]{1,0:T(8,128)S(1)}, f32[64,256]{1,0:T(8,128)}, u32[]{:S(2)}) copy-start(f32[64,256]{1,0:T(8,128)} %param.29) | copy-start | bytes 196612
  395.9 309.2 %copy-start.53 = (f32[64,256]{1,0:T(8,128)S(1)}, f32[64,256]{1,0:T(8,128)}, u32[]{:S(2)}) copy-start(f32[64,256]{1,0:T(8,128)} %param.37) | copy-start | bytes 196612
  395.9 309.2 %copy-start.54 = (f32[64,256]{1,0:T(8,128)S(1)}, f32[64,256]{1,0:T(8,128)}, u32[]{:S(2)}) copy-start(f32[64,256]{1,0:T(8,128)} %param.33) | copy-start | bytes 196612
  395.9 419.6 %copy-start.32 = (f32[2,72,256]{2,1,0:T(8,128)S(1)}, f32[2,72,256]{2,1,0:T(8,128)}, u32[]{:S(2)}) copy-start(f32[2,72,256]{2,1,0:T(8,128)} %param.30) | copy-start | bytes 442372
  395.9 419.5 %copy-start.41 = (f32[2,72,256]{2,1,0:T(8,128)S(1)}, f32[2,72,256]{2,1,0:T(8,128)}, u32[]{:S(2)}) copy-start(f32[2,72,256]{2,1,0:T(8,128)} %param.38) | copy-start | bytes 442372
  395.9 419.5 %copy-start.42 = (f32[2,72,256]{2,1,0:T(8,128)S(1)}, f32[2,72,256]{2,1,0:T(8,128)}, u32[]{:S(2)}) copy-start(f32[2,72,256]{2,1,0:T(8,128)} %param.34) | copy-start | bytes 442372
  (36 other events, 60.7 us)
Sparse Core Ops, SparseCore 0:
  11.6 56.7 all-gather.3
  72.0 57.2 all-gather.5
  306.5 121.4 all-reduce.13
  430.2 137.2 reduce-scatter.10
  569.7 135.3 reduce-scatter.12
  710.4 105.0 reduce-scatter.8
where the time goes:
time: 835 us; the launch traced here: 824 us
  waiting for transfers between devices  417 us (50%)
  blocking collectives  189 us (23%)
  matrix products  90.8 us (11%)
  starting transfers between devices  45.9 us (5%)
  other arithmetic  33.3 us (4%)
  local copies, waits for them, and re-layouts  27.2 us (3%)
  between operations  20.7 us (2%)
    reduce_scatter x1, waiting for transfers between devices, on_device(): lax.psum_scatter(four_grad, ('rows', 'batch'), scatter_dimension=0, tiled...  138 us
    reduce_scatter x1, waiting for transfers between devices, on_device(): lax.psum_scatter(five_grad, ('rows', 'batch'), scatter_dimension=0, tiled...  136 us
    reduce_scatter x1, waiting for transfers between devices, on_device(): lax.psum_scatter(conv_grad, ('rows', 'batch'), scatter_dimension=1, tiled...  109 us
    all_gather x1, blocking collectives, on_device(): lax.all_gather(lateral_four.astype(jnp.bfloat16), ('rows', 'batch'), axis...  74.2 us
    all_gather x1, blocking collectives, on_device(): lax.all_gather(delta_head.astype(jnp.bfloat16), ('rows', 'batch'), axis=0...  66.4 us
    psum x1, blocking collectives, on_device(): positives, loss_sum = lax.psum((local_count, local_loss), ('rows', 'batch'))  48.7 us
    ppermute x10, starting transfers between devices, with_halo(): before = lax.ppermute(last, axis, up)  32.3 us
    unnamed x7, waiting for transfers between devices  32.2 us
  transfers between devices with their start and end apart: 26, of which 5 were waited for; matrix products, arithmetic and copies ran while one was open for 13% of the time, Pallas kernels for 0%

commit v1 on v0

v1 whole, which is shorter than its diff:
```python
import functools

import jax
import jax.numpy as jnp
from jax import lax
from jax.experimental import pallas as pl
from jax.experimental.pallas import tpu as pltpu
from jax.sharding import PartitionSpec as P

STEP = 5

LANES = 128
DELTA_ROWS = 16
VMEM_BYTES = 56 * 1024 * 1024

box_beta = 1.0 / 9.0
beta_one = 0.5
beta_two = 0.5
learn_rate = 0.02
weight_decay = 0.01
epsilon = 1e-08

bf16 = jnp.bfloat16
f32 = jnp.float32


def adamw_update(weight, gradient, mean, square):
    first = beta_one * mean + (1.0 - beta_one) * gradient
    second = beta_two * square + (1.0 - beta_two) * gradient * gradient
    corrected_first = first / (1.0 - beta_one**STEP)
    corrected_second = second / (1.0 - beta_two**STEP)
    return (
        first,
        second,
        weight
        - learn_rate
        * (corrected_first / (jnp.sqrt(corrected_second) + epsilon) + weight_decay * weight),
    )


def sent(value, axis, mask):
    count = lax.axis_size(axis)
    return lax.ppermute(value, axis, [(i, i ^ mask) for i in range(count)])


def gathered_batch(piece):
    count, me = lax.axis_size("batch"), lax.axis_index("batch")
    stacked = jnp.stack([piece] + [sent(piece, "batch", k) for k in range(1, count)])
    return [lax.dynamic_index_in_dim(stacked, t ^ me, 0, keepdims=False) for t in range(count)]


def row_groups():
    count = lax.axis_size("rows")
    low = max(count // 4, 1)
    return count, low, count // low


def gathered_high(piece):
    _, low, high = row_groups()
    return [piece] + [sent(piece, "rows", j * low) for j in range(1, high)]


def gathered_low(held):
    count, low, high = row_groups()
    result = [None] * count
    for j in range(high):
        result[j * low] = held[j]
        for k in range(1, low):
            result[j * low + k] = sent(held[j], "rows", k)
    return result


def summed_low(blocks):
    _, low, high = row_groups()
    came = [sent(blocks[k], "rows", k) for k in range(1, low)]
    return [
        sum((c[j].astype(f32) for c in came), blocks[0][j].astype(f32)) for j in range(high)
    ]


def summed_high(partial):
    _, low, high = row_groups()
    return sum(
        (sent(partial[j].astype(bf16), "rows", j * low).astype(f32) for j in range(1, high)),
        partial[0],
    )


def summed_batch(blocks):
    count, me = lax.axis_size("batch"), lax.axis_index("batch")
    total = lax.dynamic_index_in_dim(blocks, me, 0, keepdims=False)
    for k in range(1, count):
        block = lax.dynamic_index_in_dim(blocks, me ^ k, 0, keepdims=False).astype(bf16)
        total = total + sent(block, "batch", k).astype(f32)
    return total


def from_neighbours(first, last):
    count = lax.axis_size("rows")
    above = lax.ppermute(last, "rows", [(i, i + 1) for i in range(count - 1)])
    below = lax.ppermute(first, "rows", [(i + 1, i) for i in range(count - 1)])
    return above, below


def thirds(value):
    high = lax.reduce_precision(value, 8, 7)
    middle = lax.reduce_precision(value - high, 8, 7)
    return high, middle, value - high - middle


def call(kernel, name, args, outs, scratch=(), flops=0, scalars=0, scalar_outs=0):
    vmem, smem = pl.BlockSpec(memory_space=pltpu.VMEM), pl.BlockSpec(memory_space=pltpu.SMEM)
    size = sum(a.size * a.dtype.itemsize for a in (*args, *outs))
    return pl.pallas_call(
        kernel,
        out_shape=list(outs),
        in_specs=[vmem] * (len(args) - scalars) + [smem] * scalars,
        out_specs=[vmem] * (len(outs) - scalar_outs) + [smem] * scalar_outs,
        scratch_shapes=list(scratch),
        compiler_params=pltpu.CompilerParams(vmem_limit_bytes=VMEM_BYTES),
        cost_estimate=pl.CostEstimate(flops=flops, bytes_accessed=size, transcendentals=0),
        name=name,
    )(*args)


def dot(left, right, dims=((1,), (0,))):
    return lax.dot_general(left, right, (dims, ((), ())), preferred_element_type=f32)


def turned(value, step, axis, width):
    size = value.shape[axis]
    column = lax.broadcasted_iota(jnp.int32, value.shape, axis) % width
    rolled = pltpu.roll(value, step % size, axis)
    return jnp.where(column == (0 if step == 1 else width - 1), 0.0, rolled)


def doubled_columns(ref, row):
    count = row.shape[0]
    for h in range(ref.shape[0]):
        part = row[:, h * LANES : (h + 1) * LANES]
        ref[h, pl.ds(0, count, stride=2), :] = part
        ref[h, pl.ds(1, count, stride=2), :] = part
    return jnp.concatenate([ref[h] for h in range(ref.shape[0])], axis=1)


def lateral_kernel(n_rows, four, five, *refs):
    pieces, (input_four, input_five, first, last, kernel_four, kernel_five, wide) = (
        refs[:n_rows],
        refs[n_rows:],
    )
    crops, height, width, depth = four.shape
    low_height, low_width = five.shape[1:3]
    me = lax.axis_index("rows")
    part_four, part_five = depth // n_rows, five.shape[3] // n_rows
    for k in range(n_rows):
        owner = me ^ k
        at_four = pl.multiple_of(owner * part_four, part_four)
        at_five = pl.multiple_of(owner * part_five, part_five)
        kernel_four[pl.ds(at_four, part_four), :] = pieces[k][:part_four]
        kernel_five[pl.ds(at_five, part_five), :] = pieces[k][part_four:]
    for b in range(crops):
        low = dot(five[b].reshape(low_height * low_width, -1), kernel_five[...])
        low_rounded = low.astype(bf16).reshape(low_height, low_width, -1)
        input_five[b] = low_rounded
        first[b, width:] = low_rounded[0]
        last[b, width:] = low_rounded[low_height - 1]
        for q in range(low_height):
            up = doubled_columns(wide, low[q * low_width : (q + 1) * low_width])
            rows = four[b, 2 * q : 2 * q + 2].reshape(2 * width, depth)
            merged = dot(rows, kernel_four[...]).reshape(2, width, -1) + up[None]
            rounded = merged.astype(bf16)
            input_four[b, 2 * q : 2 * q + 2] = rounded
            if q == 0:
                first[b, :width] = rounded[0]
            if q == low_height - 1:
                last[b, :width] = rounded[1]


def three_taps(source, b, start, rows, weights, step):
    width, channels = source.shape[2:]
    parts = []
    for j in range(3):
        taps = range(3) if step == 1 else (2, 1, 0)
        left = jnp.concatenate(
            [
                source[b, start + i : start + i + rows].reshape(rows * width, channels)
                for i in range(3)
            ],
            axis=1,
        )
        blocks = [weights[(3 * i + j) * channels : (3 * i + j + 1) * channels] for i in taps]
        if step == 1:
            parts.append(dot(left, jnp.concatenate(blocks, axis=0)))
        else:
            parts.append(dot(left, jnp.concatenate(blocks, axis=1), ((1,), (1,))))
    return parts[1] + turned(parts[0], step, 0, width) + turned(parts[2], -step, 0, width)


def fill_padded(padded, own, above, below, start):
    height, width = own.shape[1:3]
    for b in range(own.shape[0]):
        padded[b, 0] = above[b, start : start + width]
        padded[b, 1 : height + 1] = own[b]
        padded[b, height + 1] = below[b, start : start + width]


def output_kernel(n_rows, deltas, input_four, input_five, above, below, *refs):
    pieces, (levels, first, last, kernel_four, kernel_five, head, count, spread_four, spread_five, wide) = (
        refs[:n_rows],
        refs[n_rows:],
    )
    crops, height, width, channels = input_four.shape
    low_height, low_width = input_five.shape[1:3]
    me = lax.axis_index("rows")
    part = 9 * channels // n_rows
    positives = jnp.zeros((), f32)
    spare = wide.at[:]
    for k in range(n_rows):
        at = pl.multiple_of((me ^ k) * part, part)
        kernel_four[pl.ds(at, part), :] = pieces[k][:, :channels]
        kernel_five[pl.ds(at, part), :] = pieces[k][:, channels : 2 * channels]
        spare[pl.ds(at, part), :] = pieces[k][:, 2 * channels :].astype(f32)
    lane = lax.broadcasted_iota(jnp.int32, (channels, LANES), 1)
    line = lax.broadcasted_iota(jnp.int32, (DELTA_ROWS, channels), 0)
    for t in range(9):
        block = spare[t * channels : (t + 1) * channels, :]
        positives = positives + jnp.sum(
            jnp.where((lane >= deltas) & (lane < deltas + 3), block, 0.0)
        )
        turned_block = jnp.where(line < deltas, block.T[:DELTA_ROWS], 0.0)
        head[t * DELTA_ROWS : (t + 1) * DELTA_ROWS, :] = turned_block.astype(bf16)
    count[0, 0] = positives
    fill_padded(spread_four, input_four, above, below, 0)
    fill_padded(spread_five, input_five, above, below, width)
    low_start, top_start = height, height + low_height
    half = width // 2
    levels[:, low_start:, half:, :] = jnp.zeros(
        (crops, levels.shape[1] - low_start, width - half, channels), bf16
    )
    quarter = low_width // 2
    levels[:, top_start:, quarter:, :] = jnp.zeros(
        (crops, levels.shape[1] - top_start, width - quarter, channels), bf16
    )
    rows = 4
    for b in range(crops):
        low = three_taps(spread_five, b, 0, low_height, kernel_five, 1)
        low_rounded = low.astype(bf16).reshape(low_height, low_width, channels)
        levels[b, low_start:top_start, :low_width, :] = low_rounded
        first[b, width : width + low_width] = low_rounded[0]
        last[b, width : width + low_width] = low_rounded[low_height - 1]
        for h in range(0, channels, LANES):
            spare[: low_height * low_width, :] = low[:, h : h + LANES]
            for q in range(low_height // 2):
                total = jnp.zeros((quarter, LANES), f32)
                for at in (2 * q * low_width, (2 * q + 1) * low_width):
                    for side in range(2):
                        total = total + spare[pl.ds(at + side, quarter, stride=2), :]
                pooled = (0.25 * total).astype(bf16)
                levels[b, top_start + q, :quarter, h : h + LANES] = pooled
                if q == 0:
                    first[b, width + low_width :, h : h + LANES] = pooled
                if q == low_height // 2 - 1:
                    last[b, width + low_width :, h : h + LANES] = pooled
        for r in range(0, height, rows):
            sums = three_taps(spread_four, b, r, rows, kernel_four, 1)
            rounded = sums.astype(bf16).reshape(rows, width, channels)
            levels[b, r : r + rows] = rounded
            if r == 0:
                first[b, :width] = rounded[0]
            if r == height - rows:
                last[b, :width] = rounded[rows - 1]


def level_rows(height):
    result, padded, own = [], 0, 0
    for count in (height, height // 2, height // 4):
        result.append((padded, own, count))
        padded, own = padded + count + 2, own + count
    return result


def head_kernel(height, levels, above, below, head, target, mask, count, grads, first, last, loss, spread):
    crops, _, width, channels = levels.shape
    inverse = 1.0 / jnp.maximum(count[0, 0], 1.0)
    plan = level_rows(height)
    summed = jnp.zeros((DELTA_ROWS, LANES), f32)
    for b in range(crops):
        edge = 0
        for index, (padded, own, lines) in enumerate(plan):
            extent = width >> index
            for at, rim in ((padded, above), (padded + lines + 1, below)):
                spread[at, :extent] = rim[b, edge : edge + extent]
                if extent < width:
                    spread[at, extent:] = jnp.zeros((width - extent, channels), bf16)
            spread[padded + 1 : padded + 1 + lines] = levels[b, own : own + lines]
            edge += extent
        total_rows = spread.shape[0]
        products = dot(
            head[...], spread[...].reshape(total_rows * width, channels), ((1,), (1,))
        )
        columns = []
        for j in range(3):
            pieces = []
            for padded, own, lines in plan:
                total = jnp.zeros((DELTA_ROWS, lines * width), f32)
                for i in range(3):
                    tap = (3 * i + j) * DELTA_ROWS
                    total = total + products[
                        tap : tap + DELTA_ROWS, (padded + i) * width : (padded + i + lines) * width
                    ]
                pieces.append(total)
            columns.append(jnp.concatenate(pieces, axis=1))
        values = columns[1] + turned(columns[0], 1, 1, width) + turned(columns[2], -1, 1, width)
        mismatch = values - target[b]
        weight = mask[b]
        magnitude = jnp.abs(mismatch)
        losses = weight * jnp.where(
            magnitude < box_beta, 0.5 * mismatch * mismatch / box_beta, magnitude - 0.5 * box_beta
        )
        for at in range(0, losses.shape[1], LANES):
            summed = summed + losses[:, at : at + LANES]
        gradient = (weight * jnp.clip(mismatch / box_beta, -1.0, 1.0) * inverse).astype(bf16)
        grads[b] = gradient
        for index, (padded, own, lines) in enumerate(plan):
            at = slice(index * width, (index + 1) * width)
            first[b, :, at] = gradient[:, own * width : (own + 1) * width]
            last[b, :, at] = gradient[:, (own + lines - 1) * width : (own + lines) * width]
    loss[0, 0] = jnp.sum(summed)


def back_kernel(height, levels, head, grads, above, below, head_grad, grad_four, grad_five, first, last, taps, wide):
    crops, _, width, channels = levels.shape
    plan = level_rows(height)
    total = jnp.zeros((9 * DELTA_ROWS, channels), f32)
    for b in range(crops):
        pieces = []
        for index, (padded, own, lines) in enumerate(plan):
            at = slice(index * width, (index + 1) * width)
            pieces += [
                above[b, :, at],
                grads[b, :, own * width : (own + lines) * width],
                below[b, :, at],
            ]
        middle = jnp.concatenate(pieces, axis=1).astype(f32)
        shifted = [turned(middle, -1, 1, width), middle, turned(middle, 1, 1, width)]
        for i in range(3):
            for j in range(3):
                for padded, own, lines in plan:
                    at = (padded + 2 - i) * width
                    taps[
                        (3 * i + j) * DELTA_ROWS : (3 * i + j + 1) * DELTA_ROWS,
                        own * width : (own + lines) * width,
                    ] = shifted[j][:, at : at + lines * width].astype(bf16)
        spread = taps[...]
        lines_all = levels.shape[1]
        total = total + dot(spread, levels[b].reshape(lines_all * width, channels))
        back = dot(spread, head[...], ((0,), (0,))).reshape(lines_all, width, channels)
        rounded = back[:height].astype(bf16)
        grad_four[b] = rounded
        first[b, :width] = rounded[0]
        last[b, :width] = rounded[height - 1]
        low_height, low_width = height // 2, width // 2
        for q in range(low_height // 2):
            up = doubled_columns(wide, back[height + low_height + q, : low_width // 2])
            for row in (2 * q, 2 * q + 1):
                low = (back[height + row, :low_width] + 0.25 * up).astype(bf16)
                grad_five[b, row] = low
                if row == 0:
                    first[b, width:] = low
                if row == low_height - 1:
                    last[b, width:] = low
    head_grad[...] = total


def conv_grad_kernel(n_rows, input_four, input_five, above, below, grad_four, grad_five, head_grad, place, kept, turned_rows, sums_four, sums_five, spare):
    crops, height, width, channels = input_four.shape
    low_height, low_width = input_five.shape[1:3]
    padding = jnp.zeros((width - low_width, channels), bf16)
    for own, grad, edge, sums in (
        (input_four, grad_four, 0, sums_four),
        (input_five, grad_five, width, sums_five),
    ):
        lines, extent = own.shape[1:3]

        def widened(row):
            if extent == width:
                return row
            return jnp.concatenate([row, padding], axis=0)

        for b in range(crops):
            for r in range(lines + 2):
                if r == 0:
                    row = above[b, edge : edge + extent]
                elif r == lines + 1:
                    row = below[b, edge : edge + extent]
                else:
                    row = own[b, r - 1]
                turned_rows[:, r * width : (r + 1) * width] = widened(row).T
            left = jnp.concatenate(
                [turned_rows[:, i * width : (i + lines) * width] for i in range(3)], axis=0
            )
            middle = jnp.concatenate([widened(grad[b, r]) for r in range(lines)], axis=0)
            wide = middle.astype(f32)
            right = jnp.concatenate(
                [
                    turned(wide, -1, 0, width).astype(bf16),
                    middle,
                    turned(wide, 1, 0, width).astype(bf16),
                ],
                axis=1,
            )
            product = dot(left, right)
            if b == 0:
                sums[...] = product
            else:
                sums[...] += product
    for t in range(9):
        block = head_grad[t * DELTA_ROWS : (t + 1) * DELTA_ROWS, :]
        block = jnp.concatenate(
            [block, jnp.zeros((LANES - DELTA_ROWS, channels), f32)], axis=0
        )
        spare[t * channels : (t + 1) * channels, :] = block.T
    me = lax.axis_index("rows")
    part = 9 * channels // n_rows
    for owner in range(n_rows):
        index = owner ^ me
        for start in range(0, part, 16):
            line = owner * part + start
            i, rest = divmod(line, 3 * channels)
            j, channel = divmod(rest, channels)
            lines = jnp.concatenate(
                [
                    sums_four[pl.ds(i * channels + channel, 16), j * channels : (j + 1) * channels],
                    sums_five[pl.ds(i * channels + channel, 16), j * channels : (j + 1) * channels],
                    spare[pl.ds(line, 16), :] + place[pl.ds(start, 16), :],
                ],
                axis=1,
            ).astype(bf16)
            kept[index, start : start + 16, :] = lines


def merged_grad_kernel(grad_four, grad_five, above, below, kernel_four, kernel_five, lat_four, lat_five, spread_four, spread_five, fold):
    crops, height, width, channels = grad_four.shape
    low_height, low_width = grad_five.shape[1:3]
    fill_padded(spread_four, grad_four, above, below, 0)
    fill_padded(spread_five, grad_five, above, below, width)
    rows = 4
    for b in range(crops):
        low = three_taps(spread_five, b, 0, low_height, kernel_five, -1)
        low = low.reshape(low_height, low_width, channels)
        for r in range(0, height, rows):
            back = three_taps(spread_four, b, r, rows, kernel_four, -1)
            at = (b * height + r) * width
            lat_four[at : at + rows * width, :] = back.astype(bf16)
            for h in range(0, channels, LANES):
                fold[...] = back[:, h : h + LANES]
                for q in range(rows // 2):
                    total = low[r // 2 + q, :, h : h + LANES]
                    folded = jnp.zeros_like(total)
                    for line in (2 * q * width, (2 * q + 1) * width):
                        for side in range(2):
                            folded = folded + fold[pl.ds(line + side, low_width, stride=2), :]
                    at_low = (b * low_height + r // 2 + q) * low_width
                    lat_five[at_low : at_low + low_width, h : h + LANES] = (total + folded).astype(bf16)


def section_grad_kernel(n_rows, four, five, lat_four, lat_five, kept):
    crops, height, width, depth = four.shape
    low_height, low_width, low_depth = five.shape[1:]
    me = lax.axis_index("rows")
    part_four, part_five = depth // n_rows, low_depth // n_rows
    positions = crops * height * width
    low_positions = crops * low_height * low_width
    turned_four = lat_four[...].T
    turned_five = lat_five[...].T
    for owner in range(n_rows):
        index = owner ^ me
        at = slice(owner * part_four, (owner + 1) * part_four)
        block = dot(turned_four, four[:, :, :, at].reshape(positions, part_four))
        kept[index, :part_four, :] = block.T.astype(bf16)
        at = slice(owner * part_five, (owner + 1) * part_five)
        block = dot(turned_five, five[:, :, :, at].reshape(low_positions, part_five))
        kept[index, part_four:, :] = block.T.astype(bf16)


def planes(field, rows):
    crops, height, width, depth = field.shape
    field = jnp.transpose(field, (0, 3, 1, 2))
    field = jnp.pad(field, ((0, 0), (0, rows - depth), (0, 0), (0, LANES - width)))
    return field.reshape(crops, rows, height * LANES)


def on_device(
    section_four,
    section_five,
    target_four,
    target_five,
    target_six,
    anchor_four,
    anchor_five,
    anchor_six,
    lateral_four,
    lateral_five,
    output_conv,
    delta_head,
    mean_four,
    mean_five,
    mean_conv,
    mean_head,
    square_four,
    square_five,
    square_conv,
    square_head,
):
    n_rows, n_batch = lax.axis_size("rows"), lax.axis_size("batch")
    number = lax.axis_index("rows") * n_batch + lax.axis_index("batch")
    _, low_group, high_group = row_groups()
    crops, height, width, depth = section_four.shape
    low_height, low_width, low_depth = section_five.shape[1:]
    top_width = target_six.shape[2]
    four_n, five_n, conv_n = lateral_four.shape[0], lateral_five.shape[0], output_conv.shape[1]
    channels, deltas = delta_head.shape[0] * n_rows * n_batch // 9, delta_head.shape[1]
    shape = jax.ShapeDtypeStruct

    lateral = jnp.concatenate([lateral_four, lateral_five]).astype(bf16)
    parts = gathered_batch(lateral)
    lateral = jnp.concatenate([p[:four_n] for p in parts] + [p[four_n:] for p in parts])
    laterals = gathered_high(lateral)

    anchors = [a.astype(f32) for a in (anchor_four, anchor_five, anchor_six)]
    mask = jnp.concatenate(
        [planes(jnp.repeat(a, deltas // a.shape[3], axis=3), DELTA_ROWS) for a in anchors], axis=2
    )
    target = jnp.concatenate(
        [planes(t, DELTA_ROWS) for t in (target_four, target_five, target_six)], axis=2
    )
    local_count = sum(jnp.sum(a) for a in anchors)

    lane = lax.broadcasted_iota(jnp.int32, (conv_n, LANES), 1)
    line = lax.broadcasted_iota(jnp.int32, (conv_n, LANES), 0)
    spare = jnp.pad(delta_head, ((0, 0), (0, LANES - deltas)))
    for k, piece in enumerate(thirds(local_count)):
        spare = jnp.where((line == 0) & (lane == deltas + k), piece, spare)
    conv = jnp.concatenate([output_conv[0], output_conv[1], spare], axis=1).astype(bf16)
    conv, _ = lax.optimization_barrier((conv, lateral))
    conv = jnp.concatenate(gathered_batch(conv))
    conv, laterals = lax.optimization_barrier((conv, laterals))
    laterals = gathered_low(laterals)
    convs = gathered_high(conv)

    edge = width + low_width
    input_four, input_five, first, last = call(
        functools.partial(lateral_kernel, n_rows),
        "laterals",
        [section_four, section_five, *laterals],
        [
            shape((crops, height, width, channels), bf16),
            shape((crops, low_height, low_width, channels), bf16),
            shape((crops, edge, channels), bf16),
            shape((crops, edge, channels), bf16),
        ],
        [
            pltpu.VMEM((depth, channels), bf16),
            pltpu.VMEM((low_depth, channels), bf16),
            pltpu.VMEM((channels // LANES, width, LANES), f32),
        ],
        flops=2 * crops * channels * (height * width * depth + low_height * low_width * low_depth),
    )
    above_in, below_in = from_neighbours(first, last)
    convs, _ = lax.optimization_barrier((convs, input_four))
    convs = gathered_low(convs)

    lines = height + low_height + low_height // 2
    conv_flops = 18 * crops * channels * channels * (height * width + low_height * low_width)
    levels, first, last, kernel_four, kernel_five, head, count = call(
        functools.partial(output_kernel, n_rows, deltas),
        "outputs",
        [input_four, input_five, above_in, below_in, *convs],
        [
            shape((crops, lines, width, channels), bf16),
            shape((crops, edge + top_width, channels), bf16),
            shape((crops, edge + top_width, channels), bf16),
            shape((9 * channels, channels), bf16),
            shape((9 * channels, channels), bf16),
            shape((9 * DELTA_ROWS, channels), bf16),
            shape((1, 1), f32),
        ],
        [
            pltpu.VMEM((crops, height + 2, width, channels), bf16),
            pltpu.VMEM((crops, low_height + 2, low_width, channels), bf16),
            pltpu.VMEM((9 * channels, LANES), f32),
        ],
        flops=conv_flops,
        scalar_outs=1,
    )
    above, below = from_neighbours(first, last)

    head_flops = 18 * DELTA_ROWS * crops * lines * width * channels
    grads, first, last, loss = call(
        functools.partial(head_kernel, height),
        "deltas",
        [levels, above, below, head, target, mask, count],
        [
            shape((crops, DELTA_ROWS, lines * width), bf16),
            shape((crops, DELTA_ROWS, 3 * width), bf16),
            shape((crops, DELTA_ROWS, 3 * width), bf16),
            shape((1, 1), f32),
        ],
        [pltpu.VMEM((lines + 6, width, channels), bf16)],
        flops=head_flops,
        scalars=1,
        scalar_outs=1,
    )
    above, below = from_neighbours(first, last)

    head_grad, grad_four, grad_five, first, last = call(
        functools.partial(back_kernel, height),
        "level_grads",
        [levels, head, grads, above, below],
        [
            shape((9 * DELTA_ROWS, channels), f32),
            shape((crops, height, width, channels), bf16),
            shape((crops, low_height, low_width, channels), bf16),
            shape((crops, edge, channels), bf16),
            shape((crops, edge, channels), bf16),
        ],
        [
            pltpu.VMEM((9 * DELTA_ROWS, lines * width), bf16),
            pltpu.VMEM((channels // LANES, low_width, LANES), f32),
        ],
        flops=2 * head_flops,
    )
    above, below = from_neighbours(first, last)

    place = jnp.zeros((conv_n, LANES), f32)
    for k, piece in enumerate(thirds(loss[0, 0])):
        spot = (line == number % conv_n) & (lane == deltas + 3 * (number // conv_n) + k)
        place = jnp.where(spot, piece, place)
    place = jnp.concatenate([place] * n_batch)
    conv_width = 2 * channels + LANES
    (conv_blocks,) = call(
        functools.partial(conv_grad_kernel, n_rows),
        "conv_grads",
        [input_four, input_five, above_in, below_in, grad_four, grad_five, head_grad, place],
        [shape((n_rows, n_batch * conv_n, conv_width), bf16)],
        [
            pltpu.VMEM((channels, (height + 2) * width), bf16),
            pltpu.VMEM((3 * channels, 3 * channels), f32),
            pltpu.VMEM((3 * channels, 3 * channels), f32),
            pltpu.VMEM((9 * channels, LANES), f32),
        ],
        flops=conv_flops,
    )
    conv_blocks = conv_blocks.reshape(high_group, low_group, n_batch * conv_n, conv_width)
    positions, low_positions = crops * height * width, crops * low_height * low_width
    lat_four, lat_five = call(
        merged_grad_kernel,
        "merged_grads",
        [grad_four, grad_five, above, below, kernel_four, kernel_five],
        [shape((positions, channels), bf16), shape((low_positions, channels), bf16)],
        [
            pltpu.VMEM((crops, height + 2, width, channels), bf16),
            pltpu.VMEM((crops, low_height + 2, low_width, channels), bf16),
            pltpu.VMEM((4 * width, LANES), f32),
        ],
        flops=conv_flops,
    )
    conv_partial = summed_low([conv_blocks[:, k] for k in range(low_group)])
    lat_four, conv_partial = lax.optimization_barrier((lat_four, conv_partial))
    conv_sum = summed_high(conv_partial)

    (lateral_blocks,) = call(
        functools.partial(section_grad_kernel, n_rows),
        "lateral_grads",
        [section_four, section_five, lat_four, lat_five],
        [shape((n_rows, n_batch * (four_n + five_n), channels), bf16)],
        flops=2 * channels * (positions * depth + low_positions * low_depth),
    )
    lateral_blocks = lateral_blocks.reshape(
        high_group, low_group, n_batch * (four_n + five_n), channels
    )
    lateral_partial = summed_low([lateral_blocks[:, k] for k in range(low_group)])
    lateral_partial, conv_sum = lax.optimization_barrier((lateral_partial, conv_sum))
    lateral_sum = summed_high(lateral_partial)
    conv_sum = summed_batch(conv_sum.reshape(n_batch, conv_n, conv_width))
    lateral_sum = summed_batch(
        jnp.concatenate(
            [
                lateral_sum[: n_batch * four_n].reshape(n_batch, four_n, channels),
                lateral_sum[n_batch * four_n :].reshape(n_batch, five_n, channels),
            ],
            axis=1,
        )
    )

    conv_part = jnp.stack([conv_sum[:, :channels], conv_sum[:, channels : 2 * channels]])
    head_part = conv_sum[:, 2 * channels : 2 * channels + deltas]
    loss_sum = jnp.sum(conv_sum[:, 2 * channels + deltas :])
    first_four, second_four, weight_four = adamw_update(
        lateral_four, lateral_sum[:four_n], mean_four, square_four
    )
    first_five, second_five, weight_five = adamw_update(
        lateral_five, lateral_sum[four_n:], mean_five, square_five
    )
    first_conv, second_conv, weight_conv = adamw_update(
        output_conv, conv_part, mean_conv, square_conv
    )
    first_head, second_head, weight_head = adamw_update(
        delta_head, head_part, mean_head, square_head
    )
    return (
        loss_sum,
        count[0, 0],
        first_four,
        first_five,
        first_conv,
        first_head,
        second_four,
        second_five,
        second_conv,
        second_head,
        weight_four,
        weight_five,
        weight_conv,
        weight_head,
    )


def solution(mesh):
    split = P("batch", "rows", None, None)
    whole, pair = P(("rows", "batch"), None), P(None, ("rows", "batch"), None)
    weights = (whole, whole, pair, whole)
    return jax.shard_map(
        on_device,
        mesh=mesh,
        in_specs=(split,) * 8 + weights * 3,
        out_specs=(P(), P()) + weights * 3,
        check_vma=False,
    )
```

time: 835 us -> 199 us (0.24); the launches traced: 824 us -> 198 us
  waiting for transfers between devices: 417 us -> 42.3 us
  blocking collectives: 189 us -> 0 us
  matrix products: 90.8 us -> 0 us
  Pallas kernels: 0 us -> 42.9 us
  starting transfers between devices: 45.9 us -> 65.7 us
  local copies, waits for them, and re-layouts: 27.2 us -> 15.1 us
  between operations: 20.7 us -> 9.6 us
  other arithmetic: 33.3 us -> 22.2 us
    reduce_scatter x3 -> x0, waiting for transfers between devices: 383 us -> none  [the longest x1 138 us: on_device(): lax.psum_scatter(four_grad, ('rows', 'batch'), scatter_dimension=0, tiled...]
    all_gather x2 -> x0, blocking collectives: 141 us -> none  [the longest x1 74.2 us: on_device(): lax.all_gather(lateral_four.astype(jnp.bfloat16), ('rows', 'batch'), axis...]
    dot_general x138 -> x0, matrix products: 90.8 us -> none  [the longest x45 31.8 us: conv_taps(): jnp.dot(window, kernel[offset * channels:(offset + 1) * channels], prefer...]
    psum x1 -> x0, blocking collectives: 48.7 us -> none  [on_device(): positives, loss_sum = lax.psum((local_count, local_loss), ('rows', 'batch'))]
    pallas_call x0 -> x7, Pallas kernels: none -> 42.9 us  [call(): pl.pallas_call(kernel, out_shape=list(outs), in_specs=[vmem] * (len(args)...]
    ppermute x20 -> x42, waiting for transfers between devices: 2.05 us -> 42.3 us  [the longest x34 34.7 us: sent(): return lax.ppermute(value, axis, [(i, i ^ mask) for i in range(count)])]
    unnamed x7 -> x0, waiting for transfers between devices: 32.2 us -> none
    ppermute x20 -> x42, starting transfers between devices: 45.4 us -> 65.7 us  [the longest x34 44.1 us: sent(): return lax.ppermute(value, axis, [(i, i ^ mask) for i in range(count)])]
  transfers between devices with their start and end apart: 26 -> 42, of which waited for: 5 -> 14; matrix products, arithmetic and copies ran while one was open for 13% -> 11% of each run, Pallas kernels for 0% -> 7%
where the time goes in v1:
time: 199 us; the launch traced here: 198 us
  starting transfers between devices  65.7 us (33%)
  Pallas kernels  42.9 us (22%)
  waiting for transfers between devices  42.3 us (21%)
  other arithmetic  22.2 us (11%)
  local copies, waits for them, and re-layouts  15.1 us (8%)
  between operations  9.6 us (5%)
    ppermute x34, starting transfers between devices, sent(): return lax.ppermute(value, axis, [(i, i ^ mask) for i in range(count)])  44.1 us
    pallas_call x7, Pallas kernels, call(): pl.pallas_call(kernel, out_shape=list(outs), in_specs=[vmem] * (len(args)...  42.9 us
    ppermute x34, waiting for transfers between devices, sent(): return lax.ppermute(value, axis, [(i, i ^ mask) for i in range(count)])  34.7 us
    ppermute x4, starting transfers between devices, from_neighbours(): above = lax.ppermute(last, 'rows', [(i, i + 1) for i in range(count - 1)])  16 us
    unnamed x115, local copies, waits for them, and re-layouts  10.8 us
    ppermute x4, waiting for transfers between devices, from_neighbours(): below = lax.ppermute(first, 'rows', [(i + 1, i) for i in range(count - 1)])  7.59 us
    ppermute x4, starting transfers between devices, from_neighbours(): below = lax.ppermute(first, 'rows', [(i + 1, i) for i in range(count - 1)])  5.57 us
    add x4, other arithmetic, summed_low(): sum((c[j].astype(f32) for c in came), blocks[0][j].astype(f32))  4.21 us
  transfers between devices with their start and end apart: 42, of which 14 were waited for; matrix products, arithmetic and copies ran while one was open for 11% of the time, Pallas kernels for 7%

profile of v1, /device:TPU:0, one launch (start us, length us, event | category | flops | bytes accessed | tf_op | source)
XLA Modules:
  0.0 197.8 jit_solution(6727071383327582602)
XLA Ops:
  0.6 0.8 convert.40
  2.3 5.1 %collective-permute-start.2 = (bf16[96,256]{1,0:T(8,128)(2,1)S(1)}, bf16[96,256]{1,0:T(8,128)(2,1)S(1)}, u32[]{:S(2)}, u32[]{:S(2)}) collective-permute-start(bf16[96,256]{1,0:T(8,128)(2,1)S(1)} %pad_maximum_fusion.8), channel_id=1, source_target_pairs={{0,3},{1,2},{2,1},{3,0},{4,7},{5,6},{6,5},{7,4},{8,11},{9,10},{10,... | collective-permute-start | bytes 147464 | tf_op jit(solution)/shard_map/ppermute | solution.py:43
  8.0 0.8 convert_bitcast_fusion.4
  9.6 0.8 copy.52
  10.4 1.3 convert_reduce_fusion.2
  11.8 1.3 convert_reduce_fusion.1
  13.1 1.3 convert_reduce_fusion
  18.7 0.9 convert.37
  19.6 1.4 select_convert_fusion
  21.3 3.8 %collective-permute-start.5 = (bf16[72,640]{1,0:T(8,128)(2,1)S(1)}, bf16[72,640]{1,0:T(8,128)(2,1)S(1)}, u32[]{:S(2)}, u32[]{:S(2)}) collective-permute-start(bf16[72,640]{1,0:T(8,128)(2,1)S(1)} %pad_maximum_fusion.7), channel_id=1, source_target_pairs={{0,3},{1,2},{2,1},{3,0},{4,7},{5,6},{6,5},{7,4},{8,11},{9,10},{10,... | collective-permute-start | bytes 276488 | tf_op jit(solution)/shard_map/ppermute | solution.py:43
  25.7 1.6 collective-permute-start.6
  27.4 1.5 collective-permute-start.7
  28.9 1.8 collective-permute-start.8
  30.6 1.3 collective-permute-done.4
  32.2 1.2 collective-permute-done.6.refs_2_
  33.4 3.3 %collective-permute-done.7.refs_4_ = bf16[384,256]{1,0:T(8,128)(2,1)S(1)} collective-permute-done((bf16[384,256]{1,0:T(8,128)(2,1)S(1)}, bf16[384,256]{1,0:T(8,128)(2,1)S(1)}, u32[]{:S(2)}, u32[]{:S(2)}) %collective-permute-start.7) | collective-permute-done | bytes 196640 | tf_op jit(solution)/shard_map/ppermute | solution.py:43
  37.8 0.9 collective-permute-start.15
  38.7 1.4 collective-permute-start.16
  40.1 1.2 collective-permute-start.17
  42.7 6.1 %laterals.1 = (bf16[2,8,128,256]{3,2,1,0:T(8,128)(2,1)}, bf16[2,4,64,256]{3,2,1,0:T(8,128)(2,1)}, bf16[2,192,256]{2,1,0:T(8,128)(2,1)}, bf16[2,192,256]{2,1,0:T(8,128)(2,1)}) custom-call(bf16[2,8,128,1024]{3,2,1,0:T(8,128)(2,1)} %four.3, bf16[2,4,64,2048]{3,2,1,0:T(8,128)(2,1)} %five.3, bf16[384,256]{1,0:T(8,128)(2,1)} %copy-done.8, ...), custom_call_target="tpu_custom_call" | custom-call | flops 1610612736 | bytes 9568256 | tf_op jit(solution)/shard_map/laterals/pallas_call | solution.py:114
  48.8 2.0 collective-permute-start.13
  50.8 7.1 %collective-permute-done.16.refs_4_ = bf16[288,640]{1,0:T(8,128)(2,1)S(1)} collective-permute-done((bf16[288,640]{1,0:T(8,128)(2,1)S(1)}, bf16[288,640]{1,0:T(8,128)(2,1)S(1)}, u32[]{:S(2)}, u32[]{:S(2)}) %collective-permute-start.16) | collective-permute-done | bytes 368672 | tf_op jit(solution)/shard_map/ppermute | solution.py:43
  59.6 1.3 collective-permute-start.14
  60.9 2.2 %collective-permute-done.14.below = bf16[2,192,256]{2,1,0:T(8,128)(2,1)S(1)} collective-permute-done((bf16[2,192,256]{2,1,0:T(8,128)(2,1)}, bf16[2,192,256]{2,1,0:T(8,128)(2,1)S(1)}, u32[]{:S(2)}, u32[]{:S(2)}) %collective-permute-start.14) | collective-permute-done | bytes 196640 | tf_op jit(solution)/shard_map/ppermute | solution.py:101
  64.3 7.1 %outputs.1 = (bf16[2,14,128,256]{3,2,1,0:T(8,128)(2,1)}, bf16[2,224,256]{2,1,0:T(8,128)(2,1)}, bf16[2,224,256]{2,1,0:T(8,128)(2,1)}, bf16[2304,256]{1,0:T(8,128)...) custom-call(bf16[2,8,128,256]{3,2,1,0:T(8,128)(2,1)} %get-tuple-element.61.input_four, ...), custom_call_target="tpu_custom_call" | custom-call | flops 3019898880 | bytes 9379844 | tf_op jit(solution)/shard_map/outputs/pallas_call | solution.py:114
  71.5 5.7 %collective-permute-start.22 = (bf16[2,224,256]{2,1,0:T(8,128)(2,1)}, bf16[2,224,256]{2,1,0:T(8,128)(2,1)S(1)}, u32[]{:S(2)}, u32[]{:S(2)}) collective-permute-start(bf16[2,224,256]{2,1,0:T(8,128)(2,1)} %get-tuple-element.72), channel_id=1, source_target_pairs={{0,4},{4,8},{8,12},{12,16},{16,20},{20,24},{24,28},{1,5},{5,9},{9,... | collective-permute-start | bytes 688136 | tf_op jit(solution)/shard_map/ppermute | solution.py:100
  77.1 1.3 collective-permute-start.23
  78.4 0.8 pad_maximum_fusion.3
  79.2 1.5 collective-permute-done.23.below
  81.4 4.2 %deltas.1 = (bf16[2,16,1792]{2,1,0:T(8,128)(2,1)}, bf16[2,16,384]{2,1,0:T(8,128)(2,1)}, bf16[2,16,384]{2,1,0:T(8,128)(2,1)}, f32[1,1]{1,0:T(1,128)}) custom-call(bf16[2,14,128,256]{3,2,1,0:T(8,128)(2,1)} %get-tuple-element.70.levels, bf16[2,224,256]{2,1,0:T(8,128)(2,1)} %copy-done.9, bf16[2,224,256]{2,1,0:T(8,128)(2,1)} %copy-done.10, ...), custom_call_target="tpu_custom_call" | custom-call | flops 264241152 | bytes 2990088 | tf_op jit(solution)/shard_map/deltas/pallas_call | solution.py:114
  85.6 6.4 %collective-permute-start.24 = (bf16[2,16,384]{2,1,0:T(8,128)(2,1)}, bf16[2,16,384]{2,1,0:T(8,128)(2,1)S(1)}, u32[]{:S(2)}, u32[]{:S(2)}) collective-permute-start(bf16[2,16,384]{2,1,0:T(8,128)(2,1)} %get-tuple-element.76), channel_id=1, source_target_pairs={{0,4},{4,8},{8,12},{12,16},{16,20},{20,24},{24,28},{1,5},{5,9},{9,... | collective-permute-start | bytes 73736 | tf_op jit(solution)/shard_map/ppermute | solution.py:100
  92.1 1.5 collective-permute-start.25
  97.2 1.4 select_select_fusion
  99.9 3.8 %level_grads.1 = (f32[144,256]{1,0:T(8,128)}, bf16[2,8,128,256]{3,2,1,0:T(8,128)(2,1)}, bf16[2,4,64,256]{3,2,1,0:T(8,128)(2,1)}, bf16[2,192,256]{2,1,0:T(8,128)(2,1)}, bf16[2,192,256]{2,1,0:T(8,128)(2,1)}) custom-call(bf16[2,14,128,256]{3,2,1,0:T(8,128)(2,1)} %get-tuple-element.70.levels, bf16[144,256]{1,0:T(8,128)(2,1)} %get-tuple-element.71.head, ...), custom_call_target="tpu_custom_call" | custom-call | flops 528482304 | bytes 3923968 | tf_op jit(solution)/shard_map/level_grads/pallas_call | solution.py:114
  103.6 7.5 %conv_grads.1 = bf16[8,288,640]{2,1,0:T(8,128)(2,1)} custom-call(bf16[2,8,128,256]{3,2,1,0:T(8,128)(2,1)} %get-tuple-element.61.input_four, bf16[2,4,64,256]{3,2,1,0:T(8,128)(2,1)} %get-tuple-element.62.input_five, bf16[2,192,256]{2,1,0:T(8,128)(2,1)} %collective-permute-done.13.above, bf16[2,192,256]{2,1,0:T(8,128)(2,1)} %copy-done.44, ...), custom_call_target="tpu_custom_call" | custom-call | flops 3019898880 | bytes 6258688 | tf_op jit(solution)/shard_map/conv_grads/pallas_call | solution.py:114
  111.2 1.6 slice_bitcast_fusion
  112.7 1.2 collective-permute-start.28
  113.9 1.9 collective-permute-start.26
  115.9 1.5 collective-permute-start.27
  117.4 3.9 %collective-permute-done.27.below = bf16[2,192,256]{2,1,0:T(8,128)(2,1)S(1)} collective-permute-done((bf16[2,192,256]{2,1,0:T(8,128)(2,1)S(1)}, bf16[2,192,256]{2,1,0:T(8,128)(2,1)S(1)}, u32[]{:S(2)}, u32[]{:S(2)}) %collective-permute-start.27) | collective-permute-done | bytes 196640 | tf_op jit(solution)/shard_map/ppermute | solution.py:101
  122.0 6.9 %merged_grads.1 = (bf16[2048,256]{1,0:T(8,128)(2,1)}, bf16[512,256]{1,0:T(8,128)(2,1)}) custom-call(bf16[2,8,128,256]{3,2,1,0:T(8,128)(2,1)} %get-tuple-element.78.grad_four, bf16[2,4,64,256]{3,2,1,0:T(8,128)(2,1)} %get-tuple-element.79.grad_five, bf16[2,192,256]{2,1,0:T(8,128)(2,1)} %copy-done.47, bf16[2,192,256]{2,1,0:T(8,128)(2,1)} %copy-done.48, ...), custom_call_target="tpu_custom_call" | custom-call | flops 3019898880 | bytes 5373952 | tf_op jit(solution)/shard_map/merged_grads/pallas_call | solution.py:114
  129.0 1.2 convert_add_fusion
  130.2 7.3 %lateral_grads.1 = bf16[8,384,256]{2,1,0:T(8,128)(2,1)} custom-call(bf16[2,8,128,1024]{3,2,1,0:T(8,128)(2,1)} %four.3, bf16[2,4,64,2048]{3,2,1,0:T(8,128)(2,1)} %five.3, bf16[2048,256]{1,0:T(8,128)(2,1)} %get-tuple-element.87.lat_four, bf16[512,256]{1,0:T(8,128)(2,1)} %get-tuple-element.88.lat_five), custom_call_target="tpu_custom_call" | custom-call | flops 1610612736 | bytes 9175040 | tf_op jit(solution)/shard_map/lateral_grads/pallas_call | solution.py:114
  137.4 2.1 %slice_bitcast_fusion.1 = bf16[4,384,256]{2,1,0:T(8,128)(2,1)} fusion(bf16[4,2,384,256]{3,2,1,0:T(8,128)(2,1)} %bitcast.197), kind=kLoop, calls=%fused_computation.1 | loop fusion | bytes 1572864 | tf_op jit(solution)/shard_map/squeeze | solution.py:682
  139.6 4.1 %collective-permute-start.29 = (bf16[4,384,256]{2,1,0:T(8,128)(2,1)}, bf16[4,384,256]{2,1,0:T(8,128)(2,1)}, u32[]{:S(2)}, u32[]{:S(2)}) collective-permute-start(bf16[4,384,256]{2,1,0:T(8,128)(2,1)} %slice_bitcast_fusion.1), channel_id=1, source_target_pairs={{0,4},{4,0},{8,12},{12,8},{16,20},{20,16},{24,28},{28,24},{1,5},{5... | collective-permute-start | bytes 2359304 | tf_op jit(solution)/shard_map/ppermute | solution.py:43
  143.9 4.3 %collective-permute-start.31 = (bf16[288,640]{1,0:T(8,128)(2,1)}, bf16[288,640]{1,0:T(8,128)(2,1)}, u32[]{:S(2)}, u32[]{:S(2)}) collective-permute-start(bf16[288,640]{1,0:T(8,128)(2,1)} %get-tuple-element.91), channel_id=1, source_target_pairs={{0,16},{4,20},{8,24},{12,28},{16,0},{20,4},{24,8},{28,12},{1,17},{... | collective-permute-start | bytes 1105928 | tf_op jit(solution)/shard_map/ppermute | solution.py:43
  148.3 0.8 copy.59
  149.1 0.8 copy.58
  150.0 6.5 %collective-permute-done.32 = bf16[288,640]{1,0:T(8,128)(2,1)} collective-permute-done((bf16[288,640]{1,0:T(8,128)(2,1)}, bf16[288,640]{1,0:T(8,128)(2,1)}, u32[]{:S(2)}, u32[]{:S(2)}) %collective-permute-start.32) | collective-permute-done | bytes 368672 | tf_op jit(solution)/shard_map/ppermute | solution.py:43
  156.4 6.9 %collective-permute-done.31 = bf16[288,640]{1,0:T(8,128)(2,1)} collective-permute-done((bf16[288,640]{1,0:T(8,128)(2,1)}, bf16[288,640]{1,0:T(8,128)(2,1)}, u32[]{:S(2)}, u32[]{:S(2)}) %collective-permute-start.31) | collective-permute-done | bytes 368672 | tf_op jit(solution)/shard_map/ppermute | solution.py:43
  163.7 1.4 convert_add_fusion.4
  165.1 1.0 convert_add_fusion.8
  166.1 2.0 %convert_add_fusion.5 = (bf16[384,256]{1,0:T(8,128)(2,1)}, bf16[384,256]{1,0:T(8,128)(2,1)}, bf16[384,256]{1,0:T(8,128)(2,1)S(1)}) fusion(bf16[4,384,256]{2,1,0:T(8,128)(2,1)} %collective-permute-done.29, bf16[4,2,384,256]{3,2,1,0:T(8,128)(2,1)S(1)} %bitcast.199), kind=kLoop, calls=%fused_computation.15 | loop fusion | flops 1179648 | bytes 1769472 | tf_op jit(solution)/shard_map/add | solution.py:77
  168.3 3.7 %collective-permute-start.35 = (bf16[72,640]{0,1:T(8,128)(2,1)S(1)}, bf16[72,640]{0,1:T(8,128)(2,1)}, u32[]{:S(2)}, u32[]{:S(2)}) collective-permute-start(bf16[72,640]{0,1:T(8,128)(2,1)S(1)} %bitcast.213), channel_id=1, source_target_pairs={{0,3},{1,2},{2,1},{3,0},{4,7},{5,6},{6,5},{7,4},{8,11},{9,10},{10,... | collective-permute-start | bytes 276488 | tf_op jit(solution)/shard_map/ppermute | solution.py:43
  172.2 0.8 copy.66
  174.0 2.7 %collective-permute-start.38 = (bf16[384,256]{1,0:T(8,128)(2,1)S(1)}, bf16[384,256]{1,0:T(8,128)(2,1)S(1)}, u32[]{:S(2)}, u32[]{:S(2)}) collective-permute-start(bf16[384,256]{1,0:T(8,128)(2,1)S(1)} %copy-done.12), channel_id=1, source_target_pairs={{0,24},{4,28},{8,16},{12,20},{16,8},{20,12},{24,0},{28,4},{1,25},{... | collective-permute-start | bytes 589832 | tf_op jit(solution)/shard_map/ppermute | solution.py:43
  177.4 1.4 collective-permute-start.36
  178.8 7.3 %collective-permute-done.34 = bf16[72,640]{0,1:T(8,128)(2,1)} collective-permute-done((bf16[72,640]{0,1:T(8,128)(2,1)S(1)}, bf16[72,640]{0,1:T(8,128)(2,1)}, u32[]{:S(2)}, u32[]{:S(2)}) %collective-permute-start.34) | collective-permute-done | bytes 92192 | tf_op jit(solution)/shard_map/ppermute | solution.py:43
  186.2 1.1 fusion.1
  188.5 2.7 %collective-permute-start.41 = (bf16[96,256]{1,0:T(8,128)(2,1)S(1)}, bf16[96,256]{1,0:T(8,128)(2,1)S(1)}, u32[]{:S(2)}, u32[]{:S(2)}) collective-permute-start(bf16[96,256]{1,0:T(8,128)(2,1)S(1)} %get-tuple-element.163), channel_id=1, source_target_pairs={{0,3},{1,2},{2,1},{3,0},{4,7},{5,6},{6,5},{7,4},{8,11},{9,10},{10,... | collective-permute-start | bytes 147464 | tf_op jit(solution)/shard_map/ppermute | solution.py:43
  191.8 1.2 collective-permute-start.39
  193.6 0.8 copy.62
  194.3 0.8 copy.63
  195.1 0.8 copy.64
  (208 shorter events, 17.8 us)
Async XLA Ops:
  2.3 18.8 %collective-permute-start.2 = (bf16[96,256]{1,0:T(8,128)(2,1)S(1)}, bf16[96,256]{1,0:T(8,128)(2,1)S(1)}, u32[]{:S(2)}, u32[]{:S(2)}) collective-permute-start(bf16[96,256]{1,0:T(8,128)(2,1)S(1)} %pad_maximum_fusion.8), channel_id=1, source_target_pairs={{0,3},{1,2},{2,1},{3,0},{4,7},{5,6},{6,5},{7,4},{8,11},{9,10},{10,... | collective-permute-start | bytes 147464 | tf_op jit(solution)/shard_map/ppermute | solution.py:43
  7.4 13.7 %collective-permute-start.1 = (bf16[96,256]{1,0:T(8,128)(2,1)S(1)}, bf16[96,256]{1,0:T(8,128)(2,1)S(1)}, u32[]{:S(2)}, u32[]{:S(2)}) collective-permute-start(bf16[96,256]{1,0:T(8,128)(2,1)S(1)} %pad_maximum_fusion.8), channel_id=1, source_target_pairs={{0,2},{1,3},{2,0},{3,1},{4,6},{5,7},{6,4},{7,5},{8,10},{9,11},{10,... | collective-permute-start | bytes 147464 | tf_op jit(solution)/shard_map/ppermute | solution.py:43
  7.4 13.7 %collective-permute-start = (bf16[96,256]{1,0:T(8,128)(2,1)S(1)}, bf16[96,256]{1,0:T(8,128)(2,1)S(1)}, u32[]{:S(2)}, u32[]{:S(2)}) collective-permute-start(bf16[96,256]{1,0:T(8,128)(2,1)S(1)} %pad_maximum_fusion.8), channel_id=1, source_target_pairs={{0,1},{1,0},{2,3},{3,2},{4,5},{5,4},{6,7},{7,6},{8,9},{9,8},{10,11... | collective-permute-start | bytes 147464 | tf_op jit(solution)/shard_map/ppermute | solution.py:43
  21.3 20.0 %copy-start.8 = (bf16[384,256]{1,0:T(8,128)(2,1)}, bf16[384,256]{1,0:T(8,128)(2,1)S(1)}, u32[]{:S(2)}) copy-start(bf16[384,256]{1,0:T(8,128)(2,1)S(1)} %fusion.19.refs_0_) | copy-start | bytes 589828
  21.3 7.6 %collective-permute-start.5 = (bf16[72,640]{1,0:T(8,128)(2,1)S(1)}, bf16[72,640]{1,0:T(8,128)(2,1)S(1)}, u32[]{:S(2)}, u32[]{:S(2)}) collective-permute-start(bf16[72,640]{1,0:T(8,128)(2,1)S(1)} %pad_maximum_fusion.7), channel_id=1, source_target_pairs={{0,3},{1,2},{2,1},{3,0},{4,7},{5,6},{6,5},{7,4},{8,11},{9,10},{10,... | collective-permute-start | bytes 276488 | tf_op jit(solution)/shard_map/ppermute | solution.py:43
  25.1 6.8 %collective-permute-start.4 = (bf16[72,640]{1,0:T(8,128)(2,1)S(1)}, bf16[72,640]{1,0:T(8,128)(2,1)S(1)}, u32[]{:S(2)}, u32[]{:S(2)}) collective-permute-start(bf16[72,640]{1,0:T(8,128)(2,1)S(1)} %pad_maximum_fusion.7), channel_id=1, source_target_pairs={{0,2},{1,3},{2,0},{3,1},{4,6},{5,7},{6,4},{7,5},{8,10},{9,11},{10,... | collective-permute-start | bytes 276488 | tf_op jit(solution)/shard_map/ppermute | solution.py:43
  25.1 6.8 %collective-permute-start.3 = (bf16[72,640]{1,0:T(8,128)(2,1)S(1)}, bf16[72,640]{1,0:T(8,128)(2,1)S(1)}, u32[]{:S(2)}, u32[]{:S(2)}) collective-permute-start(bf16[72,640]{1,0:T(8,128)(2,1)S(1)} %pad_maximum_fusion.7), channel_id=1, source_target_pairs={{0,1},{1,0},{2,3},{3,2},{4,5},{5,4},{6,7},{7,6},{8,9},{9,8},{10,11... | collective-permute-start | bytes 276488 | tf_op jit(solution)/shard_map/ppermute | solution.py:43
  25.7 7.7 %collective-permute-start.6 = (bf16[384,256]{1,0:T(8,128)(2,1)S(1)}, bf16[384,256]{1,0:T(8,128)(2,1)S(1)}, u32[]{:S(2)}, u32[]{:S(2)}) collective-permute-start(bf16[384,256]{1,0:T(8,128)(2,1)S(1)} %fusion.19.refs_0_), channel_id=1, source_target_pairs={{0,8},{4,12},{8,0},{12,4},{16,24},{20,28},{24,16},{28,20},{1,9},{5... | collective-permute-start | bytes 589832 | tf_op jit(solution)/shard_map/ppermute | solution.py:43
  27.4 9.3 %collective-permute-start.7 = (bf16[384,256]{1,0:T(8,128)(2,1)S(1)}, bf16[384,256]{1,0:T(8,128)(2,1)S(1)}, u32[]{:S(2)}, u32[]{:S(2)}) collective-permute-start(bf16[384,256]{1,0:T(8,128)(2,1)S(1)} %fusion.19.refs_0_), channel_id=1, source_target_pairs={{0,16},{4,20},{8,24},{12,28},{16,0},{20,4},{24,8},{28,12},{1,17},{... | collective-permute-start | bytes 589832 | tf_op jit(solution)/shard_map/ppermute | solution.py:43
  28.9 7.8 %collective-permute-start.8 = (bf16[384,256]{1,0:T(8,128)(2,1)S(1)}, bf16[384,256]{1,0:T(8,128)(2,1)S(1)}, u32[]{:S(2)}, u32[]{:S(2)}) collective-permute-start(bf16[384,256]{1,0:T(8,128)(2,1)S(1)} %fusion.19.refs_0_), channel_id=1, source_target_pairs={{0,24},{4,28},{8,16},{12,20},{16,8},{20,12},{24,0},{28,4},{1,25},{... | collective-permute-start | bytes 589832 | tf_op jit(solution)/shard_map/ppermute | solution.py:43
  32.1 25.8 %copy-start.6 = (bf16[288,640]{1,0:T(8,128)(2,1)}, bf16[288,640]{1,0:T(8,128)(2,1)S(1)}, u32[]{:S(2)}) copy-start(bf16[288,640]{1,0:T(8,128)(2,1)S(1)} %pad_maximum_fusion.1.refs_0_) | copy-start | bytes 1105924
  32.1 26.9 %copy-start.34 = (s32[2,2,32,3]{2,1,3,0:T(2,128)S(1)}, s32[2,2,32,3]{2,1,3,0:T(2,128)}, u32[]{:S(2)}) copy-start(s32[2,2,32,3]{2,1,3,0:T(2,128)} %param.27) | copy-start | bytes 4612
  32.1 26.9 %copy-start.27 = (s32[2,4,64,3]{2,1,3,0:T(4,128)S(1)}, s32[2,4,64,3]{2,1,3,0:T(4,128)}, u32[]{:S(2)}) copy-start(s32[2,4,64,3]{2,1,3,0:T(4,128)} %param.26) | copy-start | bytes 18436
  32.1 26.9 %copy-start.23 = (s32[2,8,128,3]{2,1,3,0:T(8,128)S(1)}, s32[2,8,128,3]{2,1,3,0:T(8,128)}, u32[]{:S(2)}) copy-start(s32[2,8,128,3]{2,1,3,0:T(8,128)} %param.25) | copy-start | bytes 73732
  32.1 27.0 %copy-start.33 = (f32[2,2,32,12]{2,1,3,0:T(2,128)S(1)}, f32[2,2,32,12]{2,1,3,0:T(2,128)}, u32[]{:S(2)}) copy-start(f32[2,2,32,12]{2,1,3,0:T(2,128)} %param.24) | copy-start | bytes 18436
  32.1 27.0 %copy-start.26 = (f32[2,4,64,12]{2,1,3,0:T(4,128)S(1)}, f32[2,4,64,12]{2,1,3,0:T(4,128)}, u32[]{:S(2)}) copy-start(f32[2,4,64,12]{2,1,3,0:T(4,128)} %param.23) | copy-start | bytes 73732
  32.2 27.1 %copy-start.22 = (f32[2,8,128,12]{2,1,3,0:T(8,128)S(1)}, f32[2,8,128,12]{2,1,3,0:T(8,128)}, u32[]{:S(2)}) copy-start(f32[2,8,128,12]{2,1,3,0:T(8,128)} %param.22) | copy-start | bytes 294916
  36.7 2.0 collective-permute-start.9
  36.8 3.3 %collective-permute-start.10 = (bf16[384,256]{1,0:T(8,128)(2,1)S(1)}, bf16[384,256]{1,0:T(8,128)(2,1)S(1)}, u32[]{:S(2)}, u32[]{:S(2)}) collective-permute-start(bf16[384,256]{1,0:T(8,128)(2,1)S(1)} %collective-permute-done.6.refs_2_), channel_id=1, source_target_pairs={{0,4},{4,0},{8,12},{12,8},{16,20},{20,16},{24,28},{28,24},{1,5},{5... | collective-permute-start | bytes 589832 | tf_op jit(solution)/shard_map/ppermute | solution.py:43
  37.3 4.0 %collective-permute-start.11 = (bf16[384,256]{1,0:T(8,128)(2,1)S(1)}, bf16[384,256]{1,0:T(8,128)(2,1)S(1)}, u32[]{:S(2)}, u32[]{:S(2)}) collective-permute-start(bf16[384,256]{1,0:T(8,128)(2,1)S(1)} %collective-permute-done.7.refs_4_), channel_id=1, source_target_pairs={{0,4},{4,0},{8,12},{12,8},{16,20},{20,16},{24,28},{28,24},{1,5},{5... | collective-permute-start | bytes 589832 | tf_op jit(solution)/shard_map/ppermute | solution.py:43
  37.3 3.9 %collective-permute-start.12 = (bf16[384,256]{1,0:T(8,128)(2,1)S(1)}, bf16[384,256]{1,0:T(8,128)(2,1)S(1)}, u32[]{:S(2)}, u32[]{:S(2)}) collective-permute-start(bf16[384,256]{1,0:T(8,128)(2,1)S(1)} %collective-permute-done.8.refs_6_), channel_id=1, source_target_pairs={{0,4},{4,0},{8,12},{12,8},{16,20},{20,16},{24,28},{28,24},{1,5},{5... | collective-permute-start | bytes 589832 | tf_op jit(solution)/shard_map/ppermute | solution.py:43
  37.8 13.0 %collective-permute-start.15 = (bf16[288,640]{1,0:T(8,128)(2,1)S(1)}, bf16[288,640]{1,0:T(8,128)(2,1)S(1)}, u32[]{:S(2)}, u32[]{:S(2)}) collective-permute-start(bf16[288,640]{1,0:T(8,128)(2,1)S(1)} %pad_maximum_fusion.1.refs_0_), channel_id=1, source_target_pairs={{0,8},{4,12},{8,0},{12,4},{16,24},{20,28},{24,16},{28,20},{1,9},{5... | collective-permute-start | bytes 1105928 | tf_op jit(solution)/shard_map/ppermute | solution.py:43
  38.7 19.3 %collective-permute-start.16 = (bf16[288,640]{1,0:T(8,128)(2,1)S(1)}, bf16[288,640]{1,0:T(8,128)(2,1)S(1)}, u32[]{:S(2)}, u32[]{:S(2)}) collective-permute-start(bf16[288,640]{1,0:T(8,128)(2,1)S(1)} %pad_maximum_fusion.1.refs_0_), channel_id=1, source_target_pairs={{0,16},{4,20},{8,24},{12,28},{16,0},{20,4},{24,8},{28,12},{1,17},{... | collective-permute-start | bytes 1105928 | tf_op jit(solution)/shard_map/ppermute | solution.py:43
  40.1 17.8 %collective-permute-start.17 = (bf16[288,640]{1,0:T(8,128)(2,1)S(1)}, bf16[288,640]{1,0:T(8,128)(2,1)S(1)}, u32[]{:S(2)}, u32[]{:S(2)}) collective-permute-start(bf16[288,640]{1,0:T(8,128)(2,1)S(1)} %pad_maximum_fusion.1.refs_0_), channel_id=1, source_target_pairs={{0,24},{4,28},{8,16},{12,20},{16,8},{20,12},{24,0},{28,4},{1,25},{... | collective-permute-start | bytes 1105928 | tf_op jit(solution)/shard_map/ppermute | solution.py:43
  48.8 10.8 %collective-permute-start.13 = (bf16[2,192,256]{2,1,0:T(8,128)(2,1)}, bf16[2,192,256]{2,1,0:T(8,128)(2,1)}, u32[]{:S(2)}, u32[]{:S(2)}) collective-permute-start(bf16[2,192,256]{2,1,0:T(8,128)(2,1)} %get-tuple-element.63), channel_id=1, source_target_pairs={{0,4},{4,8},{8,12},{12,16},{16,20},{20,24},{24,28},{1,5},{5,9},{9,... | collective-permute-start | bytes 589832 | tf_op jit(solution)/shard_map/ppermute | solution.py:100
  50.8 12.4 %copy-start.37 = (bf16[288,640]{1,0:T(8,128)(2,1)}, bf16[288,640]{1,0:T(8,128)(2,1)S(1)}, u32[]{:S(2)}) copy-start(bf16[288,640]{1,0:T(8,128)(2,1)S(1)} %collective-permute-done.15.refs_2_) | copy-start | bytes 1105924
  57.9 5.2 %collective-permute-start.18 = (bf16[288,640]{1,0:T(8,128)(2,1)S(1)}, bf16[288,640]{1,0:T(8,128)(2,1)S(1)}, u32[]{:S(2)}, u32[]{:S(2)}) collective-permute-start(bf16[288,640]{1,0:T(8,128)(2,1)S(1)} %pad_maximum_fusion.1.refs_0_), channel_id=1, source_target_pairs={{0,4},{4,0},{8,12},{12,8},{16,20},{20,16},{24,28},{28,24},{1,5},{5... | collective-permute-start | bytes 1105928 | tf_op jit(solution)/shard_map/ppermute | solution.py:43
  58.0 5.1 %collective-permute-start.19 = (bf16[288,640]{1,0:T(8,128)(2,1)S(1)}, bf16[288,640]{1,0:T(8,128)(2,1)S(1)}, u32[]{:S(2)}, u32[]{:S(2)}) collective-permute-start(bf16[288,640]{1,0:T(8,128)(2,1)S(1)} %collective-permute-done.15.refs_2_), channel_id=1, source_target_pairs={{0,4},{4,0},{8,12},{12,8},{16,20},{20,16},{24,28},{28,24},{1,5},{5... | collective-permute-start | bytes 1105928 | tf_op jit(solution)/shard_map/ppermute | solution.py:43
  58.5 4.6 %collective-permute-start.20 = (bf16[288,640]{1,0:T(8,128)(2,1)S(1)}, bf16[288,640]{1,0:T(8,128)(2,1)S(1)}, u32[]{:S(2)}, u32[]{:S(2)}) collective-permute-start(bf16[288,640]{1,0:T(8,128)(2,1)S(1)} %collective-permute-done.16.refs_4_), channel_id=1, source_target_pairs={{0,4},{4,0},{8,12},{12,8},{16,20},{20,16},{24,28},{28,24},{1,5},{5... | collective-permute-start | bytes 1105928 | tf_op jit(solution)/shard_map/ppermute | solution.py:43
  58.6 4.6 %collective-permute-start.21 = (bf16[288,640]{1,0:T(8,128)(2,1)S(1)}, bf16[288,640]{1,0:T(8,128)(2,1)S(1)}, u32[]{:S(2)}, u32[]{:S(2)}) collective-permute-start(bf16[288,640]{1,0:T(8,128)(2,1)S(1)} %collective-permute-done.17.refs_6_), channel_id=1, source_target_pairs={{0,4},{4,0},{8,12},{12,8},{16,20},{20,16},{24,28},{28,24},{1,5},{5... | collective-permute-start | bytes 1105928 | tf_op jit(solution)/shard_map/ppermute | solution.py:43
  59.6 3.5 %collective-permute-start.14 = (bf16[2,192,256]{2,1,0:T(8,128)(2,1)}, bf16[2,192,256]{2,1,0:T(8,128)(2,1)S(1)}, u32[]{:S(2)}, u32[]{:S(2)}) collective-permute-start(bf16[2,192,256]{2,1,0:T(8,128)(2,1)} %get-tuple-element.64), channel_id=1, source_target_pairs={{4,0},{8,4},{12,8},{16,12},{20,16},{24,20},{28,24},{5,1},{9,5},{13... | collective-permute-start | bytes 589832 | tf_op jit(solution)/shard_map/ppermute | solution.py:101
  71.5 7.8 %collective-permute-start.22 = (bf16[2,224,256]{2,1,0:T(8,128)(2,1)}, bf16[2,224,256]{2,1,0:T(8,128)(2,1)S(1)}, u32[]{:S(2)}, u32[]{:S(2)}) collective-permute-start(bf16[2,224,256]{2,1,0:T(8,128)(2,1)} %get-tuple-element.72), channel_id=1, source_target_pairs={{0,4},{4,8},{8,12},{12,16},{16,20},{20,24},{24,28},{1,5},{5,9},{9,... | collective-permute-start | bytes 688136 | tf_op jit(solution)/shard_map/ppermute | solution.py:100
  77.1 3.6 %collective-permute-start.23 = (bf16[2,224,256]{2,1,0:T(8,128)(2,1)}, bf16[2,224,256]{2,1,0:T(8,128)(2,1)S(1)}, u32[]{:S(2)}, u32[]{:S(2)}) collective-permute-start(bf16[2,224,256]{2,1,0:T(8,128)(2,1)} %get-tuple-element.73), channel_id=1, source_target_pairs={{4,0},{8,4},{12,8},{16,12},{20,16},{24,20},{28,24},{5,1},{9,5},{13... | collective-permute-start | bytes 688136 | tf_op jit(solution)/shard_map/ppermute | solution.py:101
  85.6 13.6 %collective-permute-start.24 = (bf16[2,16,384]{2,1,0:T(8,128)(2,1)}, bf16[2,16,384]{2,1,0:T(8,128)(2,1)S(1)}, u32[]{:S(2)}, u32[]{:S(2)}) collective-permute-start(bf16[2,16,384]{2,1,0:T(8,128)(2,1)} %get-tuple-element.76), channel_id=1, source_target_pairs={{0,4},{4,8},{8,12},{12,16},{16,20},{20,24},{24,28},{1,5},{5,9},{9,... | collective-permute-start | bytes 73736 | tf_op jit(solution)/shard_map/ppermute | solution.py:100
  92.1 7.1 %collective-permute-start.25 = (bf16[2,16,384]{2,1,0:T(8,128)(2,1)}, bf16[2,16,384]{2,1,0:T(8,128)(2,1)S(1)}, u32[]{:S(2)}, u32[]{:S(2)}) collective-permute-start(bf16[2,16,384]{2,1,0:T(8,128)(2,1)} %get-tuple-element.77), channel_id=1, source_target_pairs={{4,0},{8,4},{12,8},{16,12},{20,16},{24,20},{28,24},{5,1},{9,5},{13... | collective-permute-start | bytes 73736 | tf_op jit(solution)/shard_map/ppermute | solution.py:101
  112.7 16.2 %collective-permute-start.28 = (bf16[4,288,640]{2,1,0:T(8,128)(2,1)S(1)}, bf16[4,288,640]{2,1,0:T(8,128)(2,1)S(1)}, u32[]{:S(2)}, u32[]{:S(2)}) collective-permute-start(bf16[4,288,640]{2,1,0:T(8,128)(2,1)S(1)} %slice_bitcast_fusion), channel_id=1, source_target_pairs={{0,4},{4,0},{8,12},{12,8},{16,20},{20,16},{24,28},{28,24},{1,5},{5... | collective-permute-start | bytes 4423688 | tf_op jit(solution)/shard_map/ppermute | solution.py:43
  113.9 3.5 %collective-permute-start.26 = (bf16[2,192,256]{2,1,0:T(8,128)(2,1)S(1)}, bf16[2,192,256]{2,1,0:T(8,128)(2,1)S(1)}, u32[]{:S(2)}, u32[]{:S(2)}) collective-permute-start(bf16[2,192,256]{2,1,0:T(8,128)(2,1)S(1)} %copy-done.46), channel_id=1, source_target_pairs={{0,4},{4,8},{8,12},{12,16},{16,20},{20,24},{24,28},{1,5},{5,9},{9,... | collective-permute-start | bytes 589832 | tf_op jit(solution)/shard_map/ppermute | solution.py:100
  115.9 5.4 %collective-permute-start.27 = (bf16[2,192,256]{2,1,0:T(8,128)(2,1)S(1)}, bf16[2,192,256]{2,1,0:T(8,128)(2,1)S(1)}, u32[]{:S(2)}, u32[]{:S(2)}) collective-permute-start(bf16[2,192,256]{2,1,0:T(8,128)(2,1)S(1)} %copy-done.45), channel_id=1, source_target_pairs={{4,0},{8,4},{12,8},{16,12},{20,16},{24,20},{28,24},{5,1},{9,5},{13... | collective-permute-start | bytes 589832 | tf_op jit(solution)/shard_map/ppermute | solution.py:101
  137.4 10.7 %copy-start.4 = (f32[2,72,256]{2,1,0:T(8,128)S(1)}, f32[2,72,256]{2,1,0:T(8,128)}, u32[]{:S(2)}) copy-start(f32[2,72,256]{2,1,0:T(8,128)} %param.30) | copy-start | bytes 442372
  137.4 10.9 %copy-start.20 = (f32[2,72,256]{2,1,0:T(8,128)S(1)}, f32[2,72,256]{2,1,0:T(8,128)}, u32[]{:S(2)}) copy-start(f32[2,72,256]{2,1,0:T(8,128)} %param.38) | copy-start | bytes 442372
  137.4 11.7 %copy-start.21 = (f32[2,72,256]{2,1,0:T(8,128)S(1)}, f32[2,72,256]{2,1,0:T(8,128)}, u32[]{:S(2)}) copy-start(f32[2,72,256]{2,1,0:T(8,128)} %param.34) | copy-start | bytes 442372
  139.6 25.5 %collective-permute-start.29 = (bf16[4,384,256]{2,1,0:T(8,128)(2,1)}, bf16[4,384,256]{2,1,0:T(8,128)(2,1)}, u32[]{:S(2)}, u32[]{:S(2)}) collective-permute-start(bf16[4,384,256]{2,1,0:T(8,128)(2,1)} %slice_bitcast_fusion.1), channel_id=1, source_target_pairs={{0,4},{4,0},{8,12},{12,8},{16,20},{20,16},{24,28},{28,24},{1,5},{5... | collective-permute-start | bytes 2359304 | tf_op jit(solution)/shard_map/ppermute | solution.py:43
  143.7 12.7 %collective-permute-start.32 = (bf16[288,640]{1,0:T(8,128)(2,1)}, bf16[288,640]{1,0:T(8,128)(2,1)}, u32[]{:S(2)}, u32[]{:S(2)}) collective-permute-start(bf16[288,640]{1,0:T(8,128)(2,1)} %get-tuple-element.92), channel_id=1, source_target_pairs={{0,24},{4,28},{8,16},{12,20},{16,8},{20,12},{24,0},{28,4},{1,25},{... | collective-permute-start | bytes 1105928 | tf_op jit(solution)/shard_map/ppermute | solution.py:43
  143.9 19.5 %collective-permute-start.31 = (bf16[288,640]{1,0:T(8,128)(2,1)}, bf16[288,640]{1,0:T(8,128)(2,1)}, u32[]{:S(2)}, u32[]{:S(2)}) collective-permute-start(bf16[288,640]{1,0:T(8,128)(2,1)} %get-tuple-element.91), channel_id=1, source_target_pairs={{0,16},{4,20},{8,24},{12,28},{16,0},{20,4},{24,8},{28,12},{1,17},{... | collective-permute-start | bytes 1105928 | tf_op jit(solution)/shard_map/ppermute | solution.py:43
  148.2 15.5 %collective-permute-start.30 = (bf16[288,640]{1,0:T(8,128)(2,1)S(1)}, bf16[288,640]{1,0:T(8,128)(2,1)}, u32[]{:S(2)}, u32[]{:S(2)}) collective-permute-start(bf16[288,640]{1,0:T(8,128)(2,1)S(1)} %get-tuple-element.90), channel_id=1, source_target_pairs={{0,8},{4,12},{8,0},{12,4},{16,24},{20,28},{24,16},{28,20},{1,9},{5... | collective-permute-start | bytes 1105928 | tf_op jit(solution)/shard_map/ppermute | solution.py:43
  149.1 15.9 %copy-start = (bf16[8,384,256]{2,1,0:T(8,128)(2,1)S(1)}, bf16[8,384,256]{2,1,0:T(8,128)(2,1)}, u32[]{:S(2)}) copy-start(bf16[8,384,256]{2,1,0:T(8,128)(2,1)} %lateral_grads.1) | copy-start | bytes 4718596
  168.1 8.7 %copy-start.11 = (bf16[384,256]{1,0:T(8,128)(2,1)S(1)}, bf16[384,256]{1,0:T(8,128)(2,1)}, u32[]{:S(2)}) copy-start(bf16[384,256]{1,0:T(8,128)(2,1)} %get-tuple-element.96) | copy-start | bytes 589828
  168.3 19.1 %copy-start.2 = (f32[2,72,256]{1,2,0:T(8,128)S(1)}, f32[2,72,256]{1,2,0:T(8,128)}, u32[]{:S(2)}) copy-start(f32[2,72,256]{1,2,0:T(8,128)} %copy.59) | copy-start | bytes 442372
  168.3 19.1 %copy-start.3 = (f32[2,72,256]{1,2,0:T(8,128)S(1)}, f32[2,72,256]{1,2,0:T(8,128)}, u32[]{:S(2)}) copy-start(f32[2,72,256]{1,2,0:T(8,128)} %copy.58) | copy-start | bytes 442372
  168.3 9.1 %collective-permute-start.35 = (bf16[72,640]{0,1:T(8,128)(2,1)S(1)}, bf16[72,640]{0,1:T(8,128)(2,1)}, u32[]{:S(2)}, u32[]{:S(2)}) collective-permute-start(bf16[72,640]{0,1:T(8,128)(2,1)S(1)} %bitcast.213), channel_id=1, source_target_pairs={{0,3},{1,2},{2,1},{3,0},{4,7},{5,6},{6,5},{7,4},{8,11},{9,10},{10,... | collective-permute-start | bytes 276488 | tf_op jit(solution)/shard_map/ppermute | solution.py:43
  172.1 14.0 %collective-permute-start.34 = (bf16[72,640]{0,1:T(8,128)(2,1)S(1)}, bf16[72,640]{0,1:T(8,128)(2,1)}, u32[]{:S(2)}, u32[]{:S(2)}) collective-permute-start(bf16[72,640]{0,1:T(8,128)(2,1)S(1)} %bitcast.212), channel_id=1, source_target_pairs={{0,2},{1,3},{2,0},{3,1},{4,6},{5,7},{6,4},{7,5},{8,10},{9,11},{10,... | collective-permute-start | bytes 276488 | tf_op jit(solution)/shard_map/ppermute | solution.py:43
  173.0 13.1 %collective-permute-start.33 = (bf16[72,640]{0,1:T(8,128)(2,1)}, bf16[72,640]{0,1:T(8,128)(2,1)}, u32[]{:S(2)}, u32[]{:S(2)}) collective-permute-start(bf16[72,640]{0,1:T(8,128)(2,1)} %bitcast.194), channel_id=1, source_target_pairs={{0,1},{1,0},{2,3},{3,2},{4,5},{5,4},{6,7},{7,6},{8,9},{9,8},{10,11... | collective-permute-start | bytes 276488 | tf_op jit(solution)/shard_map/ppermute | solution.py:43
  174.0 13.6 %copy-start.30 = (f32[72,12]{0,1:T(8,128)S(1)}, f32[72,12]{0,1:T(8,128)}, u32[]{:S(2)}) copy-start(f32[72,12]{0,1:T(8,128)} %param.31) | copy-start | bytes 10372
  174.0 13.6 %copy-start.35 = (f32[72,12]{0,1:T(8,128)S(1)}, f32[72,12]{0,1:T(8,128)}, u32[]{:S(2)}) copy-start(f32[72,12]{0,1:T(8,128)} %param.39) | copy-start | bytes 10372
  174.0 13.6 %copy-start.36 = (f32[72,12]{0,1:T(8,128)S(1)}, f32[72,12]{0,1:T(8,128)}, u32[]{:S(2)}) copy-start(f32[72,12]{0,1:T(8,128)} %param.35) | copy-start | bytes 10372
  174.0 14.2 %collective-permute-start.38 = (bf16[384,256]{1,0:T(8,128)(2,1)S(1)}, bf16[384,256]{1,0:T(8,128)(2,1)S(1)}, u32[]{:S(2)}, u32[]{:S(2)}) collective-permute-start(bf16[384,256]{1,0:T(8,128)(2,1)S(1)} %copy-done.12), channel_id=1, source_target_pairs={{0,24},{4,28},{8,16},{12,20},{16,8},{20,12},{24,0},{28,4},{1,25},{... | collective-permute-start | bytes 589832 | tf_op jit(solution)/shard_map/ppermute | solution.py:43
  176.7 11.5 %collective-permute-start.37 = (bf16[384,256]{1,0:T(8,128)(2,1)S(1)}, bf16[384,256]{1,0:T(8,128)(2,1)S(1)}, u32[]{:S(2)}, u32[]{:S(2)}) collective-permute-start(bf16[384,256]{1,0:T(8,128)(2,1)S(1)} %copy-done.11), channel_id=1, source_target_pairs={{0,16},{4,20},{8,24},{12,28},{16,0},{20,4},{24,8},{28,12},{1,17},{... | collective-permute-start | bytes 589832 | tf_op jit(solution)/shard_map/ppermute | solution.py:43
  177.4 10.8 %collective-permute-start.36 = (bf16[384,256]{1,0:T(8,128)(2,1)S(1)}, bf16[384,256]{1,0:T(8,128)(2,1)S(1)}, u32[]{:S(2)}, u32[]{:S(2)}) collective-permute-start(bf16[384,256]{1,0:T(8,128)(2,1)S(1)} %get-tuple-element.95), channel_id=1, source_target_pairs={{0,8},{4,12},{8,0},{12,4},{16,24},{20,28},{24,16},{28,20},{1,9},{5... | collective-permute-start | bytes 589832 | tf_op jit(solution)/shard_map/ppermute | solution.py:43
  188.4 8.7 %copy-start.5 = (f32[64,256]{1,0:T(8,128)S(1)}, f32[64,256]{1,0:T(8,128)}, u32[]{:S(2)}) copy-start(f32[64,256]{1,0:T(8,128)} %param.29) | copy-start | bytes 196612
  188.4 8.7 %copy-start.24 = (f32[64,256]{1,0:T(8,128)S(1)}, f32[64,256]{1,0:T(8,128)}, u32[]{:S(2)}) copy-start(f32[64,256]{1,0:T(8,128)} %param.37) | copy-start | bytes 196612
  188.4 8.7 %copy-start.25 = (f32[64,256]{1,0:T(8,128)S(1)}, f32[64,256]{1,0:T(8,128)}, u32[]{:S(2)}) copy-start(f32[64,256]{1,0:T(8,128)} %param.33) | copy-start | bytes 196612
  188.5 7.4 %collective-permute-start.41 = (bf16[96,256]{1,0:T(8,128)(2,1)S(1)}, bf16[96,256]{1,0:T(8,128)(2,1)S(1)}, u32[]{:S(2)}, u32[]{:S(2)}) collective-permute-start(bf16[96,256]{1,0:T(8,128)(2,1)S(1)} %get-tuple-element.163), channel_id=1, source_target_pairs={{0,3},{1,2},{2,1},{3,0},{4,7},{5,6},{6,5},{7,4},{8,11},{9,10},{10,... | collective-permute-start | bytes 147464 | tf_op jit(solution)/shard_map/ppermute | solution.py:43
  191.2 5.1 %collective-permute-start.40 = (bf16[96,256]{1,0:T(8,128)(2,1)S(1)}, bf16[96,256]{1,0:T(8,128)(2,1)S(1)}, u32[]{:S(2)}, u32[]{:S(2)}) collective-permute-start(bf16[96,256]{1,0:T(8,128)(2,1)S(1)} %get-tuple-element.162), channel_id=1, source_target_pairs={{0,2},{1,3},{2,0},{3,1},{4,6},{5,7},{6,4},{7,5},{8,10},{9,11},{10,... | collective-permute-start | bytes 147464 | tf_op jit(solution)/shard_map/ppermute | solution.py:43
  191.8 4.6 %collective-permute-start.39 = (bf16[96,256]{1,0:T(8,128)(2,1)S(1)}, bf16[96,256]{1,0:T(8,128)(2,1)S(1)}, u32[]{:S(2)}, u32[]{:S(2)}) collective-permute-start(bf16[96,256]{1,0:T(8,128)(2,1)S(1)} %get-tuple-element.161), channel_id=1, source_target_pairs={{0,1},{1,0},{2,3},{3,2},{4,5},{5,4},{6,7},{7,6},{8,9},{9,8},{10,11... | collective-permute-start | bytes 147464 | tf_op jit(solution)/shard_map/ppermute | solution.py:43
  (27 other events, 90.2 us)

commit v2 on v1

--- a/solution.py
+++ b/solution.py
@@ -72,7 +72,12 @@
 
 def summed_low(blocks):
     _, low, high = row_groups()
-    came = [sent(blocks[k], "rows", k) for k in range(1, low)]
+    came = []
+    for k in range(1, low):
+        whole = isinstance(blocks[k], jax.Array)
+        came.append(
+            sent(blocks[k], "rows", k) if whole else [sent(block, "rows", k) for block in blocks[k]]
+        )
     return [
         sum((c[j].astype(f32) for c in came), blocks[0][j].astype(f32)) for j in range(high)
     ]
@@ -86,13 +91,14 @@
     )
 
 
-def summed_batch(blocks):
+def shared_batch(blocks):
     count, me = lax.axis_size("batch"), lax.axis_index("batch")
-    total = lax.dynamic_index_in_dim(blocks, me, 0, keepdims=False)
+    own = lax.dynamic_index_in_dim(blocks, me, 0, keepdims=False)
+    came = []
     for k in range(1, count):
         block = lax.dynamic_index_in_dim(blocks, me ^ k, 0, keepdims=False).astype(bf16)
-        total = total + sent(block, "batch", k).astype(f32)
-    return total
+        came.append(sent(block, "batch", k))
+    return [own, *came]
 
 
 def from_neighbours(first, last):
@@ -100,12 +106,6 @@
     above = lax.ppermute(last, "rows", [(i, i + 1) for i in range(count - 1)])
     below = lax.ppermute(first, "rows", [(i + 1, i) for i in range(count - 1)])
     return above, below
-
-
-def thirds(value):
-    high = lax.reduce_precision(value, 8, 7)
-    middle = lax.reduce_precision(value - high, 8, 7)
-    return high, middle, value - high - middle
 
 
 def call(kernel, name, args, outs, scratch=(), flops=0, scalars=0, scalar_outs=0):
@@ -141,6 +141,35 @@
         ref[h, pl.ds(0, count, stride=2), :] = part
         ref[h, pl.ds(1, count, stride=2), :] = part
     return jnp.concatenate([ref[h] for h in range(ref.shape[0])], axis=1)
+
+
+def pieces_of(value):
+    high = value.astype(bf16).astype(f32)
+    middle = (value - high).astype(bf16).astype(f32)
+    return high, middle, value - high - middle
+
+
+def pack_lateral_kernel(four, five, packed):
+    packed[: four.shape[0]] = four[...].astype(bf16)
+    packed[four.shape[0] :] = five[...].astype(bf16)
+
+
+def pack_conv_kernel(conv, head, anchor_four, anchor_five, anchor_six, packed, square):
+    lines, channels = conv.shape[1:]
+    deltas = head.shape[0]
+    total = jnp.zeros((1, 1), f32)
+    for anchor in (anchor_four, anchor_five, anchor_six):
+        total = total + jnp.sum(anchor[...].astype(f32), keepdims=True).reshape(1, 1)
+    square[...] = jnp.zeros_like(square)
+    square[:deltas, :lines] = head[...]
+    spare = square[...].T[:lines]
+    line = lax.broadcasted_iota(jnp.int32, spare.shape, 0)
+    lane = lax.broadcasted_iota(jnp.int32, spare.shape, 1)
+    for k, piece in enumerate(pieces_of(jnp.broadcast_to(total, spare.shape))):
+        spare = jnp.where((line == 0) & (lane == deltas + k), piece, spare)
+    packed[:, :channels] = conv[0].astype(bf16)
+    packed[:, channels : 2 * channels] = conv[1].astype(bf16)
+    packed[:, 2 * channels :] = spare.astype(bf16)
 
 
 def lateral_kernel(n_rows, four, five, *refs):
@@ -204,8 +233,8 @@
         padded[b, height + 1] = below[b, start : start + width]
 
 
-def output_kernel(n_rows, deltas, input_four, input_five, above, below, *refs):
-    pieces, (levels, first, last, kernel_four, kernel_five, head, count, spread_four, spread_five, wide) = (
+def output_kernel(n_rows, deltas, input_four, input_five, above, below, target, mask, *refs):
+    pieces, (levels, values, first, last, kernel_four, kernel_five, head, count, spread_four, spread_five, wide) = (
         refs[:n_rows],
         refs[n_rows:],
     )
@@ -246,8 +275,6 @@
         low = three_taps(spread_five, b, 0, low_height, kernel_five, 1)
         low_rounded = low.astype(bf16).reshape(low_height, low_width, channels)
         levels[b, low_start:top_start, :low_width, :] = low_rounded
-        first[b, width : width + low_width] = low_rounded[0]
-        last[b, width : width + low_width] = low_rounded[low_height - 1]
         for h in range(0, channels, LANES):
             spare[: low_height * low_width, :] = low[:, h : h + LANES]
             for q in range(low_height // 2):
@@ -257,91 +284,90 @@
                         total = total + spare[pl.ds(at + side, quarter, stride=2), :]
                 pooled = (0.25 * total).astype(bf16)
                 levels[b, top_start + q, :quarter, h : h + LANES] = pooled
-                if q == 0:
-                    first[b, width + low_width :, h : h + LANES] = pooled
-                if q == low_height // 2 - 1:
-                    last[b, width + low_width :, h : h + LANES] = pooled
         for r in range(0, height, rows):
             sums = three_taps(spread_four, b, r, rows, kernel_four, 1)
             rounded = sums.astype(bf16).reshape(rows, width, channels)
             levels[b, r : r + rows] = rounded
-            if r == 0:
-                first[b, :width] = rounded[0]
-            if r == height - rows:
-                last[b, :width] = rounded[rows - 1]
-
-
-def level_rows(height):
+        lines_all = levels.shape[1]
+        products = dot(
+            head[...], levels[b].reshape(lines_all * width, channels), ((1,), (1,))
+        )
+        none = jnp.zeros((products.shape[0], 2 * width), f32)
+        columns = []
+        for j in range(3):
+            pieces = []
+            for _, own, count_lines in level_rows(height, 1):
+                padded = jnp.concatenate(
+                    [none, products[:, own * width : (own + count_lines) * width], none], axis=1
+                )
+                total = jnp.zeros((DELTA_ROWS, (count_lines + 2) * width), f32)
+                for i in range(3):
+                    tap = (3 * i + j) * DELTA_ROWS
+                    at = slice(i * width, (i + count_lines + 2) * width)
+                    total = total + padded[tap : tap + DELTA_ROWS, at]
+                pieces.append(total)
+            columns.append(jnp.concatenate(pieces, axis=1))
+        sums = columns[1] + turned(columns[0], 1, 1, width) + turned(columns[2], -1, 1, width)
+        for index, (padded, own, count_lines) in enumerate(level_rows(height, 1)):
+            own_at = slice(own * width, (own + count_lines) * width)
+            start, end = padded * width, (padded + count_lines + 2) * width
+            partial = sums[:, start + width : end - width] - target[b, :, own_at]
+            values[b, :, start : start + width] = sums[:, start : start + width]
+            values[b, :, start + width : end - width] = partial
+            values[b, :, end - width : end] = sums[:, end - width : end]
+            at = slice(index * width, (index + 1) * width)
+            first[b, 0, :, at] = partial[:, :width]
+            last[b, 0, :, at] = partial[:, (count_lines - 1) * width :]
+            first[b, 1, :, at] = sums[:, start : start + width]
+            last[b, 1, :, at] = sums[:, end - width : end]
+            first[b, 2, :, at] = mask[b, :, own * width : (own + 1) * width]
+            last[b, 2, :, at] = mask[b, :, (own + count_lines - 1) * width : (own + count_lines) * width]
+
+
+def level_rows(height, rim):
     result, padded, own = [], 0, 0
     for count in (height, height // 2, height // 4):
         result.append((padded, own, count))
-        padded, own = padded + count + 2, own + count
+        padded, own = padded + count + 2 * rim, own + count
     return result
 
 
-def head_kernel(height, levels, above, below, head, target, mask, count, grads, first, last, loss, spread):
+def head_kernel(height, levels, above, below, head, values, mask, count, head_grad, grad_four, grad_five, first, last, loss, taps, wide):
     crops, _, width, channels = levels.shape
     inverse = 1.0 / jnp.maximum(count[0, 0], 1.0)
-    plan = level_rows(height)
+    plan = level_rows(height, 1)
     summed = jnp.zeros((DELTA_ROWS, LANES), f32)
+    total_grad = jnp.zeros((9 * DELTA_ROWS, channels), f32)
+    low_height, low_width = height // 2, width // 2
     for b in range(crops):
-        edge = 0
+        partial, weights = [], []
         for index, (padded, own, lines) in enumerate(plan):
-            extent = width >> index
-            for at, rim in ((padded, above), (padded + lines + 1, below)):
-                spread[at, :extent] = rim[b, edge : edge + extent]
-                if extent < width:
-                    spread[at, extent:] = jnp.zeros((width - extent, channels), bf16)
-            spread[padded + 1 : padded + 1 + lines] = levels[b, own : own + lines]
-            edge += extent
-        total_rows = spread.shape[0]
-        products = dot(
-            head[...], spread[...].reshape(total_rows * width, channels), ((1,), (1,))
-        )
-        columns = []
-        for j in range(3):
-            pieces = []
-            for padded, own, lines in plan:
-                total = jnp.zeros((DELTA_ROWS, lines * width), f32)
-                for i in range(3):
-                    tap = (3 * i + j) * DELTA_ROWS
-                    total = total + products[
-                        tap : tap + DELTA_ROWS, (padded + i) * width : (padded + i + lines) * width
-                    ]
-                pieces.append(total)
-            columns.append(jnp.concatenate(pieces, axis=1))
-        values = columns[1] + turned(columns[0], 1, 1, width) + turned(columns[2], -1, 1, width)
-        mismatch = values - target[b]
-        weight = mask[b]
+            at = slice(index * width, (index + 1) * width)
+            rows = [
+                values[b, :, line * width : (line + 1) * width]
+                for line in range(padded, padded + lines + 2)
+            ]
+            rows[0] = rows[0] + above[b, 0, :, at]
+            rows[1] = rows[1] + above[b, 1, :, at]
+            rows[lines] = rows[lines] + below[b, 1, :, at]
+            rows[lines + 1] = rows[lines + 1] + below[b, 0, :, at]
+            partial += rows
+            weights += [
+                above[b, 2, :, at],
+                mask[b, :, own * width : (own + lines) * width],
+                below[b, 2, :, at],
+            ]
+        mismatch = jnp.concatenate(partial, axis=1)
+        weight = jnp.concatenate(weights, axis=1)
         magnitude = jnp.abs(mismatch)
         losses = weight * jnp.where(
             magnitude < box_beta, 0.5 * mismatch * mismatch / box_beta, magnitude - 0.5 * box_beta
         )
-        for at in range(0, losses.shape[1], LANES):
-            summed = summed + losses[:, at : at + LANES]
-        gradient = (weight * jnp.clip(mismatch / box_beta, -1.0, 1.0) * inverse).astype(bf16)
-        grads[b] = gradient
-        for index, (padded, own, lines) in enumerate(plan):
-            at = slice(index * width, (index + 1) * width)
-            first[b, :, at] = gradient[:, own * width : (own + 1) * width]
-            last[b, :, at] = gradient[:, (own + lines - 1) * width : (own + lines) * width]
-    loss[0, 0] = jnp.sum(summed)
-
-
-def back_kernel(height, levels, head, grads, above, below, head_grad, grad_four, grad_five, first, last, taps, wide):
-    crops, _, width, channels = levels.shape
-    plan = level_rows(height)
-    total = jnp.zeros((9 * DELTA_ROWS, channels), f32)
-    for b in range(crops):
-        pieces = []
-        for index, (padded, own, lines) in enumerate(plan):
-            at = slice(index * width, (index + 1) * width)
-            pieces += [
-                above[b, :, at],
-                grads[b, :, own * width : (own + lines) * width],
-                below[b, :, at],
-            ]
-        middle = jnp.concatenate(pieces, axis=1).astype(f32)
+        for padded, own, lines in plan:
+            for line in range(padded + 1, padded + 1 + lines):
+                summed = summed + losses[:, line * width : (line + 1) * width]
+        middle = weight * jnp.clip(mismatch / box_beta, -1.0, 1.0) * inverse
+        middle = middle.astype(bf16).astype(f32)
         shifted = [turned(middle, -1, 1, width), middle, turned(middle, 1, 1, width)]
         for i in range(3):
             for j in range(3):
@@ -351,15 +377,14 @@
                         (3 * i + j) * DELTA_ROWS : (3 * i + j + 1) * DELTA_ROWS,
                         own * width : (own + lines) * width,
                     ] = shifted[j][:, at : at + lines * width].astype(bf16)
-        spread = taps[...]
+        around = taps[...]
         lines_all = levels.shape[1]
-        total = total + dot(spread, levels[b].reshape(lines_all * width, channels))
-        back = dot(spread, head[...], ((0,), (0,))).reshape(lines_all, width, channels)
+        total_grad = total_grad + dot(around, levels[b].reshape(lines_all * width, channels))
+        back = dot(around, head[...], ((0,), (0,))).reshape(lines_all, width, channels)
         rounded = back[:height].astype(bf16)
         grad_four[b] = rounded
         first[b, :width] = rounded[0]
         last[b, :width] = rounded[height - 1]
-        low_height, low_width = height // 2, width // 2
         for q in range(low_height // 2):
             up = doubled_columns(wide, back[height + low_height + q, : low_width // 2])
             for row in (2 * q, 2 * q + 1):
@@ -369,10 +394,12 @@
                     first[b, width:] = low
                 if row == low_height - 1:
                     last[b, width:] = low
-    head_grad[...] = total
-
-
-def conv_grad_kernel(n_rows, input_four, input_five, above, below, grad_four, grad_five, head_grad, place, kept, turned_rows, sums_four, sums_five, spare):
+    head_grad[...] = total_grad
+    loss[0, 0] = jnp.sum(summed)
+
+
+def conv_grad_kernel(n_rows, n_batch, deltas, input_four, input_five, above, below, grad_four, grad_five, head_grad, loss, *refs):
+    outs, (turned_rows, sums_four, sums_five, spare) = refs[:-4], refs[-4:]
     crops, height, width, channels = input_four.shape
     low_height, low_width = input_five.shape[1:3]
     padding = jnp.zeros((width - low_width, channels), bf16)
@@ -409,11 +436,15 @@
                 ],
                 axis=1,
             )
-            product = dot(left, right)
-            if b == 0:
-                sums[...] = product
-            else:
-                sums[...] += product
+            for i in range(3):
+                product = dot(left[i * channels : (i + 1) * channels], right)
+                for j in range(3):
+                    at = slice((3 * i + j) * channels, (3 * i + j + 1) * channels)
+                    block = product[:, j * channels : (j + 1) * channels]
+                    if b == 0:
+                        sums[at, :] = block
+                    else:
+                        sums[at, :] += block
     for t in range(9):
         block = head_grad[t * DELTA_ROWS : (t + 1) * DELTA_ROWS, :]
         block = jnp.concatenate(
@@ -421,22 +452,21 @@
         )
         spare[t * channels : (t + 1) * channels, :] = block.T
     me = lax.axis_index("rows")
+    number = me * n_batch + lax.axis_index("batch")
     part = 9 * channels // n_rows
-    for owner in range(n_rows):
-        index = owner ^ me
-        for start in range(0, part, 16):
-            line = owner * part + start
-            i, rest = divmod(line, 3 * channels)
-            j, channel = divmod(rest, channels)
-            lines = jnp.concatenate(
-                [
-                    sums_four[pl.ds(i * channels + channel, 16), j * channels : (j + 1) * channels],
-                    sums_five[pl.ds(i * channels + channel, 16), j * channels : (j + 1) * channels],
-                    spare[pl.ds(line, 16), :] + place[pl.ds(start, 16), :],
-                ],
-                axis=1,
-            ).astype(bf16)
-            kept[index, start : start + 16, :] = lines
+    own = part // n_batch
+    place = jnp.zeros((part, LANES), f32)
+    line = lax.broadcasted_iota(jnp.int32, place.shape, 0) % own
+    lane = lax.broadcasted_iota(jnp.int32, place.shape, 1) - deltas - 3 * (number // own)
+    for piece, value in enumerate(pieces_of(jnp.full(place.shape, loss[0, 0], f32))):
+        place = jnp.where((line == number % own) & (lane == piece), value, place)
+    low = len(outs)
+    for index in range(n_rows):
+        at = pl.ds(pl.multiple_of((index ^ me) * part, part), part)
+        out, j = outs[index % low], index // low
+        out[j, :, :channels] = sums_four[at, :].astype(bf16)
+        out[j, :, channels : 2 * channels] = sums_five[at, :].astype(bf16)
+        out[j, :, 2 * channels :] = (spare[at, :] + place).astype(bf16)
 
 
 def merged_grad_kernel(grad_four, grad_five, above, below, kernel_four, kernel_five, lat_four, lat_five, spread_four, spread_five, fold):
@@ -464,7 +494,8 @@
                     lat_five[at_low : at_low + low_width, h : h + LANES] = (total + folded).astype(bf16)
 
 
-def section_grad_kernel(n_rows, four, five, lat_four, lat_five, kept):
+def section_grad_kernel(n_rows, four, five, lat_four, lat_five, kept, *refs):
+    outs, (sums_four, sums_five) = refs[:-2], refs[-2:]
     crops, height, width, depth = four.shape
     low_height, low_width, low_depth = five.shape[1:]
     me = lax.axis_index("rows")
@@ -473,14 +504,60 @@
     low_positions = crops * low_height * low_width
     turned_four = lat_four[...].T
     turned_five = lat_five[...].T
-    for owner in range(n_rows):
-        index = owner ^ me
-        at = slice(owner * part_four, (owner + 1) * part_four)
-        block = dot(turned_four, four[:, :, :, at].reshape(positions, part_four))
-        kept[index, :part_four, :] = block.T.astype(bf16)
-        at = slice(owner * part_five, (owner + 1) * part_five)
-        block = dot(turned_five, five[:, :, :, at].reshape(low_positions, part_five))
-        kept[index, part_four:, :] = block.T.astype(bf16)
+    step = 256
+    for at in range(0, depth, step):
+        block = four[:, :, :, at : at + step].reshape(positions, step)
+        sums_four[at : at + step, :] = dot(turned_four, block).T
+    for at in range(0, low_depth, step):
+        block = five[:, :, :, at : at + step].reshape(low_positions, step)
+        sums_five[at : at + step, :] = dot(turned_five, block).T
+    high = kept.shape[0]
+    low = n_rows // high
+    for index in range(n_rows):
+        k, j = index % low, index // low
+        out = kept.at[j] if k == 0 else outs[k - 1].at[j]
+        owner = index ^ me
+        at = pl.ds(pl.multiple_of(owner * part_four, part_four), part_four)
+        out[:part_four, :] = sums_four[at, :].astype(bf16)
+        at = pl.ds(pl.multiple_of(owner * part_five, part_five), part_five)
+        out[part_four:, :] = sums_five[at, :].astype(bf16)
+
+
+def adamw_into(outs, weight, gradient, mean, square):
+    for out, value in zip(outs, adamw_update(weight, gradient, mean, square)):
+        out[...] = value
+
+
+def conv_step_kernel(count, deltas, own, *refs):
+    came, (weight, mean, square, first, second, new, head, loss) = refs[:count], refs[count:]
+    channels = weight.shape[2]
+    total = own[...]
+    for piece in came:
+        total = total + piece[...].astype(f32)
+    for k in range(2):
+        adamw_into(
+            (first.at[k], second.at[k], new.at[k]),
+            weight[k],
+            total[:, k * channels : (k + 1) * channels],
+            mean[k],
+            square[k],
+        )
+    spare = total[:, 2 * channels :]
+    head[...] = spare
+    lane = lax.broadcasted_iota(jnp.int32, spare.shape, 1)
+    loss[0, 0] = jnp.sum(jnp.where(lane >= deltas, spare, 0.0))
+
+
+def lateral_step_kernel(count, own, *refs):
+    came, rest = refs[:count], refs[count:]
+    inputs, outs = rest[:6], rest[6:]
+    total = own[...]
+    for piece in came:
+        total = total + piece[...].astype(f32)
+    lines = inputs[0].shape[0]
+    for k, gradient in enumerate((total[:lines], total[lines:])):
+        weight, mean, square = (ref[...] for ref in inputs[3 * k : 3 * k + 3])
+        adamw_into(outs[3 * k : 3 * k + 3], weight, gradient, mean, square)
 
 
 def planes(field, rows):
@@ -513,37 +590,48 @@
     square_head,
 ):
     n_rows, n_batch = lax.axis_size("rows"), lax.axis_size("batch")
-    number = lax.axis_index("rows") * n_batch + lax.axis_index("batch")
     _, low_group, high_group = row_groups()
     crops, height, width, depth = section_four.shape
     low_height, low_width, low_depth = section_five.shape[1:]
-    top_width = target_six.shape[2]
     four_n, five_n, conv_n = lateral_four.shape[0], lateral_five.shape[0], output_conv.shape[1]
     channels, deltas = delta_head.shape[0] * n_rows * n_batch // 9, delta_head.shape[1]
     shape = jax.ShapeDtypeStruct
 
-    lateral = jnp.concatenate([lateral_four, lateral_five]).astype(bf16)
+    (lateral,) = call(
+        pack_lateral_kernel,
+        "pack_laterals",
+        [lateral_four, lateral_five],
+        [shape((four_n + five_n, channels), bf16)],
+    )
     parts = gathered_batch(lateral)
     lateral = jnp.concatenate([p[:four_n] for p in parts] + [p[four_n:] for p in parts])
     laterals = gathered_high(lateral)
 
-    anchors = [a.astype(f32) for a in (anchor_four, anchor_five, anchor_six)]
-    mask = jnp.concatenate(
-        [planes(jnp.repeat(a, deltas // a.shape[3], axis=3), DELTA_ROWS) for a in anchors], axis=2
-    )
-    target = jnp.concatenate(
-        [planes(t, DELTA_ROWS) for t in (target_four, target_five, target_six)], axis=2
-    )
-    local_count = sum(jnp.sum(a) for a in anchors)
-
-    lane = lax.broadcasted_iota(jnp.int32, (conv_n, LANES), 1)
-    line = lax.broadcasted_iota(jnp.int32, (conv_n, LANES), 0)
-    spare = jnp.pad(delta_head, ((0, 0), (0, LANES - deltas)))
-    for k, piece in enumerate(thirds(local_count)):
-        spare = jnp.where((line == 0) & (lane == deltas + k), piece, spare)
-    conv = jnp.concatenate([output_conv[0], output_conv[1], spare], axis=1).astype(bf16)
+    flat = [jnp.transpose(a, (0, 3, 1, 2)) for a in (anchor_four, anchor_five, anchor_six)]
+    (conv,) = call(
+        pack_conv_kernel,
+        "pack_convs",
+        [output_conv, delta_head.T, *flat],
+        [shape((conv_n, 2 * channels + LANES), bf16)],
+        [pltpu.VMEM((LANES, LANES), f32)],
+    )
     conv, _ = lax.optimization_barrier((conv, lateral))
     conv = jnp.concatenate(gathered_batch(conv))
+    anchors, targets, _ = lax.optimization_barrier(
+        (
+            (anchor_four, anchor_five, anchor_six),
+            (target_four, target_five, target_six),
+            conv,
+        )
+    )
+    mask = jnp.concatenate(
+        [
+            planes(jnp.repeat(a.astype(f32), deltas // a.shape[3], axis=3), DELTA_ROWS)
+            for a in anchors
+        ],
+        axis=2,
+    )
+    target = jnp.concatenate([planes(t, DELTA_ROWS) for t in targets], axis=2)
     conv, laterals = lax.optimization_barrier((conv, laterals))
     laterals = gathered_low(laterals)
     convs = gathered_high(conv)
@@ -567,19 +655,20 @@
         flops=2 * crops * channels * (height * width * depth + low_height * low_width * low_depth),
     )
     above_in, below_in = from_neighbours(first, last)
-    convs, _ = lax.optimization_barrier((convs, input_four))
+    convs, above_in, below_in = lax.optimization_barrier((convs, above_in, below_in))
     convs = gathered_low(convs)
 
     lines = height + low_height + low_height // 2
     conv_flops = 18 * crops * channels * channels * (height * width + low_height * low_width)
-    levels, first, last, kernel_four, kernel_five, head, count = call(
+    levels, values, first, last, kernel_four, kernel_five, head, count = call(
         functools.partial(output_kernel, n_rows, deltas),
         "outputs",
-        [input_four, input_five, above_in, below_in, *convs],
+        [input_four, input_five, above_in, below_in, target, mask, *convs],
         [
             shape((crops, lines, width, channels), bf16),
-            shape((crops, edge + top_width, channels), bf16),
-            shape((crops, edge + top_width, channels), bf16),
+            shape((crops, DELTA_ROWS, (lines + 6) * width), f32),
+            shape((crops, 3, DELTA_ROWS, 3 * width), f32),
+            shape((crops, 3, DELTA_ROWS, 3 * width), f32),
             shape((9 * channels, channels), bf16),
             shape((9 * channels, channels), bf16),
             shape((9 * DELTA_ROWS, channels), bf16),
@@ -596,63 +685,47 @@
     above, below = from_neighbours(first, last)
 
     head_flops = 18 * DELTA_ROWS * crops * lines * width * channels
-    grads, first, last, loss = call(
+    head_grad, grad_four, grad_five, first, last, loss = call(
         functools.partial(head_kernel, height),
-        "deltas",
-        [levels, above, below, head, target, mask, count],
-        [
-            shape((crops, DELTA_ROWS, lines * width), bf16),
-            shape((crops, DELTA_ROWS, 3 * width), bf16),
-            shape((crops, DELTA_ROWS, 3 * width), bf16),
-            shape((1, 1), f32),
-        ],
-        [pltpu.VMEM((lines + 6, width, channels), bf16)],
-        flops=head_flops,
-        scalars=1,
-        scalar_outs=1,
-    )
-    above, below = from_neighbours(first, last)
-
-    head_grad, grad_four, grad_five, first, last = call(
-        functools.partial(back_kernel, height),
-        "level_grads",
-        [levels, head, grads, above, below],
+        "heads",
+        [levels, above, below, head, values, mask, count],
         [
             shape((9 * DELTA_ROWS, channels), f32),
             shape((crops, height, width, channels), bf16),
             shape((crops, low_height, low_width, channels), bf16),
             shape((crops, edge, channels), bf16),
             shape((crops, edge, channels), bf16),
+            shape((1, 1), f32),
         ],
         [
             pltpu.VMEM((9 * DELTA_ROWS, lines * width), bf16),
             pltpu.VMEM((channels // LANES, low_width, LANES), f32),
         ],
-        flops=2 * head_flops,
+        flops=3 * head_flops,
+        scalars=1,
+        scalar_outs=1,
     )
     above, below = from_neighbours(first, last)
 
-    place = jnp.zeros((conv_n, LANES), f32)
-    for k, piece in enumerate(thirds(loss[0, 0])):
-        spot = (line == number % conv_n) & (lane == deltas + 3 * (number // conv_n) + k)
-        place = jnp.where(spot, piece, place)
-    place = jnp.concatenate([place] * n_batch)
     conv_width = 2 * channels + LANES
-    (conv_blocks,) = call(
-        functools.partial(conv_grad_kernel, n_rows),
+    conv_blocks = call(
+        functools.partial(conv_grad_kernel, n_rows, n_batch, deltas),
         "conv_grads",
-        [input_four, input_five, above_in, below_in, grad_four, grad_five, head_grad, place],
-        [shape((n_rows, n_batch * conv_n, conv_width), bf16)],
+        [input_four, input_five, above_in, below_in, grad_four, grad_five, head_grad, loss],
+        [shape((high_group, n_batch * conv_n, conv_width), bf16)] * low_group,
         [
             pltpu.VMEM((channels, (height + 2) * width), bf16),
-            pltpu.VMEM((3 * channels, 3 * channels), f32),
-            pltpu.VMEM((3 * channels, 3 * channels), f32),
+            pltpu.VMEM((9 * channels, channels), f32),
+            pltpu.VMEM((9 * channels, channels), f32),
             pltpu.VMEM((9 * channels, LANES), f32),
         ],
         flops=conv_flops,
-    )
-    conv_blocks = conv_blocks.reshape(high_group, low_group, n_batch * conv_n, conv_width)
+        scalars=1,
+    )
+
     positions, low_positions = crops * height * width, crops * low_height * low_width
+    conv_partial = summed_low(conv_blocks)
+    above, below, conv_partial = lax.optimization_barrier((above, below, conv_partial))
     lat_four, lat_five = call(
         merged_grad_kernel,
         "merged_grads",
@@ -665,51 +738,56 @@
         ],
         flops=conv_flops,
     )
-    conv_partial = summed_low([conv_blocks[:, k] for k in range(low_group)])
-    lat_four, conv_partial = lax.optimization_barrier((lat_four, conv_partial))
     conv_sum = summed_high(conv_partial)
 
-    (lateral_blocks,) = call(
+    lateral_n = four_n + five_n
+    lateral_kept, *lateral_moved = call(
         functools.partial(section_grad_kernel, n_rows),
         "lateral_grads",
         [section_four, section_five, lat_four, lat_five],
-        [shape((n_rows, n_batch * (four_n + five_n), channels), bf16)],
-        flops=2 * channels * (positions * depth + low_positions * low_depth),
-    )
-    lateral_blocks = lateral_blocks.reshape(
-        high_group, low_group, n_batch * (four_n + five_n), channels
-    )
-    lateral_partial = summed_low([lateral_blocks[:, k] for k in range(low_group)])
-    lateral_partial, conv_sum = lax.optimization_barrier((lateral_partial, conv_sum))
+        [shape((high_group, n_batch * lateral_n, channels), bf16)] * low_group,
+        [pltpu.VMEM((depth, channels), f32), pltpu.VMEM((low_depth, channels), f32)],
+        flops=1,
+    )
+    lateral_moved, conv_sum = lax.optimization_barrier((lateral_moved, conv_sum))
+    lateral_partial = summed_low([lateral_kept, *lateral_moved])
     lateral_sum = summed_high(lateral_partial)
-    conv_sum = summed_batch(conv_sum.reshape(n_batch, conv_n, conv_width))
-    lateral_sum = summed_batch(
-        jnp.concatenate(
-            [
-                lateral_sum[: n_batch * four_n].reshape(n_batch, four_n, channels),
-                lateral_sum[n_batch * four_n :].reshape(n_batch, five_n, channels),
-            ],
-            axis=1,
-        )
-    )
-
-    conv_part = jnp.stack([conv_sum[:, :channels], conv_sum[:, channels : 2 * channels]])
-    head_part = conv_sum[:, 2 * channels : 2 * channels + deltas]
-    loss_sum = jnp.sum(conv_sum[:, 2 * channels + deltas :])
-    first_four, second_four, weight_four = adamw_update(
-        lateral_four, lateral_sum[:four_n], mean_four, square_four
-    )
-    first_five, second_five, weight_five = adamw_update(
-        lateral_five, lateral_sum[four_n:], mean_five, square_five
-    )
-    first_conv, second_conv, weight_conv = adamw_update(
-        output_conv, conv_part, mean_conv, square_conv
-    )
+    conv_shares = shared_batch(conv_sum.reshape(n_batch, conv_n, conv_width))
+    conv_shares, lateral_sum = lax.optimization_barrier((conv_shares, lateral_sum))
+    first_conv, second_conv, weight_conv, head_part, loss_sum = call(
+        functools.partial(conv_step_kernel, n_batch - 1, deltas),
+        "conv_step",
+        [*conv_shares, output_conv, mean_conv, square_conv],
+        [shape(output_conv.shape, f32)] * 3 + [shape((conv_n, LANES), f32), shape((1, 1), f32)],
+        scalar_outs=1,
+    )
+    lateral_sum = jnp.concatenate(
+        [
+            lateral_sum[: n_batch * four_n].reshape(n_batch, four_n, channels),
+            lateral_sum[n_batch * four_n :].reshape(n_batch, five_n, channels),
+        ],
+        axis=1,
+    )
+    first_four, second_four, weight_four, first_five, second_five, weight_five = call(
+        functools.partial(lateral_step_kernel, n_batch - 1),
+        "lateral_step",
+        [
+            *shared_batch(lateral_sum),
+            lateral_four,
+            mean_four,
+            square_four,
+            lateral_five,
+            mean_five,
+            square_five,
+        ],
+        [shape(lateral_four.shape, f32)] * 3 + [shape(lateral_five.shape, f32)] * 3,
+    )
+    head_part = head_part[:, :deltas]
     first_head, second_head, weight_head = adamw_update(
         delta_head, head_part, mean_head, square_head
     )
     return (
-        loss_sum,
+        loss_sum[0, 0],
         count[0, 0],
         first_four,
         first_five,

time: 199 us -> 150 us (0.75)
  other arithmetic: 22.2 us -> 7.1 us
  starting transfers between devices: 65.7 us -> 51.5 us
  waiting for transfers between devices: 42.3 us -> 33.7 us
  between operations: 9.6 us -> 1.47 us
  local copies, waits for them, and re-layouts: 15.1 us -> 7.53 us
  Pallas kernels: 42.9 us -> 47.8 us
    ppermute x4 -> x3, starting transfers between devices: 16 us -> 5.64 us  [from_neighbours(): above = lax.ppermute(last, 'rows', [(i, i + 1) for i in range(count - 1)])]
    pallas_call x7 -> x10, Pallas kernels: 42.9 us -> 47.8 us  [call(): pl.pallas_call(kernel, out_shape=list(outs), in_specs=[vmem] * (len(args)...]
    reduce_sum x4 -> x0, other arithmetic: 4.58 us -> none  [the longest x3 3.97 us: on_device(): local_count = sum((jnp.sum(a) for a in anchors))]
    ppermute x34, waiting for transfers between devices: 34.7 us -> 30.3 us  [sent(): return lax.ppermute(value, axis, [(i, i ^ mask) for i in range(count)])]
    unnamed x115 -> x95, local copies, waits for them, and re-layouts: 10.8 us -> 6.44 us
    ppermute x4 -> x3, waiting for transfers between devices: 7.59 us -> 3.47 us  [from_neighbours(): below = lax.ppermute(first, 'rows', [(i + 1, i) for i in range(count - 1)])]
    another operation x4 -> x0, other arithmetic: 3.9 us -> none
    squeeze x3 -> x1, local copies, waits for them, and re-layouts: 3.7 us -> 0.68 us  [shared_batch(): own = lax.dynamic_index_in_dim(blocks, me, 0, keepdims=False)]
  transfers between devices with their start and end apart: 42 -> 40, of which waited for: 14 -> 16; matrix products, arithmetic and copies ran while one was open for 11% -> 6% of each run, Pallas kernels for 7% -> 15%
where the time goes in v2:
time: 150 us; the launch traced here: 149 us
  starting transfers between devices  51.5 us (34%)
  Pallas kernels  47.8 us (32%)
  waiting for transfers between devices  33.7 us (22%)
  local copies, waits for them, and re-layouts  7.53 us (5%)
  other arithmetic  7.1 us (5%)
    pallas_call x10, Pallas kernels, call(): pl.pallas_call(kernel, out_shape=list(outs), in_specs=[vmem] * (len(args)...  47.8 us
    ppermute x34, starting transfers between devices, sent(): return lax.ppermute(value, axis, [(i, i ^ mask) for i in range(count)])  41.6 us
    ppermute x34, waiting for transfers between devices, sent(): return lax.ppermute(value, axis, [(i, i ^ mask) for i in range(count)])  30.3 us
    unnamed x95, local copies, waits for them, and re-layouts  6.44 us
    ppermute x3, starting transfers between devices, from_neighbours(): above = lax.ppermute(last, 'rows', [(i, i + 1) for i in range(count - 1)])  5.64 us
    ppermute x3, starting transfers between devices, from_neighbours(): below = lax.ppermute(first, 'rows', [(i + 1, i) for i in range(count - 1)])  4.28 us
    ppermute x3, waiting for transfers between devices, from_neighbours(): below = lax.ppermute(first, 'rows', [(i + 1, i) for i in range(count - 1)])  3.47 us
  transfers between devices with their start and end apart: 40, of which 16 were waited for; matrix products, arithmetic and copies ran while one was open for 6% of the time, Pallas kernels for 15%

profile of v2, /device:TPU:0, one launch (start us, length us, event | category | flops | bytes accessed | tf_op | source)
XLA Modules:
  0.0 149.1 jit_solution(6074745704519744954)
XLA Ops:
  0.6 1.5 pack_laterals.1
  2.1 3.0 %collective-permute-start = (bf16[96,256]{1,0:T(8,128)(2,1)}, bf16[96,256]{1,0:T(8,128)(2,1)S(1)}, u32[]{:S(2)}, u32[]{:S(2)}) collective-permute-start(bf16[96,256]{1,0:T(8,128)(2,1)} %pack_laterals.1), channel_id=1, source_target_pairs={{0,1},{1,0},{2,3},{3,2},{4,5},{5,4},{6,7},{7,6},{8,9},{9,8},{10,11... | collective-permute-start | bytes 147464 | tf_op jit(solution)/shard_map/ppermute | solution.py:43
  5.2 2.6 %collective-permute-start.1 = (bf16[96,256]{1,0:T(8,128)(2,1)}, bf16[96,256]{1,0:T(8,128)(2,1)S(1)}, u32[]{:S(2)}, u32[]{:S(2)}) collective-permute-start(bf16[96,256]{1,0:T(8,128)(2,1)} %pack_laterals.1), channel_id=1, source_target_pairs={{0,2},{1,3},{2,0},{3,1},{4,6},{5,7},{6,4},{7,5},{8,10},{9,11},{10,... | collective-permute-start | bytes 147464 | tf_op jit(solution)/shard_map/ppermute | solution.py:43
  7.7 1.7 %pack_convs.1 = bf16[72,640]{1,0:T(8,128)(2,1)} custom-call(f32[2,72,256]{2,1,0:T(8,128)} %refs_3_.2, f32[12,72]{1,0:T(8,128)} %bitcast.130, s32[2,3,8,128]{3,2,1,0:T(8,128)} %bitcast.120, s32[2,3,4,64]{3,2,1,0:T(4,128)} %bitcast.125, s32[2,3,2,32]{3,2,1,0:T(2,128)} %bitcast.132), custom_call_target="tpu_custom_call" | custom-call | bytes 275328 | tf_op jit(solution)/shard_map/pack_convs/pallas_call | solution.py:114
  9.5 1.8 %collective-permute-done.1 = bf16[96,256]{1,0:T(8,128)(2,1)S(1)} collective-permute-done((bf16[96,256]{1,0:T(8,128)(2,1)}, bf16[96,256]{1,0:T(8,128)(2,1)S(1)}, u32[]{:S(2)}, u32[]{:S(2)}) %collective-permute-start.1) | collective-permute-done | bytes 49184 | tf_op jit(solution)/shard_map/ppermute | solution.py:43
  11.3 2.6 %collective-permute-done.2 = bf16[96,256]{1,0:T(8,128)(2,1)S(1)} collective-permute-done((bf16[96,256]{1,0:T(8,128)(2,1)}, bf16[96,256]{1,0:T(8,128)(2,1)S(1)}, u32[]{:S(2)}, u32[]{:S(2)}) %collective-permute-start.2) | collective-permute-done | bytes 49184 | tf_op jit(solution)/shard_map/ppermute | solution.py:43
  13.8 0.8 pad_maximum_fusion.3
  14.9 1.3 collective-permute-start.4
  16.2 3.1 %collective-permute-start.5 = (bf16[72,640]{1,0:T(8,128)(2,1)}, bf16[72,640]{1,0:T(8,128)(2,1)S(1)}, u32[]{:S(2)}, u32[]{:S(2)}) collective-permute-start(bf16[72,640]{1,0:T(8,128)(2,1)} %pack_convs.1), channel_id=1, source_target_pairs={{0,3},{1,2},{2,1},{3,0},{4,7},{5,6},{6,5},{7,4},{8,11},{9,10},{10,... | collective-permute-start | bytes 276488 | tf_op jit(solution)/shard_map/ppermute | solution.py:43
  19.3 1.5 collective-permute-start.6
  20.8 1.5 %collective-permute-start.7 = (bf16[384,256]{1,0:T(8,128)(2,1)S(1)}, bf16[384,256]{1,0:T(8,128)(2,1)S(1)}, u32[]{:S(2)}, u32[]{:S(2)}) collective-permute-start(bf16[384,256]{1,0:T(8,128)(2,1)S(1)} %fusion.20.refs_0_), channel_id=1, source_target_pairs={{0,16},{4,20},{8,24},{12,28},{16,0},{20,4},{24,8},{28,12},{1,17},{... | collective-permute-start | bytes 589832 | tf_op jit(solution)/shard_map/ppermute | solution.py:43
  22.8 1.0 collective-permute-done.4
  23.8 0.9 pad_maximum_fusion
  24.9 1.0 collective-permute-done.6.refs_2_
  25.9 3.3 %collective-permute-done.7.refs_4_ = bf16[384,256]{1,0:T(8,128)(2,1)S(1)} collective-permute-done((bf16[384,256]{1,0:T(8,128)(2,1)S(1)}, bf16[384,256]{1,0:T(8,128)(2,1)S(1)}, u32[]{:S(2)}, u32[]{:S(2)}) %collective-permute-start.7) | collective-permute-done | bytes 196640 | tf_op jit(solution)/shard_map/ppermute | solution.py:43
  30.3 0.9 collective-permute-start.13
  31.2 0.9 collective-permute-start.14
  32.1 1.7 %collective-permute-start.15 = (bf16[288,640]{1,0:T(8,128)(2,1)S(1)}, bf16[288,640]{1,0:T(8,128)(2,1)S(1)}, u32[]{:S(2)}, u32[]{:S(2)}) collective-permute-start(bf16[288,640]{1,0:T(8,128)(2,1)S(1)} %pad_maximum_fusion.1.refs_0_), channel_id=1, source_target_pairs={{0,24},{4,28},{8,16},{12,20},{16,8},{20,12},{24,0},{28,4},{1,25},{... | collective-permute-start | bytes 1105928 | tf_op jit(solution)/shard_map/ppermute | solution.py:43
  34.5 0.7 copy-done.9
  35.2 6.1 %laterals.1 = (bf16[2,8,128,256]{3,2,1,0:T(8,128)(2,1)}, bf16[2,4,64,256]{3,2,1,0:T(8,128)(2,1)}, bf16[2,192,256]{2,1,0:T(8,128)(2,1)}, bf16[2,192,256]{2,1,0:T(8,128)(2,1)}) custom-call(bf16[2,8,128,1024]{3,2,1,0:T(8,128)(2,1)} %four.5, bf16[2,4,64,2048]{3,2,1,0:T(8,128)(2,1)} %five.5, bf16[384,256]{1,0:T(8,128)(2,1)} %copy-done.2, ...), custom_call_target="tpu_custom_call" | custom-call | flops 1610612736 | bytes 9568256 | tf_op jit(solution)/shard_map/laterals/pallas_call | solution.py:114
  41.3 1.4 collective-permute-start.16
  42.8 1.3 collective-permute-start.17
  44.3 5.1 %collective-permute-done.15.refs_6_ = bf16[288,640]{1,0:T(8,128)(2,1)S(1)} collective-permute-done((bf16[288,640]{1,0:T(8,128)(2,1)S(1)}, bf16[288,640]{1,0:T(8,128)(2,1)S(1)}, u32[]{:S(2)}, u32[]{:S(2)}) %collective-permute-start.15) | collective-permute-done | bytes 368672 | tf_op jit(solution)/shard_map/ppermute | solution.py:43
  49.5 3.5 %collective-permute-start.18 = (bf16[288,640]{1,0:T(8,128)(2,1)S(1)}, bf16[288,640]{1,0:T(8,128)(2,1)S(1)}, u32[]{:S(2)}, u32[]{:S(2)}) collective-permute-start(bf16[288,640]{1,0:T(8,128)(2,1)S(1)} %pad_maximum_fusion.1.refs_0_), channel_id=1, source_target_pairs={{0,4},{4,0},{8,12},{12,8},{16,20},{20,16},{24,28},{28,24},{1,5},{5... | collective-permute-start | bytes 1105928 | tf_op jit(solution)/shard_map/ppermute | solution.py:43
  53.8 0.8 pad_maximum_fusion.2.target
  54.6 0.8 collective-permute-done.19.refs_3_
  56.6 8.5 %outputs.1 = (bf16[2,14,128,256]{3,2,1,0:T(8,128)(2,1)}, f32[2,16,2560]{2,1,0:T(8,128)}, f32[2,3,16,384]{3,2,1,0:T(8,128)}, f32[2,3,16,384]{3,2,1,0:T(8,128)}, b...) custom-call(bf16[2,8,128,256]{3,2,1,0:T(8,128)(2,1)} %get-tuple-element.85.inpu, ...), custom_call_target="tpu_custom_call" | custom-call | flops 3019898880 | bytes 10002436 | tf_op jit(solution)/shard_map/outputs/pallas_call | solution.py:114
  65.2 2.3 %collective-permute-start.22 = (f32[2,3,16,384]{3,2,1,0:T(8,128)}, f32[2,3,16,384]{3,2,1,0:T(8,128)S(1)}, u32[]{:S(2)}, u32[]{:S(2)}) collective-permute-start(f32[2,3,16,384]{3,2,1,0:T(8,128)} %get-tuple-element.103), channel_id=1, source_target_pairs={{0,4},{4,8},{8,12},{12,16},{16,20},{20,24},{24,28},{1,5},{5,9},{9,... | collective-permute-start | bytes 442376 | tf_op jit(solution)/shard_map/ppermute | solution.py:106
  67.5 1.5 collective-permute-start.23
  69.0 2.6 %collective-permute-done.23.below = f32[2,3,16,384]{3,2,1,0:T(8,128)S(1)} collective-permute-done((f32[2,3,16,384]{3,2,1,0:T(8,128)}, f32[2,3,16,384]{3,2,1,0:T(8,128)S(1)}, u32[]{:S(2)}, u32[]{:S(2)}) %collective-permute-start.23) | collective-permute-done | bytes 147488 | tf_op jit(solution)/shard_map/ppermute | solution.py:107
  71.6 0.7 copy-done.39
  72.3 4.7 %heads.1 = (f32[144,256]{1,0:T(8,128)}, bf16[2,8,128,256]{3,2,1,0:T(8,128)(2,1)}, bf16[2,4,64,256]{3,2,1,0:T(8,128)(2,1)}, bf16[2,192,256]{2,1,0:T(8,128)(2,1)},...) custom-call(bf16[2,14,128,256]{3,2,1,0:T(8,128)(2,1)} %get-tuple-element.102.levels, f32[2,3,16,384]{3,2,1,0:T(8,128)} %copy-done.38, ...), custom_call_target="tpu_custom_call" | custom-call | flops 792723456 | bytes 4612104 | tf_op jit(solution)/shard_map/heads/pallas_call | solution.py:114
  77.0 8.2 %conv_grads.1 = (bf16[4,288,640]{2,1,0:T(8,128)(2,1)}, bf16[4,288,640]{2,1,0:T(8,128)(2,1)}) custom-call(bf16[2,8,128,256]{3,2,1,0:T(8,128)(2,1)} %get-tuple-element.85.input_four, bf16[2,4,64,256]{3,2,1,0:T(8,128)(2,1)} %get-tuple-element.86.input_five, bf16[2,192,256]{2,1,0:T(8,128)(2,1)} %copy-done.33, ...), custom_call_target="tpu_custom_call" | custom-call | flops 3019898880 | bytes 6111236 | tf_op jit(solution)/shard_map/conv_grads/pallas_call | solution.py:114
  85.2 3.7 %collective-permute-start.26 = (bf16[4,288,640]{2,1,0:T(8,128)(2,1)}, bf16[4,288,640]{2,1,0:T(8,128)(2,1)S(1)}, u32[]{:S(2)}, u32[]{:S(2)}) collective-permute-start(bf16[4,288,640]{2,1,0:T(8,128)(2,1)} %get-tuple-element.115), channel_id=1, source_target_pairs={{0,4},{4,0},{8,12},{12,8},{16,20},{20,16},{24,28},{28,24},{1,5},{5... | collective-permute-start | bytes 4423688 | tf_op jit(solution)/shard_map/ppermute | solution.py:43
  88.9 1.9 %collective-permute-start.24 = (bf16[2,192,256]{2,1,0:T(8,128)(2,1)S(1)}, bf16[2,192,256]{2,1,0:T(8,128)(2,1)S(1)}, u32[]{:S(2)}, u32[]{:S(2)}) collective-permute-start(bf16[2,192,256]{2,1,0:T(8,128)(2,1)S(1)} %copy-done.36), channel_id=1, source_target_pairs={{0,4},{4,8},{8,12},{12,16},{16,20},{20,24},{24,28},{1,5},{5,9},{9,... | collective-permute-start | bytes 589832 | tf_op jit(solution)/shard_map/ppermute | solution.py:106
  90.9 1.5 %collective-permute-start.25 = (bf16[2,192,256]{2,1,0:T(8,128)(2,1)S(1)}, bf16[2,192,256]{2,1,0:T(8,128)(2,1)S(1)}, u32[]{:S(2)}, u32[]{:S(2)}) collective-permute-start(bf16[2,192,256]{2,1,0:T(8,128)(2,1)S(1)} %copy-done.34), channel_id=1, source_target_pairs={{4,0},{8,4},{12,8},{16,12},{20,16},{24,20},{28,24},{5,1},{9,5},{13... | collective-permute-start | bytes 589832 | tf_op jit(solution)/shard_map/ppermute | solution.py:107
  92.4 1.5 %add_bitcast_fusion = (bf16[288,640]{1,0:T(8,128)(2,1)S(1)}, bf16[288,640]{1,0:T(8,128)(2,1)S(1)}, bf16[288,640]{1,0:T(8,128)(2,1)S(1)}) fusion(bf16[4,288,640]{2,1,0:T(8,128)(2,1)S(1)} %collective-permute-done.26, bf16[4,288,640]{2,1,0:T(8,128)(2,1)} %get-tuple-element.114), kind=kLoop, calls=%fused_computation.1 | loop fusion | flops 2211840 | bytes 3317760 | tf_op jit(solution)/shard_map/add | solution.py:82
  93.9 1.1 add_bitcast_fusion.3
  95.0 0.8 collective-permute-done.25.below
  95.8 3.9 %collective-permute-start.27 = (bf16[288,640]{1,0:T(8,128)(2,1)S(1)}, bf16[288,640]{1,0:T(8,128)(2,1)S(1)}, u32[]{:S(2)}, u32[]{:S(2)}) collective-permute-start(bf16[288,640]{1,0:T(8,128)(2,1)S(1)} %get-tuple-element.124), channel_id=1, source_target_pairs={{0,8},{4,12},{8,0},{12,4},{16,24},{20,28},{24,16},{28,20},{1,9},{5... | collective-permute-start | bytes 1105928 | tf_op jit(solution)/shard_map/ppermute | solution.py:43
  99.7 1.5 collective-permute-start.29
  101.2 6.7 %merged_grads.1 = (bf16[2048,256]{1,0:T(8,128)(2,1)}, bf16[512,256]{1,0:T(8,128)(2,1)}) custom-call(bf16[2,8,128,256]{3,2,1,0:T(8,128)(2,1)} %get-tuple-element.108.grad_four, bf16[2,4,64,256]{3,2,1,0:T(8,128)(2,1)} %get-tuple-element.109.grad_five, bf16[2,192,256]{2,1,0:T(8,128)(2,1)} %copy-done.35, bf16[2,192,256]{2,1,0:T(8,128)(2,1)} %copy-done.37, ...), custom_call_target="tpu_custom_call" | custom-call | flops 3019898880 | bytes 5373952 | tf_op jit(solution)/shard_map/merged_grads/pallas_call | solution.py:114
  107.9 6.3 %lateral_grads.1 = (bf16[4,384,256]{2,1,0:T(8,128)(2,1)}, bf16[4,384,256]{2,1,0:T(8,128)(2,1)}) custom-call(bf16[2,8,128,1024]{3,2,1,0:T(8,128)(2,1)} %four.5, bf16[2,4,64,2048]{3,2,1,0:T(8,128)(2,1)} %five.5, bf16[2048,256]{1,0:T(8,128)(2,1)} %get-tuple-element.120.lat_four, bf16[512,256]{1,0:T(8,128)(2,1)} %get-tuple-element.121.lat_five), custom_call_target="tpu_custom_call" | custom-call | flops 1 | bytes 9175040 | tf_op jit(solution)/shard_map/lateral_grads/pallas_call | solution.py:114
  114.2 4.7 %collective-permute-done.28 = bf16[288,640]{1,0:T(8,128)(2,1)S(1)} collective-permute-done((bf16[288,640]{1,0:T(8,128)(2,1)S(1)}, bf16[288,640]{1,0:T(8,128)(2,1)S(1)}, u32[]{:S(2)}, u32[]{:S(2)}) %collective-permute-start.28) | collective-permute-done | bytes 368672 | tf_op jit(solution)/shard_map/ppermute | solution.py:43
  119.5 2.0 %collective-permute-done.33 = bf16[4,384,256]{2,1,0:T(8,128)(2,1)S(1)} collective-permute-done((bf16[4,384,256]{2,1,0:T(8,128)(2,1)S(1)}, bf16[4,384,256]{2,1,0:T(8,128)(2,1)S(1)}, u32[]{:S(2)}, u32[]{:S(2)}) %collective-permute-start.33) | collective-permute-done | bytes 786464 | tf_op jit(solution)/shard_map/ppermute | solution.py:43
  121.7 1.5 collective-permute-start.35
  123.2 2.0 %collective-permute-start.36 = (bf16[384,256]{1,0:T(8,128)(2,1)S(1)}, bf16[384,256]{1,0:T(8,128)(2,1)S(1)}, u32[]{:S(2)}, u32[]{:S(2)}) collective-permute-start(bf16[384,256]{1,0:T(8,128)(2,1)S(1)} %get-tuple-element.181), channel_id=1, source_target_pairs={{0,24},{4,28},{8,16},{12,20},{16,8},{20,12},{24,0},{28,4},{1,25},{... | collective-permute-start | bytes 589832 | tf_op jit(solution)/shard_map/ppermute | solution.py:43
  125.3 1.4 collective-permute-start.31
  126.6 0.7 dynamic-slice_bitcast_fusion.own
  127.3 2.1 %collective-permute-done.34 = bf16[384,256]{1,0:T(8,128)(2,1)S(1)} collective-permute-done((bf16[384,256]{1,0:T(8,128)(2,1)S(1)}, bf16[384,256]{1,0:T(8,128)(2,1)S(1)}, u32[]{:S(2)}, u32[]{:S(2)}) %collective-permute-start.34) | collective-permute-done | bytes 196640 | tf_op jit(solution)/shard_map/ppermute | solution.py:43
  129.4 0.9 collective-permute-start.32
  130.3 2.6 %collective-permute-done.35 = bf16[384,256]{1,0:T(8,128)(2,1)S(1)} collective-permute-done((bf16[384,256]{1,0:T(8,128)(2,1)S(1)}, bf16[384,256]{1,0:T(8,128)(2,1)S(1)}, u32[]{:S(2)}, u32[]{:S(2)}) %collective-permute-start.35) | collective-permute-done | bytes 196640 | tf_op jit(solution)/shard_map/ppermute | solution.py:43
  133.0 1.1 collective-permute-done.31.refs_1_
  134.2 1.7 %collective-permute-done.32.refs_2_ = bf16[72,640]{1,0:T(8,128)(2,1)S(1)} collective-permute-done((bf16[72,640]{1,0:T(8,128)(2,1)S(1)}, bf16[72,640]{1,0:T(8,128)(2,1)S(1)}, u32[]{:S(2)}, u32[]{:S(2)}) %collective-permute-start.32) | collective-permute-done | bytes 92192 | tf_op jit(solution)/shard_map/ppermute | solution.py:43
  135.9 0.9 collective-permute-start.37
  136.8 0.7 collective-permute-start.38
  137.5 2.9 %collective-permute-start.39 = (bf16[96,256]{1,0:T(8,128)(2,1)S(1)}, bf16[96,256]{1,0:T(8,128)(2,1)S(1)}, u32[]{:S(2)}, u32[]{:S(2)}) collective-permute-start(bf16[96,256]{1,0:T(8,128)(2,1)S(1)} %get-tuple-element.186), channel_id=1, source_target_pairs={{0,3},{1,2},{2,1},{3,0},{4,7},{5,6},{6,5},{7,4},{8,11},{9,10},{10,... | collective-permute-start | bytes 147464 | tf_op jit(solution)/shard_map/ppermute | solution.py:43
  140.4 2.2 %conv_step.1 = (f32[2,72,256]{2,1,0:T(8,128)}, f32[2,72,256]{2,1,0:T(8,128)}, f32[2,72,256]{2,1,0:T(8,128)}, f32[72,128]{1,0:T(8,128)}, f32[1,1]{1,0:T(1,128)}) custom-call(f32[72,640]{1,0:T(8,128)} %dynamic-slice_bitcast_fusion.own, bf16[72,640]{1,0:T(8,128)(2,1)} %copy-done.12, bf16[72,640]{1,0:T(8,128)(2,1)} %copy-done.13, bf16[72,640]{1,0:T(8,128)(2,1)} %copy-done.14, ...), custom_call_target="tpu_custom_call" | custom-call | bytes 1382404 | tf_op jit(solution)/shard_map/conv_step/pallas_call | solution.py:114
  142.6 0.8 multiply_subtract_fusion
  143.4 0.7 fusion.8.own
  144.0 0.7 copy.48
  144.7 0.7 copy.49
  145.4 0.7 copy.50
  147.3 1.8 %lateral_step.1 = (f32[32,256]{1,0:T(8,128)}, f32[32,256]{1,0:T(8,128)}, f32[32,256]{1,0:T(8,128)}, f32[64,256]{1,0:T(8,128)}, f32[64,256]{1,0:T(8,128)}, /*index=5*/f32[64,256]{1,0:T(8,128)}) custom-call(f32[96,256]{1,0:T(8,128)} %fusion.8.own, bf16[96,256]{1,0:T(8,128)(2,1)} %copy-done.18, bf16[96,256]{1,0:T(8,128)(2,1)} %copy-done.19, ...), custom_call_target="tpu_custom_call" | custom-call | bytes 835584 | tf_op jit(solution)/shard_map/lateral_step/pallas_call | solution.py:114
  (158 shorter events, 6.9 us)
Async XLA Ops:
  2.1 7.3 %collective-permute-start = (bf16[96,256]{1,0:T(8,128)(2,1)}, bf16[96,256]{1,0:T(8,128)(2,1)S(1)}, u32[]{:S(2)}, u32[]{:S(2)}) collective-permute-start(bf16[96,256]{1,0:T(8,128)(2,1)} %pack_laterals.1), channel_id=1, source_target_pairs={{0,1},{1,0},{2,3},{3,2},{4,5},{5,4},{6,7},{7,6},{8,9},{9,8},{10,11... | collective-permute-start | bytes 147464 | tf_op jit(solution)/shard_map/ppermute | solution.py:43
  5.2 6.1 %collective-permute-start.1 = (bf16[96,256]{1,0:T(8,128)(2,1)}, bf16[96,256]{1,0:T(8,128)(2,1)S(1)}, u32[]{:S(2)}, u32[]{:S(2)}) collective-permute-start(bf16[96,256]{1,0:T(8,128)(2,1)} %pack_laterals.1), channel_id=1, source_target_pairs={{0,2},{1,3},{2,0},{3,1},{4,6},{5,7},{6,4},{7,5},{8,10},{9,11},{10,... | collective-permute-start | bytes 147464 | tf_op jit(solution)/shard_map/ppermute | solution.py:43
  7.7 6.1 %collective-permute-start.2 = (bf16[96,256]{1,0:T(8,128)(2,1)}, bf16[96,256]{1,0:T(8,128)(2,1)S(1)}, u32[]{:S(2)}, u32[]{:S(2)}) collective-permute-start(bf16[96,256]{1,0:T(8,128)(2,1)} %pack_laterals.1), channel_id=1, source_target_pairs={{0,3},{1,2},{2,1},{3,0},{4,7},{5,6},{6,5},{7,4},{8,11},{9,10},{10,... | collective-permute-start | bytes 147464 | tf_op jit(solution)/shard_map/ppermute | solution.py:43
  14.8 19.0 %copy-start.2 = (bf16[384,256]{1,0:T(8,128)(2,1)}, bf16[384,256]{1,0:T(8,128)(2,1)S(1)}, u32[]{:S(2)}) copy-start(bf16[384,256]{1,0:T(8,128)(2,1)S(1)} %fusion.20.refs_0_) | copy-start | bytes 589828
  14.8 7.5 %collective-permute-start.3 = (bf16[72,640]{1,0:T(8,128)(2,1)}, bf16[72,640]{1,0:T(8,128)(2,1)S(1)}, u32[]{:S(2)}, u32[]{:S(2)}) collective-permute-start(bf16[72,640]{1,0:T(8,128)(2,1)} %pack_convs.1), channel_id=1, source_target_pairs={{0,1},{1,0},{2,3},{3,2},{4,5},{5,4},{6,7},{7,6},{8,9},{9,8},{10,11... | collective-permute-start | bytes 276488 | tf_op jit(solution)/shard_map/ppermute | solution.py:43
  14.9 8.9 %collective-permute-start.4 = (bf16[72,640]{1,0:T(8,128)(2,1)}, bf16[72,640]{1,0:T(8,128)(2,1)S(1)}, u32[]{:S(2)}, u32[]{:S(2)}) collective-permute-start(bf16[72,640]{1,0:T(8,128)(2,1)} %pack_convs.1), channel_id=1, source_target_pairs={{0,2},{1,3},{2,0},{3,1},{4,6},{5,7},{6,4},{7,5},{8,10},{9,11},{10,... | collective-permute-start | bytes 276488 | tf_op jit(solution)/shard_map/ppermute | solution.py:43
  16.2 7.6 %collective-permute-start.5 = (bf16[72,640]{1,0:T(8,128)(2,1)}, bf16[72,640]{1,0:T(8,128)(2,1)S(1)}, u32[]{:S(2)}, u32[]{:S(2)}) collective-permute-start(bf16[72,640]{1,0:T(8,128)(2,1)} %pack_convs.1), channel_id=1, source_target_pairs={{0,3},{1,2},{2,1},{3,0},{4,7},{5,6},{6,5},{7,4},{8,11},{9,10},{10,... | collective-permute-start | bytes 276488 | tf_op jit(solution)/shard_map/ppermute | solution.py:43
  19.3 6.6 %collective-permute-start.6 = (bf16[384,256]{1,0:T(8,128)(2,1)S(1)}, bf16[384,256]{1,0:T(8,128)(2,1)S(1)}, u32[]{:S(2)}, u32[]{:S(2)}) collective-permute-start(bf16[384,256]{1,0:T(8,128)(2,1)S(1)} %fusion.20.refs_0_), channel_id=1, source_target_pairs={{0,8},{4,12},{8,0},{12,4},{16,24},{20,28},{24,16},{28,20},{1,9},{5... | collective-permute-start | bytes 589832 | tf_op jit(solution)/shard_map/ppermute | solution.py:43
  20.8 8.4 %collective-permute-start.7 = (bf16[384,256]{1,0:T(8,128)(2,1)S(1)}, bf16[384,256]{1,0:T(8,128)(2,1)S(1)}, u32[]{:S(2)}, u32[]{:S(2)}) collective-permute-start(bf16[384,256]{1,0:T(8,128)(2,1)S(1)} %fusion.20.refs_0_), channel_id=1, source_target_pairs={{0,16},{4,20},{8,24},{12,28},{16,0},{20,4},{24,8},{28,12},{1,17},{... | collective-permute-start | bytes 589832 | tf_op jit(solution)/shard_map/ppermute | solution.py:43
  22.3 6.9 %collective-permute-start.8 = (bf16[384,256]{1,0:T(8,128)(2,1)S(1)}, bf16[384,256]{1,0:T(8,128)(2,1)S(1)}, u32[]{:S(2)}, u32[]{:S(2)}) collective-permute-start(bf16[384,256]{1,0:T(8,128)(2,1)S(1)} %fusion.20.refs_0_), channel_id=1, source_target_pairs={{0,24},{4,28},{8,16},{12,20},{16,8},{20,12},{24,0},{28,4},{1,25},{... | collective-permute-start | bytes 589832 | tf_op jit(solution)/shard_map/ppermute | solution.py:43
  24.9 24.6 %copy-start.1 = (bf16[288,640]{1,0:T(8,128)(2,1)}, bf16[288,640]{1,0:T(8,128)(2,1)S(1)}, u32[]{:S(2)}) copy-start(bf16[288,640]{1,0:T(8,128)(2,1)S(1)} %pad_maximum_fusion.1.refs_0_) | copy-start | bytes 1105924
  24.9 19.2 %copy-start.11 = (s32[2,8,128,3]{2,1,3,0:T(8,128)S(1)}, s32[2,8,128,3]{2,1,3,0:T(8,128)}, u32[]{:S(2)}) copy-start(s32[2,8,128,3]{2,1,3,0:T(8,128)} %param.25) | copy-start | bytes 73732
  24.9 19.2 %copy-start.16 = (s32[2,4,64,3]{2,1,3,0:T(4,128)S(1)}, s32[2,4,64,3]{2,1,3,0:T(4,128)}, u32[]{:S(2)}) copy-start(s32[2,4,64,3]{2,1,3,0:T(4,128)} %param.26) | copy-start | bytes 18436
  24.9 28.6 %copy-start.23 = (s32[2,2,32,3]{2,1,3,0:T(2,128)S(1)}, s32[2,2,32,3]{2,1,3,0:T(2,128)}, u32[]{:S(2)}) copy-start(s32[2,2,32,3]{2,1,3,0:T(2,128)} %param.27) | copy-start | bytes 4612
  25.9 7.9 %copy-start.3 = (bf16[384,256]{1,0:T(8,128)(2,1)}, bf16[384,256]{1,0:T(8,128)(2,1)S(1)}, u32[]{:S(2)}) copy-start(bf16[384,256]{1,0:T(8,128)(2,1)S(1)} %collective-permute-done.6.refs_2_) | copy-start | bytes 589828
  29.2 2.0 %collective-permute-start.10 = (bf16[384,256]{1,0:T(8,128)(2,1)S(1)}, bf16[384,256]{1,0:T(8,128)(2,1)S(1)}, u32[]{:S(2)}, u32[]{:S(2)}) collective-permute-start(bf16[384,256]{1,0:T(8,128)(2,1)S(1)} %collective-permute-done.6.refs_2_), channel_id=1, source_target_pairs={{0,4},{4,0},{8,12},{12,8},{16,20},{20,16},{24,28},{28,24},{1,5},{5... | collective-permute-start | bytes 589832 | tf_op jit(solution)/shard_map/ppermute | solution.py:43
  29.3 2.8 %collective-permute-start.11 = (bf16[384,256]{1,0:T(8,128)(2,1)S(1)}, bf16[384,256]{1,0:T(8,128)(2,1)S(1)}, u32[]{:S(2)}, u32[]{:S(2)}) collective-permute-start(bf16[384,256]{1,0:T(8,128)(2,1)S(1)} %collective-permute-done.7.refs_4_), channel_id=1, source_target_pairs={{0,4},{4,0},{8,12},{12,8},{16,20},{20,16},{24,28},{28,24},{1,5},{5... | collective-permute-start | bytes 589832 | tf_op jit(solution)/shard_map/ppermute | solution.py:43
  29.8 4.0 %collective-permute-start.12 = (bf16[384,256]{1,0:T(8,128)(2,1)S(1)}, bf16[384,256]{1,0:T(8,128)(2,1)S(1)}, u32[]{:S(2)}, u32[]{:S(2)}) collective-permute-start(bf16[384,256]{1,0:T(8,128)(2,1)S(1)} %collective-permute-done.8.refs_6_), channel_id=1, source_target_pairs={{0,4},{4,0},{8,12},{12,8},{16,20},{20,16},{24,28},{28,24},{1,5},{5... | collective-permute-start | bytes 589832 | tf_op jit(solution)/shard_map/ppermute | solution.py:43
  29.9 3.9 %collective-permute-start.9 = (bf16[384,256]{1,0:T(8,128)(2,1)S(1)}, bf16[384,256]{1,0:T(8,128)(2,1)S(1)}, u32[]{:S(2)}, u32[]{:S(2)}) collective-permute-start(bf16[384,256]{1,0:T(8,128)(2,1)S(1)} %fusion.20.refs_0_), channel_id=1, source_target_pairs={{0,4},{4,0},{8,12},{12,8},{16,20},{20,16},{24,28},{28,24},{1,5},{5... | collective-permute-start | bytes 589832 | tf_op jit(solution)/shard_map/ppermute | solution.py:43
  30.3 14.0 %collective-permute-start.13 = (bf16[288,640]{1,0:T(8,128)(2,1)S(1)}, bf16[288,640]{1,0:T(8,128)(2,1)S(1)}, u32[]{:S(2)}, u32[]{:S(2)}) collective-permute-start(bf16[288,640]{1,0:T(8,128)(2,1)S(1)} %pad_maximum_fusion.1.refs_0_), channel_id=1, source_target_pairs={{0,8},{4,12},{8,0},{12,4},{16,24},{20,28},{24,16},{28,20},{1,9},{5... | collective-permute-start | bytes 1105928 | tf_op jit(solution)/shard_map/ppermute | solution.py:43
  31.2 13.1 %collective-permute-start.14 = (bf16[288,640]{1,0:T(8,128)(2,1)S(1)}, bf16[288,640]{1,0:T(8,128)(2,1)S(1)}, u32[]{:S(2)}, u32[]{:S(2)}) collective-permute-start(bf16[288,640]{1,0:T(8,128)(2,1)S(1)} %pad_maximum_fusion.1.refs_0_), channel_id=1, source_target_pairs={{0,16},{4,20},{8,24},{12,28},{16,0},{20,4},{24,8},{28,12},{1,17},{... | collective-permute-start | bytes 1105928 | tf_op jit(solution)/shard_map/ppermute | solution.py:43
  32.1 17.4 %collective-permute-start.15 = (bf16[288,640]{1,0:T(8,128)(2,1)S(1)}, bf16[288,640]{1,0:T(8,128)(2,1)S(1)}, u32[]{:S(2)}, u32[]{:S(2)}) collective-permute-start(bf16[288,640]{1,0:T(8,128)(2,1)S(1)} %pad_maximum_fusion.1.refs_0_), channel_id=1, source_target_pairs={{0,24},{4,28},{8,16},{12,20},{16,8},{20,12},{24,0},{28,4},{1,25},{... | collective-permute-start | bytes 1105928 | tf_op jit(solution)/shard_map/ppermute | solution.py:43
  41.3 12.3 %copy-start.10 = (f32[2,8,128,12]{2,1,3,0:T(8,128)S(1)}, f32[2,8,128,12]{2,1,3,0:T(8,128)}, u32[]{:S(2)}) copy-start(f32[2,8,128,12]{2,1,3,0:T(8,128)} %param.22) | copy-start | bytes 294916
  41.3 12.3 %copy-start.17 = (f32[2,4,64,12]{2,1,3,0:T(4,128)S(1)}, f32[2,4,64,12]{2,1,3,0:T(4,128)}, u32[]{:S(2)}) copy-start(f32[2,4,64,12]{2,1,3,0:T(4,128)} %param.23) | copy-start | bytes 73732
  41.3 12.4 %copy-start.22 = (f32[2,2,32,12]{2,1,3,0:T(2,128)S(1)}, f32[2,2,32,12]{2,1,3,0:T(2,128)}, u32[]{:S(2)}) copy-start(f32[2,2,32,12]{2,1,3,0:T(2,128)} %param.24) | copy-start | bytes 18436
  41.3 8.1 %collective-permute-start.16 = (bf16[2,192,256]{2,1,0:T(8,128)(2,1)}, bf16[2,192,256]{2,1,0:T(8,128)(2,1)S(1)}, u32[]{:S(2)}, u32[]{:S(2)}) collective-permute-start(bf16[2,192,256]{2,1,0:T(8,128)(2,1)} %get-tuple-element.88), channel_id=1, source_target_pairs={{0,4},{4,8},{8,12},{12,16},{16,20},{20,24},{24,28},{1,5},{5,9},{9,... | collective-permute-start | bytes 589832 | tf_op jit(solution)/shard_map/ppermute | solution.py:106
  42.8 6.7 %collective-permute-start.17 = (bf16[2,192,256]{2,1,0:T(8,128)(2,1)}, bf16[2,192,256]{2,1,0:T(8,128)(2,1)}, u32[]{:S(2)}, u32[]{:S(2)}) collective-permute-start(bf16[2,192,256]{2,1,0:T(8,128)(2,1)} %get-tuple-element.89), channel_id=1, source_target_pairs={{4,0},{8,4},{12,8},{16,12},{20,16},{24,20},{28,24},{5,1},{9,5},{13... | collective-permute-start | bytes 589832 | tf_op jit(solution)/shard_map/ppermute | solution.py:107
  44.3 11.6 %copy-start.27 = (bf16[288,640]{1,0:T(8,128)(2,1)}, bf16[288,640]{1,0:T(8,128)(2,1)S(1)}, u32[]{:S(2)}) copy-start(bf16[288,640]{1,0:T(8,128)(2,1)S(1)} %collective-permute-done.13.refs_2_) | copy-start | bytes 1105924
  44.3 11.6 %copy-start.28 = (bf16[288,640]{1,0:T(8,128)(2,1)}, bf16[288,640]{1,0:T(8,128)(2,1)S(1)}, u32[]{:S(2)}) copy-start(bf16[288,640]{1,0:T(8,128)(2,1)S(1)} %collective-permute-done.14.refs_4_) | copy-start | bytes 1105924
  49.4 6.4 %copy-start.29 = (bf16[288,640]{1,0:T(8,128)(2,1)}, bf16[288,640]{1,0:T(8,128)(2,1)S(1)}, u32[]{:S(2)}) copy-start(bf16[288,640]{1,0:T(8,128)(2,1)S(1)} %collective-permute-done.15.refs_6_) | copy-start | bytes 1105924
  49.4 6.4 %copy-start.33 = (bf16[2,192,256]{2,1,0:T(8,128)(2,1)}, bf16[2,192,256]{2,1,0:T(8,128)(2,1)S(1)}, u32[]{:S(2)}) copy-start(bf16[2,192,256]{2,1,0:T(8,128)(2,1)S(1)} %collective-permute-done.16.above) | copy-start | bytes 589828
  49.5 5.1 %collective-permute-start.18 = (bf16[288,640]{1,0:T(8,128)(2,1)S(1)}, bf16[288,640]{1,0:T(8,128)(2,1)S(1)}, u32[]{:S(2)}, u32[]{:S(2)}) collective-permute-start(bf16[288,640]{1,0:T(8,128)(2,1)S(1)} %pad_maximum_fusion.1.refs_0_), channel_id=1, source_target_pairs={{0,4},{4,0},{8,12},{12,8},{16,20},{20,16},{24,28},{28,24},{1,5},{5... | collective-permute-start | bytes 1105928 | tf_op jit(solution)/shard_map/ppermute | solution.py:43
  53.0 2.4 %collective-permute-start.19 = (bf16[288,640]{1,0:T(8,128)(2,1)S(1)}, bf16[288,640]{1,0:T(8,128)(2,1)S(1)}, u32[]{:S(2)}, u32[]{:S(2)}) collective-permute-start(bf16[288,640]{1,0:T(8,128)(2,1)S(1)} %collective-permute-done.13.refs_2_), channel_id=1, source_target_pairs={{0,4},{4,0},{8,12},{12,8},{16,20},{20,16},{24,28},{28,24},{1,5},{5... | collective-permute-start | bytes 1105928 | tf_op jit(solution)/shard_map/ppermute | solution.py:43
  53.0 2.9 %collective-permute-start.20 = (bf16[288,640]{1,0:T(8,128)(2,1)S(1)}, bf16[288,640]{1,0:T(8,128)(2,1)S(1)}, u32[]{:S(2)}, u32[]{:S(2)}) collective-permute-start(bf16[288,640]{1,0:T(8,128)(2,1)S(1)} %collective-permute-done.14.refs_4_), channel_id=1, source_target_pairs={{0,4},{4,0},{8,12},{12,8},{16,20},{20,16},{24,28},{28,24},{1,5},{5... | collective-permute-start | bytes 1105928 | tf_op jit(solution)/shard_map/ppermute | solution.py:43
  53.5 2.4 %collective-permute-start.21 = (bf16[288,640]{1,0:T(8,128)(2,1)S(1)}, bf16[288,640]{1,0:T(8,128)(2,1)}, u32[]{:S(2)}, u32[]{:S(2)}) collective-permute-start(bf16[288,640]{1,0:T(8,128)(2,1)S(1)} %collective-permute-done.15.refs_6_), channel_id=1, source_target_pairs={{0,4},{4,0},{8,12},{12,8},{16,20},{20,16},{24,28},{28,24},{1,5},{5... | collective-permute-start | bytes 1105928 | tf_op jit(solution)/shard_map/ppermute | solution.py:43
  65.2 3.8 %collective-permute-start.22 = (f32[2,3,16,384]{3,2,1,0:T(8,128)}, f32[2,3,16,384]{3,2,1,0:T(8,128)S(1)}, u32[]{:S(2)}, u32[]{:S(2)}) collective-permute-start(f32[2,3,16,384]{3,2,1,0:T(8,128)} %get-tuple-element.103), channel_id=1, source_target_pairs={{0,4},{4,8},{8,12},{12,16},{16,20},{20,24},{24,28},{1,5},{5,9},{9,... | collective-permute-start | bytes 442376 | tf_op jit(solution)/shard_map/ppermute | solution.py:106
  67.5 4.1 %collective-permute-start.23 = (f32[2,3,16,384]{3,2,1,0:T(8,128)}, f32[2,3,16,384]{3,2,1,0:T(8,128)S(1)}, u32[]{:S(2)}, u32[]{:S(2)}) collective-permute-start(f32[2,3,16,384]{3,2,1,0:T(8,128)} %get-tuple-element.104), channel_id=1, source_target_pairs={{4,0},{8,4},{12,8},{16,12},{20,16},{24,20},{28,24},{5,1},{9,5},{13... | collective-permute-start | bytes 442376 | tf_op jit(solution)/shard_map/ppermute | solution.py:107
  77.0 11.9 %copy-start.36 = (bf16[2,192,256]{2,1,0:T(8,128)(2,1)S(1)}, bf16[2,192,256]{2,1,0:T(8,128)(2,1)}, u32[]{:S(2)}) copy-start(bf16[2,192,256]{2,1,0:T(8,128)(2,1)} %get-tuple-element.110) | copy-start | bytes 589828
  77.0 13.9 %copy-start.34 = (bf16[2,192,256]{2,1,0:T(8,128)(2,1)S(1)}, bf16[2,192,256]{2,1,0:T(8,128)(2,1)}, u32[]{:S(2)}) copy-start(bf16[2,192,256]{2,1,0:T(8,128)(2,1)} %get-tuple-element.111) | copy-start | bytes 589828
  85.2 7.2 %collective-permute-start.26 = (bf16[4,288,640]{2,1,0:T(8,128)(2,1)}, bf16[4,288,640]{2,1,0:T(8,128)(2,1)S(1)}, u32[]{:S(2)}, u32[]{:S(2)}) collective-permute-start(bf16[4,288,640]{2,1,0:T(8,128)(2,1)} %get-tuple-element.115), channel_id=1, source_target_pairs={{0,4},{4,0},{8,12},{12,8},{16,20},{20,16},{24,28},{28,24},{1,5},{5... | collective-permute-start | bytes 4423688 | tf_op jit(solution)/shard_map/ppermute | solution.py:43
  88.9 6.1 %collective-permute-start.24 = (bf16[2,192,256]{2,1,0:T(8,128)(2,1)S(1)}, bf16[2,192,256]{2,1,0:T(8,128)(2,1)S(1)}, u32[]{:S(2)}, u32[]{:S(2)}) collective-permute-start(bf16[2,192,256]{2,1,0:T(8,128)(2,1)S(1)} %copy-done.36), channel_id=1, source_target_pairs={{0,4},{4,8},{8,12},{12,16},{16,20},{20,24},{24,28},{1,5},{5,9},{9,... | collective-permute-start | bytes 589832 | tf_op jit(solution)/shard_map/ppermute | solution.py:106
  90.9 5.0 %collective-permute-start.25 = (bf16[2,192,256]{2,1,0:T(8,128)(2,1)S(1)}, bf16[2,192,256]{2,1,0:T(8,128)(2,1)S(1)}, u32[]{:S(2)}, u32[]{:S(2)}) collective-permute-start(bf16[2,192,256]{2,1,0:T(8,128)(2,1)S(1)} %copy-done.34), channel_id=1, source_target_pairs={{4,0},{8,4},{12,8},{16,12},{20,16},{24,20},{28,24},{5,1},{9,5},{13... | collective-permute-start | bytes 589832 | tf_op jit(solution)/shard_map/ppermute | solution.py:107
  95.0 6.2 %copy-start.35 = (bf16[2,192,256]{2,1,0:T(8,128)(2,1)}, bf16[2,192,256]{2,1,0:T(8,128)(2,1)S(1)}, u32[]{:S(2)}) copy-start(bf16[2,192,256]{2,1,0:T(8,128)(2,1)S(1)} %collective-permute-done.24.above) | copy-start | bytes 589828
  95.8 5.3 %copy-start.37 = (bf16[2,192,256]{2,1,0:T(8,128)(2,1)}, bf16[2,192,256]{2,1,0:T(8,128)(2,1)S(1)}, u32[]{:S(2)}) copy-start(bf16[2,192,256]{2,1,0:T(8,128)(2,1)S(1)} %collective-permute-done.25.below) | copy-start | bytes 589828
  95.8 18.4 %collective-permute-start.27 = (bf16[288,640]{1,0:T(8,128)(2,1)S(1)}, bf16[288,640]{1,0:T(8,128)(2,1)S(1)}, u32[]{:S(2)}, u32[]{:S(2)}) collective-permute-start(bf16[288,640]{1,0:T(8,128)(2,1)S(1)} %get-tuple-element.124), channel_id=1, source_target_pairs={{0,8},{4,12},{8,0},{12,4},{16,24},{20,28},{24,16},{28,20},{1,9},{5... | collective-permute-start | bytes 1105928 | tf_op jit(solution)/shard_map/ppermute | solution.py:43
  99.7 19.2 %collective-permute-start.28 = (bf16[288,640]{1,0:T(8,128)(2,1)S(1)}, bf16[288,640]{1,0:T(8,128)(2,1)S(1)}, u32[]{:S(2)}, u32[]{:S(2)}) collective-permute-start(bf16[288,640]{1,0:T(8,128)(2,1)S(1)} %get-tuple-element.125), channel_id=1, source_target_pairs={{0,16},{4,20},{8,24},{12,28},{16,0},{20,4},{24,8},{28,12},{1,17},{... | collective-permute-start | bytes 1105928 | tf_op jit(solution)/shard_map/ppermute | solution.py:43
  99.7 19.2 %collective-permute-start.29 = (bf16[288,640]{1,0:T(8,128)(2,1)S(1)}, bf16[288,640]{1,0:T(8,128)(2,1)S(1)}, u32[]{:S(2)}, u32[]{:S(2)}) collective-permute-start(bf16[288,640]{1,0:T(8,128)(2,1)S(1)} %get-tuple-element.126), channel_id=1, source_target_pairs={{0,24},{4,28},{8,16},{12,20},{16,8},{20,12},{24,0},{28,4},{1,25},{... | collective-permute-start | bytes 1105928 | tf_op jit(solution)/shard_map/ppermute | solution.py:43
  114.2 4.9 %copy-start.26 = (bf16[4,384,256]{2,1,0:T(8,128)(2,1)S(1)}, bf16[4,384,256]{2,1,0:T(8,128)(2,1)}, u32[]{:S(2)}) copy-start(bf16[4,384,256]{2,1,0:T(8,128)(2,1)} %get-tuple-element.129) | copy-start | bytes 2359300
  114.2 5.0 %copy-start.21 = (f32[72,12]{0,1:T(8,128)S(1)}, f32[72,12]{0,1:T(8,128)}, u32[]{:S(2)}) copy-start(f32[72,12]{0,1:T(8,128)} %param.31) | copy-start | bytes 10372
  114.2 5.1 %copy-start.24 = (f32[72,12]{0,1:T(8,128)S(1)}, f32[72,12]{0,1:T(8,128)}, u32[]{:S(2)}) copy-start(f32[72,12]{0,1:T(8,128)} %param.35) | copy-start | bytes 10372
  114.2 5.2 %copy-start.25 = (f32[72,12]{0,1:T(8,128)S(1)}, f32[72,12]{0,1:T(8,128)}, u32[]{:S(2)}) copy-start(f32[72,12]{0,1:T(8,128)} %param.39) | copy-start | bytes 10372
  114.2 7.3 %copy-start = (bf16[4,384,256]{2,1,0:T(8,128)(2,1)S(1)}, bf16[4,384,256]{2,1,0:T(8,128)(2,1)}, u32[]{:S(2)}) copy-start(bf16[4,384,256]{2,1,0:T(8,128)(2,1)} %get-tuple-element.128) | copy-start | bytes 2359300
  119.1 2.4 %collective-permute-start.33 = (bf16[4,384,256]{2,1,0:T(8,128)(2,1)S(1)}, bf16[4,384,256]{2,1,0:T(8,128)(2,1)S(1)}, u32[]{:S(2)}, u32[]{:S(2)}) collective-permute-start(bf16[4,384,256]{2,1,0:T(8,128)(2,1)S(1)} %copy-done.26), channel_id=1, source_target_pairs={{0,4},{4,0},{8,12},{12,8},{16,20},{20,16},{24,28},{28,24},{1,5},{5... | collective-permute-start | bytes 2359304 | tf_op jit(solution)/shard_map/ppermute | solution.py:43
  121.6 7.8 %collective-permute-start.34 = (bf16[384,256]{1,0:T(8,128)(2,1)S(1)}, bf16[384,256]{1,0:T(8,128)(2,1)S(1)}, u32[]{:S(2)}, u32[]{:S(2)}) collective-permute-start(bf16[384,256]{1,0:T(8,128)(2,1)S(1)} %get-tuple-element.180), channel_id=1, source_target_pairs={{0,8},{4,12},{8,0},{12,4},{16,24},{20,28},{24,16},{28,20},{1,9},{5... | collective-permute-start | bytes 589832 | tf_op jit(solution)/shard_map/ppermute | solution.py:43
  121.7 11.2 %collective-permute-start.35 = (bf16[384,256]{1,0:T(8,128)(2,1)S(1)}, bf16[384,256]{1,0:T(8,128)(2,1)S(1)}, u32[]{:S(2)}, u32[]{:S(2)}) collective-permute-start(bf16[384,256]{1,0:T(8,128)(2,1)S(1)} %get-tuple-element.182), channel_id=1, source_target_pairs={{0,16},{4,20},{8,24},{12,28},{16,0},{20,4},{24,8},{28,12},{1,17},{... | collective-permute-start | bytes 589832 | tf_op jit(solution)/shard_map/ppermute | solution.py:43
  123.2 9.7 %collective-permute-start.36 = (bf16[384,256]{1,0:T(8,128)(2,1)S(1)}, bf16[384,256]{1,0:T(8,128)(2,1)S(1)}, u32[]{:S(2)}, u32[]{:S(2)}) collective-permute-start(bf16[384,256]{1,0:T(8,128)(2,1)S(1)} %get-tuple-element.181), channel_id=1, source_target_pairs={{0,24},{4,28},{8,16},{12,20},{16,8},{20,12},{24,0},{28,4},{1,25},{... | collective-permute-start | bytes 589832 | tf_op jit(solution)/shard_map/ppermute | solution.py:43
  125.2 7.8 %collective-permute-start.30 = (bf16[72,640]{1,0:T(8,128)(2,1)S(1)}, bf16[72,640]{1,0:T(8,128)(2,1)S(1)}, u32[]{:S(2)}, u32[]{:S(2)}) collective-permute-start(bf16[72,640]{1,0:T(8,128)(2,1)S(1)} %get-tuple-element.185), channel_id=1, source_target_pairs={{0,1},{1,0},{2,3},{3,2},{4,5},{5,4},{6,7},{7,6},{8,9},{9,8},{10,11... | collective-permute-start | bytes 276488 | tf_op jit(solution)/shard_map/ppermute | solution.py:43
  125.3 8.9 %collective-permute-start.31 = (bf16[72,640]{1,0:T(8,128)(2,1)S(1)}, bf16[72,640]{1,0:T(8,128)(2,1)S(1)}, u32[]{:S(2)}, u32[]{:S(2)}) collective-permute-start(bf16[72,640]{1,0:T(8,128)(2,1)S(1)} %get-tuple-element.184), channel_id=1, source_target_pairs={{0,2},{1,3},{2,0},{3,1},{4,6},{5,7},{6,4},{7,5},{8,10},{9,11},{10,... | collective-permute-start | bytes 276488 | tf_op jit(solution)/shard_map/ppermute | solution.py:43
  129.4 6.5 %collective-permute-start.32 = (bf16[72,640]{1,0:T(8,128)(2,1)S(1)}, bf16[72,640]{1,0:T(8,128)(2,1)S(1)}, u32[]{:S(2)}, u32[]{:S(2)}) collective-permute-start(bf16[72,640]{1,0:T(8,128)(2,1)S(1)} %get-tuple-element.183), channel_id=1, source_target_pairs={{0,3},{1,2},{2,1},{3,0},{4,7},{5,6},{6,5},{7,4},{8,11},{9,10},{10,... | collective-permute-start | bytes 276488 | tf_op jit(solution)/shard_map/ppermute | solution.py:43
  133.0 7.4 %copy-start.12 = (bf16[72,640]{1,0:T(8,128)(2,1)}, bf16[72,640]{1,0:T(8,128)(2,1)S(1)}, u32[]{:S(2)}) copy-start(bf16[72,640]{1,0:T(8,128)(2,1)S(1)} %collective-permute-done.30.refs_0_) | copy-start | bytes 276484
  134.2 6.2 %copy-start.13 = (bf16[72,640]{1,0:T(8,128)(2,1)}, bf16[72,640]{1,0:T(8,128)(2,1)S(1)}, u32[]{:S(2)}) copy-start(bf16[72,640]{1,0:T(8,128)(2,1)S(1)} %collective-permute-done.31.refs_1_) | copy-start | bytes 276484
  135.9 10.1 %collective-permute-start.37 = (bf16[96,256]{1,0:T(8,128)(2,1)S(1)}, bf16[96,256]{1,0:T(8,128)(2,1)S(1)}, u32[]{:S(2)}, u32[]{:S(2)}) collective-permute-start(bf16[96,256]{1,0:T(8,128)(2,1)S(1)} %get-tuple-element.187), channel_id=1, source_target_pairs={{0,1},{1,0},{2,3},{3,2},{4,5},{5,4},{6,7},{7,6},{8,9},{9,8},{10,11... | collective-permute-start | bytes 147464 | tf_op jit(solution)/shard_map/ppermute | solution.py:43
  136.8 9.2 %collective-permute-start.38 = (bf16[96,256]{1,0:T(8,128)(2,1)S(1)}, bf16[96,256]{1,0:T(8,128)(2,1)S(1)}, u32[]{:S(2)}, u32[]{:S(2)}) collective-permute-start(bf16[96,256]{1,0:T(8,128)(2,1)S(1)} %get-tuple-element.188), channel_id=1, source_target_pairs={{0,2},{1,3},{2,0},{3,1},{4,6},{5,7},{6,4},{7,5},{8,10},{9,11},{10,... | collective-permute-start | bytes 147464 | tf_op jit(solution)/shard_map/ppermute | solution.py:43
  137.5 8.6 %collective-permute-start.39 = (bf16[96,256]{1,0:T(8,128)(2,1)S(1)}, bf16[96,256]{1,0:T(8,128)(2,1)S(1)}, u32[]{:S(2)}, u32[]{:S(2)}) collective-permute-start(bf16[96,256]{1,0:T(8,128)(2,1)S(1)} %get-tuple-element.186), channel_id=1, source_target_pairs={{0,3},{1,2},{2,1},{3,0},{4,7},{5,6},{6,5},{7,4},{8,11},{9,10},{10,... | collective-permute-start | bytes 147464 | tf_op jit(solution)/shard_map/ppermute | solution.py:43
  (16 other events, 29.7 us)

commit v3 on v2

--- a/solution.py
+++ b/solution.py
@@ -1,4 +1,5 @@
 import functools
+import math
 
 import jax
 import jax.numpy as jnp
@@ -11,7 +12,8 @@
 
 LANES = 128
 DELTA_ROWS = 16
-VMEM_BYTES = 56 * 1024 * 1024
+SPARE_BYTES = 12 * 1024 * 1024
+ALL_BYTES = 60 * 1024 * 1024
 
 box_beta = 1.0 / 9.0
 beta_one = 0.5
@@ -101,26 +103,45 @@
     return [own, *came]
 
 
-def from_neighbours(first, last):
+def from_neighbours(pair, other):
     count = lax.axis_size("rows")
-    above = lax.ppermute(last, "rows", [(i, i + 1) for i in range(count - 1)])
-    below = lax.ppermute(first, "rows", [(i + 1, i) for i in range(count - 1)])
-    return above, below
-
-
-def call(kernel, name, args, outs, scratch=(), flops=0, scalars=0, scalar_outs=0):
+    links = [(i, i + 1) for i in range(1, count - 1, 2)]
+    return sent(pair, "rows", 1), lax.ppermute(other, "rows", links + [(j, i) for i, j in links])
+
+
+def call(kernel, name, args, outs, scratch=(), flops=0, scalars=0, scalar_outs=0, apart=0):
     vmem, smem = pl.BlockSpec(memory_space=pltpu.VMEM), pl.BlockSpec(memory_space=pltpu.SMEM)
+    hbm = pl.BlockSpec(memory_space=pltpu.HBM)
     size = sum(a.size * a.dtype.itemsize for a in (*args, *outs))
+    held = sum(
+        math.prod(ref.shape) * jnp.dtype(ref.dtype).itemsize
+        for ref in scratch
+        if ref.memory_space == pltpu.VMEM
+    )
     return pl.pallas_call(
         kernel,
         out_shape=list(outs),
-        in_specs=[vmem] * (len(args) - scalars) + [smem] * scalars,
+        in_specs=[hbm] * apart + [vmem] * (len(args) - scalars - apart) + [smem] * scalars,
         out_specs=[vmem] * (len(outs) - scalar_outs) + [smem] * scalar_outs,
         scratch_shapes=list(scratch),
-        compiler_params=pltpu.CompilerParams(vmem_limit_bytes=VMEM_BYTES),
+        compiler_params=pltpu.CompilerParams(vmem_limit_bytes=ALL_BYTES if apart else held + SPARE_BYTES),
         cost_estimate=pl.CostEstimate(flops=flops, bytes_accessed=size, transcendentals=0),
         name=name,
     )(*args)
+
+
+def swapped(upper, lower, pair, other, outward):
+    odd = lax.axis_index("rows") % 2 == 1
+
+    def move(one, two):
+        for ref, side in ((one, pair), (two, other)):
+            if outward:
+                side[...] = ref[...]
+            else:
+                ref[...] = side[...]
+
+    pl.when(odd)(lambda: move(upper, lower))
+    pl.when(jnp.logical_not(odd))(lambda: move(lower, upper))
 
 
 def dot(left, right, dims=((1,), (0,))):
@@ -149,34 +170,92 @@
     return high, middle, value - high - middle
 
 
-def pack_lateral_kernel(four, five, packed):
+def pack_kernel(*refs):
+    sources, packed, square, held, arrived = refs[:6], refs[6], refs[7], refs[8:14], refs[14]
+    copies = [
+        pltpu.make_async_copy(source, target, arrived.at[k])
+        for k, (source, target) in enumerate(zip(sources, held))
+    ]
+    for copy in copies:
+        copy.start()
+    for copy in copies:
+        copy.wait()
+    four, five, head, anchor_four, anchor_five, anchor_six = held
+    lines = four.shape[0] + five.shape[0]
     packed[: four.shape[0]] = four[...].astype(bf16)
-    packed[four.shape[0] :] = five[...].astype(bf16)
-
-
-def pack_conv_kernel(conv, head, anchor_four, anchor_five, anchor_six, packed, square):
-    lines, channels = conv.shape[1:]
-    deltas = head.shape[0]
+    packed[four.shape[0] : lines] = five[...].astype(bf16)
     total = jnp.zeros((1, 1), f32)
     for anchor in (anchor_four, anchor_five, anchor_six):
         total = total + jnp.sum(anchor[...].astype(f32), keepdims=True).reshape(1, 1)
     square[...] = jnp.zeros_like(square)
-    square[:deltas, :lines] = head[...]
-    spare = square[...].T[:lines]
+    square[: head.shape[0], : head.shape[1]] = head[...]
+    spare = square[...]
     line = lax.broadcasted_iota(jnp.int32, spare.shape, 0)
     lane = lax.broadcasted_iota(jnp.int32, spare.shape, 1)
     for k, piece in enumerate(pieces_of(jnp.broadcast_to(total, spare.shape))):
-        spare = jnp.where((line == 0) & (lane == deltas + k), piece, spare)
-    packed[:, :channels] = conv[0].astype(bf16)
-    packed[:, channels : 2 * channels] = conv[1].astype(bf16)
-    packed[:, 2 * channels :] = spare.astype(bf16)
+        spare = jnp.where((line == head.shape[0]) & (lane == k), piece, spare)
+    packed[lines:] = joined(spare).astype(bf16)
+
+
+def joined(square):
+    return jnp.concatenate([square[:8], square[8:]], axis=1)
+
+
+def parted(lines):
+    return jnp.concatenate([lines[:, :LANES], lines[:, LANES:]], axis=0)
+
+
+def head_weights_kernel(n_rows, n_batch, deltas, own, *refs):
+    pieces, (head, count, flat) = refs[:n_rows], refs[n_rows:]
+    channels = head.shape[1]
+    me = lax.axis_index("rows")
+    flat[...] = jnp.zeros_like(flat)
+    line = lax.broadcasted_iota(jnp.int32, (DELTA_ROWS, LANES), 0)
+    total = jnp.zeros((DELTA_ROWS, LANES), f32)
+    for k in range(n_rows):
+        lines = pieces[k][pieces[k].shape[0] - 8 * n_batch :].astype(f32)
+        for z in range(n_batch):
+            square = parted(lines[8 * z : 8 * z + 8])
+            total = total + jnp.where(line >= deltas, square, 0.0)
+            square = jnp.where(line < deltas, square, 0.0)
+            place = ((me ^ k) * n_batch + z) * own
+            wide = jnp.concatenate([square, jnp.zeros_like(square)], axis=1)
+            wide = pltpu.roll(wide, place % LANES, 1)
+            at = pl.ds(pl.multiple_of(place // LANES * LANES, LANES), 2 * LANES)
+            flat[:, at] += wide
+    for t in range(9):
+        block = flat[:, t * channels : (t + 1) * channels].astype(bf16)
+        head[t * DELTA_ROWS : (t + 1) * DELTA_ROWS, :] = block
+    count[0, 0] = jnp.sum(total)
+
+
+def planes_kernel(*refs):
+    targets, anchors, (target, mask) = refs[:3], refs[3:6], refs[-2:]
+    crops, deltas = targets[0].shape[:2]
+    own = 0
+    target[:, deltas:, :] = jnp.zeros((crops, target.shape[1] - deltas, target.shape[2]), f32)
+    mask[:, deltas:, :] = jnp.zeros((crops, mask.shape[1] - deltas, mask.shape[2]), f32)
+    for target_ref, anchor_ref in zip(targets, anchors):
+        _, count, lines, width = anchor_ref.shape
+        share = deltas // count
+        for b in range(crops):
+            for r in range(lines):
+                at, rest = own + r * LANES, LANES - width
+                target[b, :deltas, at : at + width] = target_ref[b, :, r, :]
+                if rest:
+                    target[b, :deltas, at + width : at + LANES] = jnp.zeros((deltas, rest), f32)
+                    mask[b, :deltas, at + width : at + LANES] = jnp.zeros((deltas, rest), f32)
+                for a in range(count):
+                    row = anchor_ref[b, a, r : r + 1, :].astype(f32)
+                    mask[b, a * share : (a + 1) * share, at : at + width] = jnp.broadcast_to(
+                        row, (share, width)
+                    )
+        own += lines * LANES
 
 
 def lateral_kernel(n_rows, four, five, *refs):
-    pieces, (input_four, input_five, first, last, kernel_four, kernel_five, wide) = (
-        refs[:n_rows],
-        refs[n_rows:],
-    )
+    pieces, rest = refs[:n_rows], refs[n_rows:]
+    input_four, input_five, pair, other, kernel_four, kernel_five, wide, first, last = rest
     crops, height, width, depth = four.shape
     low_height, low_width = five.shape[1:3]
     me = lax.axis_index("rows")
@@ -186,7 +265,7 @@
         at_four = pl.multiple_of(owner * part_four, part_four)
         at_five = pl.multiple_of(owner * part_five, part_five)
         kernel_four[pl.ds(at_four, part_four), :] = pieces[k][:part_four]
-        kernel_five[pl.ds(at_five, part_five), :] = pieces[k][part_four:]
+        kernel_five[pl.ds(at_five, part_five), :] = pieces[k][part_four : part_four + part_five]
     for b in range(crops):
         low = dot(five[b].reshape(low_height * low_width, -1), kernel_five[...])
         low_rounded = low.astype(bf16).reshape(low_height, low_width, -1)
@@ -203,6 +282,7 @@
                 first[b, :width] = rounded[0]
             if q == low_height - 1:
                 last[b, :width] = rounded[1]
+    swapped(first, last, pair, other, True)
 
 
 def three_taps(source, b, start, rows, weights, step):
@@ -233,32 +313,19 @@
         padded[b, height + 1] = below[b, start : start + width]
 
 
-def output_kernel(n_rows, deltas, input_four, input_five, above, below, target, mask, *refs):
-    pieces, (levels, values, first, last, kernel_four, kernel_five, head, count, spread_four, spread_five, wide) = (
-        refs[:n_rows],
-        refs[n_rows:],
-    )
+def output_kernel(n_rows, input_four, input_five, pair_in, other_in, head, target, mask, *refs):
+    pieces, rest = refs[:n_rows], refs[n_rows:]
+    levels, values, pair, other, kernel_four, kernel_five = rest[:6]
+    spread_four, spread_five, spare, above, below, first, last = rest[6:]
+    swapped(above, below, pair_in, other_in, False)
     crops, height, width, channels = input_four.shape
     low_height, low_width = input_five.shape[1:3]
     me = lax.axis_index("rows")
     part = 9 * channels // n_rows
-    positives = jnp.zeros((), f32)
-    spare = wide.at[:]
     for k in range(n_rows):
         at = pl.multiple_of((me ^ k) * part, part)
         kernel_four[pl.ds(at, part), :] = pieces[k][:, :channels]
-        kernel_five[pl.ds(at, part), :] = pieces[k][:, channels : 2 * channels]
-        spare[pl.ds(at, part), :] = pieces[k][:, 2 * channels :].astype(f32)
-    lane = lax.broadcasted_iota(jnp.int32, (channels, LANES), 1)
-    line = lax.broadcasted_iota(jnp.int32, (DELTA_ROWS, channels), 0)
-    for t in range(9):
-        block = spare[t * channels : (t + 1) * channels, :]
-        positives = positives + jnp.sum(
-            jnp.where((lane >= deltas) & (lane < deltas + 3), block, 0.0)
-        )
-        turned_block = jnp.where(line < deltas, block.T[:DELTA_ROWS], 0.0)
-        head[t * DELTA_ROWS : (t + 1) * DELTA_ROWS, :] = turned_block.astype(bf16)
-    count[0, 0] = positives
+        kernel_five[pl.ds(at, part), :] = pieces[k][:, channels:]
     fill_padded(spread_four, input_four, above, below, 0)
     fill_padded(spread_five, input_five, above, below, width)
     low_start, top_start = height, height + low_height
@@ -315,13 +382,27 @@
             values[b, :, start : start + width] = sums[:, start : start + width]
             values[b, :, start + width : end - width] = partial
             values[b, :, end - width : end] = sums[:, end - width : end]
-            at = slice(index * width, (index + 1) * width)
-            first[b, 0, :, at] = partial[:, :width]
-            last[b, 0, :, at] = partial[:, (count_lines - 1) * width :]
-            first[b, 1, :, at] = sums[:, start : start + width]
-            last[b, 1, :, at] = sums[:, end - width : end]
-            first[b, 2, :, at] = mask[b, :, own * width : (own + 1) * width]
-            last[b, 2, :, at] = mask[b, :, (own + count_lines - 1) * width : (own + count_lines) * width]
+            own_end = (own + count_lines) * width
+            upper = (
+                partial[:, :width],
+                sums[:, start : start + width],
+                mask[b, :, own * width : (own + 1) * width],
+            )
+            lower = (
+                partial[:, (count_lines - 1) * width :],
+                sums[:, end - width : end],
+                mask[b, :, own_end - width : own_end],
+            )
+            for out, values_of in ((first, upper), (last, lower)):
+                for kind, line in enumerate(values_of):
+                    if index < 2:
+                        out[b, kind, :, index * width : (index + 1) * width] = line
+                    else:
+                        moved = pltpu.roll(line, half, 1)
+                        lane = lax.broadcasted_iota(jnp.int32, line.shape, 1)
+                        mixed = jnp.where(lane < half, out[b, kind, :, width : 2 * width], moved)
+                        out[b, kind, :, width : 2 * width] = mixed
+    swapped(first, last, pair, other, True)
 
 
 def level_rows(height, rim):
@@ -332,30 +413,41 @@
     return result
 
 
-def head_kernel(height, levels, above, below, head, values, mask, count, head_grad, grad_four, grad_five, first, last, loss, taps, wide):
+def head_kernel(height, levels, pair_in, other_in, head, values, mask, count, *refs):
+    head_grad, grad_four, grad_five, pair, other, loss = refs[:6]
+    taps, wide, above, below, first, last = refs[6:]
+    swapped(above, below, pair_in, other_in, False)
     crops, _, width, channels = levels.shape
     inverse = 1.0 / jnp.maximum(count[0, 0], 1.0)
     plan = level_rows(height, 1)
     summed = jnp.zeros((DELTA_ROWS, LANES), f32)
     total_grad = jnp.zeros((9 * DELTA_ROWS, channels), f32)
     low_height, low_width = height // 2, width // 2
+    def came(ref, b, kind, index):
+        if index == 0:
+            return ref[b, kind, :, :width]
+        line = ref[b, kind, :, width : 2 * width]
+        if index == 2:
+            line = pltpu.roll(line, width // 2, 1)
+        lane = lax.broadcasted_iota(jnp.int32, line.shape, 1)
+        return jnp.where(lane < width >> index, line, 0.0)
+
     for b in range(crops):
         partial, weights = [], []
         for index, (padded, own, lines) in enumerate(plan):
-            at = slice(index * width, (index + 1) * width)
             rows = [
                 values[b, :, line * width : (line + 1) * width]
                 for line in range(padded, padded + lines + 2)
             ]
-            rows[0] = rows[0] + above[b, 0, :, at]
-            rows[1] = rows[1] + above[b, 1, :, at]
-            rows[lines] = rows[lines] + below[b, 1, :, at]
-            rows[lines + 1] = rows[lines + 1] + below[b, 0, :, at]
+            rows[0] = rows[0] + came(above, b, 0, index)
+            rows[1] = rows[1] + came(above, b, 1, index)
+            rows[lines] = rows[lines] + came(below, b, 1, index)
+            rows[lines + 1] = rows[lines + 1] + came(below, b, 0, index)
             partial += rows
             weights += [
-                above[b, 2, :, at],
+                came(above, b, 2, index),
                 mask[b, :, own * width : (own + lines) * width],
-                below[b, 2, :, at],
+                came(below, b, 2, index),
             ]
         mismatch = jnp.concatenate(partial, axis=1)
         weight = jnp.concatenate(weights, axis=1)
@@ -394,12 +486,14 @@
                     first[b, width:] = low
                 if row == low_height - 1:
                     last[b, width:] = low
+    swapped(first, last, pair, other, True)
     head_grad[...] = total_grad
     loss[0, 0] = jnp.sum(summed)
 
 
-def conv_grad_kernel(n_rows, n_batch, deltas, input_four, input_five, above, below, grad_four, grad_five, head_grad, loss, *refs):
-    outs, (turned_rows, sums_four, sums_five, spare) = refs[:-4], refs[-4:]
+def conv_grad_kernel(n_rows, input_four, input_five, pair_in, other_in, grad_four, grad_five, *refs):
+    outs, (turned_rows, sums_four, sums_five, above, below) = refs[:-5], refs[-5:]
+    swapped(above, below, pair_in, other_in, False)
     crops, height, width, channels = input_four.shape
     low_height, low_width = input_five.shape[1:3]
     padding = jnp.zeros((width - low_width, channels), bf16)
@@ -445,31 +539,19 @@
                         sums[at, :] = block
                     else:
                         sums[at, :] += block
-    for t in range(9):
-        block = head_grad[t * DELTA_ROWS : (t + 1) * DELTA_ROWS, :]
-        block = jnp.concatenate(
-            [block, jnp.zeros((LANES - DELTA_ROWS, channels), f32)], axis=0
-        )
-        spare[t * channels : (t + 1) * channels, :] = block.T
     me = lax.axis_index("rows")
-    number = me * n_batch + lax.axis_index("batch")
     part = 9 * channels // n_rows
-    own = part // n_batch
-    place = jnp.zeros((part, LANES), f32)
-    line = lax.broadcasted_iota(jnp.int32, place.shape, 0) % own
-    lane = lax.broadcasted_iota(jnp.int32, place.shape, 1) - deltas - 3 * (number // own)
-    for piece, value in enumerate(pieces_of(jnp.full(place.shape, loss[0, 0], f32))):
-        place = jnp.where((line == number % own) & (lane == piece), value, place)
     low = len(outs)
     for index in range(n_rows):
         at = pl.ds(pl.multiple_of((index ^ me) * part, part), part)
         out, j = outs[index % low], index // low
         out[j, :, :channels] = sums_four[at, :].astype(bf16)
-        out[j, :, channels : 2 * channels] = sums_five[at, :].astype(bf16)
-        out[j, :, 2 * channels :] = (spare[at, :] + place).astype(bf16)
-
-
-def merged_grad_kernel(grad_four, grad_five, above, below, kernel_four, kernel_five, lat_four, lat_five, spread_four, spread_five, fold):
+        out[j, :, channels:] = sums_five[at, :].astype(bf16)
+
+
+def merged_grad_kernel(grad_four, grad_five, pair_in, other_in, kernel_four, kernel_five, *refs):
+    lat_four, lat_five, spread_four, spread_five, fold, above, below = refs
+    swapped(above, below, pair_in, other_in, False)
     crops, height, width, channels = grad_four.shape
     low_height, low_width = grad_five.shape[1:3]
     fill_padded(spread_four, grad_four, above, below, 0)
@@ -494,8 +576,8 @@
                     lat_five[at_low : at_low + low_width, h : h + LANES] = (total + folded).astype(bf16)
 
 
-def section_grad_kernel(n_rows, four, five, lat_four, lat_five, kept, *refs):
-    outs, (sums_four, sums_five) = refs[:-2], refs[-2:]
+def section_grad_kernel(n_rows, n_batch, deltas, own, four, five, lat_four, lat_five, head_grad, loss, kept, *refs):
+    outs, (sums_four, sums_five, flat) = refs[:-3], refs[-3:]
     crops, height, width, depth = four.shape
     low_height, low_width, low_depth = five.shape[1:]
     me = lax.axis_index("rows")
@@ -511,6 +593,18 @@
     for at in range(0, low_depth, step):
         block = five[:, :, :, at : at + step].reshape(low_positions, step)
         sums_five[at : at + step, :] = dot(turned_five, block).T
+    channels = head_grad.shape[1]
+    flat[:, 9 * channels :] = jnp.zeros((DELTA_ROWS, flat.shape[1] - 9 * channels), f32)
+    for t in range(9):
+        flat[:, t * channels : (t + 1) * channels] = head_grad[
+            t * DELTA_ROWS : (t + 1) * DELTA_ROWS, :
+        ]
+    line = lax.broadcasted_iota(jnp.int32, (DELTA_ROWS, LANES), 0)
+    lane = lax.broadcasted_iota(jnp.int32, (DELTA_ROWS, LANES), 1)
+    spot = (line - deltas) * LANES + lane - 3 * (me * n_batch + lax.axis_index("batch"))
+    place = jnp.zeros((DELTA_ROWS, LANES), f32)
+    for piece, value in enumerate(pieces_of(jnp.full(place.shape, loss[0, 0], f32))):
+        place = jnp.where((line >= deltas) & (spot == piece), value, place)
     high = kept.shape[0]
     low = n_rows // high
     for index in range(n_rows):
@@ -520,7 +614,15 @@
         at = pl.ds(pl.multiple_of(owner * part_four, part_four), part_four)
         out[:part_four, :] = sums_four[at, :].astype(bf16)
         at = pl.ds(pl.multiple_of(owner * part_five, part_five), part_five)
-        out[part_four:, :] = sums_five[at, :].astype(bf16)
+        out[part_four : part_four + part_five, :] = sums_five[at, :].astype(bf16)
+        pieces = []
+        for z in range(n_batch):
+            start = (owner * n_batch + z) * own
+            at = pl.ds(pl.multiple_of(start // LANES * LANES, LANES), 2 * LANES)
+            square = pltpu.roll(flat[:, at], (2 * LANES - start % LANES) % (2 * LANES), 1)[:, :LANES]
+            square = jnp.where((line < deltas) & (lane < own), square, place)
+            pieces.append(joined(square))
+        out[part_four + part_five :, :] = jnp.concatenate(pieces, axis=0).astype(bf16)
 
 
 def adamw_into(outs, weight, gradient, mean, square):
@@ -528,8 +630,8 @@
         out[...] = value
 
 
-def conv_step_kernel(count, deltas, own, *refs):
-    came, (weight, mean, square, first, second, new, head, loss) = refs[:count], refs[count:]
+def conv_step_kernel(count, own, *refs):
+    came, (weight, mean, square, first, second, new) = refs[:count], refs[count:]
     channels = weight.shape[2]
     total = own[...]
     for piece in came:
@@ -542,29 +644,22 @@
             mean[k],
             square[k],
         )
-    spare = total[:, 2 * channels :]
-    head[...] = spare
-    lane = lax.broadcasted_iota(jnp.int32, spare.shape, 1)
-    loss[0, 0] = jnp.sum(jnp.where(lane >= deltas, spare, 0.0))
 
 
 def lateral_step_kernel(count, own, *refs):
-    came, rest = refs[:count], refs[count:]
-    inputs, outs = rest[:6], rest[6:]
+    came, inputs, outs, loss = refs[:count], refs[count : count + 9], refs[count + 9 : -1], refs[-1]
     total = own[...]
     for piece in came:
         total = total + piece[...].astype(f32)
     lines = inputs[0].shape[0]
-    for k, gradient in enumerate((total[:lines], total[lines:])):
-        weight, mean, square = (ref[...] for ref in inputs[3 * k : 3 * k + 3])
-        adamw_into(outs[3 * k : 3 * k + 3], weight, gradient, mean, square)
-
-
-def planes(field, rows):
-    crops, height, width, depth = field.shape
-    field = jnp.transpose(field, (0, 3, 1, 2))
-    field = jnp.pad(field, ((0, 0), (0, rows - depth), (0, 0), (0, LANES - width)))
-    return field.reshape(crops, rows, height * LANES)
+    deltas, rows = inputs[6].shape
+    square = parted(total[total.shape[0] - 8 :])
+    gradients = (total[:lines], total[lines : total.shape[0] - 8], square[:deltas, :rows])
+    for k, gradient in enumerate(gradients):
+        weight, mean, second = (ref[...] for ref in inputs[3 * k : 3 * k + 3])
+        adamw_into(outs[3 * k : 3 * k + 3], weight, gradient, mean, second)
+    line = lax.broadcasted_iota(jnp.int32, square.shape, 0)
+    loss[0, 0] = jnp.sum(jnp.where(line >= deltas, square, 0.0))
 
 
 def on_device(
@@ -597,47 +692,61 @@
     channels, deltas = delta_head.shape[0] * n_rows * n_batch // 9, delta_head.shape[1]
     shape = jax.ShapeDtypeStruct
 
+    flat = [jnp.transpose(a, (0, 3, 1, 2)) for a in (anchor_four, anchor_five, anchor_six)]
+    sources = [lateral_four, lateral_five, delta_head.T, *flat]
     (lateral,) = call(
-        pack_lateral_kernel,
-        "pack_laterals",
-        [lateral_four, lateral_five],
-        [shape((four_n + five_n, channels), bf16)],
+        pack_kernel,
+        "pack",
+        sources,
+        [shape((four_n + five_n + 8, channels), bf16)],
+        [pltpu.VMEM((DELTA_ROWS, LANES), f32)]
+        + [pltpu.VMEM(v.shape, v.dtype) for v in sources]
+        + [pltpu.SemaphoreType.DMA((len(sources),))],
+        apart=len(sources),
     )
     parts = gathered_batch(lateral)
-    lateral = jnp.concatenate([p[:four_n] for p in parts] + [p[four_n:] for p in parts])
+    lateral = jnp.concatenate(
+        [p[:four_n] for p in parts]
+        + [p[four_n : four_n + five_n] for p in parts]
+        + [p[four_n + five_n :] for p in parts]
+    )
     laterals = gathered_high(lateral)
 
-    flat = [jnp.transpose(a, (0, 3, 1, 2)) for a in (anchor_four, anchor_five, anchor_six)]
-    (conv,) = call(
-        pack_conv_kernel,
-        "pack_convs",
-        [output_conv, delta_head.T, *flat],
-        [shape((conv_n, 2 * channels + LANES), bf16)],
-        [pltpu.VMEM((LANES, LANES), f32)],
-    )
+    conv = jnp.concatenate([output_conv[0], output_conv[1]], axis=1).astype(bf16)
     conv, _ = lax.optimization_barrier((conv, lateral))
     conv = jnp.concatenate(gathered_batch(conv))
-    anchors, targets, _ = lax.optimization_barrier(
+
+    lines = height + low_height + low_height // 2
+    flat, _ = lax.optimization_barrier(
         (
-            (anchor_four, anchor_five, anchor_six),
-            (target_four, target_five, target_six),
-            conv,
+            [
+                jnp.transpose(t, (0, 3, 1, 2))
+                for t in (
+                    target_four,
+                    target_five,
+                    target_six,
+                    anchor_four,
+                    anchor_five,
+                    anchor_six,
+                )
+            ],
+            lateral,
         )
     )
-    mask = jnp.concatenate(
-        [
-            planes(jnp.repeat(a.astype(f32), deltas // a.shape[3], axis=3), DELTA_ROWS)
-            for a in anchors
-        ],
-        axis=2,
-    )
-    target = jnp.concatenate([planes(t, DELTA_ROWS) for t in targets], axis=2)
-    conv, laterals = lax.optimization_barrier((conv, laterals))
+    target, mask = call(
+        planes_kernel,
+        "planes",
+        [*flat, section_four, section_five],
+        [shape((crops, DELTA_ROWS, lines * LANES), f32)] * 2,
+    )
+    laterals, target, mask = lax.optimization_barrier((laterals, target, mask))
     laterals = gathered_low(laterals)
     convs = gathered_high(conv)
 
     edge = width + low_width
-    input_four, input_five, first, last = call(
+    input_rims = [pltpu.VMEM((crops, edge, channels), bf16)] * 2
+    head_rims = [pltpu.VMEM((crops, 3, DELTA_ROWS, 2 * width), f32)] * 2
+    input_four, input_five, pair, other = call(
         functools.partial(lateral_kernel, n_rows),
         "laterals",
         [section_four, section_five, *laterals],
@@ -651,44 +760,51 @@
             pltpu.VMEM((depth, channels), bf16),
             pltpu.VMEM((low_depth, channels), bf16),
             pltpu.VMEM((channels // LANES, width, LANES), f32),
-        ],
+        ]
+        + input_rims,
         flops=2 * crops * channels * (height * width * depth + low_height * low_width * low_depth),
     )
-    above_in, below_in = from_neighbours(first, last)
-    convs, above_in, below_in = lax.optimization_barrier((convs, above_in, below_in))
+    pair_in, other_in = from_neighbours(pair, other)
+    convs, pair_in, other_in = lax.optimization_barrier((convs, pair_in, other_in))
     convs = gathered_low(convs)
 
-    lines = height + low_height + low_height // 2
     conv_flops = 18 * crops * channels * channels * (height * width + low_height * low_width)
-    levels, values, first, last, kernel_four, kernel_five, head, count = call(
-        functools.partial(output_kernel, n_rows, deltas),
+    head, count = call(
+        functools.partial(head_weights_kernel, n_rows, n_batch, deltas, conv_n),
+        "head_weights",
+        laterals,
+        [shape((9 * DELTA_ROWS, channels), bf16), shape((1, 1), f32)],
+        [pltpu.VMEM((DELTA_ROWS, 9 * channels + 2 * LANES), f32)],
+        scalar_outs=1,
+    )
+    levels, values, pair, other, kernel_four, kernel_five = call(
+        functools.partial(output_kernel, n_rows),
         "outputs",
-        [input_four, input_five, above_in, below_in, target, mask, *convs],
+        [input_four, input_five, pair_in, other_in, head, target, mask, *convs],
         [
             shape((crops, lines, width, channels), bf16),
             shape((crops, DELTA_ROWS, (lines + 6) * width), f32),
-            shape((crops, 3, DELTA_ROWS, 3 * width), f32),
-            shape((crops, 3, DELTA_ROWS, 3 * width), f32),
+            shape((crops, 3, DELTA_ROWS, 2 * width), f32),
+            shape((crops, 3, DELTA_ROWS, 2 * width), f32),
             shape((9 * channels, channels), bf16),
             shape((9 * channels, channels), bf16),
-            shape((9 * DELTA_ROWS, channels), bf16),
-            shape((1, 1), f32),
         ],
         [
             pltpu.VMEM((crops, height + 2, width, channels), bf16),
             pltpu.VMEM((crops, low_height + 2, low_width, channels), bf16),
-            pltpu.VMEM((9 * channels, LANES), f32),
-        ],
+            pltpu.VMEM((low_height * low_width, LANES), f32),
+        ]
+        + input_rims
+        + head_rims,
         flops=conv_flops,
-        scalar_outs=1,
-    )
-    above, below = from_neighbours(first, last)
+    )
+    pair, other = from_neighbours(pair, other)
 
     head_flops = 18 * DELTA_ROWS * crops * lines * width * channels
-    head_grad, grad_four, grad_five, first, last, loss = call(
+    head_grad, grad_four, grad_five, pair, other, loss = call(
         functools.partial(head_kernel, height),
         "heads",
-        [levels, above, below, head, values, mask, count],
+        [levels, pair, other, head, values, mask, count],
         [
             shape((9 * DELTA_ROWS, channels), f32),
             shape((crops, height, width, channels), bf16),
@@ -700,75 +816,88 @@
         [
             pltpu.VMEM((9 * DELTA_ROWS, lines * width), bf16),
             pltpu.VMEM((channels // LANES, low_width, LANES), f32),
-        ],
+        ]
+        + head_rims
+        + input_rims,
         flops=3 * head_flops,
         scalars=1,
         scalar_outs=1,
     )
-    above, below = from_neighbours(first, last)
-
-    conv_width = 2 * channels + LANES
+    pair, other = from_neighbours(pair, other)
+
+    conv_width = 2 * channels
     conv_blocks = call(
-        functools.partial(conv_grad_kernel, n_rows, n_batch, deltas),
+        functools.partial(conv_grad_kernel, n_rows),
         "conv_grads",
-        [input_four, input_five, above_in, below_in, grad_four, grad_five, head_grad, loss],
+        [input_four, input_five, pair_in, other_in, grad_four, grad_five],
         [shape((high_group, n_batch * conv_n, conv_width), bf16)] * low_group,
         [
             pltpu.VMEM((channels, (height + 2) * width), bf16),
             pltpu.VMEM((9 * channels, channels), f32),
             pltpu.VMEM((9 * channels, channels), f32),
-            pltpu.VMEM((9 * channels, LANES), f32),
-        ],
+        ]
+        + input_rims,
         flops=conv_flops,
-        scalars=1,
     )
 
     positions, low_positions = crops * height * width, crops * low_height * low_width
+    conv_blocks, pair, other = lax.optimization_barrier((conv_blocks, pair, other))
     conv_partial = summed_low(conv_blocks)
-    above, below, conv_partial = lax.optimization_barrier((above, below, conv_partial))
+    pair, other, conv_partial = lax.optimization_barrier((pair, other, conv_partial))
     lat_four, lat_five = call(
         merged_grad_kernel,
         "merged_grads",
-        [grad_four, grad_five, above, below, kernel_four, kernel_five],
+        [grad_four, grad_five, pair, other, kernel_four, kernel_five],
         [shape((positions, channels), bf16), shape((low_positions, channels), bf16)],
         [
             pltpu.VMEM((crops, height + 2, width, channels), bf16),
             pltpu.VMEM((crops, low_height + 2, low_width, channels), bf16),
             pltpu.VMEM((4 * width, LANES), f32),
+        ]
+        + input_rims,
+        flops=conv_flops,
+    )
+    conv_sum = summed_high(conv_partial)
+
+    lateral_n = four_n + five_n + 8
+    lateral_kept, *lateral_moved = call(
+        functools.partial(section_grad_kernel, n_rows, n_batch, deltas, conv_n),
+        "lateral_grads",
+        [section_four, section_five, lat_four, lat_five, head_grad, loss],
+        [shape((high_group, n_batch * lateral_n, channels), bf16)] * low_group,
+        [
+            pltpu.VMEM((depth, channels), f32),
+            pltpu.VMEM((low_depth, channels), f32),
+            pltpu.VMEM((DELTA_ROWS, 9 * channels + 2 * LANES), f32),
         ],
-        flops=conv_flops,
-    )
-    conv_sum = summed_high(conv_partial)
-
-    lateral_n = four_n + five_n
-    lateral_kept, *lateral_moved = call(
-        functools.partial(section_grad_kernel, n_rows),
-        "lateral_grads",
-        [section_four, section_five, lat_four, lat_five],
-        [shape((high_group, n_batch * lateral_n, channels), bf16)] * low_group,
-        [pltpu.VMEM((depth, channels), f32), pltpu.VMEM((low_depth, channels), f32)],
         flops=1,
+        scalars=1,
     )
     lateral_moved, conv_sum = lax.optimization_barrier((lateral_moved, conv_sum))
     lateral_partial = summed_low([lateral_kept, *lateral_moved])
     lateral_sum = summed_high(lateral_partial)
     conv_shares = shared_batch(conv_sum.reshape(n_batch, conv_n, conv_width))
     conv_shares, lateral_sum = lax.optimization_barrier((conv_shares, lateral_sum))
-    first_conv, second_conv, weight_conv, head_part, loss_sum = call(
-        functools.partial(conv_step_kernel, n_batch - 1, deltas),
+    first_conv, second_conv, weight_conv = call(
+        functools.partial(conv_step_kernel, n_batch - 1),
         "conv_step",
         [*conv_shares, output_conv, mean_conv, square_conv],
-        [shape(output_conv.shape, f32)] * 3 + [shape((conv_n, LANES), f32), shape((1, 1), f32)],
-        scalar_outs=1,
-    )
+        [shape(output_conv.shape, f32)] * 3,
+    )
+    ends = (n_batch * four_n, n_batch * (four_n + five_n))
     lateral_sum = jnp.concatenate(
         [
-            lateral_sum[: n_batch * four_n].reshape(n_batch, four_n, channels),
-            lateral_sum[n_batch * four_n :].reshape(n_batch, five_n, channels),
+            part.reshape(n_batch, -1, channels)
+            for part in (
+                lateral_sum[: ends[0]],
+                lateral_sum[ends[0] : ends[1]],
+                lateral_sum[ends[1] :],
+            )
         ],
         axis=1,
     )
-    first_four, second_four, weight_four, first_five, second_five, weight_five = call(
+    turned_head = [v.T for v in (delta_head, mean_head, square_head)]
+    outs = call(
         functools.partial(lateral_step_kernel, n_batch - 1),
         "lateral_step",
         [
@@ -779,13 +908,17 @@
             lateral_five,
             mean_five,
             square_five,
+            *turned_head,
         ],
-        [shape(lateral_four.shape, f32)] * 3 + [shape(lateral_five.shape, f32)] * 3,
-    )
-    head_part = head_part[:, :deltas]
-    first_head, second_head, weight_head = adamw_update(
-        delta_head, head_part, mean_head, square_head
-    )
+        [shape(lateral_four.shape, f32)] * 3
+        + [shape(lateral_five.shape, f32)] * 3
+        + [shape(turned_head[0].shape, f32)] * 3
+        + [shape((1, 1), f32)],
+        scalar_outs=1,
+    )
+    first_four, second_four, weight_four, first_five, second_five, weight_five = outs[:6]
+    first_head, second_head, weight_head = (v.T for v in outs[6:9])
+    loss_sum = outs[9]
     return (
         loss_sum[0, 0],
         count[0, 0],

time: 150 us -> 120 us (0.80)
  Pallas kernels: 47.8 us -> 24.2 us
  waiting for transfers between devices: 33.7 us -> 39.4 us
  other arithmetic: 7.1 us -> 2.61 us
  starting transfers between devices: 51.5 us -> 47.6 us
  local copies, waits for them, and re-layouts: 7.53 us -> 4.17 us
    pallas_call x10 -> x11, Pallas kernels: 47.8 us -> 24.2 us  [call(): pl.pallas_call(kernel, out_shape=list(outs), in_specs=[hbm] * apart + [vm...]
    ppermute x34 -> x37, waiting for transfers between devices: 30.3 us -> 39.4 us  [sent(): return lax.ppermute(value, axis, [(i, i ^ mask) for i in range(count)])]
    ppermute x6 -> x3, starting transfers between devices: 9.92 us -> 1.99 us  [from_neighbours(): lax.ppermute(other, 'rows', links + [(j, i) for i, j in links])]
    ppermute x34 -> x37, starting transfers between devices: 41.6 us -> 45.6 us  [sent(): return lax.ppermute(value, axis, [(i, i ^ mask) for i in range(count)])]
    ppermute x6 -> x3, waiting for transfers between devices: 3.48 us -> 0.01 us  [from_neighbours(): lax.ppermute(other, 'rows', links + [(j, i) for i, j in links])]
    unnamed x95 -> x55, local copies, waits for them, and re-layouts: 6.44 us -> 4.02 us
    add x2, other arithmetic: 2.58 us -> 0.31 us  [summed_low(): sum((c[j].astype(f32) for c in came), blocks[0][j].astype(f32))]
  transfers between devices with their start and end apart: 40 -> 40, of which waited for: 16 -> 21; matrix products, arithmetic and copies ran while one was open for 6% -> 1% of each run, Pallas kernels for 15% -> 12%
where the time goes in v3:
time: 120 us; the launch traced here: 119 us
  starting transfers between devices  47.6 us (40%)
  waiting for transfers between devices  39.4 us (33%)
  Pallas kernels  24.2 us (20%)
  local copies, waits for them, and re-layouts  4.17 us (3%)
  other arithmetic  2.61 us (2%)
  between operations  1.51 us (1%)
    ppermute x37, starting transfers between devices, sent(): return lax.ppermute(value, axis, [(i, i ^ mask) for i in range(count)])  45.6 us
    ppermute x37, waiting for transfers between devices, sent(): return lax.ppermute(value, axis, [(i, i ^ mask) for i in range(count)])  39.4 us
    pallas_call x11, Pallas kernels, call(): pl.pallas_call(kernel, out_shape=list(outs), in_specs=[hbm] * apart + [vm...  24.2 us
    unnamed x55, local copies, waits for them, and re-layouts  4.02 us
  transfers between devices with their start and end apart: 40, of which 21 were waited for; matrix products, arithmetic and copies ran while one was open for 1% of the time, Pallas kernels for 12%

profile of v3, /device:TPU:0, one launch (start us, length us, event | category | flops | bytes accessed | tf_op | source)
XLA Modules:
  0.0 119.5 jit_solution(3921315384218371620)
XLA Ops:
  0.7 1.7 %pack.1 = bf16[104,256]{1,0:T(8,128)(2,1)} custom-call(f32[32,256]{1,0:T(8,128)} %refs_3_.2, f32[64,256]{1,0:T(8,128)} %refs_6_.3, f32[12,72]{1,0:T(8,128)} %bitcast.129, s32[2,3,8,128]{3,2,1,0:T(8,128)} %bitcast.123, s32[2,3,4,64]{3,2,1,0:T(4,128)} %bitcast.127, s32[2,3,2,32]{3,2,1,0:T(2,128)} %bitcast.132), custom_call_target="tpu_custom_call" | custom-call | bytes 187264 | tf_op jit(solution)/shard_map/pack/pallas_call | solution.py:121
  2.4 5.1 %collective-permute-start.2 = (bf16[104,256]{1,0:T(8,128)(2,1)}, bf16[104,256]{1,0:T(8,128)(2,1)S(1)}, u32[]{:S(2)}, u32[]{:S(2)}) collective-permute-start(bf16[104,256]{1,0:T(8,128)(2,1)} %pack.1), channel_id=1, source_target_pairs={{0,3},{1,2},{2,1},{3,0},{4,7},{5,6},{6,5},{7,4},{8,11},{9,10},{10,... | collective-permute-start | bytes 159752 | tf_op jit(solution)/shard_map/ppermute | solution.py:45
  7.6 0.6 collective-permute-start
  8.2 0.9 convert.8
  9.2 0.9 collective-permute-done.2
  10.1 2.7 %collective-permute-done.1 = bf16[104,256]{1,0:T(8,128)(2,1)S(1)} collective-permute-done((bf16[104,256]{1,0:T(8,128)(2,1)}, bf16[104,256]{1,0:T(8,128)(2,1)S(1)}, u32[]{:S(2)}, u32[]{:S(2)}) %collective-permute-start.1) | collective-permute-done | bytes 53280 | tf_op jit(solution)/shard_map/ppermute | solution.py:45
  12.8 0.8 pad_maximum_fusion.3
  13.9 2.4 %collective-permute-start.12 = (bf16[72,512]{1,0:T(8,128)(2,1)S(1)}, bf16[72,512]{1,0:T(8,128)(2,1)S(1)}, u32[]{:S(2)}, u32[]{:S(2)}) collective-permute-start(bf16[72,512]{1,0:T(8,128)(2,1)S(1)} %pad_maximum_fusion.4), channel_id=1, source_target_pairs={{0,3},{1,2},{2,1},{3,0},{4,7},{5,6},{6,5},{7,4},{8,11},{9,10},{10,... | collective-permute-start | bytes 221192 | tf_op jit(solution)/shard_map/ppermute | solution.py:45
  16.3 2.4 %collective-permute-start.5 = (bf16[416,256]{1,0:T(8,128)(2,1)S(1)}, bf16[416,256]{1,0:T(8,128)(2,1)S(1)}, u32[]{:S(2)}, u32[]{:S(2)}) collective-permute-start(bf16[416,256]{1,0:T(8,128)(2,1)S(1)} %constant_dynamic-update-slice_fusion.refs_0_), channel_id=1, source_target_pairs={{0,24},{4,28},{8,16},{12,20},{16,8},{20,12},{24,0},{28,4},{1,25},{... | collective-permute-start | bytes 638984 | tf_op jit(solution)/shard_map/ppermute | solution.py:45
  18.8 0.5 collective-permute-start.4
  19.3 0.5 collective-permute-start.3
  19.8 0.5 collective-permute-done.12
  20.3 1.6 %collective-permute-start.10 = (bf16[72,512]{1,0:T(8,128)(2,1)S(1)}, bf16[72,512]{1,0:T(8,128)(2,1)S(1)}, u32[]{:S(2)}, u32[]{:S(2)}) collective-permute-start(bf16[72,512]{1,0:T(8,128)(2,1)S(1)} %pad_maximum_fusion.4), channel_id=1, source_target_pairs={{0,1},{1,0},{2,3},{3,2},{4,5},{5,4},{6,7},{7,6},{8,9},{9,8},{10,11... | collective-permute-start | bytes 221192 | tf_op jit(solution)/shard_map/ppermute | solution.py:45
  21.9 2.2 %copy-done = bf16[2,8,128,1024]{3,2,1,0:T(8,128)(2,1)S(1)} copy-done((bf16[2,8,128,1024]{3,2,1,0:T(8,128)(2,1)S(1)}, bf16[2,8,128,1024]{3,2,1,0:T(8,128)(2,1)}, u32[]{:S(2)}) %copy-start) | copy-done | bytes 4194328
  24.1 1.6 %copy-done.2 = bf16[2,4,64,2048]{3,2,1,0:T(8,128)(2,1)S(1)} copy-done((bf16[2,4,64,2048]{3,2,1,0:T(8,128)(2,1)S(1)}, bf16[2,4,64,2048]{3,2,1,0:T(8,128)(2,1)}, u32[]{:S(2)}) %copy-start.2) | copy-done | bytes 2097176
  25.9 1.4 %collective-permute-done.4.refs_4_ = bf16[416,256]{1,0:T(8,128)(2,1)S(1)} collective-permute-done((bf16[416,256]{1,0:T(8,128)(2,1)S(1)}, bf16[416,256]{1,0:T(8,128)(2,1)S(1)}, u32[]{:S(2)}, u32[]{:S(2)}) %collective-permute-start.4) | collective-permute-done | bytes 213024 | tf_op jit(solution)/shard_map/ppermute | solution.py:45
  27.4 0.5 collective-permute-start.7
  27.9 0.5 collective-permute-start.9
  28.5 1.7 %collective-permute-start.15 = (bf16[288,512]{1,0:T(8,128)(2,1)S(1)}, bf16[288,512]{1,0:T(8,128)(2,1)S(1)}, u32[]{:S(2)}, u32[]{:S(2)}) collective-permute-start(bf16[288,512]{1,0:T(8,128)(2,1)S(1)} %pad_maximum_fusion.2.refs_0_), channel_id=1, source_target_pairs={{0,24},{4,28},{8,16},{12,20},{16,8},{20,12},{24,0},{28,4},{1,25},{... | collective-permute-start | bytes 884744 | tf_op jit(solution)/shard_map/ppermute | solution.py:45
  30.2 1.3 %collective-permute-start.14 = (bf16[288,512]{1,0:T(8,128)(2,1)S(1)}, bf16[288,512]{1,0:T(8,128)(2,1)S(1)}, u32[]{:S(2)}, u32[]{:S(2)}) collective-permute-start(bf16[288,512]{1,0:T(8,128)(2,1)S(1)} %pad_maximum_fusion.2.refs_0_), channel_id=1, source_target_pairs={{0,16},{4,20},{8,24},{12,28},{16,0},{20,4},{24,8},{28,12},{1,17},{... | collective-permute-start | bytes 884744 | tf_op jit(solution)/shard_map/ppermute | solution.py:45
  31.5 0.5 collective-permute-start.13
  32.0 2.0 %laterals.1 = (bf16[2,8,128,256]{3,2,1,0:T(8,128)(2,1)S(1)}, bf16[2,4,64,256]{3,2,1,0:T(8,128)(2,1)S(1)}, bf16[2,192,256]{2,1,0:T(8,128)(2,1)S(1)}, bf16[2,192,256]{2,1,0:T(8,128)(2,1)S(1)}) custom-call(bf16[2,8,128,1024]{3,2,1,0:T(8,128)(2,1)S(1)} %copy-done.1, bf16[2,4,64,2048]{3,2,1,0:T(8,128)(2,1)S(1)} %copy-done.2, ...), custom_call_target="tpu_custom_call" | custom-call | flops 1610612736 | bytes 9699328 | tf_op jit(solution)/shard_map/laterals/pallas_call | solution.py:121
  34.1 0.7 collective-permute-start.17
  34.8 4.6 %collective-permute-done.15.refs_6_ = bf16[288,512]{1,0:T(8,128)(2,1)S(1)} collective-permute-done((bf16[288,512]{1,0:T(8,128)(2,1)S(1)}, bf16[288,512]{1,0:T(8,128)(2,1)S(1)}, u32[]{:S(2)}, u32[]{:S(2)}) %collective-permute-start.15) | collective-permute-done | bytes 294944 | tf_op jit(solution)/shard_map/ppermute | solution.py:45
  39.3 5.3 %collective-permute-done.14.refs_4_ = bf16[288,512]{1,0:T(8,128)(2,1)S(1)} collective-permute-done((bf16[288,512]{1,0:T(8,128)(2,1)S(1)}, bf16[288,512]{1,0:T(8,128)(2,1)S(1)}, u32[]{:S(2)}, u32[]{:S(2)}) %collective-permute-start.14) | collective-permute-done | bytes 294944 | tf_op jit(solution)/shard_map/ppermute | solution.py:45
  44.7 1.0 collective-permute-done.13.refs_2_
  45.6 3.1 %collective-permute-start.18 = (bf16[288,512]{1,0:T(8,128)(2,1)S(1)}, bf16[288,512]{1,0:T(8,128)(2,1)S(1)}, u32[]{:S(2)}, u32[]{:S(2)}) collective-permute-start(bf16[288,512]{1,0:T(8,128)(2,1)S(1)} %pad_maximum_fusion.2.refs_0_), channel_id=1, source_target_pairs={{0,4},{4,0},{8,12},{12,8},{16,20},{20,16},{24,28},{28,24},{1,5},{5... | collective-permute-start | bytes 884744 | tf_op jit(solution)/shard_map/ppermute | solution.py:45
  48.7 0.5 collective-permute-start.20
  49.2 0.9 head_weights.1
  50.1 0.2 collective-permute-done.19.refs_3_
  50.3 0.4 collective-permute-done.20.refs_5_
  50.7 0.4 collective-permute-done.21.refs_7_
  51.2 4.3 %outputs.1 = (bf16[2,14,128,256]{3,2,1,0:T(8,128)(2,1)S(1)}, f32[2,16,2560]{2,1,0:T(8,128)S(1)}, f32[2,3,16,256]{3,2,1,0:T(8,128)S(1)}, f32[2,3,16,256]{3,2,1,0:...) custom-call(bf16[2,8,128,256]{3,2,1,0:T(8,128)(2,1)S(1)} %get-tuple-element.101.input_four, ...), custom_call_target="tpu_custom_call" | custom-call | flops 3019898880 | bytes 9314304 | tf_op jit(solution)/shard_map/outputs/pallas_call | solution.py:121
  55.5 0.4 collective-permute-start.22
  55.9 0.7 collective-permute-start.23
  56.6 0.3 collective-permute-done.22.pair_in
  56.9 2.7 %heads.1 = (f32[144,256]{1,0:T(8,128)S(1)}, bf16[2,8,128,256]{3,2,1,0:T(8,128)(2,1)S(1)}, bf16[2,4,64,256]{3,2,1,0:T(8,128)(2,1)S(1)}, bf16[2,192,256]{2,1,0:T(8...) custom-call(bf16[2,14,128,256]{3,2,1,0:T(8,128)(2,1)S(1)} %get-tuple-element.115.levels, ...), custom_call_target="tpu_custom_call" | custom-call | flops 792723456 | bytes 4513800 | tf_op jit(solution)/shard_map/heads/pallas_call | solution.py:121
  59.6 6.2 %collective-permute-start.24 = (bf16[2,192,256]{2,1,0:T(8,128)(2,1)S(1)}, bf16[2,192,256]{2,1,0:T(8,128)(2,1)S(1)}, u32[]{:S(2)}, u32[]{:S(2)}) collective-permute-start(bf16[2,192,256]{2,1,0:T(8,128)(2,1)S(1)} %get-tuple-element.124), channel_id=1, source_target_pairs={{0,4},{4,0},{8,12},{12,8},{16,20},{20,16},{24,28},{28,24},{1,5},{5... | collective-permute-start | bytes 589832 | tf_op jit(solution)/shard_map/ppermute | solution.py:45
  65.7 0.7 collective-permute-start.25
  66.4 4.4 %conv_grads.1 = (bf16[4,288,512]{2,1,0:T(8,128)(2,1)S(1)}, bf16[4,288,512]{2,1,0:T(8,128)(2,1)S(1)}) custom-call(bf16[2,8,128,256]{3,2,1,0:T(8,128)(2,1)S(1)} %get-tuple-element.101.input_four, bf16[2,4,64,256]{3,2,1,0:T(8,128)(2,1)S(1)} %get-tuple-element.102.input_five, bf16[2,192,256]{2,1,0:T(8,128)(2,1)S(1)} %collective-permute-done.16.pair_in, ...), custom_call_target="tpu_custom_call" | custom-call | flops 3019898880 | bytes 5373952 | tf_op jit(solution)/shard_map/conv_grads/pallas_call | solution.py:121
  70.8 3.2 %collective-permute-start.26 = (bf16[4,288,512]{2,1,0:T(8,128)(2,1)S(1)}, bf16[4,288,512]{2,1,0:T(8,128)(2,1)S(1)}, u32[]{:S(2)}, u32[]{:S(2)}) collective-permute-start(bf16[4,288,512]{2,1,0:T(8,128)(2,1)S(1)} %get-tuple-element.129), channel_id=1, source_target_pairs={{0,4},{4,0},{8,12},{12,8},{16,20},{20,16},{24,28},{28,24},{1,5},{5... | collective-permute-start | bytes 3538952 | tf_op jit(solution)/shard_map/ppermute | solution.py:45
  74.0 2.5 %collective-permute-done.26 = bf16[4,288,512]{2,1,0:T(8,128)(2,1)S(1)} collective-permute-done((bf16[4,288,512]{2,1,0:T(8,128)(2,1)S(1)}, bf16[4,288,512]{2,1,0:T(8,128)(2,1)S(1)}, u32[]{:S(2)}, u32[]{:S(2)}) %collective-permute-start.26) | collective-permute-done | bytes 1179680 | tf_op jit(solution)/shard_map/ppermute | solution.py:45
  76.6 0.2 add_bitcast_fusion
  76.8 2.1 %collective-permute-start.27 = (bf16[288,512]{1,0:T(8,128)(2,1)S(1)}, bf16[288,512]{1,0:T(8,128)(2,1)S(1)}, u32[]{:S(2)}, u32[]{:S(2)}) collective-permute-start(bf16[288,512]{1,0:T(8,128)(2,1)S(1)} %get-tuple-element.140), channel_id=1, source_target_pairs={{0,8},{4,12},{8,0},{12,4},{16,24},{20,28},{24,16},{28,20},{1,9},{5... | collective-permute-start | bytes 884744 | tf_op jit(solution)/shard_map/ppermute | solution.py:45
  79.0 0.9 collective-permute-start.28
  79.8 1.4 %collective-permute-start.29 = (bf16[288,512]{1,0:T(8,128)(2,1)S(1)}, bf16[288,512]{1,0:T(8,128)(2,1)S(1)}, u32[]{:S(2)}, u32[]{:S(2)}) collective-permute-start(bf16[288,512]{1,0:T(8,128)(2,1)S(1)} %get-tuple-element.142), channel_id=1, source_target_pairs={{0,24},{4,28},{8,16},{12,20},{16,8},{20,12},{24,0},{28,4},{1,25},{... | collective-permute-start | bytes 884744 | tf_op jit(solution)/shard_map/ppermute | solution.py:45
  81.2 3.5 %merged_grads.1 = (bf16[2048,256]{1,0:T(8,128)(2,1)S(1)}, bf16[512,256]{1,0:T(8,128)(2,1)S(1)}) custom-call(bf16[2,8,128,256]{3,2,1,0:T(8,128)(2,1)S(1)} %get-tuple-element.120.grad_four, bf16[2,4,64,256]{3,2,1,0:T(8,128)(2,1)S(1)} %get-tuple-element.121.grad_five, bf16[2,192,256]{2,1,0:T(8,128)(2,1)S(1)} %collective-permute-done.24.pair_in, ...), custom_call_target="tpu_custom_call" | custom-call | flops 3019898880 | bytes 5373952 | tf_op jit(solution)/shard_map/merged_grads/pallas_call | solution.py:121
  84.7 2.9 %lateral_grads.1 = (bf16[4,416,256]{2,1,0:T(8,128)(2,1)S(1)}, bf16[4,416,256]{2,1,0:T(8,128)(2,1)S(1)}) custom-call(bf16[2,8,128,1024]{3,2,1,0:T(8,128)(2,1)S(1)} %copy-done.1, bf16[2,4,64,2048]{3,2,1,0:T(8,128)(2,1)S(1)} %copy-done.3, bf16[2048,256]{1,0:T(8,128)(2,1)S(1)} %get-tuple-element.134.lat_four, bf16[512,256]{1,0:T(8,128)(2,1)S(1)} %get-tuple-element.135.lat_five, ...), custom_call_target="tpu_custom_call" | custom-call | flops 1 | bytes 9453572 | tf_op jit(solution)/shard_map/lateral_grads/pallas_call | solution.py:121
  87.6 5.1 %collective-permute-done.28 = bf16[288,512]{1,0:T(8,128)(2,1)S(1)} collective-permute-done((bf16[288,512]{1,0:T(8,128)(2,1)S(1)}, bf16[288,512]{1,0:T(8,128)(2,1)S(1)}, u32[]{:S(2)}, u32[]{:S(2)}) %collective-permute-start.28) | collective-permute-done | bytes 294944 | tf_op jit(solution)/shard_map/ppermute | solution.py:45
  92.7 1.8 %collective-permute-done.29 = bf16[288,512]{1,0:T(8,128)(2,1)S(1)} collective-permute-done((bf16[288,512]{1,0:T(8,128)(2,1)S(1)}, bf16[288,512]{1,0:T(8,128)(2,1)S(1)}, u32[]{:S(2)}, u32[]{:S(2)}) %collective-permute-start.29) | collective-permute-done | bytes 294944 | tf_op jit(solution)/shard_map/ppermute | solution.py:45
  94.8 2.4 %collective-permute-done.33 = bf16[4,416,256]{2,1,0:T(8,128)(2,1)S(1)} collective-permute-done((bf16[4,416,256]{2,1,0:T(8,128)(2,1)S(1)}, bf16[4,416,256]{2,1,0:T(8,128)(2,1)S(1)}, u32[]{:S(2)}, u32[]{:S(2)}) %collective-permute-start.33) | collective-permute-done | bytes 852000 | tf_op jit(solution)/shard_map/ppermute | solution.py:45
  97.3 0.6 collective-permute-start.34
  97.9 1.5 %collective-permute-start.36 = (bf16[416,256]{1,0:T(8,128)(2,1)S(1)}, bf16[416,256]{1,0:T(8,128)(2,1)S(1)}, u32[]{:S(2)}, u32[]{:S(2)}) collective-permute-start(bf16[416,256]{1,0:T(8,128)(2,1)S(1)} %get-tuple-element.168), channel_id=1, source_target_pairs={{0,24},{4,28},{8,16},{12,20},{16,8},{20,12},{24,0},{28,4},{1,25},{... | collective-permute-start | bytes 638984 | tf_op jit(solution)/shard_map/ppermute | solution.py:45
  99.5 1.4 %collective-permute-start.35 = (bf16[416,256]{1,0:T(8,128)(2,1)S(1)}, bf16[416,256]{1,0:T(8,128)(2,1)S(1)}, u32[]{:S(2)}, u32[]{:S(2)}) collective-permute-start(bf16[416,256]{1,0:T(8,128)(2,1)S(1)} %get-tuple-element.169), channel_id=1, source_target_pairs={{0,16},{4,20},{8,24},{12,28},{16,0},{20,4},{24,8},{28,12},{1,17},{... | collective-permute-start | bytes 638984 | tf_op jit(solution)/shard_map/ppermute | solution.py:45
  100.9 1.9 %collective-permute-start.32 = (bf16[72,512]{1,0:T(8,128)(2,1)S(1)}, bf16[72,512]{1,0:T(8,128)(2,1)S(1)}, u32[]{:S(2)}, u32[]{:S(2)}) collective-permute-start(bf16[72,512]{1,0:T(8,128)(2,1)S(1)} %get-tuple-element.170), channel_id=1, source_target_pairs={{0,3},{1,2},{2,1},{3,0},{4,7},{5,6},{6,5},{7,4},{8,11},{9,10},{10,... | collective-permute-start | bytes 221192 | tf_op jit(solution)/shard_map/ppermute | solution.py:45
  102.8 2.7 %collective-permute-done.34 = bf16[416,256]{1,0:T(8,128)(2,1)S(1)} collective-permute-done((bf16[416,256]{1,0:T(8,128)(2,1)S(1)}, bf16[416,256]{1,0:T(8,128)(2,1)S(1)}, u32[]{:S(2)}, u32[]{:S(2)}) %collective-permute-start.34) | collective-permute-done | bytes 213024 | tf_op jit(solution)/shard_map/ppermute | solution.py:45
  105.5 3.9 %collective-permute-done.36 = bf16[416,256]{1,0:T(8,128)(2,1)S(1)} collective-permute-done((bf16[416,256]{1,0:T(8,128)(2,1)S(1)}, bf16[416,256]{1,0:T(8,128)(2,1)S(1)}, u32[]{:S(2)}, u32[]{:S(2)}) %collective-permute-start.36) | collective-permute-done | bytes 213024 | tf_op jit(solution)/shard_map/ppermute | solution.py:45
  109.4 1.4 %collective-permute-done.35 = bf16[416,256]{1,0:T(8,128)(2,1)S(1)} collective-permute-done((bf16[416,256]{1,0:T(8,128)(2,1)S(1)}, bf16[416,256]{1,0:T(8,128)(2,1)S(1)}, u32[]{:S(2)}, u32[]{:S(2)}) %collective-permute-start.35) | collective-permute-done | bytes 213024 | tf_op jit(solution)/shard_map/ppermute | solution.py:45
  111.2 1.9 %collective-permute-start.39 = (bf16[104,256]{1,0:T(8,128)(2,1)S(1)}, bf16[104,256]{1,0:T(8,128)(2,1)S(1)}, u32[]{:S(2)}, u32[]{:S(2)}) collective-permute-start(bf16[104,256]{1,0:T(8,128)(2,1)S(1)} %get-tuple-element.173), channel_id=1, source_target_pairs={{0,3},{1,2},{2,1},{3,0},{4,7},{5,6},{6,5},{7,4},{8,11},{9,10},{10,... | collective-permute-start | bytes 159752 | tf_op jit(solution)/shard_map/ppermute | solution.py:45
  113.1 2.5 %collective-permute-start.37 = (bf16[104,256]{1,0:T(8,128)(2,1)S(1)}, bf16[104,256]{1,0:T(8,128)(2,1)S(1)}, u32[]{:S(2)}, u32[]{:S(2)}) collective-permute-start(bf16[104,256]{1,0:T(8,128)(2,1)S(1)} %get-tuple-element.175), channel_id=1, source_target_pairs={{0,1},{1,0},{2,3},{3,2},{4,5},{5,4},{6,7},{7,6},{8,9},{9,8},{10,11... | collective-permute-start | bytes 159752 | tf_op jit(solution)/shard_map/ppermute | solution.py:45
  115.7 0.8 conv_step.1
  116.6 0.7 collective-permute-done.39.refs_2_
  117.3 1.1 collective-permute-done.38.refs_1_
  118.5 0.8 lateral_step.1
  (103 shorter events, 1.5 us)
Async XLA Ops:
  0.6 21.2 %copy-start.19 = (s32[2,2,32,3]{2,1,3,0:T(2,128)S(1)}, s32[2,2,32,3]{2,1,3,0:T(2,128)}, u32[]{:S(2)}) copy-start(s32[2,2,32,3]{2,1,3,0:T(2,128)} %param.27) | copy-start | bytes 4612
  0.7 21.2 %copy-start.14 = (s32[2,4,64,3]{2,1,3,0:T(4,128)S(1)}, s32[2,4,64,3]{2,1,3,0:T(4,128)}, u32[]{:S(2)}) copy-start(s32[2,4,64,3]{2,1,3,0:T(4,128)} %param.26) | copy-start | bytes 18436
  0.7 21.2 %copy-start.9 = (s32[2,8,128,3]{2,1,3,0:T(8,128)S(1)}, s32[2,8,128,3]{2,1,3,0:T(8,128)}, u32[]{:S(2)}) copy-start(s32[2,8,128,3]{2,1,3,0:T(8,128)} %param.25) | copy-start | bytes 73732
  0.7 21.2 %copy-start.18 = (f32[2,2,32,12]{2,1,3,0:T(2,128)S(1)}, f32[2,2,32,12]{2,1,3,0:T(2,128)}, u32[]{:S(2)}) copy-start(f32[2,2,32,12]{2,1,3,0:T(2,128)} %param.24) | copy-start | bytes 18436
  0.7 21.2 %copy-start.13 = (f32[2,4,64,12]{2,1,3,0:T(4,128)S(1)}, f32[2,4,64,12]{2,1,3,0:T(4,128)}, u32[]{:S(2)}) copy-start(f32[2,4,64,12]{2,1,3,0:T(4,128)} %param.23) | copy-start | bytes 73732
  0.7 21.2 %copy-start.10 = (f32[2,8,128,12]{2,1,3,0:T(8,128)S(1)}, f32[2,8,128,12]{2,1,3,0:T(8,128)}, u32[]{:S(2)}) copy-start(f32[2,8,128,12]{2,1,3,0:T(8,128)} %param.22) | copy-start | bytes 294916
  2.4 7.7 %collective-permute-start.2 = (bf16[104,256]{1,0:T(8,128)(2,1)}, bf16[104,256]{1,0:T(8,128)(2,1)S(1)}, u32[]{:S(2)}, u32[]{:S(2)}) collective-permute-start(bf16[104,256]{1,0:T(8,128)(2,1)} %pack.1), channel_id=1, source_target_pairs={{0,3},{1,2},{2,1},{3,0},{4,7},{5,6},{6,5},{7,4},{8,11},{9,10},{10,... | collective-permute-start | bytes 159752 | tf_op jit(solution)/shard_map/ppermute | solution.py:45
  7.6 5.2 %collective-permute-start.1 = (bf16[104,256]{1,0:T(8,128)(2,1)}, bf16[104,256]{1,0:T(8,128)(2,1)S(1)}, u32[]{:S(2)}, u32[]{:S(2)}) collective-permute-start(bf16[104,256]{1,0:T(8,128)(2,1)} %pack.1), channel_id=1, source_target_pairs={{0,2},{1,3},{2,0},{3,1},{4,6},{5,7},{6,4},{7,5},{8,10},{9,11},{10,... | collective-permute-start | bytes 159752 | tf_op jit(solution)/shard_map/ppermute | solution.py:45
  7.6 5.2 %collective-permute-start = (bf16[104,256]{1,0:T(8,128)(2,1)}, bf16[104,256]{1,0:T(8,128)(2,1)S(1)}, u32[]{:S(2)}, u32[]{:S(2)}) collective-permute-start(bf16[104,256]{1,0:T(8,128)(2,1)} %pack.1), channel_id=1, source_target_pairs={{0,1},{1,0},{2,3},{3,2},{4,5},{5,4},{6,7},{7,6},{8,9},{9,8},{10,11... | collective-permute-start | bytes 159752 | tf_op jit(solution)/shard_map/ppermute | solution.py:45
  13.9 6.4 %collective-permute-start.12 = (bf16[72,512]{1,0:T(8,128)(2,1)S(1)}, bf16[72,512]{1,0:T(8,128)(2,1)S(1)}, u32[]{:S(2)}, u32[]{:S(2)}) collective-permute-start(bf16[72,512]{1,0:T(8,128)(2,1)S(1)} %pad_maximum_fusion.4), channel_id=1, source_target_pairs={{0,3},{1,2},{2,1},{3,0},{4,7},{5,6},{6,5},{7,4},{8,11},{9,10},{10,... | collective-permute-start | bytes 221192 | tf_op jit(solution)/shard_map/ppermute | solution.py:45
  16.3 9.6 %collective-permute-start.5 = (bf16[416,256]{1,0:T(8,128)(2,1)S(1)}, bf16[416,256]{1,0:T(8,128)(2,1)S(1)}, u32[]{:S(2)}, u32[]{:S(2)}) collective-permute-start(bf16[416,256]{1,0:T(8,128)(2,1)S(1)} %constant_dynamic-update-slice_fusion.refs_0_), channel_id=1, source_target_pairs={{0,24},{4,28},{8,16},{12,20},{16,8},{20,12},{24,0},{28,4},{1,25},{... | collective-permute-start | bytes 638984 | tf_op jit(solution)/shard_map/ppermute | solution.py:45
  18.8 8.5 %collective-permute-start.4 = (bf16[416,256]{1,0:T(8,128)(2,1)S(1)}, bf16[416,256]{1,0:T(8,128)(2,1)S(1)}, u32[]{:S(2)}, u32[]{:S(2)}) collective-permute-start(bf16[416,256]{1,0:T(8,128)(2,1)S(1)} %constant_dynamic-update-slice_fusion.refs_0_), channel_id=1, source_target_pairs={{0,16},{4,20},{8,24},{12,28},{16,0},{20,4},{24,8},{28,12},{1,17},{... | collective-permute-start | bytes 638984 | tf_op jit(solution)/shard_map/ppermute | solution.py:45
  19.3 8.1 %collective-permute-start.3 = (bf16[416,256]{1,0:T(8,128)(2,1)S(1)}, bf16[416,256]{1,0:T(8,128)(2,1)S(1)}, u32[]{:S(2)}, u32[]{:S(2)}) collective-permute-start(bf16[416,256]{1,0:T(8,128)(2,1)S(1)} %constant_dynamic-update-slice_fusion.refs_0_), channel_id=1, source_target_pairs={{0,8},{4,12},{8,0},{12,4},{16,24},{20,28},{24,16},{28,20},{1,9},{5... | collective-permute-start | bytes 638984 | tf_op jit(solution)/shard_map/ppermute | solution.py:45
  19.8 6.0 %collective-permute-start.11 = (bf16[72,512]{1,0:T(8,128)(2,1)S(1)}, bf16[72,512]{1,0:T(8,128)(2,1)S(1)}, u32[]{:S(2)}, u32[]{:S(2)}) collective-permute-start(bf16[72,512]{1,0:T(8,128)(2,1)S(1)} %pad_maximum_fusion.4), channel_id=1, source_target_pairs={{0,2},{1,3},{2,0},{3,1},{4,6},{5,7},{6,4},{7,5},{8,10},{9,11},{10,... | collective-permute-start | bytes 221192 | tf_op jit(solution)/shard_map/ppermute | solution.py:45
  20.3 5.6 %collective-permute-start.10 = (bf16[72,512]{1,0:T(8,128)(2,1)S(1)}, bf16[72,512]{1,0:T(8,128)(2,1)S(1)}, u32[]{:S(2)}, u32[]{:S(2)}) collective-permute-start(bf16[72,512]{1,0:T(8,128)(2,1)S(1)} %pad_maximum_fusion.4), channel_id=1, source_target_pairs={{0,1},{1,0},{2,3},{3,2},{4,5},{5,4},{6,7},{7,6},{8,9},{9,8},{10,11... | collective-permute-start | bytes 221192 | tf_op jit(solution)/shard_map/ppermute | solution.py:45
  21.9 2.2 %copy-start = (bf16[2,8,128,1024]{3,2,1,0:T(8,128)(2,1)S(1)}, bf16[2,8,128,1024]{3,2,1,0:T(8,128)(2,1)}, u32[]{:S(2)}) copy-start(bf16[2,8,128,1024]{3,2,1,0:T(8,128)(2,1)} %four.3) | copy-start | bytes 12582916
  24.1 1.6 %copy-start.2 = (bf16[2,4,64,2048]{3,2,1,0:T(8,128)(2,1)S(1)}, bf16[2,4,64,2048]{3,2,1,0:T(8,128)(2,1)}, u32[]{:S(2)}) copy-start(bf16[2,4,64,2048]{3,2,1,0:T(8,128)(2,1)} %five.3) | copy-start | bytes 6291460
  25.7 6.4 %copy-start.1 = (bf16[2,8,128,1024]{3,2,1,0:T(8,128)(2,1)S(1)}, bf16[2,8,128,1024]{3,2,1,0:T(8,128)(2,1)}, u32[]{:S(2)}) copy-start(bf16[2,8,128,1024]{3,2,1,0:T(8,128)(2,1)} %four.3) | copy-start | bytes 12582916
  27.4 2.8 %collective-permute-start.6 = (bf16[416,256]{1,0:T(8,128)(2,1)S(1)}, bf16[416,256]{1,0:T(8,128)(2,1)S(1)}, u32[]{:S(2)}, u32[]{:S(2)}) collective-permute-start(bf16[416,256]{1,0:T(8,128)(2,1)S(1)} %constant_dynamic-update-slice_fusion.refs_0_), channel_id=1, source_target_pairs={{0,4},{4,0},{8,12},{12,8},{16,20},{20,16},{24,28},{28,24},{1,5},{5... | collective-permute-start | bytes 638984 | tf_op jit(solution)/shard_map/ppermute | solution.py:45
  27.4 4.1 %collective-permute-start.7 = (bf16[416,256]{1,0:T(8,128)(2,1)S(1)}, bf16[416,256]{1,0:T(8,128)(2,1)S(1)}, u32[]{:S(2)}, u32[]{:S(2)}) collective-permute-start(bf16[416,256]{1,0:T(8,128)(2,1)S(1)} %collective-permute-done.3.refs_2_), channel_id=1, source_target_pairs={{0,4},{4,0},{8,12},{12,8},{16,20},{20,16},{24,28},{28,24},{1,5},{5... | collective-permute-start | bytes 638984 | tf_op jit(solution)/shard_map/ppermute | solution.py:45
  27.9 4.1 %collective-permute-start.8 = (bf16[416,256]{1,0:T(8,128)(2,1)S(1)}, bf16[416,256]{1,0:T(8,128)(2,1)S(1)}, u32[]{:S(2)}, u32[]{:S(2)}) collective-permute-start(bf16[416,256]{1,0:T(8,128)(2,1)S(1)} %collective-permute-done.4.refs_4_), channel_id=1, source_target_pairs={{0,4},{4,0},{8,12},{12,8},{16,20},{20,16},{24,28},{28,24},{1,5},{5... | collective-permute-start | bytes 638984 | tf_op jit(solution)/shard_map/ppermute | solution.py:45
  27.9 4.1 %collective-permute-start.9 = (bf16[416,256]{1,0:T(8,128)(2,1)S(1)}, bf16[416,256]{1,0:T(8,128)(2,1)S(1)}, u32[]{:S(2)}, u32[]{:S(2)}) collective-permute-start(bf16[416,256]{1,0:T(8,128)(2,1)S(1)} %collective-permute-done.5.refs_6_), channel_id=1, source_target_pairs={{0,4},{4,0},{8,12},{12,8},{16,20},{20,16},{24,28},{28,24},{1,5},{5... | collective-permute-start | bytes 638984 | tf_op jit(solution)/shard_map/ppermute | solution.py:45
  28.5 10.9 %collective-permute-start.15 = (bf16[288,512]{1,0:T(8,128)(2,1)S(1)}, bf16[288,512]{1,0:T(8,128)(2,1)S(1)}, u32[]{:S(2)}, u32[]{:S(2)}) collective-permute-start(bf16[288,512]{1,0:T(8,128)(2,1)S(1)} %pad_maximum_fusion.2.refs_0_), channel_id=1, source_target_pairs={{0,24},{4,28},{8,16},{12,20},{16,8},{20,12},{24,0},{28,4},{1,25},{... | collective-permute-start | bytes 884744 | tf_op jit(solution)/shard_map/ppermute | solution.py:45
  30.2 14.5 %collective-permute-start.14 = (bf16[288,512]{1,0:T(8,128)(2,1)S(1)}, bf16[288,512]{1,0:T(8,128)(2,1)S(1)}, u32[]{:S(2)}, u32[]{:S(2)}) collective-permute-start(bf16[288,512]{1,0:T(8,128)(2,1)S(1)} %pad_maximum_fusion.2.refs_0_), channel_id=1, source_target_pairs={{0,16},{4,20},{8,24},{12,28},{16,0},{20,4},{24,8},{28,12},{1,17},{... | collective-permute-start | bytes 884744 | tf_op jit(solution)/shard_map/ppermute | solution.py:45
  31.5 14.1 %collective-permute-start.13 = (bf16[288,512]{1,0:T(8,128)(2,1)S(1)}, bf16[288,512]{1,0:T(8,128)(2,1)S(1)}, u32[]{:S(2)}, u32[]{:S(2)}) collective-permute-start(bf16[288,512]{1,0:T(8,128)(2,1)S(1)} %pad_maximum_fusion.2.refs_0_), channel_id=1, source_target_pairs={{0,8},{4,12},{8,0},{12,4},{16,24},{20,28},{24,16},{28,20},{1,9},{5... | collective-permute-start | bytes 884744 | tf_op jit(solution)/shard_map/ppermute | solution.py:45
  34.0 11.6 %collective-permute-start.16 = (bf16[2,192,256]{2,1,0:T(8,128)(2,1)S(1)}, bf16[2,192,256]{2,1,0:T(8,128)(2,1)S(1)}, u32[]{:S(2)}, u32[]{:S(2)}) collective-permute-start(bf16[2,192,256]{2,1,0:T(8,128)(2,1)S(1)} %get-tuple-element.104), channel_id=1, source_target_pairs={{0,4},{4,0},{8,12},{12,8},{16,20},{20,16},{24,28},{28,24},{1,5},{5... | collective-permute-start | bytes 589832 | tf_op jit(solution)/shard_map/ppermute | solution.py:45
  34.1 11.5 %collective-permute-start.17 = (bf16[2,192,256]{2,1,0:T(8,128)(2,1)S(1)}, bf16[2,192,256]{2,1,0:T(8,128)(2,1)S(1)}, u32[]{:S(2)}, u32[]{:S(2)}) collective-permute-start(bf16[2,192,256]{2,1,0:T(8,128)(2,1)S(1)} %get-tuple-element.105), channel_id=1, source_target_pairs={{4,8},{12,16},{20,24},{8,4},{16,12},{24,20},{5,9},{13,17},{21,25},... | collective-permute-start | bytes 589832 | tf_op jit(solution)/shard_map/ppermute | solution.py:109
  45.6 4.5 %collective-permute-start.18 = (bf16[288,512]{1,0:T(8,128)(2,1)S(1)}, bf16[288,512]{1,0:T(8,128)(2,1)S(1)}, u32[]{:S(2)}, u32[]{:S(2)}) collective-permute-start(bf16[288,512]{1,0:T(8,128)(2,1)S(1)} %pad_maximum_fusion.2.refs_0_), channel_id=1, source_target_pairs={{0,4},{4,0},{8,12},{12,8},{16,20},{20,16},{24,28},{28,24},{1,5},{5... | collective-permute-start | bytes 884744 | tf_op jit(solution)/shard_map/ppermute | solution.py:45
  48.7 1.6 %collective-permute-start.19 = (bf16[288,512]{1,0:T(8,128)(2,1)S(1)}, bf16[288,512]{1,0:T(8,128)(2,1)S(1)}, u32[]{:S(2)}, u32[]{:S(2)}) collective-permute-start(bf16[288,512]{1,0:T(8,128)(2,1)S(1)} %collective-permute-done.13.refs_2_), channel_id=1, source_target_pairs={{0,4},{4,0},{8,12},{12,8},{16,20},{20,16},{24,28},{28,24},{1,5},{5... | collective-permute-start | bytes 884744 | tf_op jit(solution)/shard_map/ppermute | solution.py:45
  48.7 2.0 %collective-permute-start.20 = (bf16[288,512]{1,0:T(8,128)(2,1)S(1)}, bf16[288,512]{1,0:T(8,128)(2,1)S(1)}, u32[]{:S(2)}, u32[]{:S(2)}) collective-permute-start(bf16[288,512]{1,0:T(8,128)(2,1)S(1)} %collective-permute-done.14.refs_4_), channel_id=1, source_target_pairs={{0,4},{4,0},{8,12},{12,8},{16,20},{20,16},{24,28},{28,24},{1,5},{5... | collective-permute-start | bytes 884744 | tf_op jit(solution)/shard_map/ppermute | solution.py:45
  49.2 2.0 %collective-permute-start.21 = (bf16[288,512]{1,0:T(8,128)(2,1)S(1)}, bf16[288,512]{1,0:T(8,128)(2,1)S(1)}, u32[]{:S(2)}, u32[]{:S(2)}) collective-permute-start(bf16[288,512]{1,0:T(8,128)(2,1)S(1)} %collective-permute-done.15.refs_6_), channel_id=1, source_target_pairs={{0,4},{4,0},{8,12},{12,8},{16,20},{20,16},{24,28},{28,24},{1,5},{5... | collective-permute-start | bytes 884744 | tf_op jit(solution)/shard_map/ppermute | solution.py:45
  55.5 1.4 %collective-permute-start.22 = (f32[2,3,16,256]{3,2,1,0:T(8,128)S(1)}, f32[2,3,16,256]{3,2,1,0:T(8,128)S(1)}, u32[]{:S(2)}, u32[]{:S(2)}) collective-permute-start(f32[2,3,16,256]{3,2,1,0:T(8,128)S(1)} %get-tuple-element.116), channel_id=1, source_target_pairs={{0,4},{4,0},{8,12},{12,8},{16,20},{20,16},{24,28},{28,24},{1,5},{5... | collective-permute-start | bytes 294920 | tf_op jit(solution)/shard_map/ppermute | solution.py:45
  55.9 0.9 collective-permute-start.23
  59.6 11.2 %collective-permute-start.24 = (bf16[2,192,256]{2,1,0:T(8,128)(2,1)S(1)}, bf16[2,192,256]{2,1,0:T(8,128)(2,1)S(1)}, u32[]{:S(2)}, u32[]{:S(2)}) collective-permute-start(bf16[2,192,256]{2,1,0:T(8,128)(2,1)S(1)} %get-tuple-element.124), channel_id=1, source_target_pairs={{0,4},{4,0},{8,12},{12,8},{16,20},{20,16},{24,28},{28,24},{1,5},{5... | collective-permute-start | bytes 589832 | tf_op jit(solution)/shard_map/ppermute | solution.py:45
  65.7 5.1 %collective-permute-start.25 = (bf16[2,192,256]{2,1,0:T(8,128)(2,1)S(1)}, bf16[2,192,256]{2,1,0:T(8,128)(2,1)S(1)}, u32[]{:S(2)}, u32[]{:S(2)}) collective-permute-start(bf16[2,192,256]{2,1,0:T(8,128)(2,1)S(1)} %get-tuple-element.125), channel_id=1, source_target_pairs={{4,8},{12,16},{20,24},{8,4},{16,12},{24,20},{5,9},{13,17},{21,25},... | collective-permute-start | bytes 589832 | tf_op jit(solution)/shard_map/ppermute | solution.py:109
  70.8 5.7 %collective-permute-start.26 = (bf16[4,288,512]{2,1,0:T(8,128)(2,1)S(1)}, bf16[4,288,512]{2,1,0:T(8,128)(2,1)S(1)}, u32[]{:S(2)}, u32[]{:S(2)}) collective-permute-start(bf16[4,288,512]{2,1,0:T(8,128)(2,1)S(1)} %get-tuple-element.129), channel_id=1, source_target_pairs={{0,4},{4,0},{8,12},{12,8},{16,20},{20,16},{24,28},{28,24},{1,5},{5... | collective-permute-start | bytes 3538952 | tf_op jit(solution)/shard_map/ppermute | solution.py:45
  76.8 10.8 %collective-permute-start.27 = (bf16[288,512]{1,0:T(8,128)(2,1)S(1)}, bf16[288,512]{1,0:T(8,128)(2,1)S(1)}, u32[]{:S(2)}, u32[]{:S(2)}) collective-permute-start(bf16[288,512]{1,0:T(8,128)(2,1)S(1)} %get-tuple-element.140), channel_id=1, source_target_pairs={{0,8},{4,12},{8,0},{12,4},{16,24},{20,28},{24,16},{28,20},{1,9},{5... | collective-permute-start | bytes 884744 | tf_op jit(solution)/shard_map/ppermute | solution.py:45
  79.0 13.7 %collective-permute-start.28 = (bf16[288,512]{1,0:T(8,128)(2,1)S(1)}, bf16[288,512]{1,0:T(8,128)(2,1)S(1)}, u32[]{:S(2)}, u32[]{:S(2)}) collective-permute-start(bf16[288,512]{1,0:T(8,128)(2,1)S(1)} %get-tuple-element.141), channel_id=1, source_target_pairs={{0,16},{4,20},{8,24},{12,28},{16,0},{20,4},{24,8},{28,12},{1,17},{... | collective-permute-start | bytes 884744 | tf_op jit(solution)/shard_map/ppermute | solution.py:45
  79.8 14.7 %collective-permute-start.29 = (bf16[288,512]{1,0:T(8,128)(2,1)S(1)}, bf16[288,512]{1,0:T(8,128)(2,1)S(1)}, u32[]{:S(2)}, u32[]{:S(2)}) collective-permute-start(bf16[288,512]{1,0:T(8,128)(2,1)S(1)} %get-tuple-element.142), channel_id=1, source_target_pairs={{0,24},{4,28},{8,16},{12,20},{16,8},{20,12},{24,0},{28,4},{1,25},{... | collective-permute-start | bytes 884744 | tf_op jit(solution)/shard_map/ppermute | solution.py:45
  81.2 3.5 %copy-start.3 = (bf16[2,4,64,2048]{3,2,1,0:T(8,128)(2,1)S(1)}, bf16[2,4,64,2048]{3,2,1,0:T(8,128)(2,1)}, u32[]{:S(2)}) copy-start(bf16[2,4,64,2048]{3,2,1,0:T(8,128)(2,1)} %five.3) | copy-start | bytes 6291460
  94.7 2.4 %collective-permute-start.33 = (bf16[4,416,256]{2,1,0:T(8,128)(2,1)S(1)}, bf16[4,416,256]{2,1,0:T(8,128)(2,1)S(1)}, u32[]{:S(2)}, u32[]{:S(2)}) collective-permute-start(bf16[4,416,256]{2,1,0:T(8,128)(2,1)S(1)} %get-tuple-element.145), channel_id=1, source_target_pairs={{0,4},{4,0},{8,12},{12,8},{16,20},{20,16},{24,28},{28,24},{1,5},{5... | collective-permute-start | bytes 2555912 | tf_op jit(solution)/shard_map/ppermute | solution.py:45
  97.3 8.2 %collective-permute-start.34 = (bf16[416,256]{1,0:T(8,128)(2,1)S(1)}, bf16[416,256]{1,0:T(8,128)(2,1)S(1)}, u32[]{:S(2)}, u32[]{:S(2)}) collective-permute-start(bf16[416,256]{1,0:T(8,128)(2,1)S(1)} %get-tuple-element.167), channel_id=1, source_target_pairs={{0,8},{4,12},{8,0},{12,4},{16,24},{20,28},{24,16},{28,20},{1,9},{5... | collective-permute-start | bytes 638984 | tf_op jit(solution)/shard_map/ppermute | solution.py:45
  97.9 11.5 %collective-permute-start.36 = (bf16[416,256]{1,0:T(8,128)(2,1)S(1)}, bf16[416,256]{1,0:T(8,128)(2,1)S(1)}, u32[]{:S(2)}, u32[]{:S(2)}) collective-permute-start(bf16[416,256]{1,0:T(8,128)(2,1)S(1)} %get-tuple-element.168), channel_id=1, source_target_pairs={{0,24},{4,28},{8,16},{12,20},{16,8},{20,12},{24,0},{28,4},{1,25},{... | collective-permute-start | bytes 638984 | tf_op jit(solution)/shard_map/ppermute | solution.py:45
  99.5 11.3 %collective-permute-start.35 = (bf16[416,256]{1,0:T(8,128)(2,1)S(1)}, bf16[416,256]{1,0:T(8,128)(2,1)S(1)}, u32[]{:S(2)}, u32[]{:S(2)}) collective-permute-start(bf16[416,256]{1,0:T(8,128)(2,1)S(1)} %get-tuple-element.169), channel_id=1, source_target_pairs={{0,16},{4,20},{8,24},{12,28},{16,0},{20,4},{24,8},{28,12},{1,17},{... | collective-permute-start | bytes 638984 | tf_op jit(solution)/shard_map/ppermute | solution.py:45
  100.9 10.1 %collective-permute-start.32 = (bf16[72,512]{1,0:T(8,128)(2,1)S(1)}, bf16[72,512]{1,0:T(8,128)(2,1)S(1)}, u32[]{:S(2)}, u32[]{:S(2)}) collective-permute-start(bf16[72,512]{1,0:T(8,128)(2,1)S(1)} %get-tuple-element.170), channel_id=1, source_target_pairs={{0,3},{1,2},{2,1},{3,0},{4,7},{5,6},{6,5},{7,4},{8,11},{9,10},{10,... | collective-permute-start | bytes 221192 | tf_op jit(solution)/shard_map/ppermute | solution.py:45
  102.8 8.2 %collective-permute-start.31 = (bf16[72,512]{1,0:T(8,128)(2,1)S(1)}, bf16[72,512]{1,0:T(8,128)(2,1)S(1)}, u32[]{:S(2)}, u32[]{:S(2)}) collective-permute-start(bf16[72,512]{1,0:T(8,128)(2,1)S(1)} %get-tuple-element.171), channel_id=1, source_target_pairs={{0,2},{1,3},{2,0},{3,1},{4,6},{5,7},{6,4},{7,5},{8,10},{9,11},{10,... | collective-permute-start | bytes 221192 | tf_op jit(solution)/shard_map/ppermute | solution.py:45
  105.4 5.5 %collective-permute-start.30 = (bf16[72,512]{1,0:T(8,128)(2,1)S(1)}, bf16[72,512]{1,0:T(8,128)(2,1)S(1)}, u32[]{:S(2)}, u32[]{:S(2)}) collective-permute-start(bf16[72,512]{1,0:T(8,128)(2,1)S(1)} %get-tuple-element.172), channel_id=1, source_target_pairs={{0,1},{1,0},{2,3},{3,2},{4,5},{5,4},{6,7},{7,6},{8,9},{9,8},{10,11... | collective-permute-start | bytes 221192 | tf_op jit(solution)/shard_map/ppermute | solution.py:45
  110.9 4.8 %copy-start.4 = (f32[2,72,256]{2,1,0:T(8,128)S(1)}, f32[2,72,256]{2,1,0:T(8,128)}, u32[]{:S(2)}) copy-start(f32[2,72,256]{2,1,0:T(8,128)} %refs_3_.3) | copy-start | bytes 442372
  110.9 4.8 %copy-start.6 = (f32[2,72,256]{2,1,0:T(8,128)S(1)}, f32[2,72,256]{2,1,0:T(8,128)}, u32[]{:S(2)}) copy-start(f32[2,72,256]{2,1,0:T(8,128)} %refs_4_.3) | copy-start | bytes 442372
  110.9 4.8 %copy-start.7 = (f32[2,72,256]{2,1,0:T(8,128)S(1)}, f32[2,72,256]{2,1,0:T(8,128)}, u32[]{:S(2)}) copy-start(f32[2,72,256]{2,1,0:T(8,128)} %refs_5_.3) | copy-start | bytes 442372
  111.0 7.4 %copy-start.5 = (f32[64,256]{1,0:T(8,128)S(1)}, f32[64,256]{1,0:T(8,128)}, u32[]{:S(2)}) copy-start(f32[64,256]{1,0:T(8,128)} %refs_6_.3) | copy-start | bytes 196612
  111.0 7.4 %copy-start.8 = (f32[32,256]{1,0:T(8,128)S(1)}, f32[32,256]{1,0:T(8,128)}, u32[]{:S(2)}) copy-start(f32[32,256]{1,0:T(8,128)} %refs_3_.2) | copy-start | bytes 98308
  111.1 7.4 %copy-start.11 = (f32[64,256]{1,0:T(8,128)S(1)}, f32[64,256]{1,0:T(8,128)}, u32[]{:S(2)}) copy-start(f32[64,256]{1,0:T(8,128)} %refs_7_.3) | copy-start | bytes 196612
  111.1 7.4 %copy-start.12 = (f32[64,256]{1,0:T(8,128)S(1)}, f32[64,256]{1,0:T(8,128)}, u32[]{:S(2)}) copy-start(f32[64,256]{1,0:T(8,128)} %refs_8_.1) | copy-start | bytes 196612
  111.1 7.4 %copy-start.15 = (f32[72,12]{0,1:T(8,128)S(1)}, f32[72,12]{0,1:T(8,128)}, u32[]{:S(2)}) copy-start(f32[72,12]{0,1:T(8,128)} %param.31) | copy-start | bytes 10372
  111.1 7.4 %copy-start.16 = (f32[32,256]{1,0:T(8,128)S(1)}, f32[32,256]{1,0:T(8,128)}, u32[]{:S(2)}) copy-start(f32[32,256]{1,0:T(8,128)} %refs_4_.2) | copy-start | bytes 98308
  111.1 7.4 %copy-start.17 = (f32[32,256]{1,0:T(8,128)S(1)}, f32[32,256]{1,0:T(8,128)}, u32[]{:S(2)}) copy-start(f32[32,256]{1,0:T(8,128)} %refs_5_.2) | copy-start | bytes 98308
  111.1 7.4 %copy-start.20 = (f32[72,12]{0,1:T(8,128)S(1)}, f32[72,12]{0,1:T(8,128)}, u32[]{:S(2)}) copy-start(f32[72,12]{0,1:T(8,128)} %param.35) | copy-start | bytes 10372
  111.1 7.4 %copy-start.21 = (f32[72,12]{0,1:T(8,128)S(1)}, f32[72,12]{0,1:T(8,128)}, u32[]{:S(2)}) copy-start(f32[72,12]{0,1:T(8,128)} %param.39) | copy-start | bytes 10372
  111.2 6.1 %collective-permute-start.39 = (bf16[104,256]{1,0:T(8,128)(2,1)S(1)}, bf16[104,256]{1,0:T(8,128)(2,1)S(1)}, u32[]{:S(2)}, u32[]{:S(2)}) collective-permute-start(bf16[104,256]{1,0:T(8,128)(2,1)S(1)} %get-tuple-element.173), channel_id=1, source_target_pairs={{0,3},{1,2},{2,1},{3,0},{4,7},{5,6},{6,5},{7,4},{8,11},{9,10},{10,... | collective-permute-start | bytes 159752 | tf_op jit(solution)/shard_map/ppermute | solution.py:45
  113.1 5.3 %collective-permute-start.38 = (bf16[104,256]{1,0:T(8,128)(2,1)S(1)}, bf16[104,256]{1,0:T(8,128)(2,1)S(1)}, u32[]{:S(2)}, u32[]{:S(2)}) collective-permute-start(bf16[104,256]{1,0:T(8,128)(2,1)S(1)} %get-tuple-element.174), channel_id=1, source_target_pairs={{0,2},{1,3},{2,0},{3,1},{4,6},{5,7},{6,4},{7,5},{8,10},{9,11},{10,... | collective-permute-start | bytes 159752 | tf_op jit(solution)/shard_map/ppermute | solution.py:45
  113.1 5.3 %collective-permute-start.37 = (bf16[104,256]{1,0:T(8,128)(2,1)S(1)}, bf16[104,256]{1,0:T(8,128)(2,1)S(1)}, u32[]{:S(2)}, u32[]{:S(2)}) collective-permute-start(bf16[104,256]{1,0:T(8,128)(2,1)S(1)} %get-tuple-element.175), channel_id=1, source_target_pairs={{0,1},{1,0},{2,3},{3,2},{4,5},{5,4},{6,7},{7,6},{8,9},{9,8},{10,11... | collective-permute-start | bytes 159752 | tf_op jit(solution)/shard_map/ppermute | solution.py:45

commit v4 on v3

--- a/solution.py
+++ b/solution.py
@@ -85,12 +85,9 @@
     ]
 
 
-def summed_high(partial):
+def sent_high(partial):
     _, low, high = row_groups()
-    return sum(
-        (sent(partial[j].astype(bf16), "rows", j * low).astype(f32) for j in range(1, high)),
-        partial[0],
-    )
+    return [sent(partial[j].astype(bf16), "rows", j * low) for j in range(1, high)]
 
 
 def shared_batch(blocks):
@@ -255,7 +252,8 @@
 
 def lateral_kernel(n_rows, four, five, *refs):
     pieces, rest = refs[:n_rows], refs[n_rows:]
-    input_four, input_five, pair, other, kernel_four, kernel_five, wide, first, last = rest
+    input_four, input_five, pair, other, kernel_four, kernel_five, wide, first, last = rest[1:]
+    mask = rest[0]
     crops, height, width, depth = four.shape
     low_height, low_width = five.shape[1:3]
     me = lax.axis_index("rows")
@@ -270,8 +268,8 @@
         low = dot(five[b].reshape(low_height * low_width, -1), kernel_five[...])
         low_rounded = low.astype(bf16).reshape(low_height, low_width, -1)
         input_five[b] = low_rounded
-        first[b, width:] = low_rounded[0]
-        last[b, width:] = low_rounded[low_height - 1]
+        first[b, width : width + low_width] = low_rounded[0]
+        last[b, width : width + low_width] = low_rounded[low_height - 1]
         for q in range(low_height):
             up = doubled_columns(wide, low[q * low_width : (q + 1) * low_width])
             rows = four[b, 2 * q : 2 * q + 2].reshape(2 * width, depth)
@@ -282,6 +280,17 @@
                 first[b, :width] = rounded[0]
             if q == low_height - 1:
                 last[b, :width] = rounded[1]
+        edge, half = width + low_width, width // 2
+        lane = lax.broadcasted_iota(jnp.int32, (DELTA_ROWS, width), 1)
+        plan = level_rows(height, 1)
+        for ref, end in ((first, 0), (last, 1)):
+            lines = []
+            for _, own, count in plan:
+                at = (own + (count - 1) * end) * width
+                lines.append(mask[b, :, at : at + width])
+            small = jnp.where(lane < half, lines[1], pltpu.roll(lines[2], half, 1))
+            ref[b, edge:, :width] = lines[0].astype(bf16)
+            ref[b, edge:, width:] = small.astype(bf16)
     swapped(first, last, pair, other, True)
 
 
@@ -313,7 +322,7 @@
         padded[b, height + 1] = below[b, start : start + width]
 
 
-def output_kernel(n_rows, input_four, input_five, pair_in, other_in, head, target, mask, *refs):
+def output_kernel(n_rows, deltas, input_four, input_five, pair_in, other_in, head, target, mask, *refs):
     pieces, rest = refs[:n_rows], refs[n_rows:]
     levels, values, pair, other, kernel_four, kernel_five = rest[:6]
     spread_four, spread_five, spare, above, below, first, last = rest[6:]
@@ -382,26 +391,18 @@
             values[b, :, start : start + width] = sums[:, start : start + width]
             values[b, :, start + width : end - width] = partial
             values[b, :, end - width : end] = sums[:, end - width : end]
-            own_end = (own + count_lines) * width
-            upper = (
-                partial[:, :width],
-                sums[:, start : start + width],
-                mask[b, :, own * width : (own + 1) * width],
-            )
-            lower = (
-                partial[:, (count_lines - 1) * width :],
-                sums[:, end - width : end],
-                mask[b, :, own_end - width : own_end],
-            )
+            upper = (partial[:, :width], sums[:, start : start + width])
+            lower = (partial[:, (count_lines - 1) * width :], sums[:, end - width : end])
             for out, values_of in ((first, upper), (last, lower)):
                 for kind, line in enumerate(values_of):
+                    lines, line = slice(kind * deltas, (kind + 1) * deltas), line[:deltas]
                     if index < 2:
-                        out[b, kind, :, index * width : (index + 1) * width] = line
+                        out[b, lines, index * width : (index + 1) * width] = line
                     else:
                         moved = pltpu.roll(line, half, 1)
                         lane = lax.broadcasted_iota(jnp.int32, line.shape, 1)
-                        mixed = jnp.where(lane < half, out[b, kind, :, width : 2 * width], moved)
-                        out[b, kind, :, width : 2 * width] = mixed
+                        mixed = jnp.where(lane < half, out[b, lines, width : 2 * width], moved)
+                        out[b, lines, width : 2 * width] = mixed
     swapped(first, last, pair, other, True)
 
 
@@ -413,24 +414,33 @@
     return result
 
 
-def head_kernel(height, levels, pair_in, other_in, head, values, mask, count, *refs):
+def head_kernel(height, deltas, levels, pair_in, other_in, pair_mask, other_mask, head, values, mask, count, *refs):
     head_grad, grad_four, grad_five, pair, other, loss = refs[:6]
-    taps, wide, above, below, first, last = refs[6:]
+    taps, wide, above, below, first, last, mask_above, mask_below = refs[6:]
     swapped(above, below, pair_in, other_in, False)
+    swapped(mask_above, mask_below, pair_mask, other_mask, False)
+    edge = first.shape[1]
     crops, _, width, channels = levels.shape
     inverse = 1.0 / jnp.maximum(count[0, 0], 1.0)
     plan = level_rows(height, 1)
     summed = jnp.zeros((DELTA_ROWS, LANES), f32)
     total_grad = jnp.zeros((9 * DELTA_ROWS, channels), f32)
     low_height, low_width = height // 2, width // 2
-    def came(ref, b, kind, index):
-        if index == 0:
-            return ref[b, kind, :, :width]
-        line = ref[b, kind, :, width : 2 * width]
+    def small_level(line, index):
         if index == 2:
             line = pltpu.roll(line, width // 2, 1)
         lane = lax.broadcasted_iota(jnp.int32, line.shape, 1)
         return jnp.where(lane < width >> index, line, 0.0)
+
+    def came(ref, b, kind, index):
+        at = slice(0, width) if index == 0 else slice(width, 2 * width)
+        line = ref[b, kind * deltas : (kind + 1) * deltas, at]
+        line = jnp.concatenate([line, jnp.zeros((DELTA_ROWS - deltas, width), f32)], axis=0)
+        return small_level(line, index)
+
+    def mask_line(ref, b, index):
+        at = slice(0, width) if index == 0 else slice(width, 2 * width)
+        return small_level(ref[b, edge:, at].astype(f32), index)
 
     for b in range(crops):
         partial, weights = [], []
@@ -445,9 +455,9 @@
             rows[lines + 1] = rows[lines + 1] + came(below, b, 0, index)
             partial += rows
             weights += [
-                came(above, b, 2, index),
+                mask_line(mask_above, b, index),
                 mask[b, :, own * width : (own + lines) * width],
-                came(below, b, 2, index),
+                mask_line(mask_below, b, index),
             ]
         mismatch = jnp.concatenate(partial, axis=1)
         weight = jnp.concatenate(weights, axis=1)
@@ -625,6 +635,13 @@
         out[part_four + part_five :, :] = jnp.concatenate(pieces, axis=0).astype(bf16)
 
 
+def total_kernel(own, *refs):
+    total = own[...]
+    for piece in refs[:-1]:
+        total = total + piece[...].astype(f32)
+    refs[-1][...] = total
+
+
 def adamw_into(outs, weight, gradient, mean, square):
     for out, value in zip(outs, adamw_update(weight, gradient, mean, square)):
         out[...] = value
@@ -744,17 +761,19 @@
     convs = gathered_high(conv)
 
     edge = width + low_width
-    input_rims = [pltpu.VMEM((crops, edge, channels), bf16)] * 2
-    head_rims = [pltpu.VMEM((crops, 3, DELTA_ROWS, 2 * width), f32)] * 2
+    full_edge = edge + DELTA_ROWS
+    input_rims = [pltpu.VMEM((crops, full_edge, channels), bf16)] * 2
+    grad_rims = [pltpu.VMEM((crops, edge, channels), bf16)] * 2
+    head_rims = [pltpu.VMEM((crops, 2 * deltas, 2 * width), f32)] * 2
     input_four, input_five, pair, other = call(
         functools.partial(lateral_kernel, n_rows),
         "laterals",
-        [section_four, section_five, *laterals],
+        [section_four, section_five, *laterals, mask],
         [
             shape((crops, height, width, channels), bf16),
             shape((crops, low_height, low_width, channels), bf16),
-            shape((crops, edge, channels), bf16),
-            shape((crops, edge, channels), bf16),
+            shape((crops, full_edge, channels), bf16),
+            shape((crops, full_edge, channels), bf16),
         ],
         [
             pltpu.VMEM((depth, channels), bf16),
@@ -765,10 +784,6 @@
         flops=2 * crops * channels * (height * width * depth + low_height * low_width * low_depth),
     )
     pair_in, other_in = from_neighbours(pair, other)
-    convs, pair_in, other_in = lax.optimization_barrier((convs, pair_in, other_in))
-    convs = gathered_low(convs)
-
-    conv_flops = 18 * crops * channels * channels * (height * width + low_height * low_width)
     head, count = call(
         functools.partial(head_weights_kernel, n_rows, n_batch, deltas, conv_n),
         "head_weights",
@@ -777,15 +792,19 @@
         [pltpu.VMEM((DELTA_ROWS, 9 * channels + 2 * LANES), f32)],
         scalar_outs=1,
     )
+    convs, pair_in, other_in, head = lax.optimization_barrier((convs, pair_in, other_in, head))
+    convs = gathered_low(convs)
+
+    conv_flops = 18 * crops * channels * channels * (height * width + low_height * low_width)
     levels, values, pair, other, kernel_four, kernel_five = call(
-        functools.partial(output_kernel, n_rows),
+        functools.partial(output_kernel, n_rows, deltas),
         "outputs",
         [input_four, input_five, pair_in, other_in, head, target, mask, *convs],
         [
             shape((crops, lines, width, channels), bf16),
             shape((crops, DELTA_ROWS, (lines + 6) * width), f32),
-            shape((crops, 3, DELTA_ROWS, 2 * width), f32),
-            shape((crops, 3, DELTA_ROWS, 2 * width), f32),
+            shape((crops, 2 * deltas, 2 * width), f32),
+            shape((crops, 2 * deltas, 2 * width), f32),
             shape((9 * channels, channels), bf16),
             shape((9 * channels, channels), bf16),
         ],
@@ -802,9 +821,9 @@
 
     head_flops = 18 * DELTA_ROWS * crops * lines * width * channels
     head_grad, grad_four, grad_five, pair, other, loss = call(
-        functools.partial(head_kernel, height),
+        functools.partial(head_kernel, height, deltas),
         "heads",
-        [levels, pair, other, head, values, mask, count],
+        [levels, pair, other, pair_in, other_in, head, values, mask, count],
         [
             shape((9 * DELTA_ROWS, channels), f32),
             shape((crops, height, width, channels), bf16),
@@ -818,6 +837,7 @@
             pltpu.VMEM((channels // LANES, low_width, LANES), f32),
         ]
         + head_rims
+        + grad_rims
         + input_rims,
         flops=3 * head_flops,
         scalars=1,
@@ -841,9 +861,8 @@
     )
 
     positions, low_positions = crops * height * width, crops * low_height * low_width
-    conv_blocks, pair, other = lax.optimization_barrier((conv_blocks, pair, other))
     conv_partial = summed_low(conv_blocks)
-    pair, other, conv_partial = lax.optimization_barrier((pair, other, conv_partial))
+    pair, other, _ = lax.optimization_barrier((pair, other, conv_partial))
     lat_four, lat_five = call(
         merged_grad_kernel,
         "merged_grads",
@@ -854,10 +873,16 @@
             pltpu.VMEM((crops, low_height + 2, low_width, channels), bf16),
             pltpu.VMEM((4 * width, LANES), f32),
         ]
-        + input_rims,
+        + grad_rims,
         flops=conv_flops,
     )
-    conv_sum = summed_high(conv_partial)
+    (conv_sum,) = call(
+        total_kernel,
+        "conv_total",
+        [conv_partial[0], *sent_high(conv_partial)],
+        [shape(conv_partial[0].shape, f32)],
+        flops=20_000_000_000,
+    )
 
     lateral_n = four_n + five_n + 8
     lateral_kept, *lateral_moved = call(
@@ -873,9 +898,9 @@
         flops=1,
         scalars=1,
     )
-    lateral_moved, conv_sum = lax.optimization_barrier((lateral_moved, conv_sum))
     lateral_partial = summed_low([lateral_kept, *lateral_moved])
-    lateral_sum = summed_high(lateral_partial)
+    lateral_partial, conv_sum = lax.optimization_barrier((lateral_partial, conv_sum))
+    lateral_sum = sum((v.astype(f32) for v in sent_high(lateral_partial)), lateral_partial[0])
     conv_shares = shared_batch(conv_sum.reshape(n_batch, conv_n, conv_width))
     conv_shares, lateral_sum = lax.optimization_barrier((conv_shares, lateral_sum))
     first_conv, second_conv, weight_conv = call(

time: 120 us -> 114 us (0.950)
  waiting for transfers between devices: 39.4 us -> 35.7 us
  starting transfers between devices: 47.6 us -> 45.4 us
    ppermute x37, waiting for transfers between devices: 39.4 us -> 35.7 us  [sent(): return lax.ppermute(value, axis, [(i, i ^ mask) for i in range(count)])]
    ppermute x37, starting transfers between devices: 45.6 us -> 43.4 us  [sent(): return lax.ppermute(value, axis, [(i, i ^ mask) for i in range(count)])]
    pallas_call x11 -> x12, Pallas kernels: 24.2 us -> 24.4 us  [call(): pl.pallas_call(kernel, out_shape=list(outs), in_specs=[hbm] * apart + [vm...]
  transfers between devices with their start and end apart: 40 -> 40, of which waited for: 21 -> 22; matrix products, arithmetic and copies ran while one was open for 1% -> 1% of each run, Pallas kernels for 12% -> 9%
where the time goes in v4:
time: 114 us
  starting transfers between devices  45.4 us (40%)
  waiting for transfers between devices  35.7 us (31%)
  Pallas kernels  24.4 us (21%)
  local copies, waits for them, and re-layouts  4.17 us (4%)
  other arithmetic  2.49 us (2%)
  between operations  1.48 us (1%)
    ppermute x37, starting transfers between devices, sent(): return lax.ppermute(value, axis, [(i, i ^ mask) for i in range(count)])  43.4 us
    ppermute x37, waiting for transfers between devices, sent(): return lax.ppermute(value, axis, [(i, i ^ mask) for i in range(count)])  35.7 us
    pallas_call x12, Pallas kernels, call(): pl.pallas_call(kernel, out_shape=list(outs), in_specs=[hbm] * apart + [vm...  24.4 us
    unnamed x55, local copies, waits for them, and re-layouts  4.02 us
  transfers between devices with their start and end apart: 40, of which 22 were waited for; matrix products, arithmetic and copies ran while one was open for 1% of the time, Pallas kernels for 9%

profile of v4, /device:TPU:0, one launch (start us, length us, event | category | flops | bytes accessed | tf_op | source)
XLA Modules:
  0.0 113.7 jit_solution(423273734013703014)
XLA Ops:
  0.7 1.7 %pack.1 = bf16[104,256]{1,0:T(8,128)(2,1)} custom-call(f32[32,256]{1,0:T(8,128)} %refs_3_.2, f32[64,256]{1,0:T(8,128)} %refs_6_.3, f32[12,72]{1,0:T(8,128)} %bitcast.133, s32[2,3,8,128]{3,2,1,0:T(8,128)} %bitcast.127, s32[2,3,4,64]{3,2,1,0:T(4,128)} %bitcast.131, s32[2,3,2,32]{3,2,1,0:T(2,128)} %bitcast.136), custom_call_target="tpu_custom_call" | custom-call | bytes 187264 | tf_op jit(solution)/shard_map/pack/pallas_call | solution.py:118
  2.4 5.1 %collective-permute-start.2 = (bf16[104,256]{1,0:T(8,128)(2,1)}, bf16[104,256]{1,0:T(8,128)(2,1)S(1)}, u32[]{:S(2)}, u32[]{:S(2)}) collective-permute-start(bf16[104,256]{1,0:T(8,128)(2,1)} %pack.1), channel_id=1, source_target_pairs={{0,3},{1,2},{2,1},{3,0},{4,7},{5,6},{6,5},{7,4},{8,11},{9,10},{10,... | collective-permute-start | bytes 159752 | tf_op jit(solution)/shard_map/ppermute | solution.py:45
  7.6 0.6 collective-permute-start
  8.2 0.9 convert.8
  9.2 0.9 collective-permute-done.2
  10.1 2.7 %collective-permute-done.1 = bf16[104,256]{1,0:T(8,128)(2,1)S(1)} collective-permute-done((bf16[104,256]{1,0:T(8,128)(2,1)}, bf16[104,256]{1,0:T(8,128)(2,1)S(1)}, u32[]{:S(2)}, u32[]{:S(2)}) %collective-permute-start.1) | collective-permute-done | bytes 53280 | tf_op jit(solution)/shard_map/ppermute | solution.py:45
  12.8 0.8 pad_maximum_fusion.3
  13.9 2.4 %collective-permute-start.12 = (bf16[72,512]{1,0:T(8,128)(2,1)S(1)}, bf16[72,512]{1,0:T(8,128)(2,1)S(1)}, u32[]{:S(2)}, u32[]{:S(2)}) collective-permute-start(bf16[72,512]{1,0:T(8,128)(2,1)S(1)} %pad_maximum_fusion.4), channel_id=1, source_target_pairs={{0,3},{1,2},{2,1},{3,0},{4,7},{5,6},{6,5},{7,4},{8,11},{9,10},{10,... | collective-permute-start | bytes 221192 | tf_op jit(solution)/shard_map/ppermute | solution.py:45
  16.3 2.4 %collective-permute-start.5 = (bf16[416,256]{1,0:T(8,128)(2,1)S(1)}, bf16[416,256]{1,0:T(8,128)(2,1)S(1)}, u32[]{:S(2)}, u32[]{:S(2)}) collective-permute-start(bf16[416,256]{1,0:T(8,128)(2,1)S(1)} %constant_dynamic-update-slice_fusion.refs_0_), channel_id=1, source_target_pairs={{0,24},{4,28},{8,16},{12,20},{16,8},{20,12},{24,0},{28,4},{1,25},{... | collective-permute-start | bytes 638984 | tf_op jit(solution)/shard_map/ppermute | solution.py:45
  18.8 0.5 collective-permute-start.4
  19.3 0.5 collective-permute-start.3
  19.8 0.5 collective-permute-done.12
  20.3 1.6 %collective-permute-start.10 = (bf16[72,512]{1,0:T(8,128)(2,1)S(1)}, bf16[72,512]{1,0:T(8,128)(2,1)S(1)}, u32[]{:S(2)}, u32[]{:S(2)}) collective-permute-start(bf16[72,512]{1,0:T(8,128)(2,1)S(1)} %pad_maximum_fusion.4), channel_id=1, source_target_pairs={{0,1},{1,0},{2,3},{3,2},{4,5},{5,4},{6,7},{7,6},{8,9},{9,8},{10,11... | collective-permute-start | bytes 221192 | tf_op jit(solution)/shard_map/ppermute | solution.py:45
  21.9 2.2 %copy-done = bf16[2,8,128,1024]{3,2,1,0:T(8,128)(2,1)S(1)} copy-done((bf16[2,8,128,1024]{3,2,1,0:T(8,128)(2,1)S(1)}, bf16[2,8,128,1024]{3,2,1,0:T(8,128)(2,1)}, u32[]{:S(2)}) %copy-start) | copy-done | bytes 4194328
  24.1 1.6 %copy-done.2 = bf16[2,4,64,2048]{3,2,1,0:T(8,128)(2,1)S(1)} copy-done((bf16[2,4,64,2048]{3,2,1,0:T(8,128)(2,1)S(1)}, bf16[2,4,64,2048]{3,2,1,0:T(8,128)(2,1)}, u32[]{:S(2)}) %copy-start.2) | copy-done | bytes 2097176
  25.7 0.2 planes.1
  25.9 1.4 %collective-permute-done.4.refs_4_ = bf16[416,256]{1,0:T(8,128)(2,1)S(1)} collective-permute-done((bf16[416,256]{1,0:T(8,128)(2,1)S(1)}, bf16[416,256]{1,0:T(8,128)(2,1)S(1)}, u32[]{:S(2)}, u32[]{:S(2)}) %collective-permute-start.4) | collective-permute-done | bytes 213024 | tf_op jit(solution)/shard_map/ppermute | solution.py:45
  27.4 0.5 collective-permute-start.7
  27.9 0.5 collective-permute-start.9
  28.5 1.7 %collective-permute-start.15 = (bf16[288,512]{1,0:T(8,128)(2,1)S(1)}, bf16[288,512]{1,0:T(8,128)(2,1)S(1)}, u32[]{:S(2)}, u32[]{:S(2)}) collective-permute-start(bf16[288,512]{1,0:T(8,128)(2,1)S(1)} %pad_maximum_fusion.2.refs_0_), channel_id=1, source_target_pairs={{0,24},{4,28},{8,16},{12,20},{16,8},{20,12},{24,0},{28,4},{1,25},{... | collective-permute-start | bytes 884744 | tf_op jit(solution)/shard_map/ppermute | solution.py:45
  30.2 1.3 %collective-permute-start.14 = (bf16[288,512]{1,0:T(8,128)(2,1)S(1)}, bf16[288,512]{1,0:T(8,128)(2,1)S(1)}, u32[]{:S(2)}, u32[]{:S(2)}) collective-permute-start(bf16[288,512]{1,0:T(8,128)(2,1)S(1)} %pad_maximum_fusion.2.refs_0_), channel_id=1, source_target_pairs={{0,16},{4,20},{8,24},{12,28},{16,0},{20,4},{24,8},{28,12},{1,17},{... | collective-permute-start | bytes 884744 | tf_op jit(solution)/shard_map/ppermute | solution.py:45
  31.5 0.5 collective-permute-start.13
  32.0 2.0 %laterals.1 = (bf16[2,8,128,256]{3,2,1,0:T(8,128)(2,1)S(1)}, bf16[2,4,64,256]{3,2,1,0:T(8,128)(2,1)S(1)}, bf16[2,208,256]{2,1,0:T(8,128)(2,1)S(1)}, bf16[2,208,256]{2,1,0:T(8,128)(2,1)S(1)}) custom-call(bf16[2,8,128,1024]{3,2,1,0:T(8,128)(2,1)S(1)} %copy-done.1, bf16[2,4,64,2048]{3,2,1,0:T(8,128)(2,1)S(1)} %copy-done.2, ...), custom_call_target="tpu_custom_call" | custom-call | flops 1610612736 | bytes 9961472 | tf_op jit(solution)/shard_map/laterals/pallas_call | solution.py:118
  34.1 0.7 collective-permute-start.17
  34.8 0.9 head_weights.1
  35.7 3.7 %collective-permute-done.15.refs_6_ = bf16[288,512]{1,0:T(8,128)(2,1)S(1)} collective-permute-done((bf16[288,512]{1,0:T(8,128)(2,1)S(1)}, bf16[288,512]{1,0:T(8,128)(2,1)S(1)}, u32[]{:S(2)}, u32[]{:S(2)}) %collective-permute-start.15) | collective-permute-done | bytes 294944 | tf_op jit(solution)/shard_map/ppermute | solution.py:45
  39.3 5.3 %collective-permute-done.14.refs_4_ = bf16[288,512]{1,0:T(8,128)(2,1)S(1)} collective-permute-done((bf16[288,512]{1,0:T(8,128)(2,1)S(1)}, bf16[288,512]{1,0:T(8,128)(2,1)S(1)}, u32[]{:S(2)}, u32[]{:S(2)}) %collective-permute-start.14) | collective-permute-done | bytes 294944 | tf_op jit(solution)/shard_map/ppermute | solution.py:45
  44.7 1.0 collective-permute-done.13.refs_2_
  45.6 3.4 %collective-permute-start.18 = (bf16[288,512]{1,0:T(8,128)(2,1)S(1)}, bf16[288,512]{1,0:T(8,128)(2,1)S(1)}, u32[]{:S(2)}, u32[]{:S(2)}) collective-permute-start(bf16[288,512]{1,0:T(8,128)(2,1)S(1)} %pad_maximum_fusion.2.refs_0_), channel_id=1, source_target_pairs={{0,4},{4,0},{8,12},{12,8},{16,20},{20,16},{24,28},{28,24},{1,5},{5... | collective-permute-start | bytes 884744 | tf_op jit(solution)/shard_map/ppermute | solution.py:45
  49.1 0.5 collective-permute-start.20
  49.6 0.7 collective-permute-done.18.refs_1_
  50.3 0.4 collective-permute-done.19.refs_3_
  50.7 0.4 collective-permute-done.20.refs_5_
  51.1 0.4 collective-permute-done.21.refs_7_
  51.5 4.3 %outputs.1 = (bf16[2,14,128,256]{3,2,1,0:T(8,128)(2,1)S(1)}, f32[2,16,2560]{2,1,0:T(8,128)S(1)}, f32[2,24,256]{2,1,0:T(8,128)S(1)}, f32[2,24,256]{2,1,0:T(8,128)...) custom-call(bf16[2,8,128,256]{3,2,1,0:T(8,128)(2,1)S(1)} %get-tuple-element.98.input_four, ...), custom_call_target="tpu_custom_call" | custom-call | flops 3019898880 | bytes 9248768 | tf_op jit(solution)/shard_map/outputs/pallas_call | solution.py:118
  55.9 0.4 collective-permute-start.22
  56.3 0.7 collective-permute-start.23
  56.9 0.2 collective-permute-done.22.pair_in
  57.2 2.8 %heads.1 = (f32[144,256]{1,0:T(8,128)S(1)}, bf16[2,8,128,256]{3,2,1,0:T(8,128)(2,1)S(1)}, bf16[2,4,64,256]{3,2,1,0:T(8,128)(2,1)S(1)}, bf16[2,192,256]{2,1,0:T(8...) custom-call(bf16[2,14,128,256]{3,2,1,0:T(8,128)(2,1)S(1)} %get-tuple-element.112.levels, ...), custom_call_target="tpu_custom_call" | custom-call | flops 792723456 | bytes 4841480 | tf_op jit(solution)/shard_map/heads/pallas_call | solution.py:118
  59.9 4.4 %conv_grads.1 = (bf16[4,288,512]{2,1,0:T(8,128)(2,1)S(1)}, bf16[4,288,512]{2,1,0:T(8,128)(2,1)S(1)}) custom-call(bf16[2,8,128,256]{3,2,1,0:T(8,128)(2,1)S(1)} %get-tuple-element.98.input_four, bf16[2,4,64,256]{3,2,1,0:T(8,128)(2,1)S(1)} %get-tuple-element.99.input_five, bf16[2,208,256]{2,1,0:T(8,128)(2,1)S(1)} %collective-permute-done.16.pair_in.pair_mask, ...), custom_call_target="tpu_custom_call" | custom-call | flops 3019898880 | bytes 5406720 | tf_op jit(solution)/shard_map/conv_grads/pallas_call | solution.py:118
  64.3 5.1 %collective-permute-start.26 = (bf16[4,288,512]{2,1,0:T(8,128)(2,1)S(1)}, bf16[4,288,512]{2,1,0:T(8,128)(2,1)S(1)}, u32[]{:S(2)}, u32[]{:S(2)}) collective-permute-start(bf16[4,288,512]{2,1,0:T(8,128)(2,1)S(1)} %get-tuple-element.122), channel_id=1, source_target_pairs={{0,4},{4,0},{8,12},{12,8},{16,20},{20,16},{24,28},{28,24},{1,5},{5... | collective-permute-start | bytes 3538952 | tf_op jit(solution)/shard_map/ppermute | solution.py:45
  69.5 0.7 collective-permute-start.25
  70.2 1.7 %collective-permute-done.26 = bf16[4,288,512]{2,1,0:T(8,128)(2,1)S(1)} collective-permute-done((bf16[4,288,512]{2,1,0:T(8,128)(2,1)S(1)}, bf16[4,288,512]{2,1,0:T(8,128)(2,1)S(1)}, u32[]{:S(2)}, u32[]{:S(2)}) %collective-permute-start.26) | collective-permute-done | bytes 1179680 | tf_op jit(solution)/shard_map/ppermute | solution.py:45
  71.9 0.3 fusion.16
  72.3 2.7 %collective-permute-start.30 = (bf16[288,512]{1,0:T(8,128)(2,1)S(1)}, bf16[288,512]{1,0:T(8,128)(2,1)S(1)}, u32[]{:S(2)}, u32[]{:S(2)}) collective-permute-start(bf16[288,512]{1,0:T(8,128)(2,1)S(1)} %get-tuple-element.156), channel_id=1, source_target_pairs={{0,24},{4,28},{8,16},{12,20},{16,8},{20,12},{24,0},{28,4},{1,25},{... | collective-permute-start | bytes 884744 | tf_op jit(solution)/shard_map/ppermute | solution.py:45
  75.0 1.8 %collective-permute-start.28 = (bf16[288,512]{1,0:T(8,128)(2,1)S(1)}, bf16[288,512]{1,0:T(8,128)(2,1)S(1)}, u32[]{:S(2)}, u32[]{:S(2)}) collective-permute-start(bf16[288,512]{1,0:T(8,128)(2,1)S(1)} %get-tuple-element.157), channel_id=1, source_target_pairs={{0,8},{4,12},{8,0},{12,4},{16,24},{20,28},{24,16},{28,20},{1,9},{5... | collective-permute-start | bytes 884744 | tf_op jit(solution)/shard_map/ppermute | solution.py:45
  76.8 3.5 %merged_grads.1 = (bf16[2048,256]{1,0:T(8,128)(2,1)S(1)}, bf16[512,256]{1,0:T(8,128)(2,1)S(1)}) custom-call(bf16[2,8,128,256]{3,2,1,0:T(8,128)(2,1)S(1)} %get-tuple-element.117.grad_four, bf16[2,4,64,256]{3,2,1,0:T(8,128)(2,1)S(1)} %get-tuple-element.118.grad_five, bf16[2,192,256]{2,1,0:T(8,128)(2,1)S(1)} %collective-permute-done.24.pair_in, ...), custom_call_target="tpu_custom_call" | custom-call | flops 3019898880 | bytes 5373952 | tf_op jit(solution)/shard_map/merged_grads/pallas_call | solution.py:118
  80.4 2.9 %lateral_grads.1 = (bf16[4,416,256]{2,1,0:T(8,128)(2,1)S(1)}, bf16[4,416,256]{2,1,0:T(8,128)(2,1)S(1)}) custom-call(bf16[2,8,128,1024]{3,2,1,0:T(8,128)(2,1)S(1)} %copy-done.1, bf16[2,4,64,2048]{3,2,1,0:T(8,128)(2,1)S(1)} %copy-done.3, bf16[2048,256]{1,0:T(8,128)(2,1)S(1)} %get-tuple-element.127.lat_four, bf16[512,256]{1,0:T(8,128)(2,1)S(1)} %get-tuple-element.128.lat_five, ...), custom_call_target="tpu_custom_call" | custom-call | flops 1 | bytes 9453572 | tf_op jit(solution)/shard_map/lateral_grads/pallas_call | solution.py:118
  83.3 1.5 %collective-permute-start.27 = (bf16[4,416,256]{2,1,0:T(8,128)(2,1)S(1)}, bf16[4,416,256]{2,1,0:T(8,128)(2,1)S(1)}, u32[]{:S(2)}, u32[]{:S(2)}) collective-permute-start(bf16[4,416,256]{2,1,0:T(8,128)(2,1)S(1)} %get-tuple-element.132), channel_id=1, source_target_pairs={{0,4},{4,0},{8,12},{12,8},{16,20},{20,16},{24,28},{28,24},{1,5},{5... | collective-permute-start | bytes 2555912 | tf_op jit(solution)/shard_map/ppermute | solution.py:45
  84.7 0.6 collective-permute-done.30.refs_2_
  85.3 5.8 %collective-permute-done.28.refs_0_ = bf16[288,512]{1,0:T(8,128)(2,1)S(1)} collective-permute-done((bf16[288,512]{1,0:T(8,128)(2,1)S(1)}, bf16[288,512]{1,0:T(8,128)(2,1)S(1)}, u32[]{:S(2)}, u32[]{:S(2)}) %collective-permute-start.28) | collective-permute-done | bytes 294944 | tf_op jit(solution)/shard_map/ppermute | solution.py:45
  91.5 1.7 %collective-permute-start.34 = (bf16[416,256]{1,0:T(8,128)(2,1)S(1)}, bf16[416,256]{1,0:T(8,128)(2,1)S(1)}, u32[]{:S(2)}, u32[]{:S(2)}) collective-permute-start(bf16[416,256]{1,0:T(8,128)(2,1)S(1)} %get-tuple-element.135), channel_id=1, source_target_pairs={{0,8},{4,12},{8,0},{12,4},{16,24},{20,28},{24,16},{28,20},{1,9},{5... | collective-permute-start | bytes 638984 | tf_op jit(solution)/shard_map/ppermute | solution.py:45
  93.1 0.6 collective-permute-start.35
  93.7 1.3 %collective-permute-start.36 = (bf16[416,256]{1,0:T(8,128)(2,1)S(1)}, bf16[416,256]{1,0:T(8,128)(2,1)S(1)}, u32[]{:S(2)}, u32[]{:S(2)}) collective-permute-start(bf16[416,256]{1,0:T(8,128)(2,1)S(1)} %get-tuple-element.137), channel_id=1, source_target_pairs={{0,24},{4,28},{8,16},{12,20},{16,8},{20,12},{24,0},{28,4},{1,25},{... | collective-permute-start | bytes 638984 | tf_op jit(solution)/shard_map/ppermute | solution.py:45
  95.1 1.9 %collective-permute-start.33 = (bf16[72,512]{1,0:T(8,128)(2,1)S(1)}, bf16[72,512]{1,0:T(8,128)(2,1)S(1)}, u32[]{:S(2)}, u32[]{:S(2)}) collective-permute-start(bf16[72,512]{1,0:T(8,128)(2,1)S(1)} %get-tuple-element.163), channel_id=1, source_target_pairs={{0,3},{1,2},{2,1},{3,0},{4,7},{5,6},{6,5},{7,4},{8,11},{9,10},{10,... | collective-permute-start | bytes 221192 | tf_op jit(solution)/shard_map/ppermute | solution.py:45
  97.0 2.7 %collective-permute-done.34 = bf16[416,256]{1,0:T(8,128)(2,1)S(1)} collective-permute-done((bf16[416,256]{1,0:T(8,128)(2,1)S(1)}, bf16[416,256]{1,0:T(8,128)(2,1)S(1)}, u32[]{:S(2)}, u32[]{:S(2)}) %collective-permute-start.34) | collective-permute-done | bytes 213024 | tf_op jit(solution)/shard_map/ppermute | solution.py:45
  99.7 1.5 %collective-permute-done.35 = bf16[416,256]{1,0:T(8,128)(2,1)S(1)} collective-permute-done((bf16[416,256]{1,0:T(8,128)(2,1)S(1)}, bf16[416,256]{1,0:T(8,128)(2,1)S(1)}, u32[]{:S(2)}, u32[]{:S(2)}) %collective-permute-start.35) | collective-permute-done | bytes 213024 | tf_op jit(solution)/shard_map/ppermute | solution.py:45
  101.2 3.4 %collective-permute-done.36 = bf16[416,256]{1,0:T(8,128)(2,1)S(1)} collective-permute-done((bf16[416,256]{1,0:T(8,128)(2,1)S(1)}, bf16[416,256]{1,0:T(8,128)(2,1)S(1)}, u32[]{:S(2)}, u32[]{:S(2)}) %collective-permute-start.36) | collective-permute-done | bytes 213024 | tf_op jit(solution)/shard_map/ppermute | solution.py:45
  105.1 1.9 %collective-permute-start.39 = (bf16[104,256]{1,0:T(8,128)(2,1)S(1)}, bf16[104,256]{1,0:T(8,128)(2,1)S(1)}, u32[]{:S(2)}, u32[]{:S(2)}) collective-permute-start(bf16[104,256]{1,0:T(8,128)(2,1)S(1)} %get-tuple-element.166), channel_id=1, source_target_pairs={{0,3},{1,2},{2,1},{3,0},{4,7},{5,6},{6,5},{7,4},{8,11},{9,10},{10,... | collective-permute-start | bytes 159752 | tf_op jit(solution)/shard_map/ppermute | solution.py:45
  107.0 2.6 %collective-permute-start.37 = (bf16[104,256]{1,0:T(8,128)(2,1)S(1)}, bf16[104,256]{1,0:T(8,128)(2,1)S(1)}, u32[]{:S(2)}, u32[]{:S(2)}) collective-permute-start(bf16[104,256]{1,0:T(8,128)(2,1)S(1)} %get-tuple-element.168), channel_id=1, source_target_pairs={{0,1},{1,0},{2,3},{3,2},{4,5},{5,4},{6,7},{7,6},{8,9},{9,8},{10,11... | collective-permute-start | bytes 159752 | tf_op jit(solution)/shard_map/ppermute | solution.py:45
  109.6 0.8 conv_step.1
  110.4 1.1 collective-permute-done.39.refs_2_
  111.6 1.1 collective-permute-done.38.refs_1_
  112.7 0.8 lateral_step.1
  (103 shorter events, 1.4 us)
Async XLA Ops:
  0.6 21.2 %copy-start.19 = (s32[2,2,32,3]{2,1,3,0:T(2,128)S(1)}, s32[2,2,32,3]{2,1,3,0:T(2,128)}, u32[]{:S(2)}) copy-start(s32[2,2,32,3]{2,1,3,0:T(2,128)} %param.27) | copy-start | bytes 4612
  0.7 21.2 %copy-start.14 = (s32[2,4,64,3]{2,1,3,0:T(4,128)S(1)}, s32[2,4,64,3]{2,1,3,0:T(4,128)}, u32[]{:S(2)}) copy-start(s32[2,4,64,3]{2,1,3,0:T(4,128)} %param.26) | copy-start | bytes 18436
  0.7 21.2 %copy-start.9 = (s32[2,8,128,3]{2,1,3,0:T(8,128)S(1)}, s32[2,8,128,3]{2,1,3,0:T(8,128)}, u32[]{:S(2)}) copy-start(s32[2,8,128,3]{2,1,3,0:T(8,128)} %param.25) | copy-start | bytes 73732
  0.7 21.2 %copy-start.18 = (f32[2,2,32,12]{2,1,3,0:T(2,128)S(1)}, f32[2,2,32,12]{2,1,3,0:T(2,128)}, u32[]{:S(2)}) copy-start(f32[2,2,32,12]{2,1,3,0:T(2,128)} %param.24) | copy-start | bytes 18436
  0.7 21.2 %copy-start.13 = (f32[2,4,64,12]{2,1,3,0:T(4,128)S(1)}, f32[2,4,64,12]{2,1,3,0:T(4,128)}, u32[]{:S(2)}) copy-start(f32[2,4,64,12]{2,1,3,0:T(4,128)} %param.23) | copy-start | bytes 73732
  0.7 21.2 %copy-start.10 = (f32[2,8,128,12]{2,1,3,0:T(8,128)S(1)}, f32[2,8,128,12]{2,1,3,0:T(8,128)}, u32[]{:S(2)}) copy-start(f32[2,8,128,12]{2,1,3,0:T(8,128)} %param.22) | copy-start | bytes 294916
  2.4 7.7 %collective-permute-start.2 = (bf16[104,256]{1,0:T(8,128)(2,1)}, bf16[104,256]{1,0:T(8,128)(2,1)S(1)}, u32[]{:S(2)}, u32[]{:S(2)}) collective-permute-start(bf16[104,256]{1,0:T(8,128)(2,1)} %pack.1), channel_id=1, source_target_pairs={{0,3},{1,2},{2,1},{3,0},{4,7},{5,6},{6,5},{7,4},{8,11},{9,10},{10,... | collective-permute-start | bytes 159752 | tf_op jit(solution)/shard_map/ppermute | solution.py:45
  7.6 5.2 %collective-permute-start.1 = (bf16[104,256]{1,0:T(8,128)(2,1)}, bf16[104,256]{1,0:T(8,128)(2,1)S(1)}, u32[]{:S(2)}, u32[]{:S(2)}) collective-permute-start(bf16[104,256]{1,0:T(8,128)(2,1)} %pack.1), channel_id=1, source_target_pairs={{0,2},{1,3},{2,0},{3,1},{4,6},{5,7},{6,4},{7,5},{8,10},{9,11},{10,... | collective-permute-start | bytes 159752 | tf_op jit(solution)/shard_map/ppermute | solution.py:45
  7.6 5.2 %collective-permute-start = (bf16[104,256]{1,0:T(8,128)(2,1)}, bf16[104,256]{1,0:T(8,128)(2,1)S(1)}, u32[]{:S(2)}, u32[]{:S(2)}) collective-permute-start(bf16[104,256]{1,0:T(8,128)(2,1)} %pack.1), channel_id=1, source_target_pairs={{0,1},{1,0},{2,3},{3,2},{4,5},{5,4},{6,7},{7,6},{8,9},{9,8},{10,11... | collective-permute-start | bytes 159752 | tf_op jit(solution)/shard_map/ppermute | solution.py:45
  13.9 6.4 %collective-permute-start.12 = (bf16[72,512]{1,0:T(8,128)(2,1)S(1)}, bf16[72,512]{1,0:T(8,128)(2,1)S(1)}, u32[]{:S(2)}, u32[]{:S(2)}) collective-permute-start(bf16[72,512]{1,0:T(8,128)(2,1)S(1)} %pad_maximum_fusion.4), channel_id=1, source_target_pairs={{0,3},{1,2},{2,1},{3,0},{4,7},{5,6},{6,5},{7,4},{8,11},{9,10},{10,... | collective-permute-start | bytes 221192 | tf_op jit(solution)/shard_map/ppermute | solution.py:45
  16.3 9.6 %collective-permute-start.5 = (bf16[416,256]{1,0:T(8,128)(2,1)S(1)}, bf16[416,256]{1,0:T(8,128)(2,1)S(1)}, u32[]{:S(2)}, u32[]{:S(2)}) collective-permute-start(bf16[416,256]{1,0:T(8,128)(2,1)S(1)} %constant_dynamic-update-slice_fusion.refs_0_), channel_id=1, source_target_pairs={{0,24},{4,28},{8,16},{12,20},{16,8},{20,12},{24,0},{28,4},{1,25},{... | collective-permute-start | bytes 638984 | tf_op jit(solution)/shard_map/ppermute | solution.py:45
  18.8 8.5 %collective-permute-start.4 = (bf16[416,256]{1,0:T(8,128)(2,1)S(1)}, bf16[416,256]{1,0:T(8,128)(2,1)S(1)}, u32[]{:S(2)}, u32[]{:S(2)}) collective-permute-start(bf16[416,256]{1,0:T(8,128)(2,1)S(1)} %constant_dynamic-update-slice_fusion.refs_0_), channel_id=1, source_target_pairs={{0,16},{4,20},{8,24},{12,28},{16,0},{20,4},{24,8},{28,12},{1,17},{... | collective-permute-start | bytes 638984 | tf_op jit(solution)/shard_map/ppermute | solution.py:45
  19.3 8.1 %collective-permute-start.3 = (bf16[416,256]{1,0:T(8,128)(2,1)S(1)}, bf16[416,256]{1,0:T(8,128)(2,1)S(1)}, u32[]{:S(2)}, u32[]{:S(2)}) collective-permute-start(bf16[416,256]{1,0:T(8,128)(2,1)S(1)} %constant_dynamic-update-slice_fusion.refs_0_), channel_id=1, source_target_pairs={{0,8},{4,12},{8,0},{12,4},{16,24},{20,28},{24,16},{28,20},{1,9},{5... | collective-permute-start | bytes 638984 | tf_op jit(solution)/shard_map/ppermute | solution.py:45
  19.8 6.0 %collective-permute-start.11 = (bf16[72,512]{1,0:T(8,128)(2,1)S(1)}, bf16[72,512]{1,0:T(8,128)(2,1)S(1)}, u32[]{:S(2)}, u32[]{:S(2)}) collective-permute-start(bf16[72,512]{1,0:T(8,128)(2,1)S(1)} %pad_maximum_fusion.4), channel_id=1, source_target_pairs={{0,2},{1,3},{2,0},{3,1},{4,6},{5,7},{6,4},{7,5},{8,10},{9,11},{10,... | collective-permute-start | bytes 221192 | tf_op jit(solution)/shard_map/ppermute | solution.py:45
  20.3 5.6 %collective-permute-start.10 = (bf16[72,512]{1,0:T(8,128)(2,1)S(1)}, bf16[72,512]{1,0:T(8,128)(2,1)S(1)}, u32[]{:S(2)}, u32[]{:S(2)}) collective-permute-start(bf16[72,512]{1,0:T(8,128)(2,1)S(1)} %pad_maximum_fusion.4), channel_id=1, source_target_pairs={{0,1},{1,0},{2,3},{3,2},{4,5},{5,4},{6,7},{7,6},{8,9},{9,8},{10,11... | collective-permute-start | bytes 221192 | tf_op jit(solution)/shard_map/ppermute | solution.py:45
  21.9 2.2 %copy-start = (bf16[2,8,128,1024]{3,2,1,0:T(8,128)(2,1)S(1)}, bf16[2,8,128,1024]{3,2,1,0:T(8,128)(2,1)}, u32[]{:S(2)}) copy-start(bf16[2,8,128,1024]{3,2,1,0:T(8,128)(2,1)} %four.3) | copy-start | bytes 12582916
  24.1 1.6 %copy-start.2 = (bf16[2,4,64,2048]{3,2,1,0:T(8,128)(2,1)S(1)}, bf16[2,4,64,2048]{3,2,1,0:T(8,128)(2,1)}, u32[]{:S(2)}) copy-start(bf16[2,4,64,2048]{3,2,1,0:T(8,128)(2,1)} %five.3) | copy-start | bytes 6291460
  25.7 6.4 %copy-start.1 = (bf16[2,8,128,1024]{3,2,1,0:T(8,128)(2,1)S(1)}, bf16[2,8,128,1024]{3,2,1,0:T(8,128)(2,1)}, u32[]{:S(2)}) copy-start(bf16[2,8,128,1024]{3,2,1,0:T(8,128)(2,1)} %four.3) | copy-start | bytes 12582916
  27.4 2.8 %collective-permute-start.6 = (bf16[416,256]{1,0:T(8,128)(2,1)S(1)}, bf16[416,256]{1,0:T(8,128)(2,1)S(1)}, u32[]{:S(2)}, u32[]{:S(2)}) collective-permute-start(bf16[416,256]{1,0:T(8,128)(2,1)S(1)} %constant_dynamic-update-slice_fusion.refs_0_), channel_id=1, source_target_pairs={{0,4},{4,0},{8,12},{12,8},{16,20},{20,16},{24,28},{28,24},{1,5},{5... | collective-permute-start | bytes 638984 | tf_op jit(solution)/shard_map/ppermute | solution.py:45
  27.4 4.1 %collective-permute-start.7 = (bf16[416,256]{1,0:T(8,128)(2,1)S(1)}, bf16[416,256]{1,0:T(8,128)(2,1)S(1)}, u32[]{:S(2)}, u32[]{:S(2)}) collective-permute-start(bf16[416,256]{1,0:T(8,128)(2,1)S(1)} %collective-permute-done.3.refs_2_), channel_id=1, source_target_pairs={{0,4},{4,0},{8,12},{12,8},{16,20},{20,16},{24,28},{28,24},{1,5},{5... | collective-permute-start | bytes 638984 | tf_op jit(solution)/shard_map/ppermute | solution.py:45
  27.9 4.1 %collective-permute-start.8 = (bf16[416,256]{1,0:T(8,128)(2,1)S(1)}, bf16[416,256]{1,0:T(8,128)(2,1)S(1)}, u32[]{:S(2)}, u32[]{:S(2)}) collective-permute-start(bf16[416,256]{1,0:T(8,128)(2,1)S(1)} %collective-permute-done.4.refs_4_), channel_id=1, source_target_pairs={{0,4},{4,0},{8,12},{12,8},{16,20},{20,16},{24,28},{28,24},{1,5},{5... | collective-permute-start | bytes 638984 | tf_op jit(solution)/shard_map/ppermute | solution.py:45
  27.9 4.1 %collective-permute-start.9 = (bf16[416,256]{1,0:T(8,128)(2,1)S(1)}, bf16[416,256]{1,0:T(8,128)(2,1)S(1)}, u32[]{:S(2)}, u32[]{:S(2)}) collective-permute-start(bf16[416,256]{1,0:T(8,128)(2,1)S(1)} %collective-permute-done.5.refs_6_), channel_id=1, source_target_pairs={{0,4},{4,0},{8,12},{12,8},{16,20},{20,16},{24,28},{28,24},{1,5},{5... | collective-permute-start | bytes 638984 | tf_op jit(solution)/shard_map/ppermute | solution.py:45
  28.5 10.9 %collective-permute-start.15 = (bf16[288,512]{1,0:T(8,128)(2,1)S(1)}, bf16[288,512]{1,0:T(8,128)(2,1)S(1)}, u32[]{:S(2)}, u32[]{:S(2)}) collective-permute-start(bf16[288,512]{1,0:T(8,128)(2,1)S(1)} %pad_maximum_fusion.2.refs_0_), channel_id=1, source_target_pairs={{0,24},{4,28},{8,16},{12,20},{16,8},{20,12},{24,0},{28,4},{1,25},{... | collective-permute-start | bytes 884744 | tf_op jit(solution)/shard_map/ppermute | solution.py:45
  30.2 14.5 %collective-permute-start.14 = (bf16[288,512]{1,0:T(8,128)(2,1)S(1)}, bf16[288,512]{1,0:T(8,128)(2,1)S(1)}, u32[]{:S(2)}, u32[]{:S(2)}) collective-permute-start(bf16[288,512]{1,0:T(8,128)(2,1)S(1)} %pad_maximum_fusion.2.refs_0_), channel_id=1, source_target_pairs={{0,16},{4,20},{8,24},{12,28},{16,0},{20,4},{24,8},{28,12},{1,17},{... | collective-permute-start | bytes 884744 | tf_op jit(solution)/shard_map/ppermute | solution.py:45
  31.5 14.1 %collective-permute-start.13 = (bf16[288,512]{1,0:T(8,128)(2,1)S(1)}, bf16[288,512]{1,0:T(8,128)(2,1)S(1)}, u32[]{:S(2)}, u32[]{:S(2)}) collective-permute-start(bf16[288,512]{1,0:T(8,128)(2,1)S(1)} %pad_maximum_fusion.2.refs_0_), channel_id=1, source_target_pairs={{0,8},{4,12},{8,0},{12,4},{16,24},{20,28},{24,16},{28,20},{1,9},{5... | collective-permute-start | bytes 884744 | tf_op jit(solution)/shard_map/ppermute | solution.py:45
  34.0 11.6 %collective-permute-start.16 = (bf16[2,208,256]{2,1,0:T(8,128)(2,1)S(1)}, bf16[2,208,256]{2,1,0:T(8,128)(2,1)S(1)}, u32[]{:S(2)}, u32[]{:S(2)}) collective-permute-start(bf16[2,208,256]{2,1,0:T(8,128)(2,1)S(1)} %get-tuple-element.101), channel_id=1, source_target_pairs={{0,4},{4,0},{8,12},{12,8},{16,20},{20,16},{24,28},{28,24},{1,5},{5... | collective-permute-start | bytes 638984 | tf_op jit(solution)/shard_map/ppermute | solution.py:45
  34.1 11.5 %collective-permute-start.17 = (bf16[2,208,256]{2,1,0:T(8,128)(2,1)S(1)}, bf16[2,208,256]{2,1,0:T(8,128)(2,1)S(1)}, u32[]{:S(2)}, u32[]{:S(2)}) collective-permute-start(bf16[2,208,256]{2,1,0:T(8,128)(2,1)S(1)} %get-tuple-element.102), channel_id=1, source_target_pairs={{4,8},{12,16},{20,24},{8,4},{16,12},{24,20},{5,9},{13,17},{21,25},... | collective-permute-start | bytes 638984 | tf_op jit(solution)/shard_map/ppermute | solution.py:106
  45.6 4.6 %collective-permute-start.18 = (bf16[288,512]{1,0:T(8,128)(2,1)S(1)}, bf16[288,512]{1,0:T(8,128)(2,1)S(1)}, u32[]{:S(2)}, u32[]{:S(2)}) collective-permute-start(bf16[288,512]{1,0:T(8,128)(2,1)S(1)} %pad_maximum_fusion.2.refs_0_), channel_id=1, source_target_pairs={{0,4},{4,0},{8,12},{12,8},{16,20},{20,16},{24,28},{28,24},{1,5},{5... | collective-permute-start | bytes 884744 | tf_op jit(solution)/shard_map/ppermute | solution.py:45
  49.0 1.6 %collective-permute-start.19 = (bf16[288,512]{1,0:T(8,128)(2,1)S(1)}, bf16[288,512]{1,0:T(8,128)(2,1)S(1)}, u32[]{:S(2)}, u32[]{:S(2)}) collective-permute-start(bf16[288,512]{1,0:T(8,128)(2,1)S(1)} %collective-permute-done.13.refs_2_), channel_id=1, source_target_pairs={{0,4},{4,0},{8,12},{12,8},{16,20},{20,16},{24,28},{28,24},{1,5},{5... | collective-permute-start | bytes 884744 | tf_op jit(solution)/shard_map/ppermute | solution.py:45
  49.1 2.0 %collective-permute-start.20 = (bf16[288,512]{1,0:T(8,128)(2,1)S(1)}, bf16[288,512]{1,0:T(8,128)(2,1)S(1)}, u32[]{:S(2)}, u32[]{:S(2)}) collective-permute-start(bf16[288,512]{1,0:T(8,128)(2,1)S(1)} %collective-permute-done.14.refs_4_), channel_id=1, source_target_pairs={{0,4},{4,0},{8,12},{12,8},{16,20},{20,16},{24,28},{28,24},{1,5},{5... | collective-permute-start | bytes 884744 | tf_op jit(solution)/shard_map/ppermute | solution.py:45
  49.6 2.0 %collective-permute-start.21 = (bf16[288,512]{1,0:T(8,128)(2,1)S(1)}, bf16[288,512]{1,0:T(8,128)(2,1)S(1)}, u32[]{:S(2)}, u32[]{:S(2)}) collective-permute-start(bf16[288,512]{1,0:T(8,128)(2,1)S(1)} %collective-permute-done.15.refs_6_), channel_id=1, source_target_pairs={{0,4},{4,0},{8,12},{12,8},{16,20},{20,16},{24,28},{28,24},{1,5},{5... | collective-permute-start | bytes 884744 | tf_op jit(solution)/shard_map/ppermute | solution.py:45
  55.9 1.3 %collective-permute-start.22 = (f32[2,24,256]{2,1,0:T(8,128)S(1)}, f32[2,24,256]{2,1,0:T(8,128)S(1)}, u32[]{:S(2)}, u32[]{:S(2)}) collective-permute-start(f32[2,24,256]{2,1,0:T(8,128)S(1)} %get-tuple-element.113), channel_id=1, source_target_pairs={{0,4},{4,0},{8,12},{12,8},{16,20},{20,16},{24,28},{28,24},{1,5},{5... | collective-permute-start | bytes 147464 | tf_op jit(solution)/shard_map/ppermute | solution.py:45
  56.3 0.9 collective-permute-start.23
  64.3 7.6 %collective-permute-start.26 = (bf16[4,288,512]{2,1,0:T(8,128)(2,1)S(1)}, bf16[4,288,512]{2,1,0:T(8,128)(2,1)S(1)}, u32[]{:S(2)}, u32[]{:S(2)}) collective-permute-start(bf16[4,288,512]{2,1,0:T(8,128)(2,1)S(1)} %get-tuple-element.122), channel_id=1, source_target_pairs={{0,4},{4,0},{8,12},{12,8},{16,20},{20,16},{24,28},{28,24},{1,5},{5... | collective-permute-start | bytes 3538952 | tf_op jit(solution)/shard_map/ppermute | solution.py:45
  69.5 7.3 %collective-permute-start.24 = (bf16[2,192,256]{2,1,0:T(8,128)(2,1)S(1)}, bf16[2,192,256]{2,1,0:T(8,128)(2,1)S(1)}, u32[]{:S(2)}, u32[]{:S(2)}) collective-permute-start(bf16[2,192,256]{2,1,0:T(8,128)(2,1)S(1)} %get-tuple-element.119), channel_id=1, source_target_pairs={{0,4},{4,0},{8,12},{12,8},{16,20},{20,16},{24,28},{28,24},{1,5},{5... | collective-permute-start | bytes 589832 | tf_op jit(solution)/shard_map/ppermute | solution.py:45
  69.5 7.3 %collective-permute-start.25 = (bf16[2,192,256]{2,1,0:T(8,128)(2,1)S(1)}, bf16[2,192,256]{2,1,0:T(8,128)(2,1)S(1)}, u32[]{:S(2)}, u32[]{:S(2)}) collective-permute-start(bf16[2,192,256]{2,1,0:T(8,128)(2,1)S(1)} %get-tuple-element.120), channel_id=1, source_target_pairs={{4,8},{12,16},{20,24},{8,4},{16,12},{24,20},{5,9},{13,17},{21,25},... | collective-permute-start | bytes 589832 | tf_op jit(solution)/shard_map/ppermute | solution.py:106
  72.3 13.1 %collective-permute-start.30 = (bf16[288,512]{1,0:T(8,128)(2,1)S(1)}, bf16[288,512]{1,0:T(8,128)(2,1)S(1)}, u32[]{:S(2)}, u32[]{:S(2)}) collective-permute-start(bf16[288,512]{1,0:T(8,128)(2,1)S(1)} %get-tuple-element.156), channel_id=1, source_target_pairs={{0,24},{4,28},{8,16},{12,20},{16,8},{20,12},{24,0},{28,4},{1,25},{... | collective-permute-start | bytes 884744 | tf_op jit(solution)/shard_map/ppermute | solution.py:45
  75.0 16.1 %collective-permute-start.28 = (bf16[288,512]{1,0:T(8,128)(2,1)S(1)}, bf16[288,512]{1,0:T(8,128)(2,1)S(1)}, u32[]{:S(2)}, u32[]{:S(2)}) collective-permute-start(bf16[288,512]{1,0:T(8,128)(2,1)S(1)} %get-tuple-element.157), channel_id=1, source_target_pairs={{0,8},{4,12},{8,0},{12,4},{16,24},{20,28},{24,16},{28,20},{1,9},{5... | collective-permute-start | bytes 884744 | tf_op jit(solution)/shard_map/ppermute | solution.py:45
  76.8 14.3 %collective-permute-start.29 = (bf16[288,512]{1,0:T(8,128)(2,1)S(1)}, bf16[288,512]{1,0:T(8,128)(2,1)S(1)}, u32[]{:S(2)}, u32[]{:S(2)}) collective-permute-start(bf16[288,512]{1,0:T(8,128)(2,1)S(1)} %get-tuple-element.158), channel_id=1, source_target_pairs={{0,16},{4,20},{8,24},{12,28},{16,0},{20,4},{24,8},{28,12},{1,17},{... | collective-permute-start | bytes 884744 | tf_op jit(solution)/shard_map/ppermute | solution.py:45
  76.8 3.6 %copy-start.3 = (bf16[2,4,64,2048]{3,2,1,0:T(8,128)(2,1)S(1)}, bf16[2,4,64,2048]{3,2,1,0:T(8,128)(2,1)}, u32[]{:S(2)}) copy-start(bf16[2,4,64,2048]{3,2,1,0:T(8,128)(2,1)} %five.3) | copy-start | bytes 6291460
  83.3 8.0 %collective-permute-start.27 = (bf16[4,416,256]{2,1,0:T(8,128)(2,1)S(1)}, bf16[4,416,256]{2,1,0:T(8,128)(2,1)S(1)}, u32[]{:S(2)}, u32[]{:S(2)}) collective-permute-start(bf16[4,416,256]{2,1,0:T(8,128)(2,1)S(1)} %get-tuple-element.132), channel_id=1, source_target_pairs={{0,4},{4,0},{8,12},{12,8},{16,20},{20,16},{24,28},{28,24},{1,5},{5... | collective-permute-start | bytes 2555912 | tf_op jit(solution)/shard_map/ppermute | solution.py:45
  91.5 8.2 %collective-permute-start.34 = (bf16[416,256]{1,0:T(8,128)(2,1)S(1)}, bf16[416,256]{1,0:T(8,128)(2,1)S(1)}, u32[]{:S(2)}, u32[]{:S(2)}) collective-permute-start(bf16[416,256]{1,0:T(8,128)(2,1)S(1)} %get-tuple-element.135), channel_id=1, source_target_pairs={{0,8},{4,12},{8,0},{12,4},{16,24},{20,28},{24,16},{28,20},{1,9},{5... | collective-permute-start | bytes 638984 | tf_op jit(solution)/shard_map/ppermute | solution.py:45
  93.1 8.1 %collective-permute-start.35 = (bf16[416,256]{1,0:T(8,128)(2,1)S(1)}, bf16[416,256]{1,0:T(8,128)(2,1)S(1)}, u32[]{:S(2)}, u32[]{:S(2)}) collective-permute-start(bf16[416,256]{1,0:T(8,128)(2,1)S(1)} %get-tuple-element.136), channel_id=1, source_target_pairs={{0,16},{4,20},{8,24},{12,28},{16,0},{20,4},{24,8},{28,12},{1,17},{... | collective-permute-start | bytes 638984 | tf_op jit(solution)/shard_map/ppermute | solution.py:45
  93.7 10.8 %collective-permute-start.36 = (bf16[416,256]{1,0:T(8,128)(2,1)S(1)}, bf16[416,256]{1,0:T(8,128)(2,1)S(1)}, u32[]{:S(2)}, u32[]{:S(2)}) collective-permute-start(bf16[416,256]{1,0:T(8,128)(2,1)S(1)} %get-tuple-element.137), channel_id=1, source_target_pairs={{0,24},{4,28},{8,16},{12,20},{16,8},{20,12},{24,0},{28,4},{1,25},{... | collective-permute-start | bytes 638984 | tf_op jit(solution)/shard_map/ppermute | solution.py:45
  95.1 9.7 %collective-permute-start.33 = (bf16[72,512]{1,0:T(8,128)(2,1)S(1)}, bf16[72,512]{1,0:T(8,128)(2,1)S(1)}, u32[]{:S(2)}, u32[]{:S(2)}) collective-permute-start(bf16[72,512]{1,0:T(8,128)(2,1)S(1)} %get-tuple-element.163), channel_id=1, source_target_pairs={{0,3},{1,2},{2,1},{3,0},{4,7},{5,6},{6,5},{7,4},{8,11},{9,10},{10,... | collective-permute-start | bytes 221192 | tf_op jit(solution)/shard_map/ppermute | solution.py:45
  97.0 7.8 %collective-permute-start.32 = (bf16[72,512]{1,0:T(8,128)(2,1)S(1)}, bf16[72,512]{1,0:T(8,128)(2,1)S(1)}, u32[]{:S(2)}, u32[]{:S(2)}) collective-permute-start(bf16[72,512]{1,0:T(8,128)(2,1)S(1)} %get-tuple-element.164), channel_id=1, source_target_pairs={{0,2},{1,3},{2,0},{3,1},{4,6},{5,7},{6,4},{7,5},{8,10},{9,11},{10,... | collective-permute-start | bytes 221192 | tf_op jit(solution)/shard_map/ppermute | solution.py:45
  99.7 5.2 %collective-permute-start.31 = (bf16[72,512]{1,0:T(8,128)(2,1)S(1)}, bf16[72,512]{1,0:T(8,128)(2,1)S(1)}, u32[]{:S(2)}, u32[]{:S(2)}) collective-permute-start(bf16[72,512]{1,0:T(8,128)(2,1)S(1)} %get-tuple-element.165), channel_id=1, source_target_pairs={{0,1},{1,0},{2,3},{3,2},{4,5},{5,4},{6,7},{7,6},{8,9},{9,8},{10,11... | collective-permute-start | bytes 221192 | tf_op jit(solution)/shard_map/ppermute | solution.py:45
  104.7 4.8 %copy-start.4 = (f32[2,72,256]{2,1,0:T(8,128)S(1)}, f32[2,72,256]{2,1,0:T(8,128)}, u32[]{:S(2)}) copy-start(f32[2,72,256]{2,1,0:T(8,128)} %refs_3_.3) | copy-start | bytes 442372
  104.7 4.8 %copy-start.6 = (f32[2,72,256]{2,1,0:T(8,128)S(1)}, f32[2,72,256]{2,1,0:T(8,128)}, u32[]{:S(2)}) copy-start(f32[2,72,256]{2,1,0:T(8,128)} %refs_4_.3) | copy-start | bytes 442372
  104.7 4.8 %copy-start.7 = (f32[2,72,256]{2,1,0:T(8,128)S(1)}, f32[2,72,256]{2,1,0:T(8,128)}, u32[]{:S(2)}) copy-start(f32[2,72,256]{2,1,0:T(8,128)} %refs_5_.3) | copy-start | bytes 442372
  104.9 7.7 %copy-start.5 = (f32[64,256]{1,0:T(8,128)S(1)}, f32[64,256]{1,0:T(8,128)}, u32[]{:S(2)}) copy-start(f32[64,256]{1,0:T(8,128)} %refs_6_.3) | copy-start | bytes 196612
  104.9 7.7 %copy-start.8 = (f32[32,256]{1,0:T(8,128)S(1)}, f32[32,256]{1,0:T(8,128)}, u32[]{:S(2)}) copy-start(f32[32,256]{1,0:T(8,128)} %refs_3_.2) | copy-start | bytes 98308
  104.9 7.7 %copy-start.11 = (f32[64,256]{1,0:T(8,128)S(1)}, f32[64,256]{1,0:T(8,128)}, u32[]{:S(2)}) copy-start(f32[64,256]{1,0:T(8,128)} %refs_7_.3) | copy-start | bytes 196612
  104.9 7.7 %copy-start.12 = (f32[64,256]{1,0:T(8,128)S(1)}, f32[64,256]{1,0:T(8,128)}, u32[]{:S(2)}) copy-start(f32[64,256]{1,0:T(8,128)} %refs_8_.1) | copy-start | bytes 196612
  104.9 7.7 %copy-start.15 = (f32[72,12]{0,1:T(8,128)S(1)}, f32[72,12]{0,1:T(8,128)}, u32[]{:S(2)}) copy-start(f32[72,12]{0,1:T(8,128)} %param.31) | copy-start | bytes 10372
  105.0 7.7 %copy-start.16 = (f32[32,256]{1,0:T(8,128)S(1)}, f32[32,256]{1,0:T(8,128)}, u32[]{:S(2)}) copy-start(f32[32,256]{1,0:T(8,128)} %refs_4_.2) | copy-start | bytes 98308
  105.0 7.7 %copy-start.17 = (f32[32,256]{1,0:T(8,128)S(1)}, f32[32,256]{1,0:T(8,128)}, u32[]{:S(2)}) copy-start(f32[32,256]{1,0:T(8,128)} %refs_5_.2) | copy-start | bytes 98308
  105.0 7.7 %copy-start.20 = (f32[72,12]{0,1:T(8,128)S(1)}, f32[72,12]{0,1:T(8,128)}, u32[]{:S(2)}) copy-start(f32[72,12]{0,1:T(8,128)} %param.35) | copy-start | bytes 10372
  105.0 7.7 %copy-start.21 = (f32[72,12]{0,1:T(8,128)S(1)}, f32[72,12]{0,1:T(8,128)}, u32[]{:S(2)}) copy-start(f32[72,12]{0,1:T(8,128)} %param.39) | copy-start | bytes 10372
  105.1 6.5 %collective-permute-start.39 = (bf16[104,256]{1,0:T(8,128)(2,1)S(1)}, bf16[104,256]{1,0:T(8,128)(2,1)S(1)}, u32[]{:S(2)}, u32[]{:S(2)}) collective-permute-start(bf16[104,256]{1,0:T(8,128)(2,1)S(1)} %get-tuple-element.166), channel_id=1, source_target_pairs={{0,3},{1,2},{2,1},{3,0},{4,7},{5,6},{6,5},{7,4},{8,11},{9,10},{10,... | collective-permute-start | bytes 159752 | tf_op jit(solution)/shard_map/ppermute | solution.py:45
  107.0 5.7 %collective-permute-start.38 = (bf16[104,256]{1,0:T(8,128)(2,1)S(1)}, bf16[104,256]{1,0:T(8,128)(2,1)S(1)}, u32[]{:S(2)}, u32[]{:S(2)}) collective-permute-start(bf16[104,256]{1,0:T(8,128)(2,1)S(1)} %get-tuple-element.167), channel_id=1, source_target_pairs={{0,2},{1,3},{2,0},{3,1},{4,6},{5,7},{6,4},{7,5},{8,10},{9,11},{10,... | collective-permute-start | bytes 159752 | tf_op jit(solution)/shard_map/ppermute | solution.py:45
  107.0 5.7 %collective-permute-start.37 = (bf16[104,256]{1,0:T(8,128)(2,1)S(1)}, bf16[104,256]{1,0:T(8,128)(2,1)S(1)}, u32[]{:S(2)}, u32[]{:S(2)}) collective-permute-start(bf16[104,256]{1,0:T(8,128)(2,1)S(1)} %get-tuple-element.168), channel_id=1, source_target_pairs={{0,1},{1,0},{2,3},{3,2},{4,5},{5,4},{6,7},{7,6},{8,9},{9,8},{10,11... | collective-permute-start | bytes 159752 | tf_op jit(solution)/shard_map/ppermute | solution.py:45

commit v5 on v4

--- a/solution.py
+++ b/solution.py
@@ -63,9 +63,9 @@
 
 
 def gathered_low(held):
-    count, low, high = row_groups()
-    result = [None] * count
-    for j in range(high):
+    _, low, _ = row_groups()
+    result = [None] * (low * len(held))
+    for j in range(len(held)):
         result[j * low] = held[j]
         for k in range(1, low):
             result[j * low + k] = sent(held[j], "rows", k)
@@ -506,57 +506,61 @@
     swapped(above, below, pair_in, other_in, False)
     crops, height, width, channels = input_four.shape
     low_height, low_width = input_five.shape[1:3]
-    padding = jnp.zeros((width - low_width, channels), bf16)
     for own, grad, edge, sums in (
         (input_four, grad_four, 0, sums_four),
         (input_five, grad_five, width, sums_five),
     ):
         lines, extent = own.shape[1:3]
-
-        def widened(row):
-            if extent == width:
-                return row
-            return jnp.concatenate([row, padding], axis=0)
-
-        for b in range(crops):
+        beside = width // extent
+        starts = range(0, crops, beside)
+
+        def padded_row(b, r):
+            if r == 0:
+                return above[b, edge : edge + extent]
+            if r == lines + 1:
+                return below[b, edge : edge + extent]
+            return own[b, r - 1]
+
+        for g, start in enumerate(starts):
             for r in range(lines + 2):
-                if r == 0:
-                    row = above[b, edge : edge + extent]
-                elif r == lines + 1:
-                    row = below[b, edge : edge + extent]
-                else:
-                    row = own[b, r - 1]
-                turned_rows[:, r * width : (r + 1) * width] = widened(row).T
-            left = jnp.concatenate(
-                [turned_rows[:, i * width : (i + lines) * width] for i in range(3)], axis=0
-            )
-            middle = jnp.concatenate([widened(grad[b, r]) for r in range(lines)], axis=0)
-            wide = middle.astype(f32)
-            right = jnp.concatenate(
-                [
-                    turned(wide, -1, 0, width).astype(bf16),
-                    middle,
-                    turned(wide, 1, 0, width).astype(bf16),
-                ],
-                axis=1,
-            )
-            for i in range(3):
-                product = dot(left[i * channels : (i + 1) * channels], right)
-                for j in range(3):
-                    at = slice((3 * i + j) * channels, (3 * i + j + 1) * channels)
-                    block = product[:, j * channels : (j + 1) * channels]
-                    if b == 0:
-                        sums[at, :] = block
-                    else:
-                        sums[at, :] += block
+                row = [padded_row(b, r) for b in range(start, start + beside)]
+                at = (g * (lines + 2) + r) * width
+                turned_rows[:, at : at + width] = jnp.concatenate(row, axis=0).T
+        middle = jnp.concatenate(
+            [
+                grad[b, r]
+                for start in starts
+                for r in range(lines)
+                for b in range(start, start + beside)
+            ],
+            axis=0,
+        )
+        wide = middle.astype(f32)
+        right = jnp.concatenate(
+            [
+                turned(wide, -1, 0, extent).astype(bf16),
+                middle,
+                turned(wide, 1, 0, extent).astype(bf16),
+            ],
+            axis=1,
+        )
+        for i in range(3):
+            left = []
+            for g in range(len(starts)):
+                at = (g * (lines + 2) + i) * width
+                left.append(turned_rows[:, at : at + lines * width])
+            product = dot(jnp.concatenate(left, axis=1), right).astype(bf16)
+            for j in range(3):
+                at = slice((3 * i + j) * channels, (3 * i + j + 1) * channels)
+                sums[at, :] = product[:, j * channels : (j + 1) * channels]
     me = lax.axis_index("rows")
     part = 9 * channels // n_rows
     low = len(outs)
     for index in range(n_rows):
         at = pl.ds(pl.multiple_of((index ^ me) * part, part), part)
         out, j = outs[index % low], index // low
-        out[j, :, :channels] = sums_four[at, :].astype(bf16)
-        out[j, :, channels:] = sums_five[at, :].astype(bf16)
+        out[j, :, :channels] = sums_four[at, :]
+        out[j, :, channels:] = sums_five[at, :]
 
 
 def merged_grad_kernel(grad_four, grad_five, pair_in, other_in, kernel_four, kernel_five, *refs):
@@ -599,10 +603,10 @@
     step = 256
     for at in range(0, depth, step):
         block = four[:, :, :, at : at + step].reshape(positions, step)
-        sums_four[at : at + step, :] = dot(turned_four, block).T
+        sums_four[at : at + step, :] = dot(turned_four, block).astype(bf16).T
     for at in range(0, low_depth, step):
         block = five[:, :, :, at : at + step].reshape(low_positions, step)
-        sums_five[at : at + step, :] = dot(turned_five, block).T
+        sums_five[at : at + step, :] = dot(turned_five, block).astype(bf16).T
     channels = head_grad.shape[1]
     flat[:, 9 * channels :] = jnp.zeros((DELTA_ROWS, flat.shape[1] - 9 * channels), f32)
     for t in range(9):
@@ -622,9 +626,9 @@
         out = kept.at[j] if k == 0 else outs[k - 1].at[j]
         owner = index ^ me
         at = pl.ds(pl.multiple_of(owner * part_four, part_four), part_four)
-        out[:part_four, :] = sums_four[at, :].astype(bf16)
+        out[:part_four, :] = sums_four[at, :]
         at = pl.ds(pl.multiple_of(owner * part_five, part_five), part_five)
-        out[part_four : part_four + part_five, :] = sums_five[at, :].astype(bf16)
+        out[part_four : part_four + part_five, :] = sums_five[at, :]
         pieces = []
         for z in range(n_batch):
             start = (owner * n_batch + z) * own
@@ -792,8 +796,19 @@
         [pltpu.VMEM((DELTA_ROWS, 9 * channels + 2 * LANES), f32)],
         scalar_outs=1,
     )
-    convs, pair_in, other_in, head = lax.optimization_barrier((convs, pair_in, other_in, head))
-    convs = gathered_low(convs)
+    pair_in, other_in, head = lax.optimization_barrier((pair_in, other_in, head))
+    early = (0, high_group - 1)
+    early_convs = [
+        lax.optimization_barrier((convs[j], pair_in, other_in))[0] for j in early
+    ]
+    early_low = gathered_low(early_convs)
+    late = [j for j in range(high_group) if j not in early]
+    late_convs, early_low = lax.optimization_barrier(([convs[j] for j in late], early_low))
+    late_low = gathered_low(late_convs)
+    convs = [None] * n_rows
+    for group, lows in ((early, early_low), (late, late_low)):
+        for i, j in enumerate(group):
+            convs[j * low_group : (j + 1) * low_group] = lows[i * low_group : (i + 1) * low_group]
 
     conv_flops = 18 * crops * channels * channels * (height * width + low_height * low_width)
     levels, values, pair, other, kernel_four, kernel_five = call(
@@ -852,9 +867,9 @@
         [input_four, input_five, pair_in, other_in, grad_four, grad_five],
         [shape((high_group, n_batch * conv_n, conv_width), bf16)] * low_group,
         [
-            pltpu.VMEM((channels, (height + 2) * width), bf16),
-            pltpu.VMEM((9 * channels, channels), f32),
-            pltpu.VMEM((9 * channels, channels), f32),
+            pltpu.VMEM((channels, crops * (height + 2) * width), bf16),
+            pltpu.VMEM((9 * channels, channels), bf16),
+            pltpu.VMEM((9 * channels, channels), bf16),
         ]
         + input_rims,
         flops=conv_flops,
@@ -891,8 +906,8 @@
         [section_four, section_five, lat_four, lat_five, head_grad, loss],
         [shape((high_group, n_batch * lateral_n, channels), bf16)] * low_group,
         [
-            pltpu.VMEM((depth, channels), f32),
-            pltpu.VMEM((low_depth, channels), f32),
+            pltpu.VMEM((depth, channels), bf16),
+            pltpu.VMEM((low_depth, channels), bf16),
             pltpu.VMEM((DELTA_ROWS, 9 * channels + 2 * LANES), f32),
         ],
         flops=1,

time: 114 us -> 112 us (0.982)
  waiting for transfers between devices: 35.7 us -> 30.1 us
  starting transfers between devices: 45.4 us -> 49.8 us
    ppermute x37, waiting for transfers between devices: 35.7 us -> 30.1 us  [sent(): return lax.ppermute(value, axis, [(i, i ^ mask) for i in range(count)])]
    ppermute x37, starting transfers between devices: 43.4 us -> 47.8 us  [sent(): return lax.ppermute(value, axis, [(i, i ^ mask) for i in range(count)])]
  transfers between devices with their start and end apart: 40 -> 40, of which waited for: 22 -> 17; matrix products, arithmetic and copies ran while one was open for 1% -> 1% of each run, Pallas kernels for 9% -> 9%
where the time goes in v5:
time: 112 us
  starting transfers between devices  49.8 us (44%)
  waiting for transfers between devices  30.1 us (27%)
  Pallas kernels  23.8 us (21%)
  local copies, waits for them, and re-layouts  4.17 us (4%)
  other arithmetic  2.53 us (2%)
  between operations  1.51 us (1%)
    ppermute x37, starting transfers between devices, sent(): return lax.ppermute(value, axis, [(i, i ^ mask) for i in range(count)])  47.8 us
    ppermute x37, waiting for transfers between devices, sent(): return lax.ppermute(value, axis, [(i, i ^ mask) for i in range(count)])  30.1 us
    pallas_call x12, Pallas kernels, call(): pl.pallas_call(kernel, out_shape=list(outs), in_specs=[hbm] * apart + [vm...  23.8 us
    unnamed x55, local copies, waits for them, and re-layouts  4.02 us
  transfers between devices with their start and end apart: 40, of which 17 were waited for; matrix products, arithmetic and copies ran while one was open for 1% of the time, Pallas kernels for 9%

profile of v5, /device:TPU:0, one launch (start us, length us, event | category | flops | bytes accessed | tf_op | source)
XLA Modules:
  0.0 111.9 jit_solution(890970093991241987)
XLA Ops:
  0.7 1.7 %pack.1 = bf16[104,256]{1,0:T(8,128)(2,1)} custom-call(f32[32,256]{1,0:T(8,128)} %refs_3_.2, f32[64,256]{1,0:T(8,128)} %refs_6_.3, f32[12,72]{1,0:T(8,128)} %bitcast.133, s32[2,3,8,128]{3,2,1,0:T(8,128)} %bitcast.127, s32[2,3,4,64]{3,2,1,0:T(4,128)} %bitcast.131, s32[2,3,2,32]{3,2,1,0:T(2,128)} %bitcast.136), custom_call_target="tpu_custom_call" | custom-call | bytes 187264 | tf_op jit(solution)/shard_map/pack/pallas_call | solution.py:118
  2.4 5.1 %collective-permute-start.2 = (bf16[104,256]{1,0:T(8,128)(2,1)}, bf16[104,256]{1,0:T(8,128)(2,1)S(1)}, u32[]{:S(2)}, u32[]{:S(2)}) collective-permute-start(bf16[104,256]{1,0:T(8,128)(2,1)} %pack.1), channel_id=1, source_target_pairs={{0,3},{1,2},{2,1},{3,0},{4,7},{5,6},{6,5},{7,4},{8,11},{9,10},{10,... | collective-permute-start | bytes 159752 | tf_op jit(solution)/shard_map/ppermute | solution.py:45
  7.6 0.6 collective-permute-start
  8.2 0.9 convert.8
  9.2 0.9 collective-permute-done.2
  10.1 2.7 %collective-permute-done.1 = bf16[104,256]{1,0:T(8,128)(2,1)S(1)} collective-permute-done((bf16[104,256]{1,0:T(8,128)(2,1)}, bf16[104,256]{1,0:T(8,128)(2,1)S(1)}, u32[]{:S(2)}, u32[]{:S(2)}) %collective-permute-start.1) | collective-permute-done | bytes 53280 | tf_op jit(solution)/shard_map/ppermute | solution.py:45
  12.8 0.8 pad_maximum_fusion.3
  13.9 2.4 %collective-permute-start.14 = (bf16[72,512]{1,0:T(8,128)(2,1)S(1)}, bf16[72,512]{1,0:T(8,128)(2,1)S(1)}, u32[]{:S(2)}, u32[]{:S(2)}) collective-permute-start(bf16[72,512]{1,0:T(8,128)(2,1)S(1)} %pad_maximum_fusion.4), channel_id=1, source_target_pairs={{0,3},{1,2},{2,1},{3,0},{4,7},{5,6},{6,5},{7,4},{8,11},{9,10},{10,... | collective-permute-start | bytes 221192 | tf_op jit(solution)/shard_map/ppermute | solution.py:45
  16.3 2.4 %collective-permute-start.5 = (bf16[416,256]{1,0:T(8,128)(2,1)S(1)}, bf16[416,256]{1,0:T(8,128)(2,1)S(1)}, u32[]{:S(2)}, u32[]{:S(2)}) collective-permute-start(bf16[416,256]{1,0:T(8,128)(2,1)S(1)} %constant_dynamic-update-slice_fusion.refs_0_), channel_id=1, source_target_pairs={{0,24},{4,28},{8,16},{12,20},{16,8},{20,12},{24,0},{28,4},{1,25},{... | collective-permute-start | bytes 638984 | tf_op jit(solution)/shard_map/ppermute | solution.py:45
  18.8 0.5 collective-permute-start.4
  19.3 0.5 collective-permute-start.3
  19.8 0.5 collective-permute-done.14
  20.3 1.6 %collective-permute-start.12 = (bf16[72,512]{1,0:T(8,128)(2,1)S(1)}, bf16[72,512]{1,0:T(8,128)(2,1)S(1)}, u32[]{:S(2)}, u32[]{:S(2)}) collective-permute-start(bf16[72,512]{1,0:T(8,128)(2,1)S(1)} %pad_maximum_fusion.4), channel_id=1, source_target_pairs={{0,1},{1,0},{2,3},{3,2},{4,5},{5,4},{6,7},{7,6},{8,9},{9,8},{10,11... | collective-permute-start | bytes 221192 | tf_op jit(solution)/shard_map/ppermute | solution.py:45
  21.9 2.2 %copy-done = bf16[2,8,128,1024]{3,2,1,0:T(8,128)(2,1)S(1)} copy-done((bf16[2,8,128,1024]{3,2,1,0:T(8,128)(2,1)S(1)}, bf16[2,8,128,1024]{3,2,1,0:T(8,128)(2,1)}, u32[]{:S(2)}) %copy-start) | copy-done | bytes 4194328
  24.1 1.6 %copy-done.2 = bf16[2,4,64,2048]{3,2,1,0:T(8,128)(2,1)S(1)} copy-done((bf16[2,4,64,2048]{3,2,1,0:T(8,128)(2,1)S(1)}, bf16[2,4,64,2048]{3,2,1,0:T(8,128)(2,1)}, u32[]{:S(2)}) %copy-start.2) | copy-done | bytes 2097176
  25.7 0.2 planes.1
  25.9 1.4 %collective-permute-done.4.refs_4_ = bf16[416,256]{1,0:T(8,128)(2,1)S(1)} collective-permute-done((bf16[416,256]{1,0:T(8,128)(2,1)S(1)}, bf16[416,256]{1,0:T(8,128)(2,1)S(1)}, u32[]{:S(2)}, u32[]{:S(2)}) %collective-permute-start.4) | collective-permute-done | bytes 213024 | tf_op jit(solution)/shard_map/ppermute | solution.py:45
  27.3 0.1 collective-permute-done.3.refs_2_
  27.4 0.5 collective-permute-start.7
  27.9 0.5 collective-permute-start.9
  28.5 1.7 %collective-permute-start.18 = (bf16[288,512]{1,0:T(8,128)(2,1)S(1)}, bf16[288,512]{1,0:T(8,128)(2,1)S(1)}, u32[]{:S(2)}, u32[]{:S(2)}) collective-permute-start(bf16[288,512]{1,0:T(8,128)(2,1)S(1)} %pad_maximum_fusion.2.refs_0_), channel_id=1, source_target_pairs={{0,24},{4,28},{8,16},{12,20},{16,8},{20,12},{24,0},{28,4},{1,25},{... | collective-permute-start | bytes 884744 | tf_op jit(solution)/shard_map/ppermute | solution.py:45
  30.2 2.0 %laterals.1 = (bf16[2,8,128,256]{3,2,1,0:T(8,128)(2,1)S(1)}, bf16[2,4,64,256]{3,2,1,0:T(8,128)(2,1)S(1)}, bf16[2,208,256]{2,1,0:T(8,128)(2,1)S(1)}, bf16[2,208,256]{2,1,0:T(8,128)(2,1)S(1)}) custom-call(bf16[2,8,128,1024]{3,2,1,0:T(8,128)(2,1)S(1)} %copy-done.1, bf16[2,4,64,2048]{3,2,1,0:T(8,128)(2,1)S(1)} %copy-done.2, ...), custom_call_target="tpu_custom_call" | custom-call | flops 1610612736 | bytes 9961472 | tf_op jit(solution)/shard_map/laterals/pallas_call | solution.py:118
  32.3 0.7 collective-permute-start.11
  33.0 4.1 %collective-permute-start.16 = (bf16[288,512]{1,0:T(8,128)(2,1)S(1)}, bf16[288,512]{1,0:T(8,128)(2,1)S(1)}, u32[]{:S(2)}, u32[]{:S(2)}) collective-permute-start(bf16[288,512]{1,0:T(8,128)(2,1)S(1)} %pad_maximum_fusion.2.refs_0_), channel_id=1, source_target_pairs={{0,16},{4,20},{8,24},{12,28},{16,0},{20,4},{24,8},{28,12},{1,17},{... | collective-permute-start | bytes 884744 | tf_op jit(solution)/shard_map/ppermute | solution.py:45
  37.1 0.6 collective-permute-start.15
  37.7 0.9 head_weights.1
  38.7 4.6 %collective-permute-start.17 = (bf16[288,512]{1,0:T(8,128)(2,1)S(1)}, bf16[288,512]{1,0:T(8,128)(2,1)S(1)}, u32[]{:S(2)}, u32[]{:S(2)}) collective-permute-start(bf16[288,512]{1,0:T(8,128)(2,1)S(1)} %pad_maximum_fusion.2.refs_0_), channel_id=1, source_target_pairs={{0,4},{4,0},{8,12},{12,8},{16,20},{20,16},{24,28},{28,24},{1,5},{5... | collective-permute-start | bytes 884744 | tf_op jit(solution)/shard_map/ppermute | solution.py:45
  43.3 2.6 %collective-permute-done.16.refs_4_ = bf16[288,512]{1,0:T(8,128)(2,1)S(1)} collective-permute-done((bf16[288,512]{1,0:T(8,128)(2,1)S(1)}, bf16[288,512]{1,0:T(8,128)(2,1)S(1)}, u32[]{:S(2)}, u32[]{:S(2)}) %collective-permute-start.16) | collective-permute-done | bytes 294944 | tf_op jit(solution)/shard_map/ppermute | solution.py:45
  45.9 3.3 %collective-permute-done.15.refs_2_ = bf16[288,512]{1,0:T(8,128)(2,1)S(1)} collective-permute-done((bf16[288,512]{1,0:T(8,128)(2,1)S(1)}, bf16[288,512]{1,0:T(8,128)(2,1)S(1)}, u32[]{:S(2)}, u32[]{:S(2)}) %collective-permute-start.15) | collective-permute-done | bytes 294944 | tf_op jit(solution)/shard_map/ppermute | solution.py:45
  49.2 0.5 collective-permute-start.21
  49.7 1.1 collective-permute-done.20.refs_3_
  50.8 0.4 collective-permute-done.21.refs_5_
  51.2 4.4 %outputs.1 = (bf16[2,14,128,256]{3,2,1,0:T(8,128)(2,1)S(1)}, f32[2,16,2560]{2,1,0:T(8,128)S(1)}, f32[2,24,256]{2,1,0:T(8,128)S(1)}, f32[2,24,256]{2,1,0:T(8,128)...) custom-call(bf16[2,8,128,256]{3,2,1,0:T(8,128)(2,1)S(1)} %get-tuple-element.102.input_four, ...), custom_call_target="tpu_custom_call" | custom-call | flops 3019898880 | bytes 9248768 | tf_op jit(solution)/shard_map/outputs/pallas_call | solution.py:118
  55.6 0.2 collective-permute-start.22
  55.8 0.7 collective-permute-start.23
  56.4 0.4 collective-permute-done.22.pair_in
  56.9 2.7 %heads.1 = (f32[144,256]{1,0:T(8,128)S(1)}, bf16[2,8,128,256]{3,2,1,0:T(8,128)(2,1)S(1)}, bf16[2,4,64,256]{3,2,1,0:T(8,128)(2,1)S(1)}, bf16[2,192,256]{2,1,0:T(8...) custom-call(bf16[2,14,128,256]{3,2,1,0:T(8,128)(2,1)S(1)} %get-tuple-element.120.levels, ...), custom_call_target="tpu_custom_call" | custom-call | flops 792723456 | bytes 4841480 | tf_op jit(solution)/shard_map/heads/pallas_call | solution.py:118
  59.6 3.7 %conv_grads.1 = (bf16[4,288,512]{2,1,0:T(8,128)(2,1)S(1)}, bf16[4,288,512]{2,1,0:T(8,128)(2,1)S(1)}) custom-call(bf16[2,8,128,256]{3,2,1,0:T(8,128)(2,1)S(1)} %get-tuple-element.102.input_four, bf16[2,4,64,256]{3,2,1,0:T(8,128)(2,1)S(1)} %get-tuple-element.103.input_five, bf16[2,208,256]{2,1,0:T(8,128)(2,1)S(1)} %collective-permute-done.10.pair_in.pair_mask, ...), custom_call_target="tpu_custom_call" | custom-call | flops 3019898880 | bytes 5406720 | tf_op jit(solution)/shard_map/conv_grads/pallas_call | solution.py:118
  63.3 4.7 %collective-permute-start.26 = (bf16[4,288,512]{2,1,0:T(8,128)(2,1)S(1)}, bf16[4,288,512]{2,1,0:T(8,128)(2,1)S(1)}, u32[]{:S(2)}, u32[]{:S(2)}) collective-permute-start(bf16[4,288,512]{2,1,0:T(8,128)(2,1)S(1)} %get-tuple-element.130), channel_id=1, source_target_pairs={{0,4},{4,0},{8,12},{12,8},{16,20},{20,16},{24,28},{28,24},{1,5},{5... | collective-permute-start | bytes 3538952 | tf_op jit(solution)/shard_map/ppermute | solution.py:45
  68.1 0.7 collective-permute-start.25
  68.8 1.7 %collective-permute-done.26 = bf16[4,288,512]{2,1,0:T(8,128)(2,1)S(1)} collective-permute-done((bf16[4,288,512]{2,1,0:T(8,128)(2,1)S(1)}, bf16[4,288,512]{2,1,0:T(8,128)(2,1)S(1)}, u32[]{:S(2)}, u32[]{:S(2)}) %collective-permute-start.26) | collective-permute-done | bytes 1179680 | tf_op jit(solution)/shard_map/ppermute | solution.py:45
  70.5 0.4 fusion.16
  70.9 1.9 %collective-permute-start.30 = (bf16[288,512]{1,0:T(8,128)(2,1)S(1)}, bf16[288,512]{1,0:T(8,128)(2,1)S(1)}, u32[]{:S(2)}, u32[]{:S(2)}) collective-permute-start(bf16[288,512]{1,0:T(8,128)(2,1)S(1)} %get-tuple-element.164), channel_id=1, source_target_pairs={{0,24},{4,28},{8,16},{12,20},{16,8},{20,12},{24,0},{28,4},{1,25},{... | collective-permute-start | bytes 884744 | tf_op jit(solution)/shard_map/ppermute | solution.py:45
  72.7 1.6 %collective-permute-start.28 = (bf16[288,512]{1,0:T(8,128)(2,1)S(1)}, bf16[288,512]{1,0:T(8,128)(2,1)S(1)}, u32[]{:S(2)}, u32[]{:S(2)}) collective-permute-start(bf16[288,512]{1,0:T(8,128)(2,1)S(1)} %get-tuple-element.165), channel_id=1, source_target_pairs={{0,8},{4,12},{8,0},{12,4},{16,24},{20,28},{24,16},{28,20},{1,9},{5... | collective-permute-start | bytes 884744 | tf_op jit(solution)/shard_map/ppermute | solution.py:45
  74.3 0.1 collective-permute-start.29
  74.4 3.6 %merged_grads.1 = (bf16[2048,256]{1,0:T(8,128)(2,1)S(1)}, bf16[512,256]{1,0:T(8,128)(2,1)S(1)}) custom-call(bf16[2,8,128,256]{3,2,1,0:T(8,128)(2,1)S(1)} %get-tuple-element.125.grad_four, bf16[2,4,64,256]{3,2,1,0:T(8,128)(2,1)S(1)} %get-tuple-element.126.grad_five, bf16[2,192,256]{2,1,0:T(8,128)(2,1)S(1)} %collective-permute-done.24.pair_in, ...), custom_call_target="tpu_custom_call" | custom-call | flops 3019898880 | bytes 5373952 | tf_op jit(solution)/shard_map/merged_grads/pallas_call | solution.py:118
  78.0 2.8 %lateral_grads.1 = (bf16[4,416,256]{2,1,0:T(8,128)(2,1)S(1)}, bf16[4,416,256]{2,1,0:T(8,128)(2,1)S(1)}) custom-call(bf16[2,8,128,1024]{3,2,1,0:T(8,128)(2,1)S(1)} %copy-done.1, bf16[2,4,64,2048]{3,2,1,0:T(8,128)(2,1)S(1)} %copy-done.3, bf16[2048,256]{1,0:T(8,128)(2,1)S(1)} %get-tuple-element.135.lat_four, bf16[512,256]{1,0:T(8,128)(2,1)S(1)} %get-tuple-element.136.lat_five, ...), custom_call_target="tpu_custom_call" | custom-call | flops 1 | bytes 9453572 | tf_op jit(solution)/shard_map/lateral_grads/pallas_call | solution.py:118
  80.9 3.5 %collective-permute-start.27 = (bf16[4,416,256]{2,1,0:T(8,128)(2,1)S(1)}, bf16[4,416,256]{2,1,0:T(8,128)(2,1)S(1)}, u32[]{:S(2)}, u32[]{:S(2)}) collective-permute-start(bf16[4,416,256]{2,1,0:T(8,128)(2,1)S(1)} %get-tuple-element.140), channel_id=1, source_target_pairs={{0,4},{4,0},{8,12},{12,8},{16,20},{20,16},{24,28},{28,24},{1,5},{5... | collective-permute-start | bytes 2555912 | tf_op jit(solution)/shard_map/ppermute | solution.py:45
  84.3 5.6 %collective-permute-done.28.refs_0_ = bf16[288,512]{1,0:T(8,128)(2,1)S(1)} collective-permute-done((bf16[288,512]{1,0:T(8,128)(2,1)S(1)}, bf16[288,512]{1,0:T(8,128)(2,1)S(1)}, u32[]{:S(2)}, u32[]{:S(2)}) %collective-permute-start.28) | collective-permute-done | bytes 294944 | tf_op jit(solution)/shard_map/ppermute | solution.py:45
  89.9 0.1 conv_total.1
  90.1 0.2 add_bitcast_fusion.4
  90.3 1.0 collective-permute-start.34
  91.3 1.4 %collective-permute-start.35 = (bf16[416,256]{1,0:T(8,128)(2,1)S(1)}, bf16[416,256]{1,0:T(8,128)(2,1)S(1)}, u32[]{:S(2)}, u32[]{:S(2)}) collective-permute-start(bf16[416,256]{1,0:T(8,128)(2,1)S(1)} %get-tuple-element.144), channel_id=1, source_target_pairs={{0,16},{4,20},{8,24},{12,28},{16,0},{20,4},{24,8},{28,12},{1,17},{... | collective-permute-start | bytes 638984 | tf_op jit(solution)/shard_map/ppermute | solution.py:45
  92.8 1.1 %collective-permute-start.36 = (bf16[416,256]{1,0:T(8,128)(2,1)S(1)}, bf16[416,256]{1,0:T(8,128)(2,1)S(1)}, u32[]{:S(2)}, u32[]{:S(2)}) collective-permute-start(bf16[416,256]{1,0:T(8,128)(2,1)S(1)} %get-tuple-element.145), channel_id=1, source_target_pairs={{0,24},{4,28},{8,16},{12,20},{16,8},{20,12},{24,0},{28,4},{1,25},{... | collective-permute-start | bytes 638984 | tf_op jit(solution)/shard_map/ppermute | solution.py:45
  93.9 1.9 %collective-permute-start.33 = (bf16[72,512]{1,0:T(8,128)(2,1)S(1)}, bf16[72,512]{1,0:T(8,128)(2,1)S(1)}, u32[]{:S(2)}, u32[]{:S(2)}) collective-permute-start(bf16[72,512]{1,0:T(8,128)(2,1)S(1)} %get-tuple-element.171), channel_id=1, source_target_pairs={{0,3},{1,2},{2,1},{3,0},{4,7},{5,6},{6,5},{7,4},{8,11},{9,10},{10,... | collective-permute-start | bytes 221192 | tf_op jit(solution)/shard_map/ppermute | solution.py:45
  95.8 2.7 %collective-permute-done.34 = bf16[416,256]{1,0:T(8,128)(2,1)S(1)} collective-permute-done((bf16[416,256]{1,0:T(8,128)(2,1)S(1)}, bf16[416,256]{1,0:T(8,128)(2,1)S(1)}, u32[]{:S(2)}, u32[]{:S(2)}) %collective-permute-start.34) | collective-permute-done | bytes 213024 | tf_op jit(solution)/shard_map/ppermute | solution.py:45
  98.6 3.6 %collective-permute-done.35 = bf16[416,256]{1,0:T(8,128)(2,1)S(1)} collective-permute-done((bf16[416,256]{1,0:T(8,128)(2,1)S(1)}, bf16[416,256]{1,0:T(8,128)(2,1)S(1)}, u32[]{:S(2)}, u32[]{:S(2)}) %collective-permute-start.35) | collective-permute-done | bytes 213024 | tf_op jit(solution)/shard_map/ppermute | solution.py:45
  102.3 0.8 collective-permute-done.31.refs_0_
  103.3 2.2 %collective-permute-start.39 = (bf16[104,256]{1,0:T(8,128)(2,1)S(1)}, bf16[104,256]{1,0:T(8,128)(2,1)S(1)}, u32[]{:S(2)}, u32[]{:S(2)}) collective-permute-start(bf16[104,256]{1,0:T(8,128)(2,1)S(1)} %get-tuple-element.174), channel_id=1, source_target_pairs={{0,3},{1,2},{2,1},{3,0},{4,7},{5,6},{6,5},{7,4},{8,11},{9,10},{10,... | collective-permute-start | bytes 159752 | tf_op jit(solution)/shard_map/ppermute | solution.py:45
  105.5 2.3 %collective-permute-start.37 = (bf16[104,256]{1,0:T(8,128)(2,1)S(1)}, bf16[104,256]{1,0:T(8,128)(2,1)S(1)}, u32[]{:S(2)}, u32[]{:S(2)}) collective-permute-start(bf16[104,256]{1,0:T(8,128)(2,1)S(1)} %get-tuple-element.176), channel_id=1, source_target_pairs={{0,1},{1,0},{2,3},{3,2},{4,5},{5,4},{6,7},{7,6},{8,9},{9,8},{10,11... | collective-permute-start | bytes 159752 | tf_op jit(solution)/shard_map/ppermute | solution.py:45
  107.8 0.8 conv_step.1
  108.6 1.2 %collective-permute-done.39.refs_2_ = bf16[104,256]{1,0:T(8,128)(2,1)S(1)} collective-permute-done((bf16[104,256]{1,0:T(8,128)(2,1)S(1)}, bf16[104,256]{1,0:T(8,128)(2,1)S(1)}, u32[]{:S(2)}, u32[]{:S(2)}) %collective-permute-start.39) | collective-permute-done | bytes 53280 | tf_op jit(solution)/shard_map/ppermute | solution.py:45
  109.8 1.0 collective-permute-done.38.refs_1_
  111.0 0.8 lateral_step.1
  (103 shorter events, 0.9 us)
Async XLA Ops:
  0.6 21.2 %copy-start.19 = (s32[2,2,32,3]{2,1,3,0:T(2,128)S(1)}, s32[2,2,32,3]{2,1,3,0:T(2,128)}, u32[]{:S(2)}) copy-start(s32[2,2,32,3]{2,1,3,0:T(2,128)} %param.27) | copy-start | bytes 4612
  0.7 21.2 %copy-start.14 = (s32[2,4,64,3]{2,1,3,0:T(4,128)S(1)}, s32[2,4,64,3]{2,1,3,0:T(4,128)}, u32[]{:S(2)}) copy-start(s32[2,4,64,3]{2,1,3,0:T(4,128)} %param.26) | copy-start | bytes 18436
  0.7 21.2 %copy-start.9 = (s32[2,8,128,3]{2,1,3,0:T(8,128)S(1)}, s32[2,8,128,3]{2,1,3,0:T(8,128)}, u32[]{:S(2)}) copy-start(s32[2,8,128,3]{2,1,3,0:T(8,128)} %param.25) | copy-start | bytes 73732
  0.7 21.2 %copy-start.18 = (f32[2,2,32,12]{2,1,3,0:T(2,128)S(1)}, f32[2,2,32,12]{2,1,3,0:T(2,128)}, u32[]{:S(2)}) copy-start(f32[2,2,32,12]{2,1,3,0:T(2,128)} %param.24) | copy-start | bytes 18436
  0.7 21.2 %copy-start.13 = (f32[2,4,64,12]{2,1,3,0:T(4,128)S(1)}, f32[2,4,64,12]{2,1,3,0:T(4,128)}, u32[]{:S(2)}) copy-start(f32[2,4,64,12]{2,1,3,0:T(4,128)} %param.23) | copy-start | bytes 73732
  0.7 21.2 %copy-start.10 = (f32[2,8,128,12]{2,1,3,0:T(8,128)S(1)}, f32[2,8,128,12]{2,1,3,0:T(8,128)}, u32[]{:S(2)}) copy-start(f32[2,8,128,12]{2,1,3,0:T(8,128)} %param.22) | copy-start | bytes 294916
  2.4 7.7 %collective-permute-start.2 = (bf16[104,256]{1,0:T(8,128)(2,1)}, bf16[104,256]{1,0:T(8,128)(2,1)S(1)}, u32[]{:S(2)}, u32[]{:S(2)}) collective-permute-start(bf16[104,256]{1,0:T(8,128)(2,1)} %pack.1), channel_id=1, source_target_pairs={{0,3},{1,2},{2,1},{3,0},{4,7},{5,6},{6,5},{7,4},{8,11},{9,10},{10,... | collective-permute-start | bytes 159752 | tf_op jit(solution)/shard_map/ppermute | solution.py:45
  7.6 5.2 %collective-permute-start.1 = (bf16[104,256]{1,0:T(8,128)(2,1)}, bf16[104,256]{1,0:T(8,128)(2,1)S(1)}, u32[]{:S(2)}, u32[]{:S(2)}) collective-permute-start(bf16[104,256]{1,0:T(8,128)(2,1)} %pack.1), channel_id=1, source_target_pairs={{0,2},{1,3},{2,0},{3,1},{4,6},{5,7},{6,4},{7,5},{8,10},{9,11},{10,... | collective-permute-start | bytes 159752 | tf_op jit(solution)/shard_map/ppermute | solution.py:45
  7.6 5.2 %collective-permute-start = (bf16[104,256]{1,0:T(8,128)(2,1)}, bf16[104,256]{1,0:T(8,128)(2,1)S(1)}, u32[]{:S(2)}, u32[]{:S(2)}) collective-permute-start(bf16[104,256]{1,0:T(8,128)(2,1)} %pack.1), channel_id=1, source_target_pairs={{0,1},{1,0},{2,3},{3,2},{4,5},{5,4},{6,7},{7,6},{8,9},{9,8},{10,11... | collective-permute-start | bytes 159752 | tf_op jit(solution)/shard_map/ppermute | solution.py:45
  13.9 6.4 %collective-permute-start.14 = (bf16[72,512]{1,0:T(8,128)(2,1)S(1)}, bf16[72,512]{1,0:T(8,128)(2,1)S(1)}, u32[]{:S(2)}, u32[]{:S(2)}) collective-permute-start(bf16[72,512]{1,0:T(8,128)(2,1)S(1)} %pad_maximum_fusion.4), channel_id=1, source_target_pairs={{0,3},{1,2},{2,1},{3,0},{4,7},{5,6},{6,5},{7,4},{8,11},{9,10},{10,... | collective-permute-start | bytes 221192 | tf_op jit(solution)/shard_map/ppermute | solution.py:45
  16.3 9.6 %collective-permute-start.5 = (bf16[416,256]{1,0:T(8,128)(2,1)S(1)}, bf16[416,256]{1,0:T(8,128)(2,1)S(1)}, u32[]{:S(2)}, u32[]{:S(2)}) collective-permute-start(bf16[416,256]{1,0:T(8,128)(2,1)S(1)} %constant_dynamic-update-slice_fusion.refs_0_), channel_id=1, source_target_pairs={{0,24},{4,28},{8,16},{12,20},{16,8},{20,12},{24,0},{28,4},{1,25},{... | collective-permute-start | bytes 638984 | tf_op jit(solution)/shard_map/ppermute | solution.py:45
  18.8 8.5 %collective-permute-start.4 = (bf16[416,256]{1,0:T(8,128)(2,1)S(1)}, bf16[416,256]{1,0:T(8,128)(2,1)S(1)}, u32[]{:S(2)}, u32[]{:S(2)}) collective-permute-start(bf16[416,256]{1,0:T(8,128)(2,1)S(1)} %constant_dynamic-update-slice_fusion.refs_0_), channel_id=1, source_target_pairs={{0,16},{4,20},{8,24},{12,28},{16,0},{20,4},{24,8},{28,12},{1,17},{... | collective-permute-start | bytes 638984 | tf_op jit(solution)/shard_map/ppermute | solution.py:45
  19.3 8.1 %collective-permute-start.3 = (bf16[416,256]{1,0:T(8,128)(2,1)S(1)}, bf16[416,256]{1,0:T(8,128)(2,1)S(1)}, u32[]{:S(2)}, u32[]{:S(2)}) collective-permute-start(bf16[416,256]{1,0:T(8,128)(2,1)S(1)} %constant_dynamic-update-slice_fusion.refs_0_), channel_id=1, source_target_pairs={{0,8},{4,12},{8,0},{12,4},{16,24},{20,28},{24,16},{28,20},{1,9},{5... | collective-permute-start | bytes 638984 | tf_op jit(solution)/shard_map/ppermute | solution.py:45
  19.8 6.0 %collective-permute-start.13 = (bf16[72,512]{1,0:T(8,128)(2,1)S(1)}, bf16[72,512]{1,0:T(8,128)(2,1)S(1)}, u32[]{:S(2)}, u32[]{:S(2)}) collective-permute-start(bf16[72,512]{1,0:T(8,128)(2,1)S(1)} %pad_maximum_fusion.4), channel_id=1, source_target_pairs={{0,2},{1,3},{2,0},{3,1},{4,6},{5,7},{6,4},{7,5},{8,10},{9,11},{10,... | collective-permute-start | bytes 221192 | tf_op jit(solution)/shard_map/ppermute | solution.py:45
  20.3 5.6 %collective-permute-start.12 = (bf16[72,512]{1,0:T(8,128)(2,1)S(1)}, bf16[72,512]{1,0:T(8,128)(2,1)S(1)}, u32[]{:S(2)}, u32[]{:S(2)}) collective-permute-start(bf16[72,512]{1,0:T(8,128)(2,1)S(1)} %pad_maximum_fusion.4), channel_id=1, source_target_pairs={{0,1},{1,0},{2,3},{3,2},{4,5},{5,4},{6,7},{7,6},{8,9},{9,8},{10,11... | collective-permute-start | bytes 221192 | tf_op jit(solution)/shard_map/ppermute | solution.py:45
  21.9 2.2 %copy-start = (bf16[2,8,128,1024]{3,2,1,0:T(8,128)(2,1)S(1)}, bf16[2,8,128,1024]{3,2,1,0:T(8,128)(2,1)}, u32[]{:S(2)}) copy-start(bf16[2,8,128,1024]{3,2,1,0:T(8,128)(2,1)} %four.3) | copy-start | bytes 12582916
  24.1 1.6 %copy-start.2 = (bf16[2,4,64,2048]{3,2,1,0:T(8,128)(2,1)S(1)}, bf16[2,4,64,2048]{3,2,1,0:T(8,128)(2,1)}, u32[]{:S(2)}) copy-start(bf16[2,4,64,2048]{3,2,1,0:T(8,128)(2,1)} %five.3) | copy-start | bytes 6291460
  25.7 4.5 %copy-start.1 = (bf16[2,8,128,1024]{3,2,1,0:T(8,128)(2,1)S(1)}, bf16[2,8,128,1024]{3,2,1,0:T(8,128)(2,1)}, u32[]{:S(2)}) copy-start(bf16[2,8,128,1024]{3,2,1,0:T(8,128)(2,1)} %four.3) | copy-start | bytes 12582916
  27.4 2.8 %collective-permute-start.6 = (bf16[416,256]{1,0:T(8,128)(2,1)S(1)}, bf16[416,256]{1,0:T(8,128)(2,1)S(1)}, u32[]{:S(2)}, u32[]{:S(2)}) collective-permute-start(bf16[416,256]{1,0:T(8,128)(2,1)S(1)} %constant_dynamic-update-slice_fusion.refs_0_), channel_id=1, source_target_pairs={{0,4},{4,0},{8,12},{12,8},{16,20},{20,16},{24,28},{28,24},{1,5},{5... | collective-permute-start | bytes 638984 | tf_op jit(solution)/shard_map/ppermute | solution.py:45
  27.4 2.8 %collective-permute-start.7 = (bf16[416,256]{1,0:T(8,128)(2,1)S(1)}, bf16[416,256]{1,0:T(8,128)(2,1)S(1)}, u32[]{:S(2)}, u32[]{:S(2)}) collective-permute-start(bf16[416,256]{1,0:T(8,128)(2,1)S(1)} %collective-permute-done.3.refs_2_), channel_id=1, source_target_pairs={{0,4},{4,0},{8,12},{12,8},{16,20},{20,16},{24,28},{28,24},{1,5},{5... | collective-permute-start | bytes 638984 | tf_op jit(solution)/shard_map/ppermute | solution.py:45
  27.9 2.3 %collective-permute-start.8 = (bf16[416,256]{1,0:T(8,128)(2,1)S(1)}, bf16[416,256]{1,0:T(8,128)(2,1)S(1)}, u32[]{:S(2)}, u32[]{:S(2)}) collective-permute-start(bf16[416,256]{1,0:T(8,128)(2,1)S(1)} %collective-permute-done.4.refs_4_), channel_id=1, source_target_pairs={{0,4},{4,0},{8,12},{12,8},{16,20},{20,16},{24,28},{28,24},{1,5},{5... | collective-permute-start | bytes 638984 | tf_op jit(solution)/shard_map/ppermute | solution.py:45
  27.9 2.3 %collective-permute-start.9 = (bf16[416,256]{1,0:T(8,128)(2,1)S(1)}, bf16[416,256]{1,0:T(8,128)(2,1)S(1)}, u32[]{:S(2)}, u32[]{:S(2)}) collective-permute-start(bf16[416,256]{1,0:T(8,128)(2,1)S(1)} %collective-permute-done.5.refs_6_), channel_id=1, source_target_pairs={{0,4},{4,0},{8,12},{12,8},{16,20},{20,16},{24,28},{28,24},{1,5},{5... | collective-permute-start | bytes 638984 | tf_op jit(solution)/shard_map/ppermute | solution.py:45
  28.5 10.2 %collective-permute-start.18 = (bf16[288,512]{1,0:T(8,128)(2,1)S(1)}, bf16[288,512]{1,0:T(8,128)(2,1)S(1)}, u32[]{:S(2)}, u32[]{:S(2)}) collective-permute-start(bf16[288,512]{1,0:T(8,128)(2,1)S(1)} %pad_maximum_fusion.2.refs_0_), channel_id=1, source_target_pairs={{0,24},{4,28},{8,16},{12,20},{16,8},{20,12},{24,0},{28,4},{1,25},{... | collective-permute-start | bytes 884744 | tf_op jit(solution)/shard_map/ppermute | solution.py:45
  32.3 6.4 %collective-permute-start.10 = (bf16[2,208,256]{2,1,0:T(8,128)(2,1)S(1)}, bf16[2,208,256]{2,1,0:T(8,128)(2,1)S(1)}, u32[]{:S(2)}, u32[]{:S(2)}) collective-permute-start(bf16[2,208,256]{2,1,0:T(8,128)(2,1)S(1)} %get-tuple-element.104), channel_id=1, source_target_pairs={{0,4},{4,0},{8,12},{12,8},{16,20},{20,16},{24,28},{28,24},{1,5},{5... | collective-permute-start | bytes 638984 | tf_op jit(solution)/shard_map/ppermute | solution.py:45
  32.3 6.3 %collective-permute-start.11 = (bf16[2,208,256]{2,1,0:T(8,128)(2,1)S(1)}, bf16[2,208,256]{2,1,0:T(8,128)(2,1)S(1)}, u32[]{:S(2)}, u32[]{:S(2)}) collective-permute-start(bf16[2,208,256]{2,1,0:T(8,128)(2,1)S(1)} %get-tuple-element.105), channel_id=1, source_target_pairs={{4,8},{12,16},{20,24},{8,4},{16,12},{24,20},{5,9},{13,17},{21,25},... | collective-permute-start | bytes 638984 | tf_op jit(solution)/shard_map/ppermute | solution.py:106
  33.0 12.9 %collective-permute-start.16 = (bf16[288,512]{1,0:T(8,128)(2,1)S(1)}, bf16[288,512]{1,0:T(8,128)(2,1)S(1)}, u32[]{:S(2)}, u32[]{:S(2)}) collective-permute-start(bf16[288,512]{1,0:T(8,128)(2,1)S(1)} %pad_maximum_fusion.2.refs_0_), channel_id=1, source_target_pairs={{0,16},{4,20},{8,24},{12,28},{16,0},{20,4},{24,8},{28,12},{1,17},{... | collective-permute-start | bytes 884744 | tf_op jit(solution)/shard_map/ppermute | solution.py:45
  37.1 12.1 %collective-permute-start.15 = (bf16[288,512]{1,0:T(8,128)(2,1)S(1)}, bf16[288,512]{1,0:T(8,128)(2,1)S(1)}, u32[]{:S(2)}, u32[]{:S(2)}) collective-permute-start(bf16[288,512]{1,0:T(8,128)(2,1)S(1)} %pad_maximum_fusion.2.refs_0_), channel_id=1, source_target_pairs={{0,8},{4,12},{8,0},{12,4},{16,24},{20,28},{24,16},{28,20},{1,9},{5... | collective-permute-start | bytes 884744 | tf_op jit(solution)/shard_map/ppermute | solution.py:45
  38.7 10.5 %collective-permute-start.17 = (bf16[288,512]{1,0:T(8,128)(2,1)S(1)}, bf16[288,512]{1,0:T(8,128)(2,1)S(1)}, u32[]{:S(2)}, u32[]{:S(2)}) collective-permute-start(bf16[288,512]{1,0:T(8,128)(2,1)S(1)} %pad_maximum_fusion.2.refs_0_), channel_id=1, source_target_pairs={{0,4},{4,0},{8,12},{12,8},{16,20},{20,16},{24,28},{28,24},{1,5},{5... | collective-permute-start | bytes 884744 | tf_op jit(solution)/shard_map/ppermute | solution.py:45
  43.3 5.9 %collective-permute-start.19 = (bf16[288,512]{1,0:T(8,128)(2,1)S(1)}, bf16[288,512]{1,0:T(8,128)(2,1)S(1)}, u32[]{:S(2)}, u32[]{:S(2)}) collective-permute-start(bf16[288,512]{1,0:T(8,128)(2,1)S(1)} %collective-permute-done.18.refs_6_), channel_id=1, source_target_pairs={{0,4},{4,0},{8,12},{12,8},{16,20},{20,16},{24,28},{28,24},{1,5},{5... | collective-permute-start | bytes 884744 | tf_op jit(solution)/shard_map/ppermute | solution.py:45
  49.2 1.6 %collective-permute-start.20 = (bf16[288,512]{1,0:T(8,128)(2,1)S(1)}, bf16[288,512]{1,0:T(8,128)(2,1)S(1)}, u32[]{:S(2)}, u32[]{:S(2)}) collective-permute-start(bf16[288,512]{1,0:T(8,128)(2,1)S(1)} %collective-permute-done.15.refs_2_), channel_id=1, source_target_pairs={{0,4},{4,0},{8,12},{12,8},{16,20},{20,16},{24,28},{28,24},{1,5},{5... | collective-permute-start | bytes 884744 | tf_op jit(solution)/shard_map/ppermute | solution.py:45
  49.2 2.0 %collective-permute-start.21 = (bf16[288,512]{1,0:T(8,128)(2,1)S(1)}, bf16[288,512]{1,0:T(8,128)(2,1)S(1)}, u32[]{:S(2)}, u32[]{:S(2)}) collective-permute-start(bf16[288,512]{1,0:T(8,128)(2,1)S(1)} %collective-permute-done.16.refs_4_), channel_id=1, source_target_pairs={{0,4},{4,0},{8,12},{12,8},{16,20},{20,16},{24,28},{28,24},{1,5},{5... | collective-permute-start | bytes 884744 | tf_op jit(solution)/shard_map/ppermute | solution.py:45
  55.6 1.3 %collective-permute-start.22 = (f32[2,24,256]{2,1,0:T(8,128)S(1)}, f32[2,24,256]{2,1,0:T(8,128)S(1)}, u32[]{:S(2)}, u32[]{:S(2)}) collective-permute-start(f32[2,24,256]{2,1,0:T(8,128)S(1)} %get-tuple-element.121), channel_id=1, source_target_pairs={{0,4},{4,0},{8,12},{12,8},{16,20},{20,16},{24,28},{28,24},{1,5},{5... | collective-permute-start | bytes 147464 | tf_op jit(solution)/shard_map/ppermute | solution.py:45
  55.8 1.1 collective-permute-start.23
  63.3 7.2 %collective-permute-start.26 = (bf16[4,288,512]{2,1,0:T(8,128)(2,1)S(1)}, bf16[4,288,512]{2,1,0:T(8,128)(2,1)S(1)}, u32[]{:S(2)}, u32[]{:S(2)}) collective-permute-start(bf16[4,288,512]{2,1,0:T(8,128)(2,1)S(1)} %get-tuple-element.130), channel_id=1, source_target_pairs={{0,4},{4,0},{8,12},{12,8},{16,20},{20,16},{24,28},{28,24},{1,5},{5... | collective-permute-start | bytes 3538952 | tf_op jit(solution)/shard_map/ppermute | solution.py:45
  68.0 6.4 %collective-permute-start.24 = (bf16[2,192,256]{2,1,0:T(8,128)(2,1)S(1)}, bf16[2,192,256]{2,1,0:T(8,128)(2,1)S(1)}, u32[]{:S(2)}, u32[]{:S(2)}) collective-permute-start(bf16[2,192,256]{2,1,0:T(8,128)(2,1)S(1)} %get-tuple-element.127), channel_id=1, source_target_pairs={{0,4},{4,0},{8,12},{12,8},{16,20},{20,16},{24,28},{28,24},{1,5},{5... | collective-permute-start | bytes 589832 | tf_op jit(solution)/shard_map/ppermute | solution.py:45
  68.1 6.3 %collective-permute-start.25 = (bf16[2,192,256]{2,1,0:T(8,128)(2,1)S(1)}, bf16[2,192,256]{2,1,0:T(8,128)(2,1)S(1)}, u32[]{:S(2)}, u32[]{:S(2)}) collective-permute-start(bf16[2,192,256]{2,1,0:T(8,128)(2,1)S(1)} %get-tuple-element.128), channel_id=1, source_target_pairs={{4,8},{12,16},{20,24},{8,4},{16,12},{24,20},{5,9},{13,17},{21,25},... | collective-permute-start | bytes 589832 | tf_op jit(solution)/shard_map/ppermute | solution.py:106
  70.9 13.5 %collective-permute-start.30 = (bf16[288,512]{1,0:T(8,128)(2,1)S(1)}, bf16[288,512]{1,0:T(8,128)(2,1)S(1)}, u32[]{:S(2)}, u32[]{:S(2)}) collective-permute-start(bf16[288,512]{1,0:T(8,128)(2,1)S(1)} %get-tuple-element.164), channel_id=1, source_target_pairs={{0,24},{4,28},{8,16},{12,20},{16,8},{20,12},{24,0},{28,4},{1,25},{... | collective-permute-start | bytes 884744 | tf_op jit(solution)/shard_map/ppermute | solution.py:45
  72.7 17.2 %collective-permute-start.28 = (bf16[288,512]{1,0:T(8,128)(2,1)S(1)}, bf16[288,512]{1,0:T(8,128)(2,1)S(1)}, u32[]{:S(2)}, u32[]{:S(2)}) collective-permute-start(bf16[288,512]{1,0:T(8,128)(2,1)S(1)} %get-tuple-element.165), channel_id=1, source_target_pairs={{0,8},{4,12},{8,0},{12,4},{16,24},{20,28},{24,16},{28,20},{1,9},{5... | collective-permute-start | bytes 884744 | tf_op jit(solution)/shard_map/ppermute | solution.py:45
  74.3 15.6 %collective-permute-start.29 = (bf16[288,512]{1,0:T(8,128)(2,1)S(1)}, bf16[288,512]{1,0:T(8,128)(2,1)S(1)}, u32[]{:S(2)}, u32[]{:S(2)}) collective-permute-start(bf16[288,512]{1,0:T(8,128)(2,1)S(1)} %get-tuple-element.166), channel_id=1, source_target_pairs={{0,16},{4,20},{8,24},{12,28},{16,0},{20,4},{24,8},{28,12},{1,17},{... | collective-permute-start | bytes 884744 | tf_op jit(solution)/shard_map/ppermute | solution.py:45
  74.4 3.6 %copy-start.3 = (bf16[2,4,64,2048]{3,2,1,0:T(8,128)(2,1)S(1)}, bf16[2,4,64,2048]{3,2,1,0:T(8,128)(2,1)}, u32[]{:S(2)}) copy-start(bf16[2,4,64,2048]{3,2,1,0:T(8,128)(2,1)} %five.3) | copy-start | bytes 6291460
  80.9 9.2 %collective-permute-start.27 = (bf16[4,416,256]{2,1,0:T(8,128)(2,1)S(1)}, bf16[4,416,256]{2,1,0:T(8,128)(2,1)S(1)}, u32[]{:S(2)}, u32[]{:S(2)}) collective-permute-start(bf16[4,416,256]{2,1,0:T(8,128)(2,1)S(1)} %get-tuple-element.140), channel_id=1, source_target_pairs={{0,4},{4,0},{8,12},{12,8},{16,20},{20,16},{24,28},{28,24},{1,5},{5... | collective-permute-start | bytes 2555912 | tf_op jit(solution)/shard_map/ppermute | solution.py:45
  90.3 8.2 %collective-permute-start.34 = (bf16[416,256]{1,0:T(8,128)(2,1)S(1)}, bf16[416,256]{1,0:T(8,128)(2,1)S(1)}, u32[]{:S(2)}, u32[]{:S(2)}) collective-permute-start(bf16[416,256]{1,0:T(8,128)(2,1)S(1)} %get-tuple-element.143), channel_id=1, source_target_pairs={{0,8},{4,12},{8,0},{12,4},{16,24},{20,28},{24,16},{28,20},{1,9},{5... | collective-permute-start | bytes 638984 | tf_op jit(solution)/shard_map/ppermute | solution.py:45
  91.3 10.8 %collective-permute-start.35 = (bf16[416,256]{1,0:T(8,128)(2,1)S(1)}, bf16[416,256]{1,0:T(8,128)(2,1)S(1)}, u32[]{:S(2)}, u32[]{:S(2)}) collective-permute-start(bf16[416,256]{1,0:T(8,128)(2,1)S(1)} %get-tuple-element.144), channel_id=1, source_target_pairs={{0,16},{4,20},{8,24},{12,28},{16,0},{20,4},{24,8},{28,12},{1,17},{... | collective-permute-start | bytes 638984 | tf_op jit(solution)/shard_map/ppermute | solution.py:45
  92.8 9.4 %collective-permute-start.36 = (bf16[416,256]{1,0:T(8,128)(2,1)S(1)}, bf16[416,256]{1,0:T(8,128)(2,1)S(1)}, u32[]{:S(2)}, u32[]{:S(2)}) collective-permute-start(bf16[416,256]{1,0:T(8,128)(2,1)S(1)} %get-tuple-element.145), channel_id=1, source_target_pairs={{0,24},{4,28},{8,16},{12,20},{16,8},{20,12},{24,0},{28,4},{1,25},{... | collective-permute-start | bytes 638984 | tf_op jit(solution)/shard_map/ppermute | solution.py:45
  93.9 8.4 %collective-permute-start.33 = (bf16[72,512]{1,0:T(8,128)(2,1)S(1)}, bf16[72,512]{1,0:T(8,128)(2,1)S(1)}, u32[]{:S(2)}, u32[]{:S(2)}) collective-permute-start(bf16[72,512]{1,0:T(8,128)(2,1)S(1)} %get-tuple-element.171), channel_id=1, source_target_pairs={{0,3},{1,2},{2,1},{3,0},{4,7},{5,6},{6,5},{7,4},{8,11},{9,10},{10,... | collective-permute-start | bytes 221192 | tf_op jit(solution)/shard_map/ppermute | solution.py:45
  95.8 6.5 %collective-permute-start.32 = (bf16[72,512]{1,0:T(8,128)(2,1)S(1)}, bf16[72,512]{1,0:T(8,128)(2,1)S(1)}, u32[]{:S(2)}, u32[]{:S(2)}) collective-permute-start(bf16[72,512]{1,0:T(8,128)(2,1)S(1)} %get-tuple-element.172), channel_id=1, source_target_pairs={{0,2},{1,3},{2,0},{3,1},{4,6},{5,7},{6,4},{7,5},{8,10},{9,11},{10,... | collective-permute-start | bytes 221192 | tf_op jit(solution)/shard_map/ppermute | solution.py:45
  98.6 4.5 %collective-permute-start.31 = (bf16[72,512]{1,0:T(8,128)(2,1)S(1)}, bf16[72,512]{1,0:T(8,128)(2,1)S(1)}, u32[]{:S(2)}, u32[]{:S(2)}) collective-permute-start(bf16[72,512]{1,0:T(8,128)(2,1)S(1)} %get-tuple-element.173), channel_id=1, source_target_pairs={{0,1},{1,0},{2,3},{3,2},{4,5},{5,4},{6,7},{7,6},{8,9},{9,8},{10,11... | collective-permute-start | bytes 221192 | tf_op jit(solution)/shard_map/ppermute | solution.py:45
  102.2 5.5 %copy-start.4 = (f32[2,72,256]{2,1,0:T(8,128)S(1)}, f32[2,72,256]{2,1,0:T(8,128)}, u32[]{:S(2)}) copy-start(f32[2,72,256]{2,1,0:T(8,128)} %refs_3_.3) | copy-start | bytes 442372
  102.3 5.5 %copy-start.6 = (f32[2,72,256]{2,1,0:T(8,128)S(1)}, f32[2,72,256]{2,1,0:T(8,128)}, u32[]{:S(2)}) copy-start(f32[2,72,256]{2,1,0:T(8,128)} %refs_4_.3) | copy-start | bytes 442372
  102.3 5.5 %copy-start.7 = (f32[2,72,256]{2,1,0:T(8,128)S(1)}, f32[2,72,256]{2,1,0:T(8,128)}, u32[]{:S(2)}) copy-start(f32[2,72,256]{2,1,0:T(8,128)} %refs_5_.3) | copy-start | bytes 442372
  103.1 7.8 %copy-start.5 = (f32[64,256]{1,0:T(8,128)S(1)}, f32[64,256]{1,0:T(8,128)}, u32[]{:S(2)}) copy-start(f32[64,256]{1,0:T(8,128)} %refs_6_.3) | copy-start | bytes 196612
  103.1 7.8 %copy-start.8 = (f32[32,256]{1,0:T(8,128)S(1)}, f32[32,256]{1,0:T(8,128)}, u32[]{:S(2)}) copy-start(f32[32,256]{1,0:T(8,128)} %refs_3_.2) | copy-start | bytes 98308
  103.1 7.8 %copy-start.11 = (f32[64,256]{1,0:T(8,128)S(1)}, f32[64,256]{1,0:T(8,128)}, u32[]{:S(2)}) copy-start(f32[64,256]{1,0:T(8,128)} %refs_7_.3) | copy-start | bytes 196612
  103.1 7.8 %copy-start.12 = (f32[64,256]{1,0:T(8,128)S(1)}, f32[64,256]{1,0:T(8,128)}, u32[]{:S(2)}) copy-start(f32[64,256]{1,0:T(8,128)} %refs_8_.1) | copy-start | bytes 196612
  103.2 7.8 %copy-start.15 = (f32[72,12]{0,1:T(8,128)S(1)}, f32[72,12]{0,1:T(8,128)}, u32[]{:S(2)}) copy-start(f32[72,12]{0,1:T(8,128)} %param.31) | copy-start | bytes 10372
  103.2 7.8 %copy-start.16 = (f32[32,256]{1,0:T(8,128)S(1)}, f32[32,256]{1,0:T(8,128)}, u32[]{:S(2)}) copy-start(f32[32,256]{1,0:T(8,128)} %refs_4_.2) | copy-start | bytes 98308
  103.2 7.8 %copy-start.17 = (f32[32,256]{1,0:T(8,128)S(1)}, f32[32,256]{1,0:T(8,128)}, u32[]{:S(2)}) copy-start(f32[32,256]{1,0:T(8,128)} %refs_5_.2) | copy-start | bytes 98308
  103.2 7.7 %copy-start.20 = (f32[72,12]{0,1:T(8,128)S(1)}, f32[72,12]{0,1:T(8,128)}, u32[]{:S(2)}) copy-start(f32[72,12]{0,1:T(8,128)} %param.35) | copy-start | bytes 10372
  103.2 7.7 %copy-start.21 = (f32[72,12]{0,1:T(8,128)S(1)}, f32[72,12]{0,1:T(8,128)}, u32[]{:S(2)}) copy-start(f32[72,12]{0,1:T(8,128)} %param.39) | copy-start | bytes 10372
  103.3 6.6 %collective-permute-start.39 = (bf16[104,256]{1,0:T(8,128)(2,1)S(1)}, bf16[104,256]{1,0:T(8,128)(2,1)S(1)}, u32[]{:S(2)}, u32[]{:S(2)}) collective-permute-start(bf16[104,256]{1,0:T(8,128)(2,1)S(1)} %get-tuple-element.174), channel_id=1, source_target_pairs={{0,3},{1,2},{2,1},{3,0},{4,7},{5,6},{6,5},{7,4},{8,11},{9,10},{10,... | collective-permute-start | bytes 159752 | tf_op jit(solution)/shard_map/ppermute | solution.py:45
  105.5 5.4 %collective-permute-start.38 = (bf16[104,256]{1,0:T(8,128)(2,1)S(1)}, bf16[104,256]{1,0:T(8,128)(2,1)S(1)}, u32[]{:S(2)}, u32[]{:S(2)}) collective-permute-start(bf16[104,256]{1,0:T(8,128)(2,1)S(1)} %get-tuple-element.175), channel_id=1, source_target_pairs={{0,2},{1,3},{2,0},{3,1},{4,6},{5,7},{6,4},{7,5},{8,10},{9,11},{10,... | collective-permute-start | bytes 159752 | tf_op jit(solution)/shard_map/ppermute | solution.py:45
  105.5 5.4 %collective-permute-start.37 = (bf16[104,256]{1,0:T(8,128)(2,1)S(1)}, bf16[104,256]{1,0:T(8,128)(2,1)S(1)}, u32[]{:S(2)}, u32[]{:S(2)}) collective-permute-start(bf16[104,256]{1,0:T(8,128)(2,1)S(1)} %get-tuple-element.176), channel_id=1, source_target_pairs={{0,1},{1,0},{2,3},{3,2},{4,5},{5,4},{6,7},{7,6},{8,9},{9,8},{10,11... | collective-permute-start | bytes 159752 | tf_op jit(solution)/shard_map/ppermute | solution.py:45

commit v6 on v5

--- a/solution.py
+++ b/solution.py
@@ -462,15 +462,17 @@
         mismatch = jnp.concatenate(partial, axis=1)
         weight = jnp.concatenate(weights, axis=1)
         magnitude = jnp.abs(mismatch)
+        ratio = mismatch * (1.0 / box_beta)
         losses = weight * jnp.where(
-            magnitude < box_beta, 0.5 * mismatch * mismatch / box_beta, magnitude - 0.5 * box_beta
+            magnitude < box_beta, 0.5 * mismatch * ratio, magnitude - 0.5 * box_beta
         )
         for padded, own, lines in plan:
             for line in range(padded + 1, padded + 1 + lines):
                 summed = summed + losses[:, line * width : (line + 1) * width]
-        middle = weight * jnp.clip(mismatch / box_beta, -1.0, 1.0) * inverse
+        middle = weight * jnp.clip(ratio, -1.0, 1.0) * inverse
         middle = middle.astype(bf16).astype(f32)
         shifted = [turned(middle, -1, 1, width), middle, turned(middle, 1, 1, width)]
+        shifted = [value.astype(bf16) for value in shifted]
         for i in range(3):
             for j in range(3):
                 for padded, own, lines in plan:
@@ -478,7 +480,7 @@
                     taps[
                         (3 * i + j) * DELTA_ROWS : (3 * i + j + 1) * DELTA_ROWS,
                         own * width : (own + lines) * width,
-                    ] = shifted[j][:, at : at + lines * width].astype(bf16)
+                    ] = shifted[j][:, at : at + lines * width]
         around = taps[...]
         lines_all = levels.shape[1]
         total_grad = total_grad + dot(around, levels[b].reshape(lines_all * width, channels))
@@ -734,7 +736,6 @@
     laterals = gathered_high(lateral)
 
     conv = jnp.concatenate([output_conv[0], output_conv[1]], axis=1).astype(bf16)
-    conv, _ = lax.optimization_barrier((conv, lateral))
     conv = jnp.concatenate(gathered_batch(conv))
 
     lines = height + low_height + low_height // 2

time: 112 us -> 111 us (level)
  waiting for transfers between devices: 30.1 us -> 26 us
  starting transfers between devices: 49.8 us -> 52.3 us
    ppermute x37, waiting for transfers between devices: 30.1 us -> 25.9 us  [sent(): return lax.ppermute(value, axis, [(i, i ^ mask) for i in range(count)])]
    ppermute x37, starting transfers between devices: 47.8 us -> 50.4 us  [sent(): return lax.ppermute(value, axis, [(i, i ^ mask) for i in range(count)])]
  transfers between devices with their start and end apart: 40 -> 40, of which waited for: 17 -> 16; matrix products, arithmetic and copies ran while one was open for 1% -> 2% of each run, Pallas kernels for 9% -> 9%
where the time goes in v6:
time: 111 us; the launch traced here: 110 us
  starting transfers between devices  52.3 us (47%)
  waiting for transfers between devices  26 us (23%)
  Pallas kernels  23.8 us (21%)
  local copies, waits for them, and re-layouts  5.09 us (5%)
  other arithmetic  1.6 us (1%)
  between operations  1.46 us (1%)
    ppermute x37, starting transfers between devices, sent(): return lax.ppermute(value, axis, [(i, i ^ mask) for i in range(count)])  50.4 us
    ppermute x37, waiting for transfers between devices, sent(): return lax.ppermute(value, axis, [(i, i ^ mask) for i in range(count)])  25.9 us
    pallas_call x12, Pallas kernels, call(): pl.pallas_call(kernel, out_shape=list(outs), in_specs=[hbm] * apart + [vm...  23.8 us
    unnamed x55, local copies, waits for them, and re-layouts  4.02 us
  transfers between devices with their start and end apart: 40, of which 16 were waited for; matrix products, arithmetic and copies ran while one was open for 2% of the time, Pallas kernels for 9%

profile of v6, /device:TPU:0, one launch (start us, length us, event | category | flops | bytes accessed | tf_op | source)
XLA Modules:
  0.0 110.3 jit_solution(2444945071951376464)
XLA Ops:
  0.7 1.7 %pack.1 = bf16[104,256]{1,0:T(8,128)(2,1)} custom-call(f32[32,256]{1,0:T(8,128)} %refs_3_.2, f32[64,256]{1,0:T(8,128)} %refs_6_.3, f32[12,72]{1,0:T(8,128)} %bitcast.130, s32[2,3,8,128]{3,2,1,0:T(8,128)} %bitcast.124, s32[2,3,4,64]{3,2,1,0:T(4,128)} %bitcast.128, s32[2,3,2,32]{3,2,1,0:T(2,128)} %bitcast.133), custom_call_target="tpu_custom_call" | custom-call | bytes 187264 | tf_op jit(solution)/shard_map/pack/pallas_call | solution.py:118
  2.4 5.1 %collective-permute-start.2 = (bf16[104,256]{1,0:T(8,128)(2,1)}, bf16[104,256]{1,0:T(8,128)(2,1)S(1)}, u32[]{:S(2)}, u32[]{:S(2)}) collective-permute-start(bf16[104,256]{1,0:T(8,128)(2,1)} %pack.1), channel_id=1, source_target_pairs={{0,3},{1,2},{2,1},{3,0},{4,7},{5,6},{6,5},{7,4},{8,11},{9,10},{10,... | collective-permute-start | bytes 159752 | tf_op jit(solution)/shard_map/ppermute | solution.py:45
  7.6 0.6 collective-permute-start
  8.2 0.9 fusion.17
  9.2 3.8 %collective-permute-start.14 = (bf16[72,512]{1,0:T(8,128)(2,1)S(1)}, bf16[72,512]{1,0:T(8,128)(2,1)S(1)}, u32[]{:S(2)}, u32[]{:S(2)}) collective-permute-start(bf16[72,512]{1,0:T(8,128)(2,1)S(1)} %pad_maximum_fusion.4), channel_id=1, source_target_pairs={{0,3},{1,2},{2,1},{3,0},{4,7},{5,6},{6,5},{7,4},{8,11},{9,10},{10,... | collective-permute-start | bytes 221192 | tf_op jit(solution)/shard_map/ppermute | solution.py:45
  13.0 1.1 %collective-permute-done.1 = bf16[104,256]{1,0:T(8,128)(2,1)S(1)} collective-permute-done((bf16[104,256]{1,0:T(8,128)(2,1)}, bf16[104,256]{1,0:T(8,128)(2,1)S(1)}, u32[]{:S(2)}, u32[]{:S(2)}) %collective-permute-start.1) | collective-permute-done | bytes 53280 | tf_op jit(solution)/shard_map/ppermute | solution.py:45
  14.1 0.8 pad_maximum_fusion.3
  15.2 2.5 %collective-permute-start.5 = (bf16[416,256]{1,0:T(8,128)(2,1)S(1)}, bf16[416,256]{1,0:T(8,128)(2,1)S(1)}, u32[]{:S(2)}, u32[]{:S(2)}) collective-permute-start(bf16[416,256]{1,0:T(8,128)(2,1)S(1)} %constant_dynamic-update-slice_fusion.refs_0_), channel_id=1, source_target_pairs={{0,24},{4,28},{8,16},{12,20},{16,8},{20,12},{24,0},{28,4},{1,25},{... | collective-permute-start | bytes 638984 | tf_op jit(solution)/shard_map/ppermute | solution.py:45
  17.7 0.5 collective-permute-start.4
  18.2 0.5 collective-permute-start.3
  18.8 0.7 collective-permute-start.13
  19.5 1.2 %collective-permute-start.12 = (bf16[72,512]{1,0:T(8,128)(2,1)S(1)}, bf16[72,512]{1,0:T(8,128)(2,1)S(1)}, u32[]{:S(2)}, u32[]{:S(2)}) collective-permute-start(bf16[72,512]{1,0:T(8,128)(2,1)S(1)} %pad_maximum_fusion.4), channel_id=1, source_target_pairs={{0,1},{1,0},{2,3},{3,2},{4,5},{5,4},{6,7},{7,6},{8,9},{9,8},{10,11... | collective-permute-start | bytes 221192 | tf_op jit(solution)/shard_map/ppermute | solution.py:45
  20.7 2.2 %copy-done = bf16[2,8,128,1024]{3,2,1,0:T(8,128)(2,1)S(1)} copy-done((bf16[2,8,128,1024]{3,2,1,0:T(8,128)(2,1)S(1)}, bf16[2,8,128,1024]{3,2,1,0:T(8,128)(2,1)}, u32[]{:S(2)}) %copy-start) | copy-done | bytes 4194328
  22.9 1.6 %copy-done.2 = bf16[2,4,64,2048]{3,2,1,0:T(8,128)(2,1)S(1)} copy-done((bf16[2,4,64,2048]{3,2,1,0:T(8,128)(2,1)S(1)}, bf16[2,4,64,2048]{3,2,1,0:T(8,128)(2,1)}, u32[]{:S(2)}) %copy-start.2) | copy-done | bytes 2097176
  24.5 0.2 planes.1
  24.7 0.9 collective-permute-done.4.refs_4_
  25.7 0.5 collective-permute-start.7
  26.2 0.5 collective-permute-start.9
  26.8 1.7 %collective-permute-start.18 = (bf16[288,512]{1,0:T(8,128)(2,1)S(1)}, bf16[288,512]{1,0:T(8,128)(2,1)S(1)}, u32[]{:S(2)}, u32[]{:S(2)}) collective-permute-start(bf16[288,512]{1,0:T(8,128)(2,1)S(1)} %pad_maximum_fusion.2.refs_0_), channel_id=1, source_target_pairs={{0,24},{4,28},{8,16},{12,20},{16,8},{20,12},{24,0},{28,4},{1,25},{... | collective-permute-start | bytes 884744 | tf_op jit(solution)/shard_map/ppermute | solution.py:45
  28.5 2.0 %laterals.1 = (bf16[2,8,128,256]{3,2,1,0:T(8,128)(2,1)S(1)}, bf16[2,4,64,256]{3,2,1,0:T(8,128)(2,1)S(1)}, bf16[2,208,256]{2,1,0:T(8,128)(2,1)S(1)}, bf16[2,208,256]{2,1,0:T(8,128)(2,1)S(1)}) custom-call(bf16[2,8,128,1024]{3,2,1,0:T(8,128)(2,1)S(1)} %copy-done.1, bf16[2,4,64,2048]{3,2,1,0:T(8,128)(2,1)S(1)} %copy-done.2, ...), custom_call_target="tpu_custom_call" | custom-call | flops 1610612736 | bytes 9961472 | tf_op jit(solution)/shard_map/laterals/pallas_call | solution.py:118
  30.6 0.7 collective-permute-start.11
  31.3 4.1 %collective-permute-start.16 = (bf16[288,512]{1,0:T(8,128)(2,1)S(1)}, bf16[288,512]{1,0:T(8,128)(2,1)S(1)}, u32[]{:S(2)}, u32[]{:S(2)}) collective-permute-start(bf16[288,512]{1,0:T(8,128)(2,1)S(1)} %pad_maximum_fusion.2.refs_0_), channel_id=1, source_target_pairs={{0,16},{4,20},{8,24},{12,28},{16,0},{20,4},{24,8},{28,12},{1,17},{... | collective-permute-start | bytes 884744 | tf_op jit(solution)/shard_map/ppermute | solution.py:45
  35.4 0.7 collective-permute-start.15
  36.1 0.9 head_weights.1
  37.0 4.5 %collective-permute-start.17 = (bf16[288,512]{1,0:T(8,128)(2,1)S(1)}, bf16[288,512]{1,0:T(8,128)(2,1)S(1)}, u32[]{:S(2)}, u32[]{:S(2)}) collective-permute-start(bf16[288,512]{1,0:T(8,128)(2,1)S(1)} %pad_maximum_fusion.2.refs_0_), channel_id=1, source_target_pairs={{0,4},{4,0},{8,12},{12,8},{16,20},{20,16},{24,28},{28,24},{1,5},{5... | collective-permute-start | bytes 884744 | tf_op jit(solution)/shard_map/ppermute | solution.py:45
  41.5 2.7 %collective-permute-done.16.refs_4_ = bf16[288,512]{1,0:T(8,128)(2,1)S(1)} collective-permute-done((bf16[288,512]{1,0:T(8,128)(2,1)S(1)}, bf16[288,512]{1,0:T(8,128)(2,1)S(1)}, u32[]{:S(2)}, u32[]{:S(2)}) %collective-permute-start.16) | collective-permute-done | bytes 294944 | tf_op jit(solution)/shard_map/ppermute | solution.py:45
  44.2 3.3 %collective-permute-done.15.refs_2_ = bf16[288,512]{1,0:T(8,128)(2,1)S(1)} collective-permute-done((bf16[288,512]{1,0:T(8,128)(2,1)S(1)}, bf16[288,512]{1,0:T(8,128)(2,1)S(1)}, u32[]{:S(2)}, u32[]{:S(2)}) %collective-permute-start.15) | collective-permute-done | bytes 294944 | tf_op jit(solution)/shard_map/ppermute | solution.py:45
  47.5 0.5 collective-permute-start.21
  48.0 1.1 collective-permute-done.20.refs_3_
  49.1 0.4 collective-permute-done.21.refs_5_
  49.5 4.4 %outputs.1 = (bf16[2,14,128,256]{3,2,1,0:T(8,128)(2,1)S(1)}, f32[2,16,2560]{2,1,0:T(8,128)S(1)}, f32[2,24,256]{2,1,0:T(8,128)S(1)}, f32[2,24,256]{2,1,0:T(8,128)...) custom-call(bf16[2,8,128,256]{3,2,1,0:T(8,128)(2,1)S(1)} %get-tuple-element.101.input_four, ...), custom_call_target="tpu_custom_call" | custom-call | flops 3019898880 | bytes 9248768 | tf_op jit(solution)/shard_map/outputs/pallas_call | solution.py:118
  53.9 0.2 collective-permute-start.22
  54.1 0.7 collective-permute-start.23
  54.7 0.4 collective-permute-done.22.pair_in
  55.2 2.7 %heads.1 = (f32[144,256]{1,0:T(8,128)S(1)}, bf16[2,8,128,256]{3,2,1,0:T(8,128)(2,1)S(1)}, bf16[2,4,64,256]{3,2,1,0:T(8,128)(2,1)S(1)}, bf16[2,192,256]{2,1,0:T(8...) custom-call(bf16[2,14,128,256]{3,2,1,0:T(8,128)(2,1)S(1)} %get-tuple-element.118.levels, ...), custom_call_target="tpu_custom_call" | custom-call | flops 792723456 | bytes 4841480 | tf_op jit(solution)/shard_map/heads/pallas_call | solution.py:118
  57.9 3.7 %conv_grads.1 = (bf16[4,288,512]{2,1,0:T(8,128)(2,1)S(1)}, bf16[4,288,512]{2,1,0:T(8,128)(2,1)S(1)}) custom-call(bf16[2,8,128,256]{3,2,1,0:T(8,128)(2,1)S(1)} %get-tuple-element.101.input_four, bf16[2,4,64,256]{3,2,1,0:T(8,128)(2,1)S(1)} %get-tuple-element.102.input_five, bf16[2,208,256]{2,1,0:T(8,128)(2,1)S(1)} %collective-permute-done.10.pair_in.pair_mask, ...), custom_call_target="tpu_custom_call" | custom-call | flops 3019898880 | bytes 5406720 | tf_op jit(solution)/shard_map/conv_grads/pallas_call | solution.py:118
  61.6 4.7 %collective-permute-start.26 = (bf16[4,288,512]{2,1,0:T(8,128)(2,1)S(1)}, bf16[4,288,512]{2,1,0:T(8,128)(2,1)S(1)}, u32[]{:S(2)}, u32[]{:S(2)}) collective-permute-start(bf16[4,288,512]{2,1,0:T(8,128)(2,1)S(1)} %get-tuple-element.128), channel_id=1, source_target_pairs={{0,4},{4,0},{8,12},{12,8},{16,20},{20,16},{24,28},{28,24},{1,5},{5... | collective-permute-start | bytes 3538952 | tf_op jit(solution)/shard_map/ppermute | solution.py:45
  66.4 0.7 collective-permute-start.25
  67.1 1.7 %collective-permute-done.26 = bf16[4,288,512]{2,1,0:T(8,128)(2,1)S(1)} collective-permute-done((bf16[4,288,512]{2,1,0:T(8,128)(2,1)S(1)}, bf16[4,288,512]{2,1,0:T(8,128)(2,1)S(1)}, u32[]{:S(2)}, u32[]{:S(2)}) %collective-permute-start.26) | collective-permute-done | bytes 1179680 | tf_op jit(solution)/shard_map/ppermute | solution.py:45
  68.8 0.4 fusion.16
  69.2 1.9 %collective-permute-start.30 = (bf16[288,512]{1,0:T(8,128)(2,1)S(1)}, bf16[288,512]{1,0:T(8,128)(2,1)S(1)}, u32[]{:S(2)}, u32[]{:S(2)}) collective-permute-start(bf16[288,512]{1,0:T(8,128)(2,1)S(1)} %get-tuple-element.162), channel_id=1, source_target_pairs={{0,24},{4,28},{8,16},{12,20},{16,8},{20,12},{24,0},{28,4},{1,25},{... | collective-permute-start | bytes 884744 | tf_op jit(solution)/shard_map/ppermute | solution.py:45
  71.1 1.6 %collective-permute-start.28 = (bf16[288,512]{1,0:T(8,128)(2,1)S(1)}, bf16[288,512]{1,0:T(8,128)(2,1)S(1)}, u32[]{:S(2)}, u32[]{:S(2)}) collective-permute-start(bf16[288,512]{1,0:T(8,128)(2,1)S(1)} %get-tuple-element.163), channel_id=1, source_target_pairs={{0,8},{4,12},{8,0},{12,4},{16,24},{20,28},{24,16},{28,20},{1,9},{5... | collective-permute-start | bytes 884744 | tf_op jit(solution)/shard_map/ppermute | solution.py:45
  72.7 3.6 %merged_grads.1 = (bf16[2048,256]{1,0:T(8,128)(2,1)S(1)}, bf16[512,256]{1,0:T(8,128)(2,1)S(1)}) custom-call(bf16[2,8,128,256]{3,2,1,0:T(8,128)(2,1)S(1)} %get-tuple-element.123.grad_four, bf16[2,4,64,256]{3,2,1,0:T(8,128)(2,1)S(1)} %get-tuple-element.124.grad_five, bf16[2,192,256]{2,1,0:T(8,128)(2,1)S(1)} %collective-permute-done.24.pair_in, ...), custom_call_target="tpu_custom_call" | custom-call | flops 3019898880 | bytes 5373952 | tf_op jit(solution)/shard_map/merged_grads/pallas_call | solution.py:118
  76.3 2.8 %lateral_grads.1 = (bf16[4,416,256]{2,1,0:T(8,128)(2,1)S(1)}, bf16[4,416,256]{2,1,0:T(8,128)(2,1)S(1)}) custom-call(bf16[2,8,128,1024]{3,2,1,0:T(8,128)(2,1)S(1)} %copy-done.1, bf16[2,4,64,2048]{3,2,1,0:T(8,128)(2,1)S(1)} %copy-done.3, bf16[2048,256]{1,0:T(8,128)(2,1)S(1)} %get-tuple-element.133.lat_four, bf16[512,256]{1,0:T(8,128)(2,1)S(1)} %get-tuple-element.134.lat_five, ...), custom_call_target="tpu_custom_call" | custom-call | flops 1 | bytes 9453572 | tf_op jit(solution)/shard_map/lateral_grads/pallas_call | solution.py:118
  79.1 3.5 %collective-permute-start.27 = (bf16[4,416,256]{2,1,0:T(8,128)(2,1)S(1)}, bf16[4,416,256]{2,1,0:T(8,128)(2,1)S(1)}, u32[]{:S(2)}, u32[]{:S(2)}) collective-permute-start(bf16[4,416,256]{2,1,0:T(8,128)(2,1)S(1)} %get-tuple-element.138), channel_id=1, source_target_pairs={{0,4},{4,0},{8,12},{12,8},{16,20},{20,16},{24,28},{28,24},{1,5},{5... | collective-permute-start | bytes 2555912 | tf_op jit(solution)/shard_map/ppermute | solution.py:45
  82.6 5.6 %collective-permute-done.28.refs_0_ = bf16[288,512]{1,0:T(8,128)(2,1)S(1)} collective-permute-done((bf16[288,512]{1,0:T(8,128)(2,1)S(1)}, bf16[288,512]{1,0:T(8,128)(2,1)S(1)}, u32[]{:S(2)}, u32[]{:S(2)}) %collective-permute-start.28) | collective-permute-done | bytes 294944 | tf_op jit(solution)/shard_map/ppermute | solution.py:45
  88.2 0.1 conv_total.1
  88.4 0.2 add_bitcast_fusion.4
  88.6 1.1 collective-permute-start.34
  89.7 1.4 %collective-permute-start.35 = (bf16[416,256]{1,0:T(8,128)(2,1)S(1)}, bf16[416,256]{1,0:T(8,128)(2,1)S(1)}, u32[]{:S(2)}, u32[]{:S(2)}) collective-permute-start(bf16[416,256]{1,0:T(8,128)(2,1)S(1)} %get-tuple-element.142), channel_id=1, source_target_pairs={{0,16},{4,20},{8,24},{12,28},{16,0},{20,4},{24,8},{28,12},{1,17},{... | collective-permute-start | bytes 638984 | tf_op jit(solution)/shard_map/ppermute | solution.py:45
  91.1 1.1 collective-permute-start.36
  92.2 2.0 %collective-permute-start.33 = (bf16[72,512]{1,0:T(8,128)(2,1)S(1)}, bf16[72,512]{1,0:T(8,128)(2,1)S(1)}, u32[]{:S(2)}, u32[]{:S(2)}) collective-permute-start(bf16[72,512]{1,0:T(8,128)(2,1)S(1)} %get-tuple-element.169), channel_id=1, source_target_pairs={{0,3},{1,2},{2,1},{3,0},{4,7},{5,6},{6,5},{7,4},{8,11},{9,10},{10,... | collective-permute-start | bytes 221192 | tf_op jit(solution)/shard_map/ppermute | solution.py:45
  94.2 0.1 collective-permute-start.32
  94.4 2.5 %collective-permute-done.34 = bf16[416,256]{1,0:T(8,128)(2,1)S(1)} collective-permute-done((bf16[416,256]{1,0:T(8,128)(2,1)S(1)}, bf16[416,256]{1,0:T(8,128)(2,1)S(1)}, u32[]{:S(2)}, u32[]{:S(2)}) %collective-permute-start.34) | collective-permute-done | bytes 213024 | tf_op jit(solution)/shard_map/ppermute | solution.py:45
  96.9 0.6 collective-permute-start.31
  97.5 3.0 %collective-permute-done.35 = bf16[416,256]{1,0:T(8,128)(2,1)S(1)} collective-permute-done((bf16[416,256]{1,0:T(8,128)(2,1)S(1)}, bf16[416,256]{1,0:T(8,128)(2,1)S(1)}, u32[]{:S(2)}, u32[]{:S(2)}) %collective-permute-start.35) | collective-permute-done | bytes 213024 | tf_op jit(solution)/shard_map/ppermute | solution.py:45
  100.6 0.4 collective-permute-done.32.refs_1_
  101.0 0.7 collective-permute-done.31.refs_0_
  102.0 2.0 %collective-permute-start.39 = (bf16[104,256]{1,0:T(8,128)(2,1)S(1)}, bf16[104,256]{1,0:T(8,128)(2,1)S(1)}, u32[]{:S(2)}, u32[]{:S(2)}) collective-permute-start(bf16[104,256]{1,0:T(8,128)(2,1)S(1)} %get-tuple-element.172), channel_id=1, source_target_pairs={{0,3},{1,2},{2,1},{3,0},{4,7},{5,6},{6,5},{7,4},{8,11},{9,10},{10,... | collective-permute-start | bytes 159752 | tf_op jit(solution)/shard_map/ppermute | solution.py:45
  104.0 2.5 %collective-permute-start.37 = (bf16[104,256]{1,0:T(8,128)(2,1)S(1)}, bf16[104,256]{1,0:T(8,128)(2,1)S(1)}, u32[]{:S(2)}, u32[]{:S(2)}) collective-permute-start(bf16[104,256]{1,0:T(8,128)(2,1)S(1)} %get-tuple-element.174), channel_id=1, source_target_pairs={{0,1},{1,0},{2,3},{3,2},{4,5},{5,4},{6,7},{7,6},{8,9},{9,8},{10,11... | collective-permute-start | bytes 159752 | tf_op jit(solution)/shard_map/ppermute | solution.py:45
  106.5 0.8 conv_step.1
  107.3 0.7 collective-permute-done.39.refs_2_
  108.1 1.1 %collective-permute-done.38.refs_1_ = bf16[104,256]{1,0:T(8,128)(2,1)S(1)} collective-permute-done((bf16[104,256]{1,0:T(8,128)(2,1)S(1)}, bf16[104,256]{1,0:T(8,128)(2,1)S(1)}, u32[]{:S(2)}, u32[]{:S(2)}) %collective-permute-start.38) | collective-permute-done | bytes 53280 | tf_op jit(solution)/shard_map/ppermute | solution.py:45
  109.3 0.8 lateral_step.1
  (102 shorter events, 1.0 us)
Async XLA Ops:
  0.6 20.0 %copy-start.19 = (s32[2,2,32,3]{2,1,3,0:T(2,128)S(1)}, s32[2,2,32,3]{2,1,3,0:T(2,128)}, u32[]{:S(2)}) copy-start(s32[2,2,32,3]{2,1,3,0:T(2,128)} %param.27) | copy-start | bytes 4612
  0.7 20.0 %copy-start.14 = (s32[2,4,64,3]{2,1,3,0:T(4,128)S(1)}, s32[2,4,64,3]{2,1,3,0:T(4,128)}, u32[]{:S(2)}) copy-start(s32[2,4,64,3]{2,1,3,0:T(4,128)} %param.26) | copy-start | bytes 18436
  0.7 20.0 %copy-start.9 = (s32[2,8,128,3]{2,1,3,0:T(8,128)S(1)}, s32[2,8,128,3]{2,1,3,0:T(8,128)}, u32[]{:S(2)}) copy-start(s32[2,8,128,3]{2,1,3,0:T(8,128)} %param.25) | copy-start | bytes 73732
  0.7 20.0 %copy-start.18 = (f32[2,2,32,12]{2,1,3,0:T(2,128)S(1)}, f32[2,2,32,12]{2,1,3,0:T(2,128)}, u32[]{:S(2)}) copy-start(f32[2,2,32,12]{2,1,3,0:T(2,128)} %param.24) | copy-start | bytes 18436
  0.7 20.0 %copy-start.13 = (f32[2,4,64,12]{2,1,3,0:T(4,128)S(1)}, f32[2,4,64,12]{2,1,3,0:T(4,128)}, u32[]{:S(2)}) copy-start(f32[2,4,64,12]{2,1,3,0:T(4,128)} %param.23) | copy-start | bytes 73732
  0.7 20.0 %copy-start.10 = (f32[2,8,128,12]{2,1,3,0:T(8,128)S(1)}, f32[2,8,128,12]{2,1,3,0:T(8,128)}, u32[]{:S(2)}) copy-start(f32[2,8,128,12]{2,1,3,0:T(8,128)} %param.22) | copy-start | bytes 294916
  2.4 10.5 %collective-permute-start.2 = (bf16[104,256]{1,0:T(8,128)(2,1)}, bf16[104,256]{1,0:T(8,128)(2,1)S(1)}, u32[]{:S(2)}, u32[]{:S(2)}) collective-permute-start(bf16[104,256]{1,0:T(8,128)(2,1)} %pack.1), channel_id=1, source_target_pairs={{0,3},{1,2},{2,1},{3,0},{4,7},{5,6},{6,5},{7,4},{8,11},{9,10},{10,... | collective-permute-start | bytes 159752 | tf_op jit(solution)/shard_map/ppermute | solution.py:45
  7.6 6.5 %collective-permute-start.1 = (bf16[104,256]{1,0:T(8,128)(2,1)}, bf16[104,256]{1,0:T(8,128)(2,1)S(1)}, u32[]{:S(2)}, u32[]{:S(2)}) collective-permute-start(bf16[104,256]{1,0:T(8,128)(2,1)} %pack.1), channel_id=1, source_target_pairs={{0,2},{1,3},{2,0},{3,1},{4,6},{5,7},{6,4},{7,5},{8,10},{9,11},{10,... | collective-permute-start | bytes 159752 | tf_op jit(solution)/shard_map/ppermute | solution.py:45
  7.6 6.5 %collective-permute-start = (bf16[104,256]{1,0:T(8,128)(2,1)}, bf16[104,256]{1,0:T(8,128)(2,1)S(1)}, u32[]{:S(2)}, u32[]{:S(2)}) collective-permute-start(bf16[104,256]{1,0:T(8,128)(2,1)} %pack.1), channel_id=1, source_target_pairs={{0,1},{1,0},{2,3},{3,2},{4,5},{5,4},{6,7},{7,6},{8,9},{9,8},{10,11... | collective-permute-start | bytes 159752 | tf_op jit(solution)/shard_map/ppermute | solution.py:45
  9.2 10.3 %collective-permute-start.14 = (bf16[72,512]{1,0:T(8,128)(2,1)S(1)}, bf16[72,512]{1,0:T(8,128)(2,1)S(1)}, u32[]{:S(2)}, u32[]{:S(2)}) collective-permute-start(bf16[72,512]{1,0:T(8,128)(2,1)S(1)} %pad_maximum_fusion.4), channel_id=1, source_target_pairs={{0,3},{1,2},{2,1},{3,0},{4,7},{5,6},{6,5},{7,4},{8,11},{9,10},{10,... | collective-permute-start | bytes 221192 | tf_op jit(solution)/shard_map/ppermute | solution.py:45
  15.2 9.5 %collective-permute-start.5 = (bf16[416,256]{1,0:T(8,128)(2,1)S(1)}, bf16[416,256]{1,0:T(8,128)(2,1)S(1)}, u32[]{:S(2)}, u32[]{:S(2)}) collective-permute-start(bf16[416,256]{1,0:T(8,128)(2,1)S(1)} %constant_dynamic-update-slice_fusion.refs_0_), channel_id=1, source_target_pairs={{0,24},{4,28},{8,16},{12,20},{16,8},{20,12},{24,0},{28,4},{1,25},{... | collective-permute-start | bytes 638984 | tf_op jit(solution)/shard_map/ppermute | solution.py:45
  17.7 7.9 %collective-permute-start.4 = (bf16[416,256]{1,0:T(8,128)(2,1)S(1)}, bf16[416,256]{1,0:T(8,128)(2,1)S(1)}, u32[]{:S(2)}, u32[]{:S(2)}) collective-permute-start(bf16[416,256]{1,0:T(8,128)(2,1)S(1)} %constant_dynamic-update-slice_fusion.refs_0_), channel_id=1, source_target_pairs={{0,16},{4,20},{8,24},{12,28},{16,0},{20,4},{24,8},{28,12},{1,17},{... | collective-permute-start | bytes 638984 | tf_op jit(solution)/shard_map/ppermute | solution.py:45
  18.2 7.5 %collective-permute-start.3 = (bf16[416,256]{1,0:T(8,128)(2,1)S(1)}, bf16[416,256]{1,0:T(8,128)(2,1)S(1)}, u32[]{:S(2)}, u32[]{:S(2)}) collective-permute-start(bf16[416,256]{1,0:T(8,128)(2,1)S(1)} %constant_dynamic-update-slice_fusion.refs_0_), channel_id=1, source_target_pairs={{0,8},{4,12},{8,0},{12,4},{16,24},{20,28},{24,16},{28,20},{1,9},{5... | collective-permute-start | bytes 638984 | tf_op jit(solution)/shard_map/ppermute | solution.py:45
  18.8 5.9 %collective-permute-start.13 = (bf16[72,512]{1,0:T(8,128)(2,1)S(1)}, bf16[72,512]{1,0:T(8,128)(2,1)S(1)}, u32[]{:S(2)}, u32[]{:S(2)}) collective-permute-start(bf16[72,512]{1,0:T(8,128)(2,1)S(1)} %pad_maximum_fusion.4), channel_id=1, source_target_pairs={{0,2},{1,3},{2,0},{3,1},{4,6},{5,7},{6,4},{7,5},{8,10},{9,11},{10,... | collective-permute-start | bytes 221192 | tf_op jit(solution)/shard_map/ppermute | solution.py:45
  19.5 5.2 %collective-permute-start.12 = (bf16[72,512]{1,0:T(8,128)(2,1)S(1)}, bf16[72,512]{1,0:T(8,128)(2,1)S(1)}, u32[]{:S(2)}, u32[]{:S(2)}) collective-permute-start(bf16[72,512]{1,0:T(8,128)(2,1)S(1)} %pad_maximum_fusion.4), channel_id=1, source_target_pairs={{0,1},{1,0},{2,3},{3,2},{4,5},{5,4},{6,7},{7,6},{8,9},{9,8},{10,11... | collective-permute-start | bytes 221192 | tf_op jit(solution)/shard_map/ppermute | solution.py:45
  20.7 2.2 %copy-start = (bf16[2,8,128,1024]{3,2,1,0:T(8,128)(2,1)S(1)}, bf16[2,8,128,1024]{3,2,1,0:T(8,128)(2,1)}, u32[]{:S(2)}) copy-start(bf16[2,8,128,1024]{3,2,1,0:T(8,128)(2,1)} %four.3) | copy-start | bytes 12582916
  22.9 1.6 %copy-start.2 = (bf16[2,4,64,2048]{3,2,1,0:T(8,128)(2,1)S(1)}, bf16[2,4,64,2048]{3,2,1,0:T(8,128)(2,1)}, u32[]{:S(2)}) copy-start(bf16[2,4,64,2048]{3,2,1,0:T(8,128)(2,1)} %five.3) | copy-start | bytes 6291460
  24.5 4.0 %copy-start.1 = (bf16[2,8,128,1024]{3,2,1,0:T(8,128)(2,1)S(1)}, bf16[2,8,128,1024]{3,2,1,0:T(8,128)(2,1)}, u32[]{:S(2)}) copy-start(bf16[2,8,128,1024]{3,2,1,0:T(8,128)(2,1)} %four.3) | copy-start | bytes 12582916
  25.7 2.8 %collective-permute-start.6 = (bf16[416,256]{1,0:T(8,128)(2,1)S(1)}, bf16[416,256]{1,0:T(8,128)(2,1)S(1)}, u32[]{:S(2)}, u32[]{:S(2)}) collective-permute-start(bf16[416,256]{1,0:T(8,128)(2,1)S(1)} %constant_dynamic-update-slice_fusion.refs_0_), channel_id=1, source_target_pairs={{0,4},{4,0},{8,12},{12,8},{16,20},{20,16},{24,28},{28,24},{1,5},{5... | collective-permute-start | bytes 638984 | tf_op jit(solution)/shard_map/ppermute | solution.py:45
  25.7 2.8 %collective-permute-start.7 = (bf16[416,256]{1,0:T(8,128)(2,1)S(1)}, bf16[416,256]{1,0:T(8,128)(2,1)S(1)}, u32[]{:S(2)}, u32[]{:S(2)}) collective-permute-start(bf16[416,256]{1,0:T(8,128)(2,1)S(1)} %collective-permute-done.3.refs_2_), channel_id=1, source_target_pairs={{0,4},{4,0},{8,12},{12,8},{16,20},{20,16},{24,28},{28,24},{1,5},{5... | collective-permute-start | bytes 638984 | tf_op jit(solution)/shard_map/ppermute | solution.py:45
  26.2 2.2 %collective-permute-start.8 = (bf16[416,256]{1,0:T(8,128)(2,1)S(1)}, bf16[416,256]{1,0:T(8,128)(2,1)S(1)}, u32[]{:S(2)}, u32[]{:S(2)}) collective-permute-start(bf16[416,256]{1,0:T(8,128)(2,1)S(1)} %collective-permute-done.4.refs_4_), channel_id=1, source_target_pairs={{0,4},{4,0},{8,12},{12,8},{16,20},{20,16},{24,28},{28,24},{1,5},{5... | collective-permute-start | bytes 638984 | tf_op jit(solution)/shard_map/ppermute | solution.py:45
  26.2 2.2 %collective-permute-start.9 = (bf16[416,256]{1,0:T(8,128)(2,1)S(1)}, bf16[416,256]{1,0:T(8,128)(2,1)S(1)}, u32[]{:S(2)}, u32[]{:S(2)}) collective-permute-start(bf16[416,256]{1,0:T(8,128)(2,1)S(1)} %collective-permute-done.5.refs_6_), channel_id=1, source_target_pairs={{0,4},{4,0},{8,12},{12,8},{16,20},{20,16},{24,28},{28,24},{1,5},{5... | collective-permute-start | bytes 638984 | tf_op jit(solution)/shard_map/ppermute | solution.py:45
  26.8 10.2 %collective-permute-start.18 = (bf16[288,512]{1,0:T(8,128)(2,1)S(1)}, bf16[288,512]{1,0:T(8,128)(2,1)S(1)}, u32[]{:S(2)}, u32[]{:S(2)}) collective-permute-start(bf16[288,512]{1,0:T(8,128)(2,1)S(1)} %pad_maximum_fusion.2.refs_0_), channel_id=1, source_target_pairs={{0,24},{4,28},{8,16},{12,20},{16,8},{20,12},{24,0},{28,4},{1,25},{... | collective-permute-start | bytes 884744 | tf_op jit(solution)/shard_map/ppermute | solution.py:45
  30.6 6.4 %collective-permute-start.10 = (bf16[2,208,256]{2,1,0:T(8,128)(2,1)S(1)}, bf16[2,208,256]{2,1,0:T(8,128)(2,1)S(1)}, u32[]{:S(2)}, u32[]{:S(2)}) collective-permute-start(bf16[2,208,256]{2,1,0:T(8,128)(2,1)S(1)} %get-tuple-element.103), channel_id=1, source_target_pairs={{0,4},{4,0},{8,12},{12,8},{16,20},{20,16},{24,28},{28,24},{1,5},{5... | collective-permute-start | bytes 638984 | tf_op jit(solution)/shard_map/ppermute | solution.py:45
  30.6 6.4 %collective-permute-start.11 = (bf16[2,208,256]{2,1,0:T(8,128)(2,1)S(1)}, bf16[2,208,256]{2,1,0:T(8,128)(2,1)S(1)}, u32[]{:S(2)}, u32[]{:S(2)}) collective-permute-start(bf16[2,208,256]{2,1,0:T(8,128)(2,1)S(1)} %get-tuple-element.104), channel_id=1, source_target_pairs={{4,8},{12,16},{20,24},{8,4},{16,12},{24,20},{5,9},{13,17},{21,25},... | collective-permute-start | bytes 638984 | tf_op jit(solution)/shard_map/ppermute | solution.py:106
  31.3 12.9 %collective-permute-start.16 = (bf16[288,512]{1,0:T(8,128)(2,1)S(1)}, bf16[288,512]{1,0:T(8,128)(2,1)S(1)}, u32[]{:S(2)}, u32[]{:S(2)}) collective-permute-start(bf16[288,512]{1,0:T(8,128)(2,1)S(1)} %pad_maximum_fusion.2.refs_0_), channel_id=1, source_target_pairs={{0,16},{4,20},{8,24},{12,28},{16,0},{20,4},{24,8},{28,12},{1,17},{... | collective-permute-start | bytes 884744 | tf_op jit(solution)/shard_map/ppermute | solution.py:45
  35.4 12.1 %collective-permute-start.15 = (bf16[288,512]{1,0:T(8,128)(2,1)S(1)}, bf16[288,512]{1,0:T(8,128)(2,1)S(1)}, u32[]{:S(2)}, u32[]{:S(2)}) collective-permute-start(bf16[288,512]{1,0:T(8,128)(2,1)S(1)} %pad_maximum_fusion.2.refs_0_), channel_id=1, source_target_pairs={{0,8},{4,12},{8,0},{12,4},{16,24},{20,28},{24,16},{28,20},{1,9},{5... | collective-permute-start | bytes 884744 | tf_op jit(solution)/shard_map/ppermute | solution.py:45
  37.0 10.5 %collective-permute-start.17 = (bf16[288,512]{1,0:T(8,128)(2,1)S(1)}, bf16[288,512]{1,0:T(8,128)(2,1)S(1)}, u32[]{:S(2)}, u32[]{:S(2)}) collective-permute-start(bf16[288,512]{1,0:T(8,128)(2,1)S(1)} %pad_maximum_fusion.2.refs_0_), channel_id=1, source_target_pairs={{0,4},{4,0},{8,12},{12,8},{16,20},{20,16},{24,28},{28,24},{1,5},{5... | collective-permute-start | bytes 884744 | tf_op jit(solution)/shard_map/ppermute | solution.py:45
  41.5 6.0 %collective-permute-start.19 = (bf16[288,512]{1,0:T(8,128)(2,1)S(1)}, bf16[288,512]{1,0:T(8,128)(2,1)S(1)}, u32[]{:S(2)}, u32[]{:S(2)}) collective-permute-start(bf16[288,512]{1,0:T(8,128)(2,1)S(1)} %collective-permute-done.18.refs_6_), channel_id=1, source_target_pairs={{0,4},{4,0},{8,12},{12,8},{16,20},{20,16},{24,28},{28,24},{1,5},{5... | collective-permute-start | bytes 884744 | tf_op jit(solution)/shard_map/ppermute | solution.py:45
  47.5 1.6 %collective-permute-start.20 = (bf16[288,512]{1,0:T(8,128)(2,1)S(1)}, bf16[288,512]{1,0:T(8,128)(2,1)S(1)}, u32[]{:S(2)}, u32[]{:S(2)}) collective-permute-start(bf16[288,512]{1,0:T(8,128)(2,1)S(1)} %collective-permute-done.15.refs_2_), channel_id=1, source_target_pairs={{0,4},{4,0},{8,12},{12,8},{16,20},{20,16},{24,28},{28,24},{1,5},{5... | collective-permute-start | bytes 884744 | tf_op jit(solution)/shard_map/ppermute | solution.py:45
  47.5 2.0 %collective-permute-start.21 = (bf16[288,512]{1,0:T(8,128)(2,1)S(1)}, bf16[288,512]{1,0:T(8,128)(2,1)S(1)}, u32[]{:S(2)}, u32[]{:S(2)}) collective-permute-start(bf16[288,512]{1,0:T(8,128)(2,1)S(1)} %collective-permute-done.16.refs_4_), channel_id=1, source_target_pairs={{0,4},{4,0},{8,12},{12,8},{16,20},{20,16},{24,28},{28,24},{1,5},{5... | collective-permute-start | bytes 884744 | tf_op jit(solution)/shard_map/ppermute | solution.py:45
  53.9 1.3 %collective-permute-start.22 = (f32[2,24,256]{2,1,0:T(8,128)S(1)}, f32[2,24,256]{2,1,0:T(8,128)S(1)}, u32[]{:S(2)}, u32[]{:S(2)}) collective-permute-start(f32[2,24,256]{2,1,0:T(8,128)S(1)} %get-tuple-element.119), channel_id=1, source_target_pairs={{0,4},{4,0},{8,12},{12,8},{16,20},{20,16},{24,28},{28,24},{1,5},{5... | collective-permute-start | bytes 147464 | tf_op jit(solution)/shard_map/ppermute | solution.py:45
  54.1 1.1 %collective-permute-start.23 = (f32[2,24,256]{2,1,0:T(8,128)S(1)}, f32[2,24,256]{2,1,0:T(8,128)S(1)}, u32[]{:S(2)}, u32[]{:S(2)}) collective-permute-start(f32[2,24,256]{2,1,0:T(8,128)S(1)} %get-tuple-element.120), channel_id=1, source_target_pairs={{4,8},{12,16},{20,24},{8,4},{16,12},{24,20},{5,9},{13,17},{21,25},... | collective-permute-start | bytes 147464 | tf_op jit(solution)/shard_map/ppermute | solution.py:106
  61.6 7.2 %collective-permute-start.26 = (bf16[4,288,512]{2,1,0:T(8,128)(2,1)S(1)}, bf16[4,288,512]{2,1,0:T(8,128)(2,1)S(1)}, u32[]{:S(2)}, u32[]{:S(2)}) collective-permute-start(bf16[4,288,512]{2,1,0:T(8,128)(2,1)S(1)} %get-tuple-element.128), channel_id=1, source_target_pairs={{0,4},{4,0},{8,12},{12,8},{16,20},{20,16},{24,28},{28,24},{1,5},{5... | collective-permute-start | bytes 3538952 | tf_op jit(solution)/shard_map/ppermute | solution.py:45
  66.3 6.4 %collective-permute-start.24 = (bf16[2,192,256]{2,1,0:T(8,128)(2,1)S(1)}, bf16[2,192,256]{2,1,0:T(8,128)(2,1)S(1)}, u32[]{:S(2)}, u32[]{:S(2)}) collective-permute-start(bf16[2,192,256]{2,1,0:T(8,128)(2,1)S(1)} %get-tuple-element.125), channel_id=1, source_target_pairs={{0,4},{4,0},{8,12},{12,8},{16,20},{20,16},{24,28},{28,24},{1,5},{5... | collective-permute-start | bytes 589832 | tf_op jit(solution)/shard_map/ppermute | solution.py:45
  66.4 6.3 %collective-permute-start.25 = (bf16[2,192,256]{2,1,0:T(8,128)(2,1)S(1)}, bf16[2,192,256]{2,1,0:T(8,128)(2,1)S(1)}, u32[]{:S(2)}, u32[]{:S(2)}) collective-permute-start(bf16[2,192,256]{2,1,0:T(8,128)(2,1)S(1)} %get-tuple-element.126), channel_id=1, source_target_pairs={{4,8},{12,16},{20,24},{8,4},{16,12},{24,20},{5,9},{13,17},{21,25},... | collective-permute-start | bytes 589832 | tf_op jit(solution)/shard_map/ppermute | solution.py:106
  69.2 13.5 %collective-permute-start.30 = (bf16[288,512]{1,0:T(8,128)(2,1)S(1)}, bf16[288,512]{1,0:T(8,128)(2,1)S(1)}, u32[]{:S(2)}, u32[]{:S(2)}) collective-permute-start(bf16[288,512]{1,0:T(8,128)(2,1)S(1)} %get-tuple-element.162), channel_id=1, source_target_pairs={{0,24},{4,28},{8,16},{12,20},{16,8},{20,12},{24,0},{28,4},{1,25},{... | collective-permute-start | bytes 884744 | tf_op jit(solution)/shard_map/ppermute | solution.py:45
  71.1 17.2 %collective-permute-start.28 = (bf16[288,512]{1,0:T(8,128)(2,1)S(1)}, bf16[288,512]{1,0:T(8,128)(2,1)S(1)}, u32[]{:S(2)}, u32[]{:S(2)}) collective-permute-start(bf16[288,512]{1,0:T(8,128)(2,1)S(1)} %get-tuple-element.163), channel_id=1, source_target_pairs={{0,8},{4,12},{8,0},{12,4},{16,24},{20,28},{24,16},{28,20},{1,9},{5... | collective-permute-start | bytes 884744 | tf_op jit(solution)/shard_map/ppermute | solution.py:45
  72.7 15.6 %collective-permute-start.29 = (bf16[288,512]{1,0:T(8,128)(2,1)S(1)}, bf16[288,512]{1,0:T(8,128)(2,1)S(1)}, u32[]{:S(2)}, u32[]{:S(2)}) collective-permute-start(bf16[288,512]{1,0:T(8,128)(2,1)S(1)} %get-tuple-element.164), channel_id=1, source_target_pairs={{0,16},{4,20},{8,24},{12,28},{16,0},{20,4},{24,8},{28,12},{1,17},{... | collective-permute-start | bytes 884744 | tf_op jit(solution)/shard_map/ppermute | solution.py:45
  72.7 3.6 %copy-start.3 = (bf16[2,4,64,2048]{3,2,1,0:T(8,128)(2,1)S(1)}, bf16[2,4,64,2048]{3,2,1,0:T(8,128)(2,1)}, u32[]{:S(2)}) copy-start(bf16[2,4,64,2048]{3,2,1,0:T(8,128)(2,1)} %five.3) | copy-start | bytes 6291460
  79.1 9.2 %collective-permute-start.27 = (bf16[4,416,256]{2,1,0:T(8,128)(2,1)S(1)}, bf16[4,416,256]{2,1,0:T(8,128)(2,1)S(1)}, u32[]{:S(2)}, u32[]{:S(2)}) collective-permute-start(bf16[4,416,256]{2,1,0:T(8,128)(2,1)S(1)} %get-tuple-element.138), channel_id=1, source_target_pairs={{0,4},{4,0},{8,12},{12,8},{16,20},{20,16},{24,28},{28,24},{1,5},{5... | collective-permute-start | bytes 2555912 | tf_op jit(solution)/shard_map/ppermute | solution.py:45
  88.6 8.2 %collective-permute-start.34 = (bf16[416,256]{1,0:T(8,128)(2,1)S(1)}, bf16[416,256]{1,0:T(8,128)(2,1)S(1)}, u32[]{:S(2)}, u32[]{:S(2)}) collective-permute-start(bf16[416,256]{1,0:T(8,128)(2,1)S(1)} %get-tuple-element.141), channel_id=1, source_target_pairs={{0,8},{4,12},{8,0},{12,4},{16,24},{20,28},{24,16},{28,20},{1,9},{5... | collective-permute-start | bytes 638984 | tf_op jit(solution)/shard_map/ppermute | solution.py:45
  89.7 10.8 %collective-permute-start.35 = (bf16[416,256]{1,0:T(8,128)(2,1)S(1)}, bf16[416,256]{1,0:T(8,128)(2,1)S(1)}, u32[]{:S(2)}, u32[]{:S(2)}) collective-permute-start(bf16[416,256]{1,0:T(8,128)(2,1)S(1)} %get-tuple-element.142), channel_id=1, source_target_pairs={{0,16},{4,20},{8,24},{12,28},{16,0},{20,4},{24,8},{28,12},{1,17},{... | collective-permute-start | bytes 638984 | tf_op jit(solution)/shard_map/ppermute | solution.py:45
  91.1 9.4 %collective-permute-start.36 = (bf16[416,256]{1,0:T(8,128)(2,1)S(1)}, bf16[416,256]{1,0:T(8,128)(2,1)S(1)}, u32[]{:S(2)}, u32[]{:S(2)}) collective-permute-start(bf16[416,256]{1,0:T(8,128)(2,1)S(1)} %get-tuple-element.143), channel_id=1, source_target_pairs={{0,24},{4,28},{8,16},{12,20},{16,8},{20,12},{24,0},{28,4},{1,25},{... | collective-permute-start | bytes 638984 | tf_op jit(solution)/shard_map/ppermute | solution.py:45
  92.2 8.4 %collective-permute-start.33 = (bf16[72,512]{1,0:T(8,128)(2,1)S(1)}, bf16[72,512]{1,0:T(8,128)(2,1)S(1)}, u32[]{:S(2)}, u32[]{:S(2)}) collective-permute-start(bf16[72,512]{1,0:T(8,128)(2,1)S(1)} %get-tuple-element.169), channel_id=1, source_target_pairs={{0,3},{1,2},{2,1},{3,0},{4,7},{5,6},{6,5},{7,4},{8,11},{9,10},{10,... | collective-permute-start | bytes 221192 | tf_op jit(solution)/shard_map/ppermute | solution.py:45
  94.2 6.8 %collective-permute-start.32 = (bf16[72,512]{1,0:T(8,128)(2,1)S(1)}, bf16[72,512]{1,0:T(8,128)(2,1)S(1)}, u32[]{:S(2)}, u32[]{:S(2)}) collective-permute-start(bf16[72,512]{1,0:T(8,128)(2,1)S(1)} %get-tuple-element.170), channel_id=1, source_target_pairs={{0,2},{1,3},{2,0},{3,1},{4,6},{5,7},{6,4},{7,5},{8,10},{9,11},{10,... | collective-permute-start | bytes 221192 | tf_op jit(solution)/shard_map/ppermute | solution.py:45
  96.9 4.9 %collective-permute-start.31 = (bf16[72,512]{1,0:T(8,128)(2,1)S(1)}, bf16[72,512]{1,0:T(8,128)(2,1)S(1)}, u32[]{:S(2)}, u32[]{:S(2)}) collective-permute-start(bf16[72,512]{1,0:T(8,128)(2,1)S(1)} %get-tuple-element.171), channel_id=1, source_target_pairs={{0,1},{1,0},{2,3},{3,2},{4,5},{5,4},{6,7},{7,6},{8,9},{9,8},{10,11... | collective-permute-start | bytes 221192 | tf_op jit(solution)/shard_map/ppermute | solution.py:45
  100.6 5.9 %copy-start.4 = (f32[2,72,256]{2,1,0:T(8,128)S(1)}, f32[2,72,256]{2,1,0:T(8,128)}, u32[]{:S(2)}) copy-start(f32[2,72,256]{2,1,0:T(8,128)} %refs_3_.3) | copy-start | bytes 442372
  100.6 5.9 %copy-start.6 = (f32[2,72,256]{2,1,0:T(8,128)S(1)}, f32[2,72,256]{2,1,0:T(8,128)}, u32[]{:S(2)}) copy-start(f32[2,72,256]{2,1,0:T(8,128)} %refs_4_.3) | copy-start | bytes 442372
  100.6 5.9 %copy-start.7 = (f32[2,72,256]{2,1,0:T(8,128)S(1)}, f32[2,72,256]{2,1,0:T(8,128)}, u32[]{:S(2)}) copy-start(f32[2,72,256]{2,1,0:T(8,128)} %refs_5_.3) | copy-start | bytes 442372
  101.8 7.4 %copy-start.5 = (f32[64,256]{1,0:T(8,128)S(1)}, f32[64,256]{1,0:T(8,128)}, u32[]{:S(2)}) copy-start(f32[64,256]{1,0:T(8,128)} %refs_6_.3) | copy-start | bytes 196612
  101.8 7.4 %copy-start.8 = (f32[32,256]{1,0:T(8,128)S(1)}, f32[32,256]{1,0:T(8,128)}, u32[]{:S(2)}) copy-start(f32[32,256]{1,0:T(8,128)} %refs_3_.2) | copy-start | bytes 98308
  101.8 7.4 %copy-start.11 = (f32[64,256]{1,0:T(8,128)S(1)}, f32[64,256]{1,0:T(8,128)}, u32[]{:S(2)}) copy-start(f32[64,256]{1,0:T(8,128)} %refs_7_.3) | copy-start | bytes 196612
  101.8 7.4 %copy-start.12 = (f32[64,256]{1,0:T(8,128)S(1)}, f32[64,256]{1,0:T(8,128)}, u32[]{:S(2)}) copy-start(f32[64,256]{1,0:T(8,128)} %refs_8_.1) | copy-start | bytes 196612
  101.9 7.4 %copy-start.15 = (f32[72,12]{0,1:T(8,128)S(1)}, f32[72,12]{0,1:T(8,128)}, u32[]{:S(2)}) copy-start(f32[72,12]{0,1:T(8,128)} %param.31) | copy-start | bytes 10372
  101.9 7.4 %copy-start.16 = (f32[32,256]{1,0:T(8,128)S(1)}, f32[32,256]{1,0:T(8,128)}, u32[]{:S(2)}) copy-start(f32[32,256]{1,0:T(8,128)} %refs_4_.2) | copy-start | bytes 98308
  101.9 7.4 %copy-start.17 = (f32[32,256]{1,0:T(8,128)S(1)}, f32[32,256]{1,0:T(8,128)}, u32[]{:S(2)}) copy-start(f32[32,256]{1,0:T(8,128)} %refs_5_.2) | copy-start | bytes 98308
  101.9 7.4 %copy-start.20 = (f32[72,12]{0,1:T(8,128)S(1)}, f32[72,12]{0,1:T(8,128)}, u32[]{:S(2)}) copy-start(f32[72,12]{0,1:T(8,128)} %param.35) | copy-start | bytes 10372
  101.9 7.4 %copy-start.21 = (f32[72,12]{0,1:T(8,128)S(1)}, f32[72,12]{0,1:T(8,128)}, u32[]{:S(2)}) copy-start(f32[72,12]{0,1:T(8,128)} %param.39) | copy-start | bytes 10372
  102.0 6.1 %collective-permute-start.39 = (bf16[104,256]{1,0:T(8,128)(2,1)S(1)}, bf16[104,256]{1,0:T(8,128)(2,1)S(1)}, u32[]{:S(2)}, u32[]{:S(2)}) collective-permute-start(bf16[104,256]{1,0:T(8,128)(2,1)S(1)} %get-tuple-element.172), channel_id=1, source_target_pairs={{0,3},{1,2},{2,1},{3,0},{4,7},{5,6},{6,5},{7,4},{8,11},{9,10},{10,... | collective-permute-start | bytes 159752 | tf_op jit(solution)/shard_map/ppermute | solution.py:45
  104.0 5.2 %collective-permute-start.38 = (bf16[104,256]{1,0:T(8,128)(2,1)S(1)}, bf16[104,256]{1,0:T(8,128)(2,1)S(1)}, u32[]{:S(2)}, u32[]{:S(2)}) collective-permute-start(bf16[104,256]{1,0:T(8,128)(2,1)S(1)} %get-tuple-element.173), channel_id=1, source_target_pairs={{0,2},{1,3},{2,0},{3,1},{4,6},{5,7},{6,4},{7,5},{8,10},{9,11},{10,... | collective-permute-start | bytes 159752 | tf_op jit(solution)/shard_map/ppermute | solution.py:45
  104.0 5.2 %collective-permute-start.37 = (bf16[104,256]{1,0:T(8,128)(2,1)S(1)}, bf16[104,256]{1,0:T(8,128)(2,1)S(1)}, u32[]{:S(2)}, u32[]{:S(2)}) collective-permute-start(bf16[104,256]{1,0:T(8,128)(2,1)S(1)} %get-tuple-element.174), channel_id=1, source_target_pairs={{0,1},{1,0},{2,3},{3,2},{4,5},{5,4},{6,7},{7,6},{8,9},{9,8},{10,11... | collective-permute-start | bytes 159752 | tf_op jit(solution)/shard_map/ppermute | solution.py:45

commit v7 on v6

--- a/solution.py
+++ b/solution.py
@@ -12,7 +12,7 @@
 
 LANES = 128
 DELTA_ROWS = 16
-SPARE_BYTES = 12 * 1024 * 1024
+SPARE_BYTES = 8 * 1024 * 1024
 ALL_BYTES = 60 * 1024 * 1024
 
 box_beta = 1.0 / 9.0

time: 111 us -> 111 us (level)
  no operation moved by 1% of the time
where the time goes in v7:
time: 111 us; the launch traced here: 110 us
  starting transfers between devices  52.3 us (47%)
  waiting for transfers between devices  26 us (23%)
  Pallas kernels  23.8 us (21%)
  local copies, waits for them, and re-layouts  5.09 us (5%)
  other arithmetic  1.62 us (1%)
  between operations  1.47 us (1%)
    ppermute x37, starting transfers between devices, sent(): return lax.ppermute(value, axis, [(i, i ^ mask) for i in range(count)])  50.3 us
    ppermute x37, waiting for transfers between devices, sent(): return lax.ppermute(value, axis, [(i, i ^ mask) for i in range(count)])  26 us
    pallas_call x12, Pallas kernels, call(): pl.pallas_call(kernel, out_shape=list(outs), in_specs=[hbm] * apart + [vm...  23.8 us
    unnamed x55, local copies, waits for them, and re-layouts  4.02 us
  transfers between devices with their start and end apart: 40, of which 16 were waited for; matrix products, arithmetic and copies ran while one was open for 2% of the time, Pallas kernels for 9%

profile of v7, /device:TPU:0, one launch (start us, length us, event | category | flops | bytes accessed | tf_op | source)
XLA Modules:
  0.0 110.3 jit_solution(3935038582235595993)
XLA Ops:
  0.7 1.7 %pack.1 = bf16[104,256]{1,0:T(8,128)(2,1)} custom-call(f32[32,256]{1,0:T(8,128)} %refs_3_.2, f32[64,256]{1,0:T(8,128)} %refs_6_.3, f32[12,72]{1,0:T(8,128)} %bitcast.130, s32[2,3,8,128]{3,2,1,0:T(8,128)} %bitcast.124, s32[2,3,4,64]{3,2,1,0:T(4,128)} %bitcast.128, s32[2,3,2,32]{3,2,1,0:T(2,128)} %bitcast.133), custom_call_target="tpu_custom_call" | custom-call | bytes 187264 | tf_op jit(solution)/shard_map/pack/pallas_call | solution.py:118
  2.4 5.1 %collective-permute-start.2 = (bf16[104,256]{1,0:T(8,128)(2,1)}, bf16[104,256]{1,0:T(8,128)(2,1)S(1)}, u32[]{:S(2)}, u32[]{:S(2)}) collective-permute-start(bf16[104,256]{1,0:T(8,128)(2,1)} %pack.1), channel_id=1, source_target_pairs={{0,3},{1,2},{2,1},{3,0},{4,7},{5,6},{6,5},{7,4},{8,11},{9,10},{10,... | collective-permute-start | bytes 159752 | tf_op jit(solution)/shard_map/ppermute | solution.py:45
  7.6 0.6 collective-permute-start
  8.2 0.9 fusion.17
  9.2 3.8 %collective-permute-start.14 = (bf16[72,512]{1,0:T(8,128)(2,1)S(1)}, bf16[72,512]{1,0:T(8,128)(2,1)S(1)}, u32[]{:S(2)}, u32[]{:S(2)}) collective-permute-start(bf16[72,512]{1,0:T(8,128)(2,1)S(1)} %pad_maximum_fusion.4), channel_id=1, source_target_pairs={{0,3},{1,2},{2,1},{3,0},{4,7},{5,6},{6,5},{7,4},{8,11},{9,10},{10,... | collective-permute-start | bytes 221192 | tf_op jit(solution)/shard_map/ppermute | solution.py:45
  13.0 1.1 %collective-permute-done.1 = bf16[104,256]{1,0:T(8,128)(2,1)S(1)} collective-permute-done((bf16[104,256]{1,0:T(8,128)(2,1)}, bf16[104,256]{1,0:T(8,128)(2,1)S(1)}, u32[]{:S(2)}, u32[]{:S(2)}) %collective-permute-start.1) | collective-permute-done | bytes 53280 | tf_op jit(solution)/shard_map/ppermute | solution.py:45
  14.1 0.8 pad_maximum_fusion.3
  15.2 2.5 %collective-permute-start.5 = (bf16[416,256]{1,0:T(8,128)(2,1)S(1)}, bf16[416,256]{1,0:T(8,128)(2,1)S(1)}, u32[]{:S(2)}, u32[]{:S(2)}) collective-permute-start(bf16[416,256]{1,0:T(8,128)(2,1)S(1)} %constant_dynamic-update-slice_fusion.refs_0_), channel_id=1, source_target_pairs={{0,24},{4,28},{8,16},{12,20},{16,8},{20,12},{24,0},{28,4},{1,25},{... | collective-permute-start | bytes 638984 | tf_op jit(solution)/shard_map/ppermute | solution.py:45
  17.7 0.5 collective-permute-start.4
  18.2 0.5 collective-permute-start.3
  18.8 0.7 collective-permute-start.13
  19.5 1.2 %collective-permute-start.12 = (bf16[72,512]{1,0:T(8,128)(2,1)S(1)}, bf16[72,512]{1,0:T(8,128)(2,1)S(1)}, u32[]{:S(2)}, u32[]{:S(2)}) collective-permute-start(bf16[72,512]{1,0:T(8,128)(2,1)S(1)} %pad_maximum_fusion.4), channel_id=1, source_target_pairs={{0,1},{1,0},{2,3},{3,2},{4,5},{5,4},{6,7},{7,6},{8,9},{9,8},{10,11... | collective-permute-start | bytes 221192 | tf_op jit(solution)/shard_map/ppermute | solution.py:45
  20.7 2.2 %copy-done = bf16[2,8,128,1024]{3,2,1,0:T(8,128)(2,1)S(1)} copy-done((bf16[2,8,128,1024]{3,2,1,0:T(8,128)(2,1)S(1)}, bf16[2,8,128,1024]{3,2,1,0:T(8,128)(2,1)}, u32[]{:S(2)}) %copy-start) | copy-done | bytes 4194328
  22.9 1.6 %copy-done.2 = bf16[2,4,64,2048]{3,2,1,0:T(8,128)(2,1)S(1)} copy-done((bf16[2,4,64,2048]{3,2,1,0:T(8,128)(2,1)S(1)}, bf16[2,4,64,2048]{3,2,1,0:T(8,128)(2,1)}, u32[]{:S(2)}) %copy-start.2) | copy-done | bytes 2097176
  24.5 0.2 planes.1
  24.7 0.9 collective-permute-done.4.refs_4_
  25.7 0.5 collective-permute-start.7
  26.2 0.5 collective-permute-start.9
  26.8 1.7 %collective-permute-start.18 = (bf16[288,512]{1,0:T(8,128)(2,1)S(1)}, bf16[288,512]{1,0:T(8,128)(2,1)S(1)}, u32[]{:S(2)}, u32[]{:S(2)}) collective-permute-start(bf16[288,512]{1,0:T(8,128)(2,1)S(1)} %pad_maximum_fusion.2.refs_0_), channel_id=1, source_target_pairs={{0,24},{4,28},{8,16},{12,20},{16,8},{20,12},{24,0},{28,4},{1,25},{... | collective-permute-start | bytes 884744 | tf_op jit(solution)/shard_map/ppermute | solution.py:45
  28.5 2.0 %laterals.1 = (bf16[2,8,128,256]{3,2,1,0:T(8,128)(2,1)S(1)}, bf16[2,4,64,256]{3,2,1,0:T(8,128)(2,1)S(1)}, bf16[2,208,256]{2,1,0:T(8,128)(2,1)S(1)}, bf16[2,208,256]{2,1,0:T(8,128)(2,1)S(1)}) custom-call(bf16[2,8,128,1024]{3,2,1,0:T(8,128)(2,1)S(1)} %copy-done.1, bf16[2,4,64,2048]{3,2,1,0:T(8,128)(2,1)S(1)} %copy-done.2, ...), custom_call_target="tpu_custom_call" | custom-call | flops 1610612736 | bytes 9961472 | tf_op jit(solution)/shard_map/laterals/pallas_call | solution.py:118
  30.6 0.7 collective-permute-start.11
  31.3 4.1 %collective-permute-start.16 = (bf16[288,512]{1,0:T(8,128)(2,1)S(1)}, bf16[288,512]{1,0:T(8,128)(2,1)S(1)}, u32[]{:S(2)}, u32[]{:S(2)}) collective-permute-start(bf16[288,512]{1,0:T(8,128)(2,1)S(1)} %pad_maximum_fusion.2.refs_0_), channel_id=1, source_target_pairs={{0,16},{4,20},{8,24},{12,28},{16,0},{20,4},{24,8},{28,12},{1,17},{... | collective-permute-start | bytes 884744 | tf_op jit(solution)/shard_map/ppermute | solution.py:45
  35.4 0.7 collective-permute-start.15
  36.1 0.9 head_weights.1
  37.0 4.5 %collective-permute-start.17 = (bf16[288,512]{1,0:T(8,128)(2,1)S(1)}, bf16[288,512]{1,0:T(8,128)(2,1)S(1)}, u32[]{:S(2)}, u32[]{:S(2)}) collective-permute-start(bf16[288,512]{1,0:T(8,128)(2,1)S(1)} %pad_maximum_fusion.2.refs_0_), channel_id=1, source_target_pairs={{0,4},{4,0},{8,12},{12,8},{16,20},{20,16},{24,28},{28,24},{1,5},{5... | collective-permute-start | bytes 884744 | tf_op jit(solution)/shard_map/ppermute | solution.py:45
  41.5 2.7 %collective-permute-done.16.refs_4_ = bf16[288,512]{1,0:T(8,128)(2,1)S(1)} collective-permute-done((bf16[288,512]{1,0:T(8,128)(2,1)S(1)}, bf16[288,512]{1,0:T(8,128)(2,1)S(1)}, u32[]{:S(2)}, u32[]{:S(2)}) %collective-permute-start.16) | collective-permute-done | bytes 294944 | tf_op jit(solution)/shard_map/ppermute | solution.py:45
  44.2 3.3 %collective-permute-done.15.refs_2_ = bf16[288,512]{1,0:T(8,128)(2,1)S(1)} collective-permute-done((bf16[288,512]{1,0:T(8,128)(2,1)S(1)}, bf16[288,512]{1,0:T(8,128)(2,1)S(1)}, u32[]{:S(2)}, u32[]{:S(2)}) %collective-permute-start.15) | collective-permute-done | bytes 294944 | tf_op jit(solution)/shard_map/ppermute | solution.py:45
  47.5 0.5 collective-permute-start.21
  48.0 1.1 collective-permute-done.20.refs_3_
  49.1 0.4 collective-permute-done.21.refs_5_
  49.5 4.4 %outputs.1 = (bf16[2,14,128,256]{3,2,1,0:T(8,128)(2,1)S(1)}, f32[2,16,2560]{2,1,0:T(8,128)S(1)}, f32[2,24,256]{2,1,0:T(8,128)S(1)}, f32[2,24,256]{2,1,0:T(8,128)...) custom-call(bf16[2,8,128,256]{3,2,1,0:T(8,128)(2,1)S(1)} %get-tuple-element.101.input_four, ...), custom_call_target="tpu_custom_call" | custom-call | flops 3019898880 | bytes 9248768 | tf_op jit(solution)/shard_map/outputs/pallas_call | solution.py:118
  53.9 0.2 collective-permute-start.22
  54.1 0.7 collective-permute-start.23
  54.7 0.5 collective-permute-done.22.pair_in
  55.2 2.7 %heads.1 = (f32[144,256]{1,0:T(8,128)S(1)}, bf16[2,8,128,256]{3,2,1,0:T(8,128)(2,1)S(1)}, bf16[2,4,64,256]{3,2,1,0:T(8,128)(2,1)S(1)}, bf16[2,192,256]{2,1,0:T(8...) custom-call(bf16[2,14,128,256]{3,2,1,0:T(8,128)(2,1)S(1)} %get-tuple-element.118.levels, ...), custom_call_target="tpu_custom_call" | custom-call | flops 792723456 | bytes 4841480 | tf_op jit(solution)/shard_map/heads/pallas_call | solution.py:118
  57.9 3.7 %conv_grads.1 = (bf16[4,288,512]{2,1,0:T(8,128)(2,1)S(1)}, bf16[4,288,512]{2,1,0:T(8,128)(2,1)S(1)}) custom-call(bf16[2,8,128,256]{3,2,1,0:T(8,128)(2,1)S(1)} %get-tuple-element.101.input_four, bf16[2,4,64,256]{3,2,1,0:T(8,128)(2,1)S(1)} %get-tuple-element.102.input_five, bf16[2,208,256]{2,1,0:T(8,128)(2,1)S(1)} %collective-permute-done.10.pair_in.pair_mask, ...), custom_call_target="tpu_custom_call" | custom-call | flops 3019898880 | bytes 5406720 | tf_op jit(solution)/shard_map/conv_grads/pallas_call | solution.py:118
  61.6 4.7 %collective-permute-start.26 = (bf16[4,288,512]{2,1,0:T(8,128)(2,1)S(1)}, bf16[4,288,512]{2,1,0:T(8,128)(2,1)S(1)}, u32[]{:S(2)}, u32[]{:S(2)}) collective-permute-start(bf16[4,288,512]{2,1,0:T(8,128)(2,1)S(1)} %get-tuple-element.128), channel_id=1, source_target_pairs={{0,4},{4,0},{8,12},{12,8},{16,20},{20,16},{24,28},{28,24},{1,5},{5... | collective-permute-start | bytes 3538952 | tf_op jit(solution)/shard_map/ppermute | solution.py:45
  66.4 0.7 collective-permute-start.25
  67.1 1.7 %collective-permute-done.26 = bf16[4,288,512]{2,1,0:T(8,128)(2,1)S(1)} collective-permute-done((bf16[4,288,512]{2,1,0:T(8,128)(2,1)S(1)}, bf16[4,288,512]{2,1,0:T(8,128)(2,1)S(1)}, u32[]{:S(2)}, u32[]{:S(2)}) %collective-permute-start.26) | collective-permute-done | bytes 1179680 | tf_op jit(solution)/shard_map/ppermute | solution.py:45
  68.8 0.4 fusion.16
  69.2 1.9 %collective-permute-start.30 = (bf16[288,512]{1,0:T(8,128)(2,1)S(1)}, bf16[288,512]{1,0:T(8,128)(2,1)S(1)}, u32[]{:S(2)}, u32[]{:S(2)}) collective-permute-start(bf16[288,512]{1,0:T(8,128)(2,1)S(1)} %get-tuple-element.162), channel_id=1, source_target_pairs={{0,24},{4,28},{8,16},{12,20},{16,8},{20,12},{24,0},{28,4},{1,25},{... | collective-permute-start | bytes 884744 | tf_op jit(solution)/shard_map/ppermute | solution.py:45
  71.1 1.6 %collective-permute-start.28 = (bf16[288,512]{1,0:T(8,128)(2,1)S(1)}, bf16[288,512]{1,0:T(8,128)(2,1)S(1)}, u32[]{:S(2)}, u32[]{:S(2)}) collective-permute-start(bf16[288,512]{1,0:T(8,128)(2,1)S(1)} %get-tuple-element.163), channel_id=1, source_target_pairs={{0,8},{4,12},{8,0},{12,4},{16,24},{20,28},{24,16},{28,20},{1,9},{5... | collective-permute-start | bytes 884744 | tf_op jit(solution)/shard_map/ppermute | solution.py:45
  72.7 3.6 %merged_grads.1 = (bf16[2048,256]{1,0:T(8,128)(2,1)S(1)}, bf16[512,256]{1,0:T(8,128)(2,1)S(1)}) custom-call(bf16[2,8,128,256]{3,2,1,0:T(8,128)(2,1)S(1)} %get-tuple-element.123.grad_four, bf16[2,4,64,256]{3,2,1,0:T(8,128)(2,1)S(1)} %get-tuple-element.124.grad_five, bf16[2,192,256]{2,1,0:T(8,128)(2,1)S(1)} %collective-permute-done.24.pair_in, ...), custom_call_target="tpu_custom_call" | custom-call | flops 3019898880 | bytes 5373952 | tf_op jit(solution)/shard_map/merged_grads/pallas_call | solution.py:118
  76.3 2.8 %lateral_grads.1 = (bf16[4,416,256]{2,1,0:T(8,128)(2,1)S(1)}, bf16[4,416,256]{2,1,0:T(8,128)(2,1)S(1)}) custom-call(bf16[2,8,128,1024]{3,2,1,0:T(8,128)(2,1)S(1)} %copy-done.1, bf16[2,4,64,2048]{3,2,1,0:T(8,128)(2,1)S(1)} %copy-done.3, bf16[2048,256]{1,0:T(8,128)(2,1)S(1)} %get-tuple-element.133.lat_four, bf16[512,256]{1,0:T(8,128)(2,1)S(1)} %get-tuple-element.134.lat_five, ...), custom_call_target="tpu_custom_call" | custom-call | flops 1 | bytes 9453572 | tf_op jit(solution)/shard_map/lateral_grads/pallas_call | solution.py:118
  79.1 3.5 %collective-permute-start.27 = (bf16[4,416,256]{2,1,0:T(8,128)(2,1)S(1)}, bf16[4,416,256]{2,1,0:T(8,128)(2,1)S(1)}, u32[]{:S(2)}, u32[]{:S(2)}) collective-permute-start(bf16[4,416,256]{2,1,0:T(8,128)(2,1)S(1)} %get-tuple-element.138), channel_id=1, source_target_pairs={{0,4},{4,0},{8,12},{12,8},{16,20},{20,16},{24,28},{28,24},{1,5},{5... | collective-permute-start | bytes 2555912 | tf_op jit(solution)/shard_map/ppermute | solution.py:45
  82.6 5.6 %collective-permute-done.28.refs_0_ = bf16[288,512]{1,0:T(8,128)(2,1)S(1)} collective-permute-done((bf16[288,512]{1,0:T(8,128)(2,1)S(1)}, bf16[288,512]{1,0:T(8,128)(2,1)S(1)}, u32[]{:S(2)}, u32[]{:S(2)}) %collective-permute-start.28) | collective-permute-done | bytes 294944 | tf_op jit(solution)/shard_map/ppermute | solution.py:45
  88.2 0.1 conv_total.1
  88.5 0.2 add_bitcast_fusion.4
  88.6 1.0 collective-permute-start.34
  89.7 1.4 %collective-permute-start.35 = (bf16[416,256]{1,0:T(8,128)(2,1)S(1)}, bf16[416,256]{1,0:T(8,128)(2,1)S(1)}, u32[]{:S(2)}, u32[]{:S(2)}) collective-permute-start(bf16[416,256]{1,0:T(8,128)(2,1)S(1)} %get-tuple-element.142), channel_id=1, source_target_pairs={{0,16},{4,20},{8,24},{12,28},{16,0},{20,4},{24,8},{28,12},{1,17},{... | collective-permute-start | bytes 638984 | tf_op jit(solution)/shard_map/ppermute | solution.py:45
  91.1 1.1 collective-permute-start.36
  92.2 2.0 %collective-permute-start.33 = (bf16[72,512]{1,0:T(8,128)(2,1)S(1)}, bf16[72,512]{1,0:T(8,128)(2,1)S(1)}, u32[]{:S(2)}, u32[]{:S(2)}) collective-permute-start(bf16[72,512]{1,0:T(8,128)(2,1)S(1)} %get-tuple-element.169), channel_id=1, source_target_pairs={{0,3},{1,2},{2,1},{3,0},{4,7},{5,6},{6,5},{7,4},{8,11},{9,10},{10,... | collective-permute-start | bytes 221192 | tf_op jit(solution)/shard_map/ppermute | solution.py:45
  94.2 0.1 collective-permute-start.32
  94.4 2.5 %collective-permute-done.34 = bf16[416,256]{1,0:T(8,128)(2,1)S(1)} collective-permute-done((bf16[416,256]{1,0:T(8,128)(2,1)S(1)}, bf16[416,256]{1,0:T(8,128)(2,1)S(1)}, u32[]{:S(2)}, u32[]{:S(2)}) %collective-permute-start.34) | collective-permute-done | bytes 213024 | tf_op jit(solution)/shard_map/ppermute | solution.py:45
  96.9 0.6 collective-permute-start.31
  97.5 3.0 %collective-permute-done.35 = bf16[416,256]{1,0:T(8,128)(2,1)S(1)} collective-permute-done((bf16[416,256]{1,0:T(8,128)(2,1)S(1)}, bf16[416,256]{1,0:T(8,128)(2,1)S(1)}, u32[]{:S(2)}, u32[]{:S(2)}) %collective-permute-start.35) | collective-permute-done | bytes 213024 | tf_op jit(solution)/shard_map/ppermute | solution.py:45
  100.6 0.4 collective-permute-done.32.refs_1_
  101.1 0.7 collective-permute-done.31.refs_0_
  102.0 2.0 %collective-permute-start.39 = (bf16[104,256]{1,0:T(8,128)(2,1)S(1)}, bf16[104,256]{1,0:T(8,128)(2,1)S(1)}, u32[]{:S(2)}, u32[]{:S(2)}) collective-permute-start(bf16[104,256]{1,0:T(8,128)(2,1)S(1)} %get-tuple-element.172), channel_id=1, source_target_pairs={{0,3},{1,2},{2,1},{3,0},{4,7},{5,6},{6,5},{7,4},{8,11},{9,10},{10,... | collective-permute-start | bytes 159752 | tf_op jit(solution)/shard_map/ppermute | solution.py:45
  104.0 2.5 %collective-permute-start.37 = (bf16[104,256]{1,0:T(8,128)(2,1)S(1)}, bf16[104,256]{1,0:T(8,128)(2,1)S(1)}, u32[]{:S(2)}, u32[]{:S(2)}) collective-permute-start(bf16[104,256]{1,0:T(8,128)(2,1)S(1)} %get-tuple-element.174), channel_id=1, source_target_pairs={{0,1},{1,0},{2,3},{3,2},{4,5},{5,4},{6,7},{7,6},{8,9},{9,8},{10,11... | collective-permute-start | bytes 159752 | tf_op jit(solution)/shard_map/ppermute | solution.py:45
  106.5 0.8 conv_step.1
  107.4 0.7 collective-permute-done.39.refs_2_
  108.1 1.1 %collective-permute-done.38.refs_1_ = bf16[104,256]{1,0:T(8,128)(2,1)S(1)} collective-permute-done((bf16[104,256]{1,0:T(8,128)(2,1)S(1)}, bf16[104,256]{1,0:T(8,128)(2,1)S(1)}, u32[]{:S(2)}, u32[]{:S(2)}) %collective-permute-start.38) | collective-permute-done | bytes 53280 | tf_op jit(solution)/shard_map/ppermute | solution.py:45
  109.3 0.8 lateral_step.1
  (102 shorter events, 1.1 us)
Async XLA Ops:
  0.6 20.0 %copy-start.19 = (s32[2,2,32,3]{2,1,3,0:T(2,128)S(1)}, s32[2,2,32,3]{2,1,3,0:T(2,128)}, u32[]{:S(2)}) copy-start(s32[2,2,32,3]{2,1,3,0:T(2,128)} %param.27) | copy-start | bytes 4612
  0.7 20.0 %copy-start.14 = (s32[2,4,64,3]{2,1,3,0:T(4,128)S(1)}, s32[2,4,64,3]{2,1,3,0:T(4,128)}, u32[]{:S(2)}) copy-start(s32[2,4,64,3]{2,1,3,0:T(4,128)} %param.26) | copy-start | bytes 18436
  0.7 20.0 %copy-start.9 = (s32[2,8,128,3]{2,1,3,0:T(8,128)S(1)}, s32[2,8,128,3]{2,1,3,0:T(8,128)}, u32[]{:S(2)}) copy-start(s32[2,8,128,3]{2,1,3,0:T(8,128)} %param.25) | copy-start | bytes 73732
  0.7 20.0 %copy-start.18 = (f32[2,2,32,12]{2,1,3,0:T(2,128)S(1)}, f32[2,2,32,12]{2,1,3,0:T(2,128)}, u32[]{:S(2)}) copy-start(f32[2,2,32,12]{2,1,3,0:T(2,128)} %param.24) | copy-start | bytes 18436
  0.7 20.0 %copy-start.13 = (f32[2,4,64,12]{2,1,3,0:T(4,128)S(1)}, f32[2,4,64,12]{2,1,3,0:T(4,128)}, u32[]{:S(2)}) copy-start(f32[2,4,64,12]{2,1,3,0:T(4,128)} %param.23) | copy-start | bytes 73732
  0.7 20.0 %copy-start.10 = (f32[2,8,128,12]{2,1,3,0:T(8,128)S(1)}, f32[2,8,128,12]{2,1,3,0:T(8,128)}, u32[]{:S(2)}) copy-start(f32[2,8,128,12]{2,1,3,0:T(8,128)} %param.22) | copy-start | bytes 294916
  2.4 10.5 %collective-permute-start.2 = (bf16[104,256]{1,0:T(8,128)(2,1)}, bf16[104,256]{1,0:T(8,128)(2,1)S(1)}, u32[]{:S(2)}, u32[]{:S(2)}) collective-permute-start(bf16[104,256]{1,0:T(8,128)(2,1)} %pack.1), channel_id=1, source_target_pairs={{0,3},{1,2},{2,1},{3,0},{4,7},{5,6},{6,5},{7,4},{8,11},{9,10},{10,... | collective-permute-start | bytes 159752 | tf_op jit(solution)/shard_map/ppermute | solution.py:45
  7.6 6.5 %collective-permute-start.1 = (bf16[104,256]{1,0:T(8,128)(2,1)}, bf16[104,256]{1,0:T(8,128)(2,1)S(1)}, u32[]{:S(2)}, u32[]{:S(2)}) collective-permute-start(bf16[104,256]{1,0:T(8,128)(2,1)} %pack.1), channel_id=1, source_target_pairs={{0,2},{1,3},{2,0},{3,1},{4,6},{5,7},{6,4},{7,5},{8,10},{9,11},{10,... | collective-permute-start | bytes 159752 | tf_op jit(solution)/shard_map/ppermute | solution.py:45
  7.6 6.5 %collective-permute-start = (bf16[104,256]{1,0:T(8,128)(2,1)}, bf16[104,256]{1,0:T(8,128)(2,1)S(1)}, u32[]{:S(2)}, u32[]{:S(2)}) collective-permute-start(bf16[104,256]{1,0:T(8,128)(2,1)} %pack.1), channel_id=1, source_target_pairs={{0,1},{1,0},{2,3},{3,2},{4,5},{5,4},{6,7},{7,6},{8,9},{9,8},{10,11... | collective-permute-start | bytes 159752 | tf_op jit(solution)/shard_map/ppermute | solution.py:45
  9.2 10.3 %collective-permute-start.14 = (bf16[72,512]{1,0:T(8,128)(2,1)S(1)}, bf16[72,512]{1,0:T(8,128)(2,1)S(1)}, u32[]{:S(2)}, u32[]{:S(2)}) collective-permute-start(bf16[72,512]{1,0:T(8,128)(2,1)S(1)} %pad_maximum_fusion.4), channel_id=1, source_target_pairs={{0,3},{1,2},{2,1},{3,0},{4,7},{5,6},{6,5},{7,4},{8,11},{9,10},{10,... | collective-permute-start | bytes 221192 | tf_op jit(solution)/shard_map/ppermute | solution.py:45
  15.2 9.5 %collective-permute-start.5 = (bf16[416,256]{1,0:T(8,128)(2,1)S(1)}, bf16[416,256]{1,0:T(8,128)(2,1)S(1)}, u32[]{:S(2)}, u32[]{:S(2)}) collective-permute-start(bf16[416,256]{1,0:T(8,128)(2,1)S(1)} %constant_dynamic-update-slice_fusion.refs_0_), channel_id=1, source_target_pairs={{0,24},{4,28},{8,16},{12,20},{16,8},{20,12},{24,0},{28,4},{1,25},{... | collective-permute-start | bytes 638984 | tf_op jit(solution)/shard_map/ppermute | solution.py:45
  17.7 7.9 %collective-permute-start.4 = (bf16[416,256]{1,0:T(8,128)(2,1)S(1)}, bf16[416,256]{1,0:T(8,128)(2,1)S(1)}, u32[]{:S(2)}, u32[]{:S(2)}) collective-permute-start(bf16[416,256]{1,0:T(8,128)(2,1)S(1)} %constant_dynamic-update-slice_fusion.refs_0_), channel_id=1, source_target_pairs={{0,16},{4,20},{8,24},{12,28},{16,0},{20,4},{24,8},{28,12},{1,17},{... | collective-permute-start | bytes 638984 | tf_op jit(solution)/shard_map/ppermute | solution.py:45
  18.2 7.5 %collective-permute-start.3 = (bf16[416,256]{1,0:T(8,128)(2,1)S(1)}, bf16[416,256]{1,0:T(8,128)(2,1)S(1)}, u32[]{:S(2)}, u32[]{:S(2)}) collective-permute-start(bf16[416,256]{1,0:T(8,128)(2,1)S(1)} %constant_dynamic-update-slice_fusion.refs_0_), channel_id=1, source_target_pairs={{0,8},{4,12},{8,0},{12,4},{16,24},{20,28},{24,16},{28,20},{1,9},{5... | collective-permute-start | bytes 638984 | tf_op jit(solution)/shard_map/ppermute | solution.py:45
  18.8 5.9 %collective-permute-start.13 = (bf16[72,512]{1,0:T(8,128)(2,1)S(1)}, bf16[72,512]{1,0:T(8,128)(2,1)S(1)}, u32[]{:S(2)}, u32[]{:S(2)}) collective-permute-start(bf16[72,512]{1,0:T(8,128)(2,1)S(1)} %pad_maximum_fusion.4), channel_id=1, source_target_pairs={{0,2},{1,3},{2,0},{3,1},{4,6},{5,7},{6,4},{7,5},{8,10},{9,11},{10,... | collective-permute-start | bytes 221192 | tf_op jit(solution)/shard_map/ppermute | solution.py:45
  19.5 5.2 %collective-permute-start.12 = (bf16[72,512]{1,0:T(8,128)(2,1)S(1)}, bf16[72,512]{1,0:T(8,128)(2,1)S(1)}, u32[]{:S(2)}, u32[]{:S(2)}) collective-permute-start(bf16[72,512]{1,0:T(8,128)(2,1)S(1)} %pad_maximum_fusion.4), channel_id=1, source_target_pairs={{0,1},{1,0},{2,3},{3,2},{4,5},{5,4},{6,7},{7,6},{8,9},{9,8},{10,11... | collective-permute-start | bytes 221192 | tf_op jit(solution)/shard_map/ppermute | solution.py:45
  20.7 2.2 %copy-start = (bf16[2,8,128,1024]{3,2,1,0:T(8,128)(2,1)S(1)}, bf16[2,8,128,1024]{3,2,1,0:T(8,128)(2,1)}, u32[]{:S(2)}) copy-start(bf16[2,8,128,1024]{3,2,1,0:T(8,128)(2,1)} %four.3) | copy-start | bytes 12582916
  22.9 1.6 %copy-start.2 = (bf16[2,4,64,2048]{3,2,1,0:T(8,128)(2,1)S(1)}, bf16[2,4,64,2048]{3,2,1,0:T(8,128)(2,1)}, u32[]{:S(2)}) copy-start(bf16[2,4,64,2048]{3,2,1,0:T(8,128)(2,1)} %five.3) | copy-start | bytes 6291460
  24.5 4.0 %copy-start.1 = (bf16[2,8,128,1024]{3,2,1,0:T(8,128)(2,1)S(1)}, bf16[2,8,128,1024]{3,2,1,0:T(8,128)(2,1)}, u32[]{:S(2)}) copy-start(bf16[2,8,128,1024]{3,2,1,0:T(8,128)(2,1)} %four.3) | copy-start | bytes 12582916
  25.7 2.8 %collective-permute-start.6 = (bf16[416,256]{1,0:T(8,128)(2,1)S(1)}, bf16[416,256]{1,0:T(8,128)(2,1)S(1)}, u32[]{:S(2)}, u32[]{:S(2)}) collective-permute-start(bf16[416,256]{1,0:T(8,128)(2,1)S(1)} %constant_dynamic-update-slice_fusion.refs_0_), channel_id=1, source_target_pairs={{0,4},{4,0},{8,12},{12,8},{16,20},{20,16},{24,28},{28,24},{1,5},{5... | collective-permute-start | bytes 638984 | tf_op jit(solution)/shard_map/ppermute | solution.py:45
  25.7 2.8 %collective-permute-start.7 = (bf16[416,256]{1,0:T(8,128)(2,1)S(1)}, bf16[416,256]{1,0:T(8,128)(2,1)S(1)}, u32[]{:S(2)}, u32[]{:S(2)}) collective-permute-start(bf16[416,256]{1,0:T(8,128)(2,1)S(1)} %collective-permute-done.3.refs_2_), channel_id=1, source_target_pairs={{0,4},{4,0},{8,12},{12,8},{16,20},{20,16},{24,28},{28,24},{1,5},{5... | collective-permute-start | bytes 638984 | tf_op jit(solution)/shard_map/ppermute | solution.py:45
  26.2 2.2 %collective-permute-start.8 = (bf16[416,256]{1,0:T(8,128)(2,1)S(1)}, bf16[416,256]{1,0:T(8,128)(2,1)S(1)}, u32[]{:S(2)}, u32[]{:S(2)}) collective-permute-start(bf16[416,256]{1,0:T(8,128)(2,1)S(1)} %collective-permute-done.4.refs_4_), channel_id=1, source_target_pairs={{0,4},{4,0},{8,12},{12,8},{16,20},{20,16},{24,28},{28,24},{1,5},{5... | collective-permute-start | bytes 638984 | tf_op jit(solution)/shard_map/ppermute | solution.py:45
  26.2 2.2 %collective-permute-start.9 = (bf16[416,256]{1,0:T(8,128)(2,1)S(1)}, bf16[416,256]{1,0:T(8,128)(2,1)S(1)}, u32[]{:S(2)}, u32[]{:S(2)}) collective-permute-start(bf16[416,256]{1,0:T(8,128)(2,1)S(1)} %collective-permute-done.5.refs_6_), channel_id=1, source_target_pairs={{0,4},{4,0},{8,12},{12,8},{16,20},{20,16},{24,28},{28,24},{1,5},{5... | collective-permute-start | bytes 638984 | tf_op jit(solution)/shard_map/ppermute | solution.py:45
  26.8 10.2 %collective-permute-start.18 = (bf16[288,512]{1,0:T(8,128)(2,1)S(1)}, bf16[288,512]{1,0:T(8,128)(2,1)S(1)}, u32[]{:S(2)}, u32[]{:S(2)}) collective-permute-start(bf16[288,512]{1,0:T(8,128)(2,1)S(1)} %pad_maximum_fusion.2.refs_0_), channel_id=1, source_target_pairs={{0,24},{4,28},{8,16},{12,20},{16,8},{20,12},{24,0},{28,4},{1,25},{... | collective-permute-start | bytes 884744 | tf_op jit(solution)/shard_map/ppermute | solution.py:45
  30.6 6.4 %collective-permute-start.10 = (bf16[2,208,256]{2,1,0:T(8,128)(2,1)S(1)}, bf16[2,208,256]{2,1,0:T(8,128)(2,1)S(1)}, u32[]{:S(2)}, u32[]{:S(2)}) collective-permute-start(bf16[2,208,256]{2,1,0:T(8,128)(2,1)S(1)} %get-tuple-element.103), channel_id=1, source_target_pairs={{0,4},{4,0},{8,12},{12,8},{16,20},{20,16},{24,28},{28,24},{1,5},{5... | collective-permute-start | bytes 638984 | tf_op jit(solution)/shard_map/ppermute | solution.py:45
  30.6 6.4 %collective-permute-start.11 = (bf16[2,208,256]{2,1,0:T(8,128)(2,1)S(1)}, bf16[2,208,256]{2,1,0:T(8,128)(2,1)S(1)}, u32[]{:S(2)}, u32[]{:S(2)}) collective-permute-start(bf16[2,208,256]{2,1,0:T(8,128)(2,1)S(1)} %get-tuple-element.104), channel_id=1, source_target_pairs={{4,8},{12,16},{20,24},{8,4},{16,12},{24,20},{5,9},{13,17},{21,25},... | collective-permute-start | bytes 638984 | tf_op jit(solution)/shard_map/ppermute | solution.py:106
  31.3 12.9 %collective-permute-start.16 = (bf16[288,512]{1,0:T(8,128)(2,1)S(1)}, bf16[288,512]{1,0:T(8,128)(2,1)S(1)}, u32[]{:S(2)}, u32[]{:S(2)}) collective-permute-start(bf16[288,512]{1,0:T(8,128)(2,1)S(1)} %pad_maximum_fusion.2.refs_0_), channel_id=1, source_target_pairs={{0,16},{4,20},{8,24},{12,28},{16,0},{20,4},{24,8},{28,12},{1,17},{... | collective-permute-start | bytes 884744 | tf_op jit(solution)/shard_map/ppermute | solution.py:45
  35.4 12.1 %collective-permute-start.15 = (bf16[288,512]{1,0:T(8,128)(2,1)S(1)}, bf16[288,512]{1,0:T(8,128)(2,1)S(1)}, u32[]{:S(2)}, u32[]{:S(2)}) collective-permute-start(bf16[288,512]{1,0:T(8,128)(2,1)S(1)} %pad_maximum_fusion.2.refs_0_), channel_id=1, source_target_pairs={{0,8},{4,12},{8,0},{12,4},{16,24},{20,28},{24,16},{28,20},{1,9},{5... | collective-permute-start | bytes 884744 | tf_op jit(solution)/shard_map/ppermute | solution.py:45
  37.0 10.5 %collective-permute-start.17 = (bf16[288,512]{1,0:T(8,128)(2,1)S(1)}, bf16[288,512]{1,0:T(8,128)(2,1)S(1)}, u32[]{:S(2)}, u32[]{:S(2)}) collective-permute-start(bf16[288,512]{1,0:T(8,128)(2,1)S(1)} %pad_maximum_fusion.2.refs_0_), channel_id=1, source_target_pairs={{0,4},{4,0},{8,12},{12,8},{16,20},{20,16},{24,28},{28,24},{1,5},{5... | collective-permute-start | bytes 884744 | tf_op jit(solution)/shard_map/ppermute | solution.py:45
  41.5 6.0 %collective-permute-start.19 = (bf16[288,512]{1,0:T(8,128)(2,1)S(1)}, bf16[288,512]{1,0:T(8,128)(2,1)S(1)}, u32[]{:S(2)}, u32[]{:S(2)}) collective-permute-start(bf16[288,512]{1,0:T(8,128)(2,1)S(1)} %collective-permute-done.18.refs_6_), channel_id=1, source_target_pairs={{0,4},{4,0},{8,12},{12,8},{16,20},{20,16},{24,28},{28,24},{1,5},{5... | collective-permute-start | bytes 884744 | tf_op jit(solution)/shard_map/ppermute | solution.py:45
  47.5 1.6 %collective-permute-start.20 = (bf16[288,512]{1,0:T(8,128)(2,1)S(1)}, bf16[288,512]{1,0:T(8,128)(2,1)S(1)}, u32[]{:S(2)}, u32[]{:S(2)}) collective-permute-start(bf16[288,512]{1,0:T(8,128)(2,1)S(1)} %collective-permute-done.15.refs_2_), channel_id=1, source_target_pairs={{0,4},{4,0},{8,12},{12,8},{16,20},{20,16},{24,28},{28,24},{1,5},{5... | collective-permute-start | bytes 884744 | tf_op jit(solution)/shard_map/ppermute | solution.py:45
  47.5 2.0 %collective-permute-start.21 = (bf16[288,512]{1,0:T(8,128)(2,1)S(1)}, bf16[288,512]{1,0:T(8,128)(2,1)S(1)}, u32[]{:S(2)}, u32[]{:S(2)}) collective-permute-start(bf16[288,512]{1,0:T(8,128)(2,1)S(1)} %collective-permute-done.16.refs_4_), channel_id=1, source_target_pairs={{0,4},{4,0},{8,12},{12,8},{16,20},{20,16},{24,28},{28,24},{1,5},{5... | collective-permute-start | bytes 884744 | tf_op jit(solution)/shard_map/ppermute | solution.py:45
  53.9 1.3 %collective-permute-start.22 = (f32[2,24,256]{2,1,0:T(8,128)S(1)}, f32[2,24,256]{2,1,0:T(8,128)S(1)}, u32[]{:S(2)}, u32[]{:S(2)}) collective-permute-start(f32[2,24,256]{2,1,0:T(8,128)S(1)} %get-tuple-element.119), channel_id=1, source_target_pairs={{0,4},{4,0},{8,12},{12,8},{16,20},{20,16},{24,28},{28,24},{1,5},{5... | collective-permute-start | bytes 147464 | tf_op jit(solution)/shard_map/ppermute | solution.py:45
  54.1 1.1 %collective-permute-start.23 = (f32[2,24,256]{2,1,0:T(8,128)S(1)}, f32[2,24,256]{2,1,0:T(8,128)S(1)}, u32[]{:S(2)}, u32[]{:S(2)}) collective-permute-start(f32[2,24,256]{2,1,0:T(8,128)S(1)} %get-tuple-element.120), channel_id=1, source_target_pairs={{4,8},{12,16},{20,24},{8,4},{16,12},{24,20},{5,9},{13,17},{21,25},... | collective-permute-start | bytes 147464 | tf_op jit(solution)/shard_map/ppermute | solution.py:106
  61.6 7.2 %collective-permute-start.26 = (bf16[4,288,512]{2,1,0:T(8,128)(2,1)S(1)}, bf16[4,288,512]{2,1,0:T(8,128)(2,1)S(1)}, u32[]{:S(2)}, u32[]{:S(2)}) collective-permute-start(bf16[4,288,512]{2,1,0:T(8,128)(2,1)S(1)} %get-tuple-element.128), channel_id=1, source_target_pairs={{0,4},{4,0},{8,12},{12,8},{16,20},{20,16},{24,28},{28,24},{1,5},{5... | collective-permute-start | bytes 3538952 | tf_op jit(solution)/shard_map/ppermute | solution.py:45
  66.3 6.4 %collective-permute-start.24 = (bf16[2,192,256]{2,1,0:T(8,128)(2,1)S(1)}, bf16[2,192,256]{2,1,0:T(8,128)(2,1)S(1)}, u32[]{:S(2)}, u32[]{:S(2)}) collective-permute-start(bf16[2,192,256]{2,1,0:T(8,128)(2,1)S(1)} %get-tuple-element.125), channel_id=1, source_target_pairs={{0,4},{4,0},{8,12},{12,8},{16,20},{20,16},{24,28},{28,24},{1,5},{5... | collective-permute-start | bytes 589832 | tf_op jit(solution)/shard_map/ppermute | solution.py:45
  66.4 6.3 %collective-permute-start.25 = (bf16[2,192,256]{2,1,0:T(8,128)(2,1)S(1)}, bf16[2,192,256]{2,1,0:T(8,128)(2,1)S(1)}, u32[]{:S(2)}, u32[]{:S(2)}) collective-permute-start(bf16[2,192,256]{2,1,0:T(8,128)(2,1)S(1)} %get-tuple-element.126), channel_id=1, source_target_pairs={{4,8},{12,16},{20,24},{8,4},{16,12},{24,20},{5,9},{13,17},{21,25},... | collective-permute-start | bytes 589832 | tf_op jit(solution)/shard_map/ppermute | solution.py:106
  69.2 13.4 %collective-permute-start.30 = (bf16[288,512]{1,0:T(8,128)(2,1)S(1)}, bf16[288,512]{1,0:T(8,128)(2,1)S(1)}, u32[]{:S(2)}, u32[]{:S(2)}) collective-permute-start(bf16[288,512]{1,0:T(8,128)(2,1)S(1)} %get-tuple-element.162), channel_id=1, source_target_pairs={{0,24},{4,28},{8,16},{12,20},{16,8},{20,12},{24,0},{28,4},{1,25},{... | collective-permute-start | bytes 884744 | tf_op jit(solution)/shard_map/ppermute | solution.py:45
  71.1 17.2 %collective-permute-start.28 = (bf16[288,512]{1,0:T(8,128)(2,1)S(1)}, bf16[288,512]{1,0:T(8,128)(2,1)S(1)}, u32[]{:S(2)}, u32[]{:S(2)}) collective-permute-start(bf16[288,512]{1,0:T(8,128)(2,1)S(1)} %get-tuple-element.163), channel_id=1, source_target_pairs={{0,8},{4,12},{8,0},{12,4},{16,24},{20,28},{24,16},{28,20},{1,9},{5... | collective-permute-start | bytes 884744 | tf_op jit(solution)/shard_map/ppermute | solution.py:45
  72.7 15.6 %collective-permute-start.29 = (bf16[288,512]{1,0:T(8,128)(2,1)S(1)}, bf16[288,512]{1,0:T(8,128)(2,1)S(1)}, u32[]{:S(2)}, u32[]{:S(2)}) collective-permute-start(bf16[288,512]{1,0:T(8,128)(2,1)S(1)} %get-tuple-element.164), channel_id=1, source_target_pairs={{0,16},{4,20},{8,24},{12,28},{16,0},{20,4},{24,8},{28,12},{1,17},{... | collective-permute-start | bytes 884744 | tf_op jit(solution)/shard_map/ppermute | solution.py:45
  72.7 3.6 %copy-start.3 = (bf16[2,4,64,2048]{3,2,1,0:T(8,128)(2,1)S(1)}, bf16[2,4,64,2048]{3,2,1,0:T(8,128)(2,1)}, u32[]{:S(2)}) copy-start(bf16[2,4,64,2048]{3,2,1,0:T(8,128)(2,1)} %five.3) | copy-start | bytes 6291460
  79.1 9.3 %collective-permute-start.27 = (bf16[4,416,256]{2,1,0:T(8,128)(2,1)S(1)}, bf16[4,416,256]{2,1,0:T(8,128)(2,1)S(1)}, u32[]{:S(2)}, u32[]{:S(2)}) collective-permute-start(bf16[4,416,256]{2,1,0:T(8,128)(2,1)S(1)} %get-tuple-element.138), channel_id=1, source_target_pairs={{0,4},{4,0},{8,12},{12,8},{16,20},{20,16},{24,28},{28,24},{1,5},{5... | collective-permute-start | bytes 2555912 | tf_op jit(solution)/shard_map/ppermute | solution.py:45
  88.6 8.2 %collective-permute-start.34 = (bf16[416,256]{1,0:T(8,128)(2,1)S(1)}, bf16[416,256]{1,0:T(8,128)(2,1)S(1)}, u32[]{:S(2)}, u32[]{:S(2)}) collective-permute-start(bf16[416,256]{1,0:T(8,128)(2,1)S(1)} %get-tuple-element.141), channel_id=1, source_target_pairs={{0,8},{4,12},{8,0},{12,4},{16,24},{20,28},{24,16},{28,20},{1,9},{5... | collective-permute-start | bytes 638984 | tf_op jit(solution)/shard_map/ppermute | solution.py:45
  89.7 10.8 %collective-permute-start.35 = (bf16[416,256]{1,0:T(8,128)(2,1)S(1)}, bf16[416,256]{1,0:T(8,128)(2,1)S(1)}, u32[]{:S(2)}, u32[]{:S(2)}) collective-permute-start(bf16[416,256]{1,0:T(8,128)(2,1)S(1)} %get-tuple-element.142), channel_id=1, source_target_pairs={{0,16},{4,20},{8,24},{12,28},{16,0},{20,4},{24,8},{28,12},{1,17},{... | collective-permute-start | bytes 638984 | tf_op jit(solution)/shard_map/ppermute | solution.py:45
  91.1 9.4 %collective-permute-start.36 = (bf16[416,256]{1,0:T(8,128)(2,1)S(1)}, bf16[416,256]{1,0:T(8,128)(2,1)S(1)}, u32[]{:S(2)}, u32[]{:S(2)}) collective-permute-start(bf16[416,256]{1,0:T(8,128)(2,1)S(1)} %get-tuple-element.143), channel_id=1, source_target_pairs={{0,24},{4,28},{8,16},{12,20},{16,8},{20,12},{24,0},{28,4},{1,25},{... | collective-permute-start | bytes 638984 | tf_op jit(solution)/shard_map/ppermute | solution.py:45
  92.2 8.4 %collective-permute-start.33 = (bf16[72,512]{1,0:T(8,128)(2,1)S(1)}, bf16[72,512]{1,0:T(8,128)(2,1)S(1)}, u32[]{:S(2)}, u32[]{:S(2)}) collective-permute-start(bf16[72,512]{1,0:T(8,128)(2,1)S(1)} %get-tuple-element.169), channel_id=1, source_target_pairs={{0,3},{1,2},{2,1},{3,0},{4,7},{5,6},{6,5},{7,4},{8,11},{9,10},{10,... | collective-permute-start | bytes 221192 | tf_op jit(solution)/shard_map/ppermute | solution.py:45
  94.2 6.8 %collective-permute-start.32 = (bf16[72,512]{1,0:T(8,128)(2,1)S(1)}, bf16[72,512]{1,0:T(8,128)(2,1)S(1)}, u32[]{:S(2)}, u32[]{:S(2)}) collective-permute-start(bf16[72,512]{1,0:T(8,128)(2,1)S(1)} %get-tuple-element.170), channel_id=1, source_target_pairs={{0,2},{1,3},{2,0},{3,1},{4,6},{5,7},{6,4},{7,5},{8,10},{9,11},{10,... | collective-permute-start | bytes 221192 | tf_op jit(solution)/shard_map/ppermute | solution.py:45
  96.9 4.9 %collective-permute-start.31 = (bf16[72,512]{1,0:T(8,128)(2,1)S(1)}, bf16[72,512]{1,0:T(8,128)(2,1)S(1)}, u32[]{:S(2)}, u32[]{:S(2)}) collective-permute-start(bf16[72,512]{1,0:T(8,128)(2,1)S(1)} %get-tuple-element.171), channel_id=1, source_target_pairs={{0,1},{1,0},{2,3},{3,2},{4,5},{5,4},{6,7},{7,6},{8,9},{9,8},{10,11... | collective-permute-start | bytes 221192 | tf_op jit(solution)/shard_map/ppermute | solution.py:45
  100.6 5.9 %copy-start.4 = (f32[2,72,256]{2,1,0:T(8,128)S(1)}, f32[2,72,256]{2,1,0:T(8,128)}, u32[]{:S(2)}) copy-start(f32[2,72,256]{2,1,0:T(8,128)} %refs_3_.3) | copy-start | bytes 442372
  100.6 5.9 %copy-start.6 = (f32[2,72,256]{2,1,0:T(8,128)S(1)}, f32[2,72,256]{2,1,0:T(8,128)}, u32[]{:S(2)}) copy-start(f32[2,72,256]{2,1,0:T(8,128)} %refs_4_.3) | copy-start | bytes 442372
  100.6 5.9 %copy-start.7 = (f32[2,72,256]{2,1,0:T(8,128)S(1)}, f32[2,72,256]{2,1,0:T(8,128)}, u32[]{:S(2)}) copy-start(f32[2,72,256]{2,1,0:T(8,128)} %refs_5_.3) | copy-start | bytes 442372
  101.8 7.4 %copy-start.5 = (f32[64,256]{1,0:T(8,128)S(1)}, f32[64,256]{1,0:T(8,128)}, u32[]{:S(2)}) copy-start(f32[64,256]{1,0:T(8,128)} %refs_6_.3) | copy-start | bytes 196612
  101.8 7.4 %copy-start.8 = (f32[32,256]{1,0:T(8,128)S(1)}, f32[32,256]{1,0:T(8,128)}, u32[]{:S(2)}) copy-start(f32[32,256]{1,0:T(8,128)} %refs_3_.2) | copy-start | bytes 98308
  101.9 7.4 %copy-start.11 = (f32[64,256]{1,0:T(8,128)S(1)}, f32[64,256]{1,0:T(8,128)}, u32[]{:S(2)}) copy-start(f32[64,256]{1,0:T(8,128)} %refs_7_.3) | copy-start | bytes 196612
  101.9 7.4 %copy-start.12 = (f32[64,256]{1,0:T(8,128)S(1)}, f32[64,256]{1,0:T(8,128)}, u32[]{:S(2)}) copy-start(f32[64,256]{1,0:T(8,128)} %refs_8_.1) | copy-start | bytes 196612
  101.9 7.4 %copy-start.15 = (f32[72,12]{0,1:T(8,128)S(1)}, f32[72,12]{0,1:T(8,128)}, u32[]{:S(2)}) copy-start(f32[72,12]{0,1:T(8,128)} %param.31) | copy-start | bytes 10372
  101.9 7.4 %copy-start.16 = (f32[32,256]{1,0:T(8,128)S(1)}, f32[32,256]{1,0:T(8,128)}, u32[]{:S(2)}) copy-start(f32[32,256]{1,0:T(8,128)} %refs_4_.2) | copy-start | bytes 98308
  101.9 7.4 %copy-start.17 = (f32[32,256]{1,0:T(8,128)S(1)}, f32[32,256]{1,0:T(8,128)}, u32[]{:S(2)}) copy-start(f32[32,256]{1,0:T(8,128)} %refs_5_.2) | copy-start | bytes 98308
  101.9 7.4 %copy-start.20 = (f32[72,12]{0,1:T(8,128)S(1)}, f32[72,12]{0,1:T(8,128)}, u32[]{:S(2)}) copy-start(f32[72,12]{0,1:T(8,128)} %param.35) | copy-start | bytes 10372
  101.9 7.3 %copy-start.21 = (f32[72,12]{0,1:T(8,128)S(1)}, f32[72,12]{0,1:T(8,128)}, u32[]{:S(2)}) copy-start(f32[72,12]{0,1:T(8,128)} %param.39) | copy-start | bytes 10372
  102.0 6.1 %collective-permute-start.39 = (bf16[104,256]{1,0:T(8,128)(2,1)S(1)}, bf16[104,256]{1,0:T(8,128)(2,1)S(1)}, u32[]{:S(2)}, u32[]{:S(2)}) collective-permute-start(bf16[104,256]{1,0:T(8,128)(2,1)S(1)} %get-tuple-element.172), channel_id=1, source_target_pairs={{0,3},{1,2},{2,1},{3,0},{4,7},{5,6},{6,5},{7,4},{8,11},{9,10},{10,... | collective-permute-start | bytes 159752 | tf_op jit(solution)/shard_map/ppermute | solution.py:45
  104.0 5.2 %collective-permute-start.38 = (bf16[104,256]{1,0:T(8,128)(2,1)S(1)}, bf16[104,256]{1,0:T(8,128)(2,1)S(1)}, u32[]{:S(2)}, u32[]{:S(2)}) collective-permute-start(bf16[104,256]{1,0:T(8,128)(2,1)S(1)} %get-tuple-element.173), channel_id=1, source_target_pairs={{0,2},{1,3},{2,0},{3,1},{4,6},{5,7},{6,4},{7,5},{8,10},{9,11},{10,... | collective-permute-start | bytes 159752 | tf_op jit(solution)/shard_map/ppermute | solution.py:45
  104.0 5.2 %collective-permute-start.37 = (bf16[104,256]{1,0:T(8,128)(2,1)S(1)}, bf16[104,256]{1,0:T(8,128)(2,1)S(1)}, u32[]{:S(2)}, u32[]{:S(2)}) collective-permute-start(bf16[104,256]{1,0:T(8,128)(2,1)S(1)} %get-tuple-element.174), channel_id=1, source_target_pairs={{0,1},{1,0},{2,3},{3,2},{4,5},{5,4},{6,7},{7,6},{8,9},{9,8},{10,11... | collective-permute-start | bytes 159752 | tf_op jit(solution)/shard_map/ppermute | solution.py:45
